TPU v7x, 32 devices: a whole 2x2x4 slice. The times are simulated.
32 devices in a mesh: dp: 8 (over y, x, core), blk: 4 (over z).
Axes of the slice: x: 2, y: 2, z: 4, core: 2. Of those that a mesh axis runs over, the one named last changes fastest.
Arguments:
- replay: float32 [42, 116736], P(None, ('dp', 'blk')), may hold values from -27 to 27, as said below
- model_rows: float32 [42, 38912], P(None, ('dp', 'blk')), may hold values from -27 to 27, as said below
- requests: int32 [256, 8], P(('dp', 'blk')), may hold values from -1 to 3647, as said below
- member_of: int32 [256, 8], P(('dp', 'blk')), may hold values from 0 to 6
- model_live: int32 [38912], P(('dp', 'blk')), may hold values from 0 to 1
- noise: float32 [2, 40960, 6], P(None, ('dp', 'blk')), may hold values from -4 to 4
- sac_hidden: float32 [3, 256, 256], P(None, 'blk'), may hold values from -0.375 to 0.375
- sac_hidden_mom: float32 [3, 256, 256], P(None, 'blk'), may hold values from -0.21875 to 0.21875
- dyn_hidden: float32 [7, 200, 200], P(None, 'blk'), may hold values from -0.4375 to 0.4375
- dyn_hidden_mom: float32 [7, 200, 200], P(None, 'blk'), may hold values from -0.046875 to 0.046875
- crit_in: float32 [2, 23, 256], replicated, may hold values from -1.25 to 1.25
- crit_in_m: float32 [2, 23, 256], replicated, may hold values from -0.0234375 to 0.0234375
- crit_in_v: float32 [2, 23, 256], replicated, may hold values from 2.4414064e-07 to 9.765625e-07
- act_in: float32 [17, 256], replicated, may hold values from -1.5 to 1.5
- act_in_m: float32 [17, 256], replicated, may hold values from -0.0234375 to 0.0234375
- act_in_v: float32 [17, 256], replicated, may hold values from 2.4414064e-07 to 9.765625e-07
- dyn_in: float32 [7, 23, 200], replicated, may hold values from -1.25 to 1.25
- dyn_in_m: float32 [7, 23, 200], replicated, may hold values from -0.00390625 to 0.00390625
- dyn_in_v: float32 [7, 23, 200], replicated, may hold values from 9.765625e-09 to 3.90625e-08
- crit_out: float32 [2, 256], replicated, may hold values from -0.375 to 0.375
- crit_out_m: float32 [2, 256], replicated, may hold values from -0.0234375 to 0.0234375
- crit_out_v: float32 [2, 256], replicated, may hold values from 2.4414064e-07 to 9.765625e-07
- act_out: float32 [256, 12], replicated, may hold values from -0.375 to 0.375
- act_out_m: float32 [256, 12], replicated, may hold values from -0.0234375 to 0.0234375
- act_out_v: float32 [256, 12], replicated, may hold values from 2.4414064e-07 to 9.765625e-07
- dyn_out: float32 [7, 200, 36], replicated, may hold values from -0.4375 to 0.4375
- dyn_out_m: float32 [7, 200, 36], replicated, may hold values from -0.00390625 to 0.00390625
- dyn_out_v: float32 [7, 200, 36], replicated, may hold values from 9.765625e-09 to 3.90625e-08
- biases: float32 [4639], replicated, may hold values from -1.5 to 1.5
- biases_m: float32 [4639], replicated, may hold values from -0.0234375 to 0.0234375
- biases_v: float32 [4639], replicated, may hold values from 2.4414064e-07 to 9.765625e-07
- targ_in: float32 [2, 23, 256], replicated, may hold values from -1.25 to 1.25
- targ_hidden: float32 [2, 256, 256], replicated, may hold values from -0.375 to 0.375
- targ_out: float32 [2, 256], replicated, may hold values from -0.375 to 0.375
- targ_bias: float32 [2, 513], replicated, may hold values from -1.5 to 1.5
Outputs:
- sac_hidden_new: float32 [3, 256, 256], P(None, 'blk')
- sac_hidden_mom_new: float32 [3, 256, 256], P(None, 'blk')
- dyn_hidden_new: float32 [7, 200, 200], P(None, 'blk')
- dyn_hidden_mom_new: float32 [7, 200, 200], P(None, 'blk')
- crit_in_new: float32 [2, 23, 256], replicated
- crit_in_m_new: float32 [2, 23, 256], replicated
- crit_in_v_new: float32 [2, 23, 256], replicated
- act_in_new: float32 [17, 256], replicated
- act_in_m_new: float32 [17, 256], replicated
- act_in_v_new: float32 [17, 256], replicated
- dyn_in_new: float32 [7, 23, 200], replicated
- dyn_in_m_new: float32 [7, 23, 200], replicated
- dyn_in_v_new: float32 [7, 23, 200], replicated
- crit_out_new: float32 [2, 256], replicated
- crit_out_m_new: float32 [2, 256], replicated
- crit_out_v_new: float32 [2, 256], replicated
- act_out_new: float32 [256, 12], replicated
- act_out_m_new: float32 [256, 12], replicated
- act_out_v_new: float32 [256, 12], replicated
- dyn_out_new: float32 [7, 200, 36], replicated
- dyn_out_m_new: float32 [7, 200, 36], replicated
- dyn_out_v_new: float32 [7, 200, 36], replicated
- biases_new: float32 [4639], replicated
- biases_m_new: float32 [4639], replicated
- biases_v_new: float32 [4639], replicated
- loss_sum: float32 [], replicated
- loss_count: float32 [], replicated
Inputs may be any that keep to these rules, and one draw needn't show every extreme that they name: `replay`: transition columns: observation entries, actions in -1..1, a reward, next observation entries, and a done flag that is 0 or 1. `model_rows`: same layout as replay. `requests`: each row of 8 slots names rows of its owner's 3648 replay rows; filled slots come first, at least one in every row, and -1 marks an empty slot. In every draw some owner receives full rows from every device that asks it.
All inputs are finite; a program needn't handle non-finite values.
Results may differ from a plain program's by a relative error of at most 0.00035.
The roundings to bfloat16 on the way count: a program that leaves them out, or rounds other values in their place, can miss the bound.
Values may be sent and summed in bfloat16 or wider, within the bound.
A program may use at most 192 MiB of HBM per device.

v0:
```python
import jax
import jax.numpy as jnp
from jax import lax
from jax.sharding import PartitionSpec as P

OBS = 17
ACT = 6
HDYN = 200
HSAC = 256
MEMBERS = 7
NS_ITERS = 5
STEP = 10


PRECISE = lax.Precision.HIGHEST
DISCOUNT = 0.99
TARGET_ENTROPY = -6.0
BOUND_WEIGHT = 0.01
MOMENTUM = 0.95
MUON_RATE = 0.4
MUON_DECAY = 0.01
ADAM_RATE = 0.1
ADAM_DECAY = 0.01
BETA_FIRST = 0.9
BETA_SECOND = 0.999
COEF_LINEAR = 3.4445
COEF_CUBIC = -4.775
COEF_QUINTIC = 2.0315


def cast_down(value):
    return lax.optimization_barrier(value.astype(jnp.bfloat16)).astype(jnp.float32)


def identity_pass(value):
    return value


def value_keep(value):
    return (cast_down(value), None)


def value_pass(kept, grad):
    return (grad,)


def grad_keep(value):
    return (value, None)


def grad_low(kept, grad):
    return (cast_down(grad),)


def rounders():
    value_round = jax.custom_vjp(cast_down)
    value_round.defvjp(value_keep, value_pass)
    grad_round = jax.custom_vjp(identity_pass)
    grad_round.defvjp(grad_keep, grad_low)
    return (value_round, grad_round)


def smooth_gate(value):
    return value * jax.nn.sigmoid(value)


def dense_layer(inputs, weights, offset):
    value_round, grad_round = rounders()
    return grad_round(
        jnp.matmul(value_round(inputs), value_round(weights), precision=PRECISE) + offset
    )


def unpack_biases(vector):
    widths = [
        2 * HSAC,
        2 * HSAC,
        2,
        HSAC,
        HSAC,
        2 * ACT,
        MEMBERS * HDYN,
        MEMBERS * HDYN,
        MEMBERS * 2 * (OBS + 1),
        OBS + 1,
        OBS + 1,
        1,
    ]
    pieces = []
    start = 0
    for width in widths:
        pieces.append(vector[start : start + width])
        start = start + width
    return (
        pieces[0].reshape(2, HSAC),
        pieces[1].reshape(2, HSAC),
        pieces[2],
        pieces[3],
        pieces[4],
        pieces[5],
        pieces[6].reshape(MEMBERS, HDYN),
        pieces[7].reshape(MEMBERS, HDYN),
        pieces[8].reshape(MEMBERS, 2 * (OBS + 1)),
        pieces[9],
        pieces[10],
        pieces[11][0],
    )


def bound_penalty(vector):
    parts = unpack_biases(vector)
    return BOUND_WEIGHT * (jnp.sum(parts[9]) - jnp.sum(parts[10]))


def critic_pair(joined, w_in, w_hidden, w_out, first_bias, second_bias, last_bias):
    layer = smooth_gate(dense_layer(joined, w_in, first_bias[:, None, :]))
    layer = smooth_gate(dense_layer(layer, w_hidden, second_bias[:, None, :]))
    return dense_layer(layer, w_out[:, :, None], last_bias[:, None, None])[:, :, 0]


def policy(states, w_in, w_hidden, w_out, first_bias, second_bias, last_bias, noise_rows):
    layer = smooth_gate(dense_layer(states, w_in, first_bias))
    layer = smooth_gate(dense_layer(layer, w_hidden, second_bias))
    output = dense_layer(layer, w_out, last_bias)
    log_scale = -5.0 + 3.5 * (jnp.tanh(output[:, ACT:]) + 1.0)
    latent = output[:, :ACT] + jnp.exp(log_scale) * noise_rows
    log_prob = jnp.sum(
        -0.5 * noise_rows * noise_rows
        - log_scale
        - 0.9189385
        - 2.0 * (0.6931472 - latent - jax.nn.softplus(-2.0 * latent)),
        axis=1,
    )
    return (jnp.tanh(latent), log_prob)


def dynamics_model(inputs, w_in, w_hidden, w_out, first_bias, second_bias, last_bias, upper, lower):
    layer = smooth_gate(dense_layer(inputs, w_in, first_bias[:, None, :]))
    layer = smooth_gate(dense_layer(layer, w_hidden, second_bias[:, None, :]))
    output = dense_layer(layer, w_out, last_bias[:, None, :])
    width = OBS + 1
    log_var = upper - jax.nn.softplus(upper - output[:, :, width:])
    log_var = lower + jax.nn.softplus(log_var - lower)
    return (output[:, :, :width], log_var)


def prepare(params, targets, batch, noise):
    sac_hidden, dyn_hidden, crit_in, act_in, dyn_in, crit_out, act_out, dyn_out, biases = params
    targ_in, targ_hidden, targ_out, targ_bias = targets
    parts = unpack_biases(biases)
    states = batch[:, :OBS]
    following = batch[:, OBS + ACT + 1 : 2 * OBS + ACT + 1]
    alpha_fixed = jnp.exp(parts[11])
    next_action, next_prob = policy(
        following, act_in, sac_hidden[2], act_out, parts[3], parts[4], parts[5], noise[1]
    )
    target_values = critic_pair(
        jnp.concatenate([following, next_action], 1),
        targ_in,
        targ_hidden,
        targ_out,
        targ_bias[:, :HSAC],
        targ_bias[:, HSAC : 2 * HSAC],
        targ_bias[:, 2 * HSAC],
    )
    reward = batch[:, OBS + ACT]
    finished = batch[:, 2 * OBS + ACT + 1]
    target_q = reward + DISCOUNT * (1.0 - finished) * (
        jnp.min(target_values, axis=0) - alpha_fixed * next_prob
    )
    unused, prob_fixed = policy(
        states, act_in, sac_hidden[2], act_out, parts[3], parts[4], parts[5], noise[0]
    )
    return (target_q, prob_fixed, alpha_fixed)


def real_pieces(real_rows, centre_in, inv_scale, member_of, filled):
    real_input = (real_rows[:, : OBS + ACT] - centre_in) * inv_scale
    real_target = jnp.concatenate(
        [
            real_rows[:, OBS + ACT + 1 : 2 * OBS + ACT + 1] - real_rows[:, :OBS],
            real_rows[:, OBS + ACT : OBS + ACT + 1],
        ],
        1,
    )
    member_weight = (
        member_of.reshape(-1)[None, :] == jnp.arange(MEMBERS, dtype=jnp.int32)[:, None]
    ).astype(jnp.float32)
    return (real_input, real_target, member_weight * filled[None, :])


def local_terms(
    params,
    frozen,
    batch,
    weight,
    real_input,
    real_target,
    member_weight,
    noise_now,
    target_q,
    prob_fixed,
    alpha_fixed,
):
    sac_hidden, dyn_hidden, crit_in, act_in, dyn_in, crit_out, act_out, dyn_out, biases = params
    parts = unpack_biases(biases)
    fixed_hidden, fixed_in, fixed_out, fixed_biases = frozen
    fixed_parts = unpack_biases(fixed_biases)
    states = batch[:, :OBS]
    values = critic_pair(
        batch[:, : OBS + ACT], crit_in, sac_hidden[:2], crit_out, parts[0], parts[1], parts[2]
    )
    critic_terms = 0.5 * jnp.sum((values - target_q[None, :]) ** 2, axis=0)
    action, log_prob = policy(
        states, act_in, sac_hidden[2], act_out, parts[3], parts[4], parts[5], noise_now
    )
    judged = critic_pair(
        jnp.concatenate([states, action], 1),
        fixed_in,
        fixed_hidden,
        fixed_out,
        fixed_parts[0],
        fixed_parts[1],
        fixed_parts[2],
    )
    actor_terms = alpha_fixed * log_prob - jnp.mean(judged, axis=0)
    alpha_terms = -parts[11] * (prob_fixed + TARGET_ENTROPY)
    sac_total = jnp.sum(weight * (critic_terms + actor_terms + alpha_terms))
    centre, log_var = dynamics_model(
        real_input, dyn_in, dyn_hidden, dyn_out, parts[6], parts[7], parts[8], parts[9], parts[10]
    )
    errors = jnp.sum((centre - real_target[None]) ** 2 * jnp.exp(-log_var) + log_var, axis=2)
    return sac_total + jnp.sum(member_weight * errors)


def schulz_step(matrix, gram):
    square = jnp.matmul(gram, gram, precision=PRECISE)
    return COEF_LINEAR * matrix + jnp.matmul(
        matrix, COEF_CUBIC * gram + COEF_QUINTIC * square, precision=PRECISE
    )


def local_gram(matrix):
    return jnp.matmul(jnp.swapaxes(matrix, 1, 2), matrix, precision=PRECISE)


def newton_schulz(moment):
    matrix = moment / (jnp.sqrt(jnp.sum(moment * moment, axis=(1, 2), keepdims=True)) + 1e-07)
    for step in range(NS_ITERS):
        matrix = schulz_step(matrix, local_gram(matrix))
    return matrix


def muon_weight(weights, direction):
    return weights * (1.0 - MUON_RATE * MUON_DECAY) - MUON_RATE * direction


def adamw_update(weights, first, second, gradient):
    first = BETA_FIRST * first + (1.0 - BETA_FIRST) * gradient
    second = BETA_SECOND * second + (1.0 - BETA_SECOND) * gradient * gradient
    first_hat = first / (1.0 - BETA_FIRST**STEP)
    second_hat = second / (1.0 - BETA_SECOND**STEP)
    weights = weights - ADAM_RATE * (
        first_hat / (jnp.sqrt(second_hat) + 1e-08) + ADAM_DECAY * weights
    )
    return (weights, first, second)


def shards(
    replay,
    model_rows,
    requests,
    member_of,
    model_live,
    noise,
    sac_hidden,
    sac_hidden_mom,
    dyn_hidden,
    dyn_hidden_mom,
    crit_in,
    crit_in_m,
    crit_in_v,
    act_in,
    act_in_m,
    act_in_v,
    dyn_in,
    dyn_in_m,
    dyn_in_v,
    crit_out,
    crit_out_m,
    crit_out_v,
    act_out,
    act_out_m,
    act_out_v,
    dyn_out,
    dyn_out_m,
    dyn_out_v,
    biases,
    biases_m,
    biases_v,
    targ_in,
    targ_hidden,
    targ_out,
    targ_bias,
):
    sac_rounded, dyn_rounded = (
        lax.all_gather(sac_hidden.astype(jnp.bfloat16), "blk", axis=1, tiled=True),
        lax.all_gather(dyn_hidden.astype(jnp.bfloat16), "blk", axis=1, tiled=True),
    )
    sac_full = sac_rounded.astype(jnp.float32)
    dyn_full = dyn_rounded.astype(jnp.float32)
    inputs = replay[: OBS + ACT]
    part_total = jnp.sum(inputs, axis=1)
    part_square = jnp.sum(inputs * inputs, axis=1)
    filled = (requests.reshape(-1) >= 0).astype(jnp.float32)
    living = model_live.astype(jnp.float32)
    local_count = jnp.sum(filled) + jnp.sum(living)
    grand_total, squares, row_count = lax.psum(
        (part_total, part_square, local_count), ("dp", "blk")
    )
    rows_all = replay.shape[1] * lax.axis_size("dp") * lax.axis_size("blk")
    centre_in = grand_total / rows_all
    inv_scale = lax.rsqrt(squares / rows_all - centre_in * centre_in + 1e-06)
    asked = lax.all_to_all(requests, "dp", split_axis=0, concat_axis=0, tiled=True)
    picked = jnp.take(replay, jnp.maximum(asked, 0).reshape(-1), axis=1)
    picked = picked.T.reshape(asked.shape[0], asked.shape[1], replay.shape[0])
    fetched = lax.all_to_all(picked, "dp", split_axis=0, concat_axis=0, tiled=True)
    real_rows = fetched.reshape(-1, replay.shape[0])
    batch = jnp.concatenate([real_rows, model_rows.T], 0)
    weight = jnp.concatenate([filled, living], 0)
    params = (sac_full, dyn_full, crit_in, act_in, dyn_in, crit_out, act_out, dyn_out, biases)
    target_q, prob_fixed, alpha_fixed = prepare(
        params, (targ_in, targ_hidden, targ_out, targ_bias), batch, noise
    )
    frozen = (sac_full[:2], crit_in, crit_out, biases)
    real_input, real_target, member_weight = real_pieces(
        real_rows, centre_in, inv_scale, member_of, filled
    )
    local_sum, pull = jax.vjp(
        lambda values: local_terms(
            values,
            frozen,
            batch,
            weight,
            real_input,
            real_target,
            member_weight,
            noise[0],
            target_q,
            prob_fixed,
            alpha_fixed,
        ),
        params,
    )
    grads = pull(jnp.float32(1.0))[0]
    sac_grad, dyn_grad = (
        lax.psum_scatter(grads[0], "blk", scatter_dimension=1, tiled=True),
        lax.psum_scatter(grads[1], "blk", scatter_dimension=1, tiled=True),
    )
    sac_grad, dyn_grad = lax.psum((sac_grad, dyn_grad), "dp")
    summed = lax.psum(
        (grads[2], grads[3], grads[4], grads[5], grads[6], grads[7], grads[8], local_sum),
        ("dp", "blk"),
    )
    loss_total = summed[7]
    sac_moment = MOMENTUM * sac_hidden_mom + sac_grad / row_count
    dyn_moment = MOMENTUM * dyn_hidden_mom + dyn_grad / row_count
    whole_sac, whole_dyn = (
        lax.all_gather(sac_moment, "blk", axis=1, tiled=True),
        lax.all_gather(dyn_moment, "blk", axis=1, tiled=True),
    )
    sac_rows = sac_moment.shape[1]
    dyn_rows = dyn_moment.shape[1]
    position = lax.axis_index("blk")
    sac_direction = lax.dynamic_slice_in_dim(
        newton_schulz(whole_sac), position * sac_rows, sac_rows, 1
    )
    dyn_direction = lax.dynamic_slice_in_dim(
        newton_schulz(whole_dyn), position * dyn_rows, dyn_rows, 1
    )
    sac_new = muon_weight(sac_hidden, sac_direction)
    dyn_new = muon_weight(dyn_hidden, dyn_direction)
    bias_grad = summed[6] / row_count + jax.grad(bound_penalty)(biases)
    ci = adamw_update(crit_in, crit_in_m, crit_in_v, summed[0] / row_count)
    ai = adamw_update(act_in, act_in_m, act_in_v, summed[1] / row_count)
    di = adamw_update(dyn_in, dyn_in_m, dyn_in_v, summed[2] / row_count)
    co = adamw_update(crit_out, crit_out_m, crit_out_v, summed[3] / row_count)
    ao = adamw_update(act_out, act_out_m, act_out_v, summed[4] / row_count)
    head_new = adamw_update(dyn_out, dyn_out_m, dyn_out_v, summed[5] / row_count)
    bi = adamw_update(biases, biases_m, biases_v, bias_grad)
    return (
        sac_new,
        sac_moment,
        dyn_new,
        dyn_moment,
        ci[0],
        ci[1],
        ci[2],
        ai[0],
        ai[1],
        ai[2],
        di[0],
        di[1],
        di[2],
        co[0],
        co[1],
        co[2],
        ao[0],
        ao[1],
        ao[2],
        head_new[0],
        head_new[1],
        head_new[2],
        bi[0],
        bi[1],
        bi[2],
        loss_total,
        row_count,
    )


def solution(mesh):
    placed = (
        P(None, ("dp", "blk")),
        P(None, ("dp", "blk")),
        P(("dp", "blk"), None),
        P(("dp", "blk"), None),
        P(("dp", "blk")),
        P(None, ("dp", "blk"), None),
        P(None, "blk", None),
        P(None, "blk", None),
        P(None, "blk", None),
        P(None, "blk", None),
        P(),
        P(),
        P(),
        P(),
        P(),
        P(),
        P(),
        P(),
        P(),
        P(),
        P(),
        P(),
        P(),
        P(),
        P(),
        P(),
        P(),
        P(),
        P(),
        P(),
        P(),
        P(),
        P(),
        P(),
        P(),
    )
    return jax.shard_map(
        shards,
        mesh=mesh,
        in_specs=placed,
        out_specs=(
            P(None, "blk", None),
            P(None, "blk", None),
            P(None, "blk", None),
            P(None, "blk", None),
            P(),
            P(),
            P(),
            P(),
            P(),
            P(),
            P(),
            P(),
            P(),
            P(),
            P(),
            P(),
            P(),
            P(),
            P(),
            P(),
            P(),
            P(),
            P(),
            P(),
            P(),
            P(),
            P(),
        ),
        check_vma=False,
    )
```

profile of v0, /device:TPU:0, one launch (start us, length us, event | category | flops | bytes accessed | tf_op | source)
XLA Modules:
  0.0 531.7 jit_solution(5798094001431112267)
XLA Ops:
  7.2 5.2 all-to-all-start
  12.4 1.3 fusion.149
  13.7 1.4 fusion.151
  15.8 1.3 fusion.152
  17.2 1.5 fusion.150
  18.6 1.3 convert_reduce_fusion.9
  20.7 1.2 convert_bitcast_fusion
  24.4 1.3 fusion.153
  25.7 1.6 fusion.148
  29.4 15.1 %all_gather.12 = bf16[3,256,256]{2,1,0:T(8,128)(2,1)S(1)} all-gather(bf16[3,64,256]{2,1,0:T(8,128)(2,1)S(1)} %convert_element_type.245), channel_id=1, replica_groups=mesh['dp'=8,'blk'=4] {'blk'}, dimensions={1}, use_global_device_ids=true | all-gather | bytes 491520 | tf_op jit(solution)/shard_map/all_gather | solution.py:307
  45.2 19.5 %all_gather.14 = bf16[7,200,200]{2,0,1:T(8,128)(2,1)} all-gather(bf16[7,50,200]{2,0,1:T(8,128)(2,1)S(1)} %copy.241), channel_id=1, replica_groups=mesh['dp'=8,'blk'=4] {'blk'}, dimensions={1}, use_global_device_ids=true | all-gather | bytes 700000 | tf_op jit(solution)/shard_map/all_gather | solution.py:308
  64.6 39.3 %all-reduce.22 = (f32[23]{0:T(128)S(1)}, f32[23]{0:T(128)S(1)}) all-reduce(f32[23]{0:T(128)S(1)} %get-tuple-element.198, f32[23]{0:T(128)S(1)} %get-tuple-element.197), channel_id=1, replica_groups=mesh['dp'=8,'blk'=4] {'dp','blk'}, use_global_device_ids=true, to_apply=%region_11.12 | all-reduce | flops 46 | bytes 368 | tf_op jit(solution)/shard_map/psum | solution.py:318
  107.4 1.2 gather_fusion
  110.2 3.6 all-to-all-start.1
  114.7 1.3 slice.133
  132.8 1.5 fusion.144
  138.9 1.5 fusion.160
  151.7 2.4 fusion.4
  154.1 1.4 fusion.154
  156.4 1.2 fusion.11
  160.6 1.2 fusion.14
  165.0 2.0 pad_add_fusion
  167.1 1.3 convert_reduce_fusion.8
  169.0 1.4 reshape.278
  170.4 1.4 reshape.277
  172.4 1.3 copy.288
  173.7 1.3 copy.287
  174.9 1.5 reduce_sum.245
  177.9 1.3 fusion.166
  182.5 43.7 %all-reduce.35 = (f32[]{:T(128)}, f32[2,23,256]{2,1,0:T(8,128)S(1)}, f32[17,256]{1,0:T(8,128)S(1)}, f32[2,256]{1,0:T(2,128)S(1)}, f32[256,12]{0,1:T(8,128)S(1)}, /*index=5*/f32[4639]{0:T(1024)S(1)}, f32[]{:T(128)}) all-reduce(f32[]{:T(128)S(6)} %add.609, f32[2,23,256]{2,1,0:T(8,128)S(1)} %fusion.35, ...), channel_id=1, replica_groups=mesh['dp'=8,'blk'=4] {'dp','blk'}, use_global_device_ids=true, to_apply=%region_6.0 | all-reduce | flops 24353 | bytes 194824 | tf_op jit(solution)/shard_map/psum | solution.py:318
  228.8 1.3 multiply_subtract_fusion.6
  230.1 1.3 multiply_subtract_fusion.5
  231.4 1.4 multiply_subtract_fusion.4
  232.7 1.3 multiply_subtract_fusion.3
  234.0 57.2 %all-reduce.32.cloned.1.call-done = (f32[7,23,200]{2,1,0:T(8,128)}, f32[7,200,36]{1,2,0:T(8,128)}) async-done(((f32[7,23,200]{2,1,0:T(8,128)}, f32[7,200,36]{1,2,0:T(8,128)}), (f32[7,23,200]{2,1,0:T(8,128)}, f32[7,200,36]{1,2,0:T(8,128)})) %all-reduce.32.cloned.1.call-update) | async-done | bytes 330416 | tf_op jit(solution)/shard_map/psum | solution.py:361
  291.3 2.7 multiply_subtract_fusion
  294.0 64.7 %all-reduce.30.cloned.1.call-done = f32[7,200,200]{2,1,0:T(8,128)} async-done(((f32[7,200,200]{2,1,0:T(8,128)}), f32[7,200,200]{2,1,0:T(8,128)}) %all-reduce.30.cloned.1.call-update) | async-done | bytes 1120016
  358.8 1.8 constant_dynamic-slice_fusion
  360.6 23.7 %reduce-scatter.3.cloned.1.call-done = f32[3,64,256]{2,1,0:T(8,128)} async-done(((f32[3,256,256]{2,1,0:T(8,128)}), f32[3,64,256]{2,1,0:T(8,128)}) %reduce-scatter.3.cloned.1.call-update) | async-done | bytes 196624 | tf_op jit(solution)/shard_map/reduce_scatter | solution.py:357
  384.3 1.5 multiply_subtract_fusion.1
  385.9 55.9 %all-reduce.34.cloned.1.call-done = (f32[3,64,256]{2,1,0:T(8,128)}, f32[7,50,200]{2,1,0:T(8,128)}) async-done(((f32[3,64,256]{2,1,0:T(8,128)}, f32[7,50,200]{2,1,0:T(8,128)}), (f32[3,64,256]{2,1,0:T(8,128)}, f32[7,50,200]{2,1,0:T(8,128)})) %all-reduce.34.cloned.1.call-update) | async-done | bytes 476624 | tf_op jit(solution)/shard_map/psum | solution.py:360
  441.8 1.8 divide_add_fusion
  445.2 27.2 %all_gather.13 = f32[3,256,256]{2,1,0:T(8,128)S(1)} all-gather(f32[3,64,256]{2,1,0:T(8,128)S(1)} %divide_add_fusion.1), channel_id=1, replica_groups=mesh['dp'=8,'blk'=4] {'blk'}, dimensions={1}, use_global_device_ids=true | all-gather | bytes 983040 | tf_op jit(solution)/shard_map/all_gather | solution.py:369
  472.6 1.5 fusion.56
  476.0 1.4 fusion.155
  479.3 1.4 fusion.156
  482.5 1.4 fusion.157
  486.0 1.4 fusion.158
  490.2 2.1 multiply_reduce_fusion
  492.3 3.3 fusion.75
  495.7 1.6 fusion.15
  497.3 2.4 convolution_add_fusion.15
  499.7 2.8 fusion.161
  502.5 1.6 fusion.16
  504.1 1.6 convolution_add_fusion.14
  505.7 2.8 fusion.162
  508.5 1.6 fusion.17
  510.1 1.6 convolution_add_fusion.13
  511.7 3.0 fusion.163
  514.7 1.6 fusion.18
  516.3 1.6 convolution_add_fusion.12
  517.9 2.8 fusion.164
  520.7 1.6 fusion.19
  522.3 1.5 fusion.165
  (308 shorter events, 67.8 us)
Async XLA Ops:
  7.2 98.6 %all-to-all-start = ((s32[8,1,8]{2,1,0:T(1,128)}), s32[8,1,8]{2,1,0:T(1,128)}, u32[]{:S(2)}, u32[]{:S(2)}) async-start(s32[8,1,8]{2,1,0:T(1,128)} %bitcast.242), calls=%async_computation | async-start | bytes 8192 | tf_op jit(solution)/shard_map/all_to_all | solution.py:324
  20.7 83.8 %copy-start.60 = (s32[64]{0:T(128)}, s32[64]{0:T(128)S(1)}, u32[]{:S(2)}) copy-start(s32[64]{0:T(128)S(1)} %eq.31) | copy-start | bytes 772
  22.6 1.1 copy-start.37
  24.4 80.1 %copy-start.51 = (f32[64]{0:T(128)}, f32[64]{0:T(128)S(1)}, u32[]{:S(2)}) copy-start(f32[64]{0:T(128)S(1)} %reshape.281) | copy-start | bytes 772
  28.2 76.3 %copy-start.39 = (s32[8,8]{1,0:T(8,128)S(1)}, s32[8,8]{1,0:T(8,128)}, u32[]{:S(2)}) copy-start(s32[8,8]{1,0:T(8,128)} %param.38) | copy-start | bytes 772
  28.2 76.9 %copy-start.5 = (f32[42,3648]{1,0:T(8,128)S(1)}, f32[42,3648]{1,0:T(8,128)}, u32[]{:S(2)}) copy-start(f32[42,3648]{1,0:T(8,128)} %param.36) | copy-start | bytes 1838596
  105.1 20.6 %copy-start.11 = (f32[7,23,200]{2,1,0:T(8,128)S(1)}, f32[7,23,200]{2,1,0:T(8,128)}, u32[]{:S(2)}) copy-start(f32[7,23,200]{2,1,0:T(8,128)} %param.52) | copy-start | bytes 386404
  105.1 20.7 %copy-start.6 = (f32[7,200,36]{1,2,0:T(8,128)S(1)}, f32[7,200,36]{1,2,0:T(8,128)}, u32[]{:S(2)}) copy-start(f32[7,200,36]{1,2,0:T(8,128)} %param.61) | copy-start | bytes 604804
  105.7 20.1 %copy-start.12 = (f32[2,256,256]{2,1,0:T(8,128)S(1)}, f32[2,256,256]{2,1,0:T(8,128)}, u32[]{:S(2)}) copy-start(f32[2,256,256]{2,1,0:T(8,128)} %param.68) | copy-start | bytes 1572868
  105.7 21.4 %copy-start.78 = (u32[32]{0:T(128)S(1)}, u32[32]{0:T(128)}, u32[]{:S(2)}) copy-start(u32[32]{0:T(128)} %constant.237) | copy-start | bytes 388
  108.6 21.4 %copy-start.1 = (f32[42,1216]{1,0:T(8,128)S(1)}, f32[42,1216]{1,0:T(8,128)}, u32[]{:S(2)}) copy-start(f32[42,1216]{1,0:T(8,128)} %param.37) | copy-start | bytes 612868
  110.2 18.3 %all-to-all-start.1 = ((f32[8,1,336]{2,1,0:T(1,128)}), f32[8,1,336]{2,1,0:T(1,128)S(1)}, u32[]{:S(2)}, u32[]{:S(2)}) async-start(f32[8,1,336]{2,1,0:T(1,128)} %reshape.319), calls=%async_computation.1 | async-start | bytes 24576 | tf_op jit(solution)/shard_map/all_to_all | solution.py:327
  113.7 177.5 %all-reduce.32.cloned.1.call-start = ((), (), s32[]{:S(2)}) async-start(), calls=%async_computation.6 | async-start | bytes 917504 | tf_op jit(solution)/shard_map/psum | solution.py:361
  119.6 36.8 %copy-start.17 = (bf16[2,256,256]{2,1,0:T(8,128)(2,1)}, bf16[2,256,256]{2,1,0:T(8,128)(2,1)S(1)}, u32[]{:S(2)}) copy-start(bf16[2,256,256]{2,1,0:T(8,128)(2,1)S(1)} %slice.164) | copy-start | bytes 786436
  124.9 5.4 %copy-start.68 = (f32[23]{0:T(128)S(1)}, f32[23]{0:T(128)}, u32[]{:S(2)}) copy-start(f32[23]{0:T(128)} %get-tuple-element.274) | copy-start | bytes 280
  124.9 5.4 %copy-start.69 = (f32[23]{0:T(128)S(1)}, f32[23]{0:T(128)}, u32[]{:S(2)}) copy-start(f32[23]{0:T(128)} %get-tuple-element.275) | copy-start | bytes 280
  130.1 1.2 copy-start.8
  130.2 17.8 %copy-start.19 = (bf16[1280,23]{0,1:T(8,128)(2,1)}, bf16[1280,23]{0,1:T(8,128)(2,1)S(1)}, u32[]{:S(2)}) copy-start(bf16[1280,23]{0,1:T(8,128)(2,1)S(1)} %fusion.60) | copy-start | bytes 176644
  136.7 3.7 copy-start.77
  143.0 1.0 copy-start.73
  143.9 0.9 copy-start.72
  148.9 1.3 copy-start.50
  149.7 1.1 slice-start
  149.8 1.2 copy-start.52
  149.8 1.9 copy-start.57
  151.6 2.5 copy-start.28
  158.8 1.8 copy-start.18
  164.1 194.7 %all-reduce.30.cloned.1.call-start = ((), (), s32[]{:S(2)}) async-start(), calls=%async_computation.5 | async-start | bytes 2867200
  164.9 3.4 copy-start.49
  165.0 219.3 %reduce-scatter.3.cloned.1.call-start = ((), (), s32[]{:S(2)}) async-start(), calls=%async_computation.3 | async-start | bytes 983040 | tf_op jit(solution)/shard_map/reduce_scatter | solution.py:357
  176.5 2.7 copy-start.29
  176.5 3.1 copy-start.20
  179.7 2.8 copy-start.33
  179.7 46.4 %copy-start.23 = (f32[2,23,256]{2,0,1:T(2,128)S(1)}, f32[2,23,256]{2,0,1:T(2,128)}, u32[]{:S(2)}) copy-start(f32[2,23,256]{2,0,1:T(2,128)} %param.46) | copy-start | bytes 141316
  179.7 46.4 %copy-start.35 = (f32[2,23,256]{2,0,1:T(2,128)S(1)}, f32[2,23,256]{2,0,1:T(2,128)}, u32[]{:S(2)}) copy-start(f32[2,23,256]{2,0,1:T(2,128)} %param.47) | copy-start | bytes 141316
  179.7 46.4 %copy-start.36 = (f32[2,23,256]{2,0,1:T(2,128)S(1)}, f32[2,23,256]{2,0,1:T(2,128)}, u32[]{:S(2)}) copy-start(f32[2,23,256]{2,0,1:T(2,128)} %param.48) | copy-start | bytes 141316
  179.7 49.1 %copy-start.56 = (f32[2,256]{1,0:T(2,128)S(1)}, f32[2,256]{1,0:T(2,128)}, u32[]{:S(2)}) copy-start(f32[2,256]{1,0:T(2,128)} %param.55) | copy-start | bytes 6148
  179.8 49.1 %copy-start.74 = (f32[2,256]{1,0:T(2,128)S(1)}, f32[2,256]{1,0:T(2,128)}, u32[]{:S(2)}) copy-start(f32[2,256]{1,0:T(2,128)} %param.56) | copy-start | bytes 6148
  179.8 49.0 %copy-start.75 = (f32[2,256]{1,0:T(2,128)S(1)}, f32[2,256]{1,0:T(2,128)}, u32[]{:S(2)}) copy-start(f32[2,256]{1,0:T(2,128)} %param.57) | copy-start | bytes 6148
  179.8 50.3 %copy-start.34 = (f32[256,12]{0,1:T(8,128)S(1)}, f32[256,12]{0,1:T(8,128)}, u32[]{:S(2)}) copy-start(f32[256,12]{0,1:T(8,128)} %param.58) | copy-start | bytes 36868
  179.8 50.3 %copy-start.47 = (f32[256,12]{0,1:T(8,128)S(1)}, f32[256,12]{0,1:T(8,128)}, u32[]{:S(2)}) copy-start(f32[256,12]{0,1:T(8,128)} %param.59) | copy-start | bytes 36868
  179.8 50.3 %copy-start.48 = (f32[256,12]{0,1:T(8,128)S(1)}, f32[256,12]{0,1:T(8,128)}, u32[]{:S(2)}) copy-start(f32[256,12]{0,1:T(8,128)} %param.60) | copy-start | bytes 36868
  179.8 51.6 %copy-start.31 = (f32[4639]{0:T(1024)S(1)}, f32[4639]{0:T(1024)}, u32[]{:S(2)}) copy-start(f32[4639]{0:T(1024)} %param.64) | copy-start | bytes 55672
  179.8 51.5 %copy-start.44 = (f32[4639]{0:T(1024)S(1)}, f32[4639]{0:T(1024)}, u32[]{:S(2)}) copy-start(f32[4639]{0:T(1024)} %param.65) | copy-start | bytes 55672
  179.8 51.5 %copy-start.45 = (f32[4639]{0:T(1024)S(1)}, f32[4639]{0:T(1024)}, u32[]{:S(2)}) copy-start(f32[4639]{0:T(1024)} %param.66) | copy-start | bytes 55672
  179.8 52.9 %copy-start.32 = (f32[17,256]{1,0:T(8,128)S(1)}, f32[17,256]{1,0:T(8,128)}, u32[]{:S(2)}) copy-start(f32[17,256]{1,0:T(8,128)} %param.49) | copy-start | bytes 52228
  179.9 52.9 %copy-start.42 = (f32[17,256]{1,0:T(8,128)S(1)}, f32[17,256]{1,0:T(8,128)}, u32[]{:S(2)}) copy-start(f32[17,256]{1,0:T(8,128)} %param.50) | copy-start | bytes 52228
  179.9 52.9 %copy-start.43 = (f32[17,256]{1,0:T(8,128)S(1)}, f32[17,256]{1,0:T(8,128)}, u32[]{:S(2)}) copy-start(f32[17,256]{1,0:T(8,128)} %param.51) | copy-start | bytes 52228
  179.9 111.4 %copy-start.7 = (f32[7,200,36]{1,2,0:T(8,128)S(1)}, f32[7,200,36]{1,2,0:T(8,128)}, u32[]{:S(2)}) copy-start(f32[7,200,36]{1,2,0:T(8,128)} %param.61) | copy-start | bytes 604804
  179.9 111.4 %copy-start.14 = (f32[7,200,36]{1,2,0:T(8,128)S(1)}, f32[7,200,36]{1,2,0:T(8,128)}, u32[]{:S(2)}) copy-start(f32[7,200,36]{1,2,0:T(8,128)} %param.62) | copy-start | bytes 604804
  179.9 111.3 %copy-start.15 = (f32[7,200,36]{1,2,0:T(8,128)S(1)}, f32[7,200,36]{1,2,0:T(8,128)}, u32[]{:S(2)}) copy-start(f32[7,200,36]{1,2,0:T(8,128)} %param.63) | copy-start | bytes 604804
  180.2 261.5 %all-reduce.34.cloned.1.call-start = ((), (), s32[]{:S(2)}) async-start(), calls=%async_computation.7 | async-start | bytes 1196032 | tf_op jit(solution)/shard_map/psum | solution.py:360
  291.3 93.1 %copy-start.24 = (f32[7,23,200]{2,1,0:T(8,128)S(1)}, f32[7,23,200]{2,1,0:T(8,128)}, u32[]{:S(2)}) copy-start(f32[7,23,200]{2,1,0:T(8,128)} %param.53) | copy-start | bytes 386404
  291.3 93.1 %copy-start.25 = (f32[7,23,200]{2,1,0:T(8,128)S(1)}, f32[7,23,200]{2,1,0:T(8,128)}, u32[]{:S(2)}) copy-start(f32[7,23,200]{2,1,0:T(8,128)} %param.54) | copy-start | bytes 386404
  291.3 93.1 %copy-start.26 = (f32[7,23,200]{2,1,0:T(8,128)S(1)}, f32[7,23,200]{2,1,0:T(8,128)}, u32[]{:S(2)}) copy-start(f32[7,23,200]{2,1,0:T(8,128)} %get-tuple-element.214) | copy-start | bytes 386404
  294.0 147.7 %copy-start.13 = (f32[7,50,200]{2,1,0:T(8,128)S(1)}, f32[7,50,200]{2,1,0:T(8,128)}, u32[]{:S(2)}) copy-start(f32[7,50,200]{2,1,0:T(8,128)} %param.45) | copy-start | bytes 840004
  384.3 106.0 %all-gather.2.cloned.1.call-start = ((), (), s32[]{:S(2)}) async-start(), calls=%async_computation.4 | async-start | bytes 2048000 | tf_op jit(solution)/shard_map/all_gather | solution.py:370
  385.9 58.6 %copy-start.21 = (f32[3,64,256]{2,1,0:T(8,128)S(1)}, f32[3,64,256]{2,1,0:T(8,128)}, u32[]{:S(2)}) copy-start(f32[3,64,256]{2,1,0:T(8,128)} %param.43) | copy-start | bytes 589828
  441.8 2.7 copy-start.22
  443.5 29.1 %copy-start.4 = (f32[7,50,200]{2,1,0:T(8,128)}, f32[7,50,200]{2,1,0:T(8,128)S(1)}, u32[]{:S(2)}) copy-start(f32[7,50,200]{2,1,0:T(8,128)S(1)} %divide_add_fusion) | copy-start | bytes 840004
  445.2 29.0 %copy-start.10 = (f32[3,64,256]{2,1,0:T(8,128)}, f32[3,64,256]{2,1,0:T(8,128)S(1)}, u32[]{:S(2)}) copy-start(f32[3,64,256]{2,1,0:T(8,128)S(1)} %divide_add_fusion.1) | copy-start | bytes 589828
  488.4 0.9 copy-start.9
  490.2 2.1 copy-start.2
  522.3 1.5 copy-start.3
  (23 other events, 18.2 us)
Sparse Core Ops, SparseCore 0:
  164.2 126.9 all-reduce.31
  293.8 64.9 all-reduce.29
  361.2 23.0 reduce-scatter.2
  388.3 53.4 all-reduce.33
  444.6 45.5 all-gather.1
where the time goes:
time: 536 us; the launch traced here: 532 us
  waiting for transfers between devices  202 us (38%)
  blocking collectives  145 us (27%)
  matrix products  71.4 us (13%)
  other arithmetic  49.9 us (9%)
  local copies, waits for them, and re-layouts  33.6 us (6%)
  between operations  21 us (4%)
  starting transfers between devices  9.11 us (2%)
    psum x2, blocking collectives, shards(): lax.psum((part_total, part_square, local_count), ('dp', 'blk'))  83 us
    unnamed x6, waiting for transfers between devices  64.8 us
    psum x1, waiting for transfers between devices, shards(): lax.psum((grads[2], grads[3], grads[4], grads[5], grads[6], grads[7], gra...  57.2 us
    psum x1, waiting for transfers between devices, shards(): sac_grad, dyn_grad = lax.psum((sac_grad, dyn_grad), 'dp')  55.9 us
    all_gather x1, blocking collectives, shards(): lax.all_gather(sac_moment, 'blk', axis=1, tiled=True)  27.2 us
    reduce_scatter x1, waiting for transfers between devices, shards(): lax.psum_scatter(grads[0], 'blk', scatter_dimension=1, tiled=True)  23.7 us
    dot_general x34, matrix products, dense_layer(): jnp.matmul(value_round(inputs), value_round(weights), precision=PRECISE)  23.5 us
    dot_general x10, matrix products, local_gram(): return jnp.matmul(jnp.swapaxes(matrix, 1, 2), matrix, precision=PRECISE)  22 us
  transfers between devices with their start and end apart: 7, of which 5 were waited for; matrix products, arithmetic and copies ran while one was open for 15% of the time, Pallas kernels for 0%

commit v1 on v0

v1 whole, which is shorter than its diff:
```python
import functools
import math

import jax
import jax.numpy as jnp
from jax import lax
from jax.experimental import pallas as pl
from jax.experimental.pallas import tpu as pltpu
from jax.sharding import PartitionSpec as P

OBS = 17
ACT = 6
IN = OBS + ACT
FEAT = 42
HDYN = 200
HSAC = 256
MEMBERS = 7
DOUT = 36
HALF = DOUT // 2
NB = 4639
NS_ITERS = 5
STEP = 10
CAP = 8
TILE = 256

DISCOUNT = 0.99
TARGET_ENTROPY = -6.0
BOUND_WEIGHT = 0.01
MOMENTUM = 0.95
MUON_RATE = 0.4
MUON_DECAY = 0.01
ADAM_RATE = 0.1
ADAM_DECAY = 0.01
BETA_FIRST = 0.9
BETA_SECOND = 0.999
COEF_LINEAR = 3.4445
COEF_CUBIC = -4.775
COEF_QUINTIC = 2.0315

CB1, CB2, CB3, AB1, AB2, AB3 = 0, 512, 1024, 1026, 1282, 1538
DB1, DB2, DB3, MAXLV, MINLV, LOGA = 1550, 2950, 4350, 4602, 4620, 4638

R_IN, R_HEAD, R_OUT, R_MISC, R_SMALL = 0, 72, 88, 96, 128
D_IN, D_OUT, D_B2, D_B3, D_UP, D_LOW, D_LOSS, D_ROWS = 0, 24, 60, 61, 62, 63, 64, 72

F32, BF16 = jnp.float32, jnp.bfloat16
MESH = pl.DeviceIdType.MESH
NN = (((1,), (0,)), ((), ()))
NT = (((1,), (1,)), ((), ()))


def dot(a, b, dims=NN):
    return lax.dot_general(a, b, dims, preferred_element_type=F32)


def rounded(v):
    return v.astype(BF16).astype(F32)


def pieces(v):
    high = v.astype(BF16)
    rest = v - high.astype(F32)
    middle = rest.astype(BF16)
    return high, middle, (rest - middle.astype(F32)).astype(BF16)


def split(v):
    high = v.astype(BF16)
    return high, (v - high.astype(F32)).astype(BF16)


def product(a, b, dims=NN):
    return dot(a[0], b[0], dims) + dot(a[0], b[1], dims) + dot(a[1], b[0], dims)


def softplus(v):
    return jnp.maximum(v, 0.0) + jnp.log1p(jnp.exp(-jnp.abs(v)))


def sigmoid(v):
    return 0.5 + 0.5 * jnp.tanh(0.5 * v)


def gate(half):
    up = 1.0 + jnp.tanh(half)
    value = half * up
    return value, up + value * (2.0 - up)


def rows_of(shape):
    return lax.broadcasted_iota(jnp.int32, shape, 0)


def schulz(ref, steps):
    @pl.loop(0, steps)
    def _(step):
        matrix = ref[...]
        parts = split(matrix)
        gram = product(parts, parts, NT)
        halves = split(gram)
        blend = COEF_CUBIC * gram + COEF_QUINTIC * product(halves, halves)
        ref[...] = COEF_LINEAR * matrix + product(split(blend), parts)


class Layout:
    def __init__(self, mesh, replay, model):
        self.n_dp = mesh.shape["dp"]
        self.n_blk = mesh.shape["blk"]
        self.bits = int(math.log2(self.n_dp))
        self.n_dev = self.n_dp * self.n_blk
        self.replay = replay
        self.model = model
        self.real = self.n_dp * CAP
        self.batch = self.real + model
        self.width = -(-(self.real + 2) // 128) * 128
        self.rows = HSAC // self.n_blk
        self.drows = HDYN // self.n_blk
        self.mat = 64 // self.n_dp
        self.sml = 32 // self.n_dp
        self.chunk = 3 * self.mat + self.sml
        self.split_z = self.chunk % self.n_blk == 0
        self.part = self.chunk // self.n_blk if self.split_z else self.chunk
        self.owners = [self.n_dp - 1 - 2 * k for k in range(3)]


def main_kernel(lay, *refs):
    (
        replay, model, requests, member, live, noise, sac_h, sac_m, dyn_h, dyn_m, crit_in, act_in,
        dyn_in, crit_out, act_out, dyn_out, biases, targ_in, targ_hidden, targ_out, targ_bias,
        sac_g, sac_x, dyn_g, dyn_x, dyn_s, small, count,
        wg, asked, owned, dhg, dmg, smg, bk, xs, nz, w1f, w1t, w1n, w2t, w2h, heads, head_t, head_f,
        rowbuf, cols, headcol, acc_h, acc_w, acc_c, acc_a, acc_m, acc_l, grid, zr, zf, mg, mat,
        grow, xrow, dcols, dacc_h, dacc_w, dacc_o, dacc_m, dacc_b, dacc_l, xt, dmat, dpack, drow_g,
        drow_x, *rest,
    ) = refs
    rs_bufs = rest[: lay.bits]
    (
        s_w, r_w, s_q, r_q, s_p, r_p, s_dh, r_dh, s_dm, r_dm, s_sm, r_sm, s_bz, r_bz, s_bp, r_bp,
        s_rs, r_rs, s_zr, r_zr, s_za, r_za, s_pl, r_pl, s_mg, r_mg, s_ds, r_ds, s_dg, r_dg, s_dx,
        r_dx, s_sg, r_sg, s_sx, r_sx,
    ) = rest[lay.bits :]
    n_dp, n_blk, bits = lay.n_dp, lay.n_blk, lay.bits
    me = lax.axis_index("dp")
    z = lax.axis_index("blk")
    is_dyn = me < MEMBERS
    owner_k = (n_dp - 1 - me) // 2
    is_sac = jnp.logical_and(lax.rem(n_dp - 1 - me, 2) == 0, owner_k < 3)
    sac_k = jnp.minimum(owner_k, 2)
    dyn_e = jnp.minimum(me, MEMBERS - 1)

    def on_plane(src, dst, ssem, rsem, peer):
        return pltpu.make_async_remote_copy(
            src_ref=src, dst_ref=dst, send_sem=ssem, recv_sem=rsem,
            device_id={"dp": peer}, device_id_type=MESH,
        )

    def on_line(src, dst, ssem, rsem, peer):
        return pltpu.make_async_remote_copy(
            src_ref=src, dst_ref=dst, send_sem=ssem, recv_sem=rsem,
            device_id={"blk": peer}, device_id_type=MESH,
        )

    def plane_peers(body):
        @pl.loop(1, n_dp)
        def _(off):
            body(lax.rem(me + off, n_dp))

    def line_peers(body):
        @pl.loop(1, n_blk)
        def _(off):
            body(lax.rem(z + off, n_blk))

    barrier = pltpu.get_barrier_semaphore()
    plane_peers(lambda peer: pl.semaphore_signal(barrier, inc=1, device_id={"dp": peer}, device_id_type=MESH))
    line_peers(lambda peer: pl.semaphore_signal(barrier, inc=1, device_id={"blk": peer}, device_id_type=MESH))
    wg[z] = sac_h[...].astype(BF16)
    pl.semaphore_wait(barrier, n_dp - 1 + n_blk - 1)

    def hidden_copy(owner, part, peer):
        at = (2, 1) if part == 0 else (0, 2)
        view = wg.at[owner, pl.ds(*at)]
        return on_line(view, view, s_w.at[part, peer], r_w.at[part, owner], peer)

    line_peers(lambda peer: hidden_copy(z, 0, peer).start())

    def list_copy(owner, peer):
        return on_plane(requests, asked.at[owner], s_q.at[peer], r_q.at[owner], peer)

    def member_copy(owner, peer):
        return on_plane(member, owned.at[owner], s_p.at[peer], r_p.at[owner], peer)

    plane_peers(lambda peer: list_copy(me, peer).start())
    plane_peers(lambda peer: member_copy(me, peer).start())
    line_peers(lambda peer: hidden_copy(z, 1, peer).start())
    asked[me] = requests[...]
    owned[me] = member[...]

    def dyn_h_copy(owner, peer):
        return on_line(dyn_h.at[dyn_e], dhg.at[owner], s_dh.at[peer], r_dh.at[owner], peer)

    def dyn_m_copy(owner, peer):
        return on_line(dyn_m.at[dyn_e], dmg.at[owner], s_dm.at[peer], r_dm.at[owner], peer)

    def sac_m_copy(owner, peer):
        return on_line(sac_m.at[sac_k], smg.at[owner], s_sm.at[peer], r_sm.at[owner], peer)

    xs[42:56, :] = jnp.zeros((14, lay.batch), F32)
    xs[0:FEAT, lay.real : lay.batch] = model[...]
    xs[42:43, lay.real : lay.batch] = live[...].astype(F32)
    nz[...] = jnp.zeros_like(nz)
    for which in range(2):
        nz[which, 1:7, :] = noise[:, which, :]
    bias = biases
    firsts = [
        (targ_in[:, 0, :], targ_bias[0:1, 0:HSAC]),
        (targ_in[:, 1, :], targ_bias[1:2, 0:HSAC]),
        (crit_in[:, 0, :], bias[:, CB1 : CB1 + HSAC]),
        (crit_in[:, 1, :], bias[:, CB1 + HSAC : CB1 + 2 * HSAC]),
        (act_in[...], bias[:, AB1 : AB1 + HSAC]),
    ]
    w1f[...] = jnp.zeros_like(w1f)
    for net, (weights, offset) in enumerate(firsts):
        w1f[net, 0 : weights.shape[0], :] = rounded(weights)
        for at, piece in enumerate(pieces(offset)):
            w1f[net, IN + at : IN + at + 1, :] = piece.astype(F32)
        w1t[net] = (0.5 * w1f[net].T).astype(BF16)
    for k in range(2):
        w1n[k] = w1f[2 + k, 16:32, :].astype(BF16)
    for net in range(2):
        w2t[net] = (0.5 * rounded(targ_hidden[net])).T.astype(BF16)
    rowbuf[...] = jnp.zeros_like(rowbuf)
    rowbuf[0:1, :] = targ_bias[0:1, HSAC : 2 * HSAC]
    rowbuf[1:2, :] = targ_bias[1:2, HSAC : 2 * HSAC]
    rowbuf[2:3, :] = bias[:, CB2 : CB2 + HSAC]
    rowbuf[3:4, :] = bias[:, CB2 + HSAC : CB2 + 2 * HSAC]
    rowbuf[4:5, :] = bias[:, AB2 : AB2 + HSAC]
    rowbuf[5:7, :] = rounded(crit_out[...])
    cols[...] = 0.5 * rowbuf[...].T
    rowbuf[...] = jnp.zeros_like(rowbuf)
    rowbuf[0:1, 1:7] = bias[:, AB3 : AB3 + ACT]
    rowbuf[0:1, 9:15] = bias[:, AB3 + ACT : AB3 + 2 * ACT]
    headcol[...] = rowbuf[:, 0:128].T
    head_f[...] = jnp.zeros_like(head_f)
    for k in range(2):
        head_f[0:1, :] = targ_out[k : k + 1, :]
        heads[k] = head_f[...].astype(BF16)
        head_f[0:1, :] = crit_out[k : k + 1, :]
        heads[2 + k] = head_f[...].astype(BF16)
    head_f[0:1, :] = jnp.zeros((1, HSAC), F32)
    head_f[1:7, :] = act_out[0:ACT, :]
    head_f[9:15, :] = act_out[ACT : 2 * ACT, :]
    heads[4] = head_f[...].astype(BF16)
    head_t[...] = (0.5 * rounded(head_f[...])).T.astype(BF16)
    for ref in (acc_h, acc_w, acc_c, acc_a, acc_m, acc_l):
        ref[...] = jnp.zeros_like(ref)

    data = replay[...]
    sums = jnp.sum(data[0:24], axis=1, keepdims=True)
    squares = jnp.sum(data[0:24] * data[0:24], axis=1, keepdims=True)
    living = jnp.sum(live[...].astype(F32), axis=1, keepdims=True)

    def wait_lists(peer):
        list_copy(peer, peer).wait_recv()
        member_copy(peer, peer).wait_recv()

    plane_peers(wait_lists)
    spread = (
        lax.rem(lax.broadcasted_iota(jnp.int32, (CAP, lay.real), 1), CAP)
        == lax.broadcasted_iota(jnp.int32, (CAP, lay.real), 0)
    ).astype(F32)
    here = (
        lax.broadcasted_iota(jnp.int32, (n_dp, lay.real), 1) // CAP
        == lax.broadcasted_iota(jnp.int32, (n_dp, lay.real), 0)
    )

    def in_lanes(ref):
        lists = ref[:, me, :].astype(F32)
        wide = lax.dot_general(
            lists, spread, NN, precision=lax.Precision.HIGHEST, preferred_element_type=F32
        )
        return jnp.sum(jnp.where(here, wide, 0.0), axis=0, keepdims=True)

    slots = in_lanes(asked)
    wanted = jnp.maximum(slots, 0.0).astype(jnp.int32)
    hot = (rows_of((lay.replay, lay.real)) == wanted).astype(BF16)
    high, middle, low = pieces(data)
    picked = dot(high, hot) + dot(middle, hot) + dot(low, hot)
    mine = me * n_blk + z
    bk[mine, 0:FEAT, 0 : lay.real] = picked
    bk[mine, 42:43, 0 : lay.real] = (slots >= 0.0).astype(F32)
    bk[mine, 43:44, 0 : lay.real] = in_lanes(owned)
    bk[mine, 44:48, 0 : lay.real] = jnp.zeros((4, lay.real), F32)
    bk[mine, :, lay.real : lay.width] = jnp.zeros((48, lay.width - lay.real), F32)
    bk[mine, 0:24, lay.real : lay.real + 1] = sums
    bk[mine, 0:24, lay.real + 1 : lay.real + 2] = squares
    bk[mine, 24:25, lay.real : lay.real + 1] = living

    def block_line(owner, peer):
        view = bk.at[me * n_blk + owner]
        return on_line(view, view, s_bz.at[peer], r_bz.at[owner], peer)

    def block_plane(owner, peer):
        view = bk.at[pl.ds(owner * n_blk, n_blk)]
        return on_plane(view, view, s_bp.at[peer], r_bp.at[owner], peer)

    line_peers(lambda peer: block_line(z, peer).start())

    @pl.when(is_dyn)
    def _():
        line_peers(lambda peer: dyn_h_copy(z, peer).start())
        line_peers(lambda peer: dyn_m_copy(z, peer).start())

    @pl.when(is_sac)
    def _():
        line_peers(lambda peer: sac_m_copy(z, peer).start())

    def wait_hidden(peer):
        hidden_copy(peer, 0, peer).wait_recv()
        hidden_copy(peer, 1, peer).wait_recv()

    line_peers(wait_hidden)
    for k in range(3):
        for block in range(n_blk):
            w2h[k, block * lay.rows : (block + 1) * lay.rows, :] = (
                0.5 * wg[block, k].astype(F32)
            ).astype(BF16)
        w2t[2 + k] = w2h[k].astype(F32).T.astype(BF16)

    log_alpha = bias[:, LOGA : LOGA + 1]
    alpha = jnp.exp(log_alpha)
    last = [
        targ_bias[0:1, 2 * HSAC : 2 * HSAC + 1],
        targ_bias[1:2, 2 * HSAC : 2 * HSAC + 1],
        bias[:, CB3 : CB3 + 1],
        bias[:, CB3 + 1 : CB3 + 2],
    ]
    n_tiles = lay.batch // TILE

    @pl.loop(0, n_tiles)
    def _(step):
        @pl.when(step == 1)
        def _():
            line_peers(lambda peer: block_line(peer, peer).wait_recv())
            plane_peers(lambda peer: block_plane(me, peer).start())

        @pl.when(step == n_tiles - 1)
        def _():
            plane_peers(lambda peer: block_plane(peer, peer).wait_recv())
            lanes = lax.broadcasted_iota(jnp.int32, (48, lay.width), 1) // CAP

            def gather(owner, total):
                turned = pltpu.roll(
                    bk[owner * n_blk + z], lax.rem((owner - me) * CAP + lay.width, lay.width), axis=1
                )
                return jnp.where(lanes == owner, turned, total)

            own = lax.fori_loop(0, n_dp, gather, jnp.zeros((48, lay.width), F32))
            xs[0:48, 0 : lay.real] = own[:, 0 : lay.real]

        where = pl.ds(pl.multiple_of(lax.rem(step + 1, n_tiles) * TILE, TILE), TILE)
        row32 = rows_of((32, TILE))
        ones3 = jnp.logical_and(row32 >= IN, row32 < IN + 3).astype(F32)
        now_f = jnp.where(row32 < IN, xs[0:32, where], ones3)
        next_f = jnp.where(row32 < OBS, xs[24:56, where], ones3)
        now_in = now_f.astype(BF16)
        reward = xs[23:24, where]
        done = xs[41:42, where]
        weight = xs[42:43, where]
        row8 = rows_of((8, TILE))
        act_rows = jnp.logical_and(row8 >= 1, row8 < 1 + ACT)
        row16 = rows_of((16, TILE))
        ones16 = jnp.ones((16, TILE), BF16)

        def hidden(inputs, net):
            first, slope1 = gate(dot(w1t[net], inputs))
            first = first.astype(BF16)
            second, slope2 = gate(dot(w2t[net], first) + cols[:, net : net + 1])
            return first, slope1, second.astype(BF16), slope2

        def policy(inputs, which):
            first, slope1, second, slope2 = hidden(inputs, 4)
            out = dot(heads[4], second) + headcol[0:16, 0:1]
            bent = jnp.tanh(out[8:16])
            log_scale = -5.0 + 3.5 * (bent + 1.0)
            draw = nz[which, :, where]
            moved = jnp.exp(log_scale) * draw
            latent = out[0:8] + moved
            terms = (
                -0.5 * draw * draw
                - log_scale
                - 0.9189385
                - 2.0 * (0.6931472 - latent - softplus(-2.0 * latent))
            )
            log_prob = jnp.sum(jnp.where(act_rows, terms, 0.0), axis=0, keepdims=True)
            action = jnp.where(act_rows, jnp.tanh(latent), 0.0)
            return action, log_prob, bent, moved, (first, slope1, second, slope2)

        def with_action(inputs, action):
            middle_rows = jnp.where(act_rows, action, inputs[16:24])
            return jnp.concatenate([inputs[0:16], middle_rows, inputs[24:32]], 0).astype(BF16)

        def critic(inputs, net):
            kept = hidden(inputs, net)
            value = dot(heads[net], kept[2])[0:1] + last[net]
            return value, kept

        def add_hidden(k, first, grad):
            acc_h[k] += dot(jnp.concatenate([first, ones16], 0), grad, NT)

        next_action, next_prob, _, _, _ = policy(next_f.astype(BF16), 1)
        aim_in = with_action(next_f, next_action)
        aim = jnp.minimum(critic(aim_in, 0)[0], critic(aim_in, 1)[0])
        target = reward + DISCOUNT * (1.0 - done) * (aim - alpha * next_prob)
        action, log_prob, bent, moved, (a1, da1, a2, da2) = policy(now_in, 0)
        judged_in = with_action(now_f, action)
        loss = alpha * log_prob - log_alpha * (log_prob + TARGET_ENTROPY)
        grad_action = jnp.zeros((8, TILE), F32)
        heads_grad = []
        for k in range(2):
            value, (c1, dc1, c2, dc2) = critic(now_in, 2 + k)
            miss = value - target
            loss += 0.5 * miss * miss
            g3 = rounded(weight * miss)
            g3_rows = jnp.where(row16 == 0, g3, 0.0).astype(BF16)
            heads_grad.append(g3_rows)
            acc_c[k] += dot(g3_rows, c2, NT)
            g2 = ((cols[:, 5 + k : 6 + k] * g3) * dc2).astype(BF16)
            add_hidden(k, c1, g2)
            g1 = (dot(w2h[k], g2) * dc1).astype(BF16)
            acc_w[k] += dot(now_in, g1, NT)
            judged, (_, df1, _, df2) = critic(judged_in, 2 + k)
            loss -= 0.5 * judged
            g2 = ((cols[:, 5 + k : 6 + k] * (-0.5 * weight)) * df2).astype(BF16)
            g1 = (dot(w2h[k], g2) * df1).astype(BF16)
            grad_action += dot(w1n[k], g1)[0:8]
        grad_latent = 2.0 * alpha * weight * action + grad_action * (1.0 - action * action)
        grad_scale = grad_latent * moved - alpha * weight
        grad_bent = grad_scale * 3.5 * (1.0 - bent * bent)
        g3 = jnp.concatenate(
            [jnp.where(act_rows, grad_latent, 0.0), jnp.where(act_rows, grad_bent, 0.0)], 0
        ).astype(BF16)
        acc_a[...] += dot(g3, a2, NT)
        acc_m[...] += dot(ones16, jnp.concatenate([g3] + heads_grad, 0), NT)
        g2 = (dot(head_t[...], g3) * da2).astype(BF16)
        add_hidden(2, a1, g2)
        g1 = (dot(w2h[2], g2) * da1).astype(BF16)
        acc_w[2] += dot(now_in, g1, NT)
        acc_l[0:1, :] += weight * loss
        acc_l[1:2, :] += weight * (log_prob + TARGET_ENTROPY)

    for k in range(3):
        for chunk in range(n_dp):
            tile = chunk * lay.mat
            side, row = tile // 32, tile % 32
            grid[chunk, k * lay.mat : (k + 1) * lay.mat] = acc_h[
                k, row * 8 : (row + lay.mat) * 8, side * 128 : (side + 1) * 128
            ].reshape(lay.mat, 8, 128)

    def put(row, value):
        for at in range(value.shape[0] // 8):
            for side in range(value.shape[1] // 128):
                tile = side * (R_SMALL // 8) + row // 8 + at
                grid[tile // lay.sml, 3 * lay.mat + tile % lay.sml] = value[
                    at * 8 : at * 8 + 8, side * 128 : (side + 1) * 128
                ]

    for k in range(3):
        put(R_IN + 24 * k, acc_w[k, 0:24, :])
    put(R_HEAD, acc_a[...])
    rowbuf[0:1, :] = acc_c[0, 0:1, :]
    rowbuf[1:2, :] = acc_c[1, 0:1, :]
    for k in range(3):
        rowbuf[2 + k : 3 + k, :] = acc_h[k, HSAC : HSAC + 1, :]
    put(R_OUT, rowbuf[...])
    folded = jnp.sum(acc_l[...], axis=1, keepdims=True)
    rowbuf[...] = jnp.zeros_like(rowbuf)
    rowbuf[0:1, 0:48] = acc_m[0:1, :]
    rowbuf[0:1, 64:65] = folded[0:1]
    rowbuf[0:1, 65:66] = folded[1:2]
    put(R_MISC, rowbuf[...])
    put(R_MISC + 8, jnp.zeros((R_SMALL - R_MISC - 8, HSAC), F32))

    core = lax.rem(me, 2)

    def bit(b):
        return lax.rem(me // (1 << b), 2)

    starts, faces, partners = [], [], []
    start = 0
    for s in range(bits):
        if s == 0:
            face, stride = core, 1
        else:
            face = (1 - core) * bit(s) + core * bit(bits - s)
            stride = (1 - core) * (1 << s) + core * (1 << (bits - s))
        starts.append(start)
        faces.append(face)
        partners.append(me + (1 - 2 * face) * stride)
        start = start + face * (n_dp >> (s + 1))
    place = start

    def fold_copy(s):
        half = n_dp >> (s + 1)
        begin = starts[s] + (1 - faces[s]) * half
        return on_plane(grid.at[pl.ds(begin, half)], rs_bufs[s], s_rs.at[s], r_rs.at[s], partners[s])

    def fold_wait(s):
        half = n_dp >> (s + 1)
        begin = starts[s] + faces[s] * half
        fold_copy(s).wait_recv()
        for at in range(half):
            grid[begin + at] += rs_bufs[s][at]

    fold_copy(0).start()

    lane0 = lay.real // 128 * 128

    def add_block(at, carry):
        sides, fills = carry
        return sides + bk[at, 0:32, lane0 : lane0 + 128], fills + bk[at, 40:48, 0 : lay.real]

    sides, fills = lax.fori_loop(
        0, lay.n_dev, add_block, (jnp.zeros((32, 128), F32), jnp.zeros((8, lay.real), F32))
    )
    at = lay.real - lane0
    rows_all = float(lay.replay * lay.n_dev)
    centre = sides[0:24, at : at + 1] / rows_all
    scale = lax.rsqrt(sides[0:24, at + 1 : at + 2] / rows_all - centre * centre + 1e-6)
    total = sides[24:25, at : at + 1] + jnp.sum(fills[2:3, :], axis=1, keepdims=True)
    count[...] = jnp.broadcast_to(total, (8, 128))

    def dyn_bias(start, width):
        row = jnp.zeros((1, width), F32)
        for e in range(MEMBERS):
            row = jnp.where(me == e, bias[:, start + width * e : start + width * (e + 1)], row)
        return row

    @pl.when(is_dyn)
    def _():
        w1f[0] = jnp.zeros((32, HSAC), F32)
        w1f[0, 0:IN, 0:HDYN] = rounded(dyn_in[dyn_e])
        for at, piece in enumerate(pieces(dyn_bias(DB1, HDYN))):
            w1f[0, IN + at : IN + at + 1, 0:HDYN] = piece.astype(F32)
        w1t[0] = (0.5 * w1f[0].T).astype(BF16)
        rowbuf[...] = jnp.zeros_like(rowbuf)
        rowbuf[0:1, 0:HDYN] = dyn_bias(DB2, HDYN)
        head_row = dyn_bias(DB3, DOUT)
        rowbuf[1:2, 0:HALF] = head_row[:, 0:HALF]
        rowbuf[1:2, 24 : 24 + HALF] = head_row[:, HALF:DOUT]
        rowbuf[2:3, 0:HALF] = bias[:, MAXLV : MAXLV + HALF]
        rowbuf[3:4, 0:HALF] = bias[:, MINLV : MINLV + HALF]
        dcols[...] = rowbuf[...].T
        dpack[...] = jnp.zeros_like(dpack)
        dpack[0:HALF, 0:HDYN] = dyn_out[dyn_e, 0:HALF, :]
        dpack[24 : 24 + HALF, 0:HDYN] = dyn_out[dyn_e, HALF:DOUT, :]
        head = dpack[0:48, :].astype(BF16)
        head_back = (0.5 * rounded(dpack[0:48, :])).T.astype(BF16)
        dpack[...] = jnp.zeros_like(dpack)

        def wait_dyn(peer):
            dyn_h_copy(peer, peer).wait_recv()
            dyn_m_copy(peer, peer).wait_recv()

        line_peers(wait_dyn)
        dhg[z] = dyn_h[dyn_e]
        dmg[z] = dyn_m[dyn_e]
        dmat[...] = jnp.zeros_like(dmat)
        for block in range(n_blk):
            dmat[block * lay.drows : (block + 1) * lay.drows, 0:HDYN] = 0.5 * rounded(dhg[block])
        w2h[0] = dmat[...].astype(BF16)
        w2t[0] = dmat[...].T.astype(BF16)
        for ref in (dacc_h, dacc_w, dacc_o, dacc_m, dacc_b, dacc_l):
            ref[...] = jnp.zeros_like(ref)
        per = TILE // lay.real

        @pl.loop(0, lay.n_dev // per)
        def _(tile):
            for at in range(per):
                xt[:, at * lay.real : (at + 1) * lay.real] = bk[tile * per + at, :, 0 : lay.real]
            now = xt[0:24, :]
            later = xt[24:48, :]
            row24 = rows_of((24, TILE))
            scaled = jnp.where(row24 < IN, (now - centre) * scale, 1.0)
            inputs = jnp.concatenate([scaled, (rows_of((8, TILE)) < 2).astype(F32)], 0).astype(BF16)
            ones16 = jnp.ones((16, TILE), BF16)
            first, slope1 = gate(dot(w1t[0], inputs))
            first = first.astype(BF16)
            second, slope2 = gate(dot(w2t[0], first) + 0.5 * dcols[:, 0:1])
            second = second.astype(BF16)
            out = dot(head, second) + dcols[0:48, 1:2]
            used = row24 < HALF
            upper = dcols[0:24, 2:3]
            lower = dcols[0:24, 3:4]
            gap1 = upper - out[24:48]
            gap2 = upper - softplus(gap1) - lower
            log_var = lower + softplus(gap2)
            error = out[0:24] - jnp.where(row24 == OBS, now[23:24], later - now)
            inverse = jnp.exp(-log_var)
            weight = xt[42:43, :] * (xt[43:44, :] == me.astype(F32)).astype(F32)
            spread_term = error * error * inverse
            nll = jnp.sum(jnp.where(used, spread_term + log_var, 0.0), axis=0, keepdims=True)
            dacc_l[0:1, :] += weight * nll
            grad_mu = 2.0 * weight * error * inverse
            grad_lv = weight * (1.0 - spread_term)
            open1 = sigmoid(gap1)
            open2 = sigmoid(gap2)
            grad_lv1 = grad_lv * open2
            dacc_b[0] += jnp.where(used, grad_lv1 * (1.0 - open1), 0.0)
            dacc_b[1] += jnp.where(used, grad_lv * (1.0 - open2), 0.0)
            g3 = jnp.concatenate(
                [jnp.where(used, grad_mu, 0.0), jnp.where(used, grad_lv1 * open1, 0.0)], 0
            ).astype(BF16)
            dacc_o[...] += dot(g3, second, NT)
            dacc_m[...] += dot(ones16, g3, NT)
            g2 = (dot(head_back, g3) * slope2).astype(BF16)
            dacc_h[...] += dot(jnp.concatenate([first, ones16], 0), g2, NT)
            g1 = (dot(w2h[0], g2) * slope1).astype(BF16)
            dacc_w[...] += dot(inputs, g1, NT)

        dpack[D_IN : D_IN + 24, :] = dacc_w[0:24, :]
        dpack[D_OUT : D_OUT + HALF, :] = dacc_o[0:HALF, :]
        dpack[D_OUT + HALF : D_OUT + DOUT, :] = dacc_o[24 : 24 + HALF, :]
        dpack[D_B2 : D_B2 + 1, :] = dacc_h[HSAC : HSAC + 1, :]
        dpack[D_B3 : D_B3 + 1, 0:48] = dacc_m[0:1, :]
        lanes = lax.broadcasted_iota(jnp.int32, (24, 128), 1)
        bound = jnp.where(
            lanes == 0,
            jnp.sum(dacc_b[0], axis=1, keepdims=True),
            jnp.where(lanes == 1, jnp.sum(dacc_b[1], axis=1, keepdims=True), 0.0),
        )
        dpack[D_UP : D_UP + 2, 0:24] = bound.T[0:2, :]
        dpack[D_LOSS : D_LOSS + 1, 0:128] = jnp.broadcast_to(
            jnp.sum(dacc_l[0:1, :], axis=1, keepdims=True), (1, 128)
        )
        dyn_s[dyn_e] = dpack[...]

    def pack_copy(owner, peer):
        at = dyn_s.at[jnp.minimum(owner, MEMBERS - 1)]
        return on_plane(dpack, at, s_ds.at[peer], r_ds.at[owner], peer)

    def dyn_g_copy(owner, peer):
        at = dyn_g.at[jnp.minimum(owner, MEMBERS - 1)]
        return on_plane(drow_g, at, s_dg.at[peer], r_dg.at[owner], peer)

    def dyn_x_copy(owner, peer):
        at = dyn_x.at[jnp.minimum(owner, MEMBERS - 1)]
        return on_plane(drow_x, at, s_dx.at[peer], r_dx.at[owner], peer)

    def line_rows(ref):
        rows = ref[0 : lay.drows, 0:HDYN]
        for block in range(1, n_blk):
            rows = jnp.where(z == block, ref[block * lay.drows : (block + 1) * lay.drows, 0:HDYN], rows)
        return rows

    fold_wait(0)
    if bits > 1:
        fold_copy(1).start()

    @pl.when(is_dyn)
    def _():
        plane_peers(lambda peer: pack_copy(me, peer).start())
        rows = line_rows(dacc_h)
        drow_g[...] = rows
        dyn_g[dyn_e] = rows
        plane_peers(lambda peer: dyn_g_copy(me, peer).start())
        dmat[...] = jnp.zeros_like(dmat)
        for block in range(n_blk):
            at = slice(block * lay.drows, (block + 1) * lay.drows)
            dmat[at, 0:HDYN] = MOMENTUM * dmg[block] + dacc_h[at, 0:HDYN] / total
        moment = dmat[...]
        norm = jnp.sqrt(jnp.sum(jnp.sum(moment * moment, axis=1, keepdims=True), axis=0, keepdims=True))
        dmat[...] = moment / (norm + 1e-7)
        schulz(dmat, 2)

    for s in range(1, bits):
        fold_wait(s)
        if s + 1 < bits:
            fold_copy(s + 1).start()

    def line_first(owner, peer):
        if lay.split_z:
            src = grid.at[place, pl.ds(peer * lay.part, lay.part)]
        else:
            src = grid.at[place]
        return on_line(src, zr.at[owner], s_zr.at[peer], r_zr.at[owner], peer)

    def line_second(owner, peer):
        view = zf.at[pl.ds(owner * lay.part, lay.part)]
        return on_line(view, view, s_za.at[peer], r_za.at[owner], peer)

    line_peers(lambda peer: line_first(z, peer).start())

    @pl.when(is_dyn)
    def _():
        schulz(dmat, NS_ITERS - 2)
        rows = line_rows(dmat)
        drow_x[...] = rows
        dyn_x[dyn_e] = rows
        plane_peers(lambda peer: dyn_x_copy(me, peer).start())

    line_peers(lambda peer: line_first(peer, peer).wait_recv())
    if lay.split_z:
        zr[z] = grid[place, pl.ds(z * lay.part, lay.part)]
    else:
        zr[z] = grid[place]
    whole = zr[0]
    for block in range(1, n_blk):
        whole = whole + zr[block]
    if lay.split_z:
        zf[pl.ds(z * lay.part, lay.part)] = whole
        line_peers(lambda peer: line_second(z, peer).start())
        line_peers(lambda peer: line_second(peer, peer).wait_recv())
    else:
        zf[...] = whole

    def tile_copy(k, owner):
        return on_plane(zf.at[pl.ds(k * lay.mat, lay.mat)], mg.at[place], s_mg.at[k], r_mg.at[place], owner)

    for k in range(3):
        @pl.when(me != lay.owners[k])
        def _():
            tile_copy(k, lay.owners[k]).start()

    def small_copy(at, peer):
        return on_plane(
            zf.at[pl.ds(3 * lay.mat, lay.sml)], small.at[pl.ds(at * lay.sml, lay.sml)],
            s_pl.at[peer], r_pl.at[at], peer,
        )

    plane_peers(lambda peer: small_copy(place, peer).start())
    small[pl.ds(place * lay.sml, lay.sml)] = zf[3 * lay.mat :]

    def sac_g_copy(k, peer):
        src = grow.at[pl.ds(pl.multiple_of(z * lay.rows, lay.rows), lay.rows)]
        return on_plane(src, sac_g.at[k], s_sg.at[peer], r_sg.at[k], peer)

    def sac_x_copy(k, peer):
        src = mat.at[pl.ds(pl.multiple_of(z * lay.rows, lay.rows), lay.rows)]
        return on_plane(src, sac_x.at[k], s_sx.at[peer], r_sx.at[k], peer)

    mine_rows = pl.ds(pl.multiple_of(z * lay.rows, lay.rows), lay.rows)

    @pl.when(is_sac)
    def _():
        line_peers(lambda peer: sac_m_copy(peer, peer).wait_recv())
        smg[z] = sac_m[sac_k]
        mg[place] = zf[pl.ds(sac_k * lay.mat, lay.mat)]

        @pl.loop(1, n_dp)
        def _(off):
            at = lax.rem(place + off, n_dp)
            on_plane(mg.at[at], mg.at[at], s_mg.at[0], r_mg.at[at], me).wait_recv()

        for chunk in range(n_dp):
            tile = chunk * lay.mat
            side, row = tile // 32, tile % 32
            grow[row * 8 : (row + lay.mat) * 8, side * 128 : (side + 1) * 128] = mg[chunk].reshape(
                lay.mat * 8, 128
            )
        sac_g[sac_k] = grow[mine_rows, :]
        plane_peers(lambda peer: sac_g_copy(sac_k, peer).start())
        for block in range(n_blk):
            at = slice(block * lay.rows, (block + 1) * lay.rows)
            mat[at, :] = MOMENTUM * smg[block] + grow[at, :] / total
        moment = mat[...]
        norm = jnp.sqrt(jnp.sum(jnp.sum(moment * moment, axis=1, keepdims=True), axis=0, keepdims=True))
        mat[...] = moment / (norm + 1e-7)
        schulz(mat, NS_ITERS)
        sac_x[sac_k] = mat[mine_rows, :]
        plane_peers(lambda peer: sac_x_copy(sac_k, peer).start())

    @pl.loop(1, n_dp)
    def _(off):
        small_copy(lax.rem(place + off, n_dp), me).wait_recv()

    def from_members(peer):
        @pl.when(peer < MEMBERS)
        def _():
            pack_copy(peer, peer).wait_recv()
            dyn_g_copy(peer, peer).wait_recv()
            dyn_x_copy(peer, peer).wait_recv()

    plane_peers(from_members)
    for k in range(3):
        @pl.when(me != lay.owners[k])
        def _():
            sac_g_copy(k, me).wait_recv()
            sac_x_copy(k, me).wait_recv()

    def sent_on_line(peer):
        hidden_copy(z, 0, peer).wait_send()
        hidden_copy(z, 1, peer).wait_send()
        block_line(z, peer).wait_send()
        line_first(z, peer).wait_send()
        if lay.split_z:
            line_second(z, peer).wait_send()

        @pl.when(is_dyn)
        def _():
            dyn_h_copy(z, peer).wait_send()
            dyn_m_copy(z, peer).wait_send()

        @pl.when(is_sac)
        def _():
            sac_m_copy(z, peer).wait_send()

    line_peers(sent_on_line)

    def sent_on_plane(peer):
        list_copy(me, peer).wait_send()
        member_copy(me, peer).wait_send()
        block_plane(me, peer).wait_send()
        small_copy(place, peer).wait_send()

        @pl.when(is_dyn)
        def _():
            pack_copy(me, peer).wait_send()
            dyn_g_copy(me, peer).wait_send()
            dyn_x_copy(me, peer).wait_send()

        @pl.when(is_sac)
        def _():
            sac_g_copy(sac_k, peer).wait_send()
            sac_x_copy(sac_k, peer).wait_send()

    plane_peers(sent_on_plane)
    for s in range(bits):
        fold_copy(s).wait_send()
    for k in range(3):
        @pl.when(me != lay.owners[k])
        def _():
            tile_copy(k, lay.owners[k]).wait_send()


def adamw(weights, first, second, gradient):
    first = BETA_FIRST * first + (1.0 - BETA_FIRST) * gradient
    second = BETA_SECOND * second + (1.0 - BETA_SECOND) * gradient * gradient
    first_hat = first / (1.0 - BETA_FIRST**STEP)
    second_hat = second / (1.0 - BETA_SECOND**STEP)
    step = first_hat / (jnp.sqrt(second_hat) + 1e-8) + ADAM_DECAY * weights
    return weights - ADAM_RATE * step, first, second


def update_kernel(*refs):
    (
        sac_g, sac_x, dyn_g, dyn_x, dyn_s, small, count, sac_h, sac_m, dyn_h, dyn_m,
        ci, ci_m, ci_v, ai, ai_m, ai_v, di, di_m, di_v, co, co_m, co_v, ao, ao_m, ao_v,
        do, do_m, do_v, bi, bi_m, bi_v,
        sac_new, sac_mom, dyn_new, dyn_mom, ci_n, ci_mn, ci_vn, ai_n, ai_mn, ai_vn, di_n, di_mn,
        di_vn, co_n, co_mn, co_vn, ao_n, ao_mn, ao_vn, do_n, do_mn, do_vn, bi_n, bi_mn, bi_vn,
        loss, counted, bg,
    ) = refs
    total = count[0:1, 0:1]
    sac_mom[...] = MOMENTUM * sac_m[...] + sac_g[...] / total.reshape(1, 1, 1)
    sac_new[...] = sac_h[...] * (1.0 - MUON_RATE * MUON_DECAY) - MUON_RATE * sac_x[...]
    dyn_mom[...] = MOMENTUM * dyn_m[...] + dyn_g[...] / total.reshape(1, 1, 1)
    dyn_new[...] = dyn_h[...] * (1.0 - MUON_RATE * MUON_DECAY) - MUON_RATE * dyn_x[...]

    def rows(row, number):
        sides = []
        for side in range(2):
            at = side * (R_SMALL // 8) + row // 8
            sides.append(small[at : at + -(-number // 8)].reshape(-1, 128))
        return jnp.concatenate(sides, 1)

    def store(outs, at, values):
        for out, value in zip(outs, values):
            out[at] = value

    outs = (ci_n, ci_mn, ci_vn)
    for k in range(2):
        at = (slice(None), k, slice(None))
        grad = rows(R_IN + 24 * k, 24)
        bg[:, CB1 + HSAC * k : CB1 + HSAC * (k + 1)] = grad[IN : IN + 1]
        store(outs, at, adamw(ci[at], ci_m[at], ci_v[at], grad[0:IN] / total))
    grad = rows(R_IN + 48, 24)
    bg[:, AB1 : AB1 + HSAC] = grad[IN : IN + 1]
    store((ai_n, ai_mn, ai_vn), ..., adamw(ai[...], ai_m[...], ai_v[...], grad[0:OBS] / total))
    grad = rows(R_HEAD, 16)
    for at, row in ((slice(0, ACT), slice(1, 1 + ACT)), (slice(ACT, 2 * ACT), slice(9, 9 + ACT))):
        store((ao_n, ao_mn, ao_vn), at, adamw(ao[at], ao_m[at], ao_v[at], grad[row] / total))
    grad = rows(R_OUT, 8)
    store((co_n, co_mn, co_vn), ..., adamw(co[...], co_m[...], co_v[...], grad[0:2] / total))
    bg[:, CB2 : CB2 + HSAC] = grad[2:3]
    bg[:, CB2 + HSAC : CB2 + 2 * HSAC] = grad[3:4]
    bg[:, AB2 : AB2 + HSAC] = grad[4:5]
    grad = rows(R_MISC, 8)
    bg[:, CB3 : CB3 + 1] = grad[0:1, 16:17]
    bg[:, CB3 + 1 : CB3 + 2] = grad[0:1, 32:33]
    bg[:, AB3 : AB3 + ACT] = grad[0:1, 1 : 1 + ACT]
    bg[:, AB3 + ACT : AB3 + 2 * ACT] = grad[0:1, 9 : 9 + ACT]
    bg[:, LOGA : LOGA + 1] = -grad[0:1, 65:66]
    total_loss = grad[0:1, 64:65]
    up = jnp.zeros((1, HALF), F32)
    low = jnp.zeros((1, HALF), F32)
    for e in range(MEMBERS):
        pack = dyn_s[e]
        total_loss = total_loss + pack[D_LOSS : D_LOSS + 1, 0:1]
        up = up + pack[D_UP : D_UP + 1, 0:HALF]
        low = low + pack[D_LOW : D_LOW + 1, 0:HALF]
        bg[:, DB1 + HDYN * e : DB1 + HDYN * (e + 1)] = pack[IN : IN + 1, 0:HDYN]
        bg[:, DB2 + HDYN * e : DB2 + HDYN * (e + 1)] = pack[D_B2 : D_B2 + 1, 0:HDYN]
        bg[:, DB3 + DOUT * e : DB3 + DOUT * e + HALF] = pack[D_B3 : D_B3 + 1, 0:HALF]
        bg[:, DB3 + DOUT * e + HALF : DB3 + DOUT * (e + 1)] = pack[D_B3 : D_B3 + 1, 24 : 24 + HALF]
        grad = pack[0:IN, 0:HDYN] / total
        store((di_n, di_mn, di_vn), e, adamw(di[e], di_m[e], di_v[e], grad))
        grad = pack[D_OUT : D_OUT + DOUT, 0:HDYN] / total
        store((do_n, do_mn, do_vn), e, adamw(do[e], do_m[e], do_v[e], grad))
    bg[:, MAXLV : MAXLV + HALF] = up
    bg[:, MINLV : MINLV + HALF] = low
    lane = lax.broadcasted_iota(jnp.int32, (1, NB), 1)
    bounds = jnp.where(
        jnp.logical_and(lane >= MAXLV, lane < MINLV),
        BOUND_WEIGHT,
        jnp.where(jnp.logical_and(lane >= MINLV, lane < LOGA), -BOUND_WEIGHT, 0.0),
    )
    grad = bg[...] / total + bounds
    store((bi_n, bi_mn, bi_vn), ..., adamw(bi[...], bi_m[...], bi_v[...], grad))
    loss[...] = total_loss
    counted[...] = total


def shards(
    lay, replay, model_rows, requests, member_of, model_live, noise, sac_hidden, sac_hidden_mom,
    dyn_hidden, dyn_hidden_mom, crit_in, crit_in_m, crit_in_v, act_in, act_in_m, act_in_v, dyn_in,
    dyn_in_m, dyn_in_v, crit_out, crit_out_m, crit_out_v, act_out, act_out_m, act_out_v, dyn_out,
    dyn_out_m, dyn_out_v, biases, biases_m, biases_v, targ_in, targ_hidden, targ_out, targ_bias,
):
    n_dp, n_blk, bits = lay.n_dp, lay.n_blk, lay.bits
    spec = pl.BlockSpec(memory_space=pltpu.VMEM)

    def flip(value):
        return jnp.transpose(value, (1, 0, 2))

    def swap(value):
        return jnp.swapaxes(value, -1, -2)

    def row(value):
        return value.reshape(1, -1)

    inputs = (
        replay, model_rows, requests, member_of, row(model_live), jnp.transpose(noise, (2, 0, 1)),
        sac_hidden, sac_hidden_mom, dyn_hidden, dyn_hidden_mom, flip(crit_in), act_in, dyn_in,
        crit_out, swap(act_out), swap(dyn_out), row(biases), flip(targ_in), targ_hidden, targ_out,
        targ_bias,
    )
    shape = jax.ShapeDtypeStruct
    rows, drows = lay.rows, lay.drows
    out_shape = (
        shape((3, rows, HSAC), F32),
        shape((3, rows, HSAC), F32),
        shape((MEMBERS, drows, HDYN), F32),
        shape((MEMBERS, drows, HDYN), F32),
        shape((MEMBERS, D_ROWS, HSAC), F32),
        shape((32, 8, 128), F32),
        shape((8, 128), F32),
    )

    def vm(*dims, kind=F32):
        return pltpu.VMEM(dims, kind)

    def sems(*dims):
        return [pltpu.SemaphoreType.DMA(dims), pltpu.SemaphoreType.DMA(dims)]

    scratch = [
        vm(n_blk, 3, rows, HSAC, kind=BF16),
        vm(n_dp, n_dp, CAP, kind=jnp.int32),
        vm(n_dp, n_dp, CAP, kind=jnp.int32),
        vm(n_blk, drows, HDYN),
        vm(n_blk, drows, HDYN),
        vm(n_blk, rows, HSAC),
        vm(lay.n_dev, 48, lay.width),
        vm(56, lay.batch),
        vm(2, 8, lay.batch),
        vm(5, 32, HSAC),
        vm(5, HSAC, 32, kind=BF16),
        vm(2, 16, HSAC, kind=BF16),
        vm(5, HSAC, HSAC, kind=BF16),
        vm(3, HSAC, HSAC, kind=BF16),
        vm(5, 16, HSAC, kind=BF16),
        vm(HSAC, 16, kind=BF16),
        vm(16, HSAC),
        vm(8, HSAC),
        vm(HSAC, 8),
        vm(128, 8),
        vm(3, HSAC + 16, HSAC),
        vm(3, 32, HSAC),
        vm(2, 16, HSAC),
        vm(16, HSAC),
        vm(16, 48),
        vm(8, TILE),
        vm(n_dp, lay.chunk, 8, 128),
        vm(n_blk, lay.part, 8, 128),
        vm(lay.chunk, 8, 128),
        vm(n_dp, lay.mat, 8, 128),
        vm(HSAC, HSAC),
        vm(HSAC, HSAC),
        vm(8, 128),
        vm(HSAC, 8),
        vm(HSAC + 16, HSAC),
        vm(32, HSAC),
        vm(48, HSAC),
        vm(16, 48),
        vm(2, 24, TILE),
        vm(8, TILE),
        vm(48, TILE),
        vm(HSAC, HSAC),
        vm(D_ROWS, HSAC),
        vm(drows, HDYN),
        vm(drows, HDYN),
    ]
    scratch += [vm(n_dp >> (s + 1), lay.chunk, 8, 128) for s in range(bits)]
    scratch += sems(2, n_blk)
    scratch += sems(n_dp) + sems(n_dp)
    scratch += sems(n_blk) + sems(n_blk) + sems(n_blk)
    scratch += sems(n_blk) + sems(n_dp)
    scratch += sems(bits) + sems(n_blk) + sems(n_blk) + sems(n_dp)
    scratch += [pltpu.SemaphoreType.DMA((3,)), pltpu.SemaphoreType.DMA((n_dp,))]
    scratch += sems(n_dp) + sems(n_dp) + sems(n_dp)
    scratch += 2 * [pltpu.SemaphoreType.DMA((n_dp,)), pltpu.SemaphoreType.DMA((3,))]
    gathered = pl.pallas_call(
        functools.partial(main_kernel, lay),
        out_shape=out_shape,
        in_specs=[spec] * len(inputs),
        out_specs=[spec] * len(out_shape),
        scratch_shapes=scratch,
        compiler_params=pltpu.CompilerParams(
            collective_id=0, has_side_effects=True, vmem_limit_bytes=60 * 2**20
        ),
        name="step",
    )(*inputs)
    params = (
        sac_hidden, sac_hidden_mom, dyn_hidden, dyn_hidden_mom,
        flip(crit_in), flip(crit_in_m), flip(crit_in_v), act_in, act_in_m, act_in_v,
        dyn_in, dyn_in_m, dyn_in_v, crit_out, crit_out_m, crit_out_v,
        swap(act_out), swap(act_out_m), swap(act_out_v),
        swap(dyn_out), swap(dyn_out_m), swap(dyn_out_v), row(biases), row(biases_m), row(biases_v),
    )
    new_shape = [shape(params[i].shape, F32) for i in (0, 1, 2, 3)]
    new_shape += [shape(params[i].shape, F32) for i in range(4, 25)]
    new_shape += [shape((1, 1), F32)] * 2
    out = pl.pallas_call(
        update_kernel,
        out_shape=tuple(new_shape),
        in_specs=[spec] * (len(gathered) + len(params)),
        out_specs=[spec] * len(new_shape),
        scratch_shapes=[vm(1, NB)],
        compiler_params=pltpu.CompilerParams(vmem_limit_bytes=40 * 2**20),
        name="update",
    )(*gathered, *params)
    out = list(out)
    for at in (4, 5, 6):
        out[at] = flip(out[at])
    for at in (16, 17, 18, 19, 20, 21):
        out[at] = swap(out[at])
    for at in (22, 23, 24):
        out[at] = out[at].reshape(-1)
    for at in (25, 26):
        out[at] = out[at].reshape(())
    return tuple(out)


def solution(mesh):
    both = ("dp", "blk")
    sharded = (
        P(None, both), P(None, both), P(both, None), P(both, None), P(both), P(None, both, None),
    )
    hidden = (P(None, "blk", None),) * 4

    def step(replay, model_rows, *others):
        lay = Layout(mesh, replay.shape[1], model_rows.shape[1])
        return shards(lay, replay, model_rows, *others)

    return jax.shard_map(
        step,
        mesh=mesh,
        in_specs=sharded + hidden + (P(),) * 25,
        out_specs=hidden + (P(),) * 23,
        check_vma=False,
    )
```

time: 536 us -> 111 us (0.21)
  waiting for transfers between devices: 202 us -> 0 us
  blocking collectives: 145 us -> 0 us
  Pallas kernels: 0 us -> 98.1 us
  matrix products: 71.4 us -> 0 us
  other arithmetic: 49.9 us -> 1.95 us
  local copies, waits for them, and re-layouts: 33.6 us -> 9.16 us
  between operations: 21 us -> 1.07 us
  starting transfers between devices: 9.11 us -> 0 us
    psum x2 -> x0, waiting for transfers between devices: 113 us -> none  [the longest x1 57.2 us: shards(): lax.psum((grads[2], grads[3], grads[4], grads[5], grads[6], grads[7], gra...]
    pallas_call x0 -> x2, Pallas kernels: none -> 98.1 us  [the longest x1 96.3 us: shards(): pl.pallas_call(functools.partial(main_kernel, lay), out_shape=out_shape,...]
    psum x2 -> x0, blocking collectives: 83 us -> none  [shards(): lax.psum((part_total, part_square, local_count), ('dp', 'blk'))]
    dot_general x64 -> x0, matrix products: 71.4 us -> none  [the longest x34 23.5 us: dense_layer(): jnp.matmul(value_round(inputs), value_round(weights), precision=PRECISE)]
    unnamed x6 -> x0, waiting for transfers between devices: 64.8 us -> none
    all_gather x3 -> x0, blocking collectives: 61.8 us -> none  [the longest x1 27.2 us: shards(): lax.all_gather(sac_moment, 'blk', axis=1, tiled=True)]
    reduce_scatter x1 -> x0, waiting for transfers between devices: 23.7 us -> none  [shards(): lax.psum_scatter(grads[0], 'blk', scatter_dimension=1, tiled=True)]
    reduce_sum x21 -> x0, other arithmetic: 17.8 us -> none  [the longest x9 7.04 us: dense_layer(): jnp.matmul(value_round(inputs), value_round(weights), precision=PRECISE)]
  transfers between devices with their start and end apart: 7 -> 0, of which waited for: 5 -> 0; matrix products, arithmetic and copies ran while one was open for 15% -> 0% of each run, Pallas kernels for 0% -> 0%
where the time goes in v1:
time: 111 us; the launch traced here: 110 us
  Pallas kernels  98.1 us (88%)
  local copies, waits for them, and re-layouts  9.16 us (8%)
  other arithmetic  1.95 us (2%)
    pallas_call x1, Pallas kernels, shards(): pl.pallas_call(functools.partial(main_kernel, lay), out_shape=out_shape,...  96.3 us
    unnamed x66, local copies, waits for them, and re-layouts  7.21 us

profile of v1, /device:TPU:0, one launch (start us, length us, event | category | flops | bytes accessed | tf_op | source)
XLA Modules:
  0.0 110.3 jit_solution(17355334084721390445)
XLA Ops:
  0.7 0.0 copy-start.30
  0.7 1.3 %reshape.82.refs_4_ = s32[1,1216]{1,0:T(1,128)} reshape(s32[1216]{0:T(1024)} %param.39) | data formatting | bytes 9728 | tf_op jit(solution)/shard_map/reshape | solution.py:939
  2.0 0.0 copy-done.30
  2.0 0.6 reshape.83.refs_16_.refs_29_
  2.6 0.1 copy-done.31
  2.7 0.7 copy-done.32
  3.5 0.0 copy-start
  3.5 0.0 copy-start.1
  3.5 0.0 copy-start.2
  3.5 0.0 copy-start.3
  3.5 0.0 copy-start.4
  3.5 0.0 copy-start.5
  3.5 0.0 copy-start.9
  3.5 0.0 copy-start.10
  3.6 0.0 copy-start.13
  3.6 0.0 copy-start.14
  3.6 0.0 copy-start.15
  3.6 0.0 copy-start.16
  3.6 0.0 copy-start.18
  3.6 0.0 copy-start.19
  3.6 0.0 copy-start.20
  3.6 0.0 copy-start.21
  3.6 0.0 copy-start.22
  3.7 0.0 copy-start.23
  3.7 0.0 copy-start.24
  3.7 0.0 copy-start.25
  3.7 0.0 copy-start.28
  3.7 0.0 copy-start.29
  3.7 96.3 %step.1 = (f32[3,64,256]{2,1,0:T(8,128)}, f32[3,64,256]{2,1,0:T(8,128)}, f32[7,50,200]{2,1,0:T(8,128)}, f32[7,50,200]{2,1,0:T(8,128)}, f32[7,72,256]{2,1,0:T(8,1...) custom-call(f32[42,3648]{1,0:T(8,128)} %refs_0_.1, f32[42,1216]{1,0:T(8,128)} %refs_1_.1, s32[8,8]{1,0:T(8,128)} %refs_2_.1, ...), custom_call_target="tpu_custom_call" | custom-call | tf_op jit(solution)/shard_map/step/pallas_call | solution.py:1021
  100.0 0.0 copy-start.27
  100.0 0.0 copy-start.26
  100.0 0.0 copy-done
  100.0 0.0 copy-done.1
  100.0 0.0 copy-done.2
  100.1 0.0 copy-done.3
  100.1 0.0 copy-done.4
  100.1 0.0 copy-done.5
  100.1 0.0 copy-done.9
  100.1 0.0 copy-done.10
  100.1 0.0 copy-done.13
  100.1 0.0 copy-done.14
  100.1 0.0 copy-done.15
  100.1 0.0 copy-done.16
  100.1 0.0 copy-done.18
  100.2 0.0 copy-done.19
  100.2 0.0 copy-done.20
  100.2 0.0 copy-done.21
  100.2 0.0 copy-done.22
  100.2 0.0 copy-done.23
  100.2 0.0 copy-done.24
  100.2 0.0 copy-done.25
  100.2 0.0 copy-done.28
  100.2 0.4 copy-done.27
  100.7 0.0 copy-done.26
  100.7 1.0 copy-done.6
  101.7 1.0 copy-done.7
  102.7 1.0 copy-done.8
  103.7 0.9 copy-done.11
  104.7 0.9 copy-done.12
  105.6 0.9 copy-done.17
  106.5 1.8 %update.1 = (f32[3,64,256]{2,1,0:T(8,128)}, f32[3,64,256]{2,1,0:T(8,128)}, f32[7,50,200]{2,1,0:T(8,128)}, f32[7,50,200]{2,1,0:T(8,128)}, f32[23,2,256]{2,1,0:T(2...) custom-call(f32[3,64,256]{2,1,0:T(8,128)S(1)} %copy-done.11, ...), custom_call_target="tpu_custom_call" | custom-call | tf_op jit(solution)/shard_map/update/pallas_call | solution.py:1042
  108.3 0.7 reduce
  109.0 0.7 reduce.1
  109.6 0.7 reduce.2
  (11 shorter events, 0.0 us)
Async XLA Ops:
  0.7 1.3 %copy-start.30 = (f32[4639]{0:T(1024)S(1)}, f32[4639]{0:T(1024)}, u32[]{:S(2)}) copy-start(f32[4639]{0:T(1024)} %param.63) | copy-start | bytes 55672
  2.0 0.7 copy-start.31
  2.7 0.7 copy-start.32
  3.5 96.6 %copy-start = (f32[7,50,200]{2,1,0:T(8,128)S(1)}, f32[7,50,200]{2,1,0:T(8,128)}, u32[]{:S(2)}) copy-start(f32[7,50,200]{2,1,0:T(8,128)} %refs_9_.3) | copy-start | bytes 840004
  3.5 96.6 %copy-start.1 = (f32[7,50,200]{2,1,0:T(8,128)S(1)}, f32[7,50,200]{2,1,0:T(8,128)}, u32[]{:S(2)}) copy-start(f32[7,50,200]{2,1,0:T(8,128)} %refs_10_.1) | copy-start | bytes 840004
  3.5 96.6 %copy-start.2 = (f32[7,200,36]{1,2,0:T(8,128)S(1)}, f32[7,200,36]{1,2,0:T(8,128)}, u32[]{:S(2)}) copy-start(f32[7,200,36]{1,2,0:T(8,128)} %param.60) | copy-start | bytes 604804
  3.5 96.6 %copy-start.3 = (f32[3,64,256]{2,1,0:T(8,128)S(1)}, f32[3,64,256]{2,1,0:T(8,128)}, u32[]{:S(2)}) copy-start(f32[3,64,256]{2,1,0:T(8,128)} %refs_7_.3) | copy-start | bytes 589828
  3.5 96.6 %copy-start.4 = (f32[3,64,256]{2,1,0:T(8,128)S(1)}, f32[3,64,256]{2,1,0:T(8,128)}, u32[]{:S(2)}) copy-start(f32[3,64,256]{2,1,0:T(8,128)} %refs_8_.3) | copy-start | bytes 589828
  3.5 96.6 %copy-start.5 = (f32[7,23,200]{2,1,0:T(8,128)S(1)}, f32[7,23,200]{2,1,0:T(8,128)}, u32[]{:S(2)}) copy-start(f32[7,23,200]{2,1,0:T(8,128)} %refs_17_.1) | copy-start | bytes 386404
  3.5 96.6 %copy-start.9 = (f32[7,200,36]{1,2,0:T(8,128)S(1)}, f32[7,200,36]{1,2,0:T(8,128)}, u32[]{:S(2)}) copy-start(f32[7,200,36]{1,2,0:T(8,128)} %param.61) | copy-start | bytes 604804
  3.5 96.6 %copy-start.10 = (f32[7,200,36]{1,2,0:T(8,128)S(1)}, f32[7,200,36]{1,2,0:T(8,128)}, u32[]{:S(2)}) copy-start(f32[7,200,36]{1,2,0:T(8,128)} %param.62) | copy-start | bytes 604804
  3.6 96.6 %copy-start.13 = (f32[2,23,256]{2,0,1:T(2,128)S(1)}, f32[2,23,256]{2,0,1:T(2,128)}, u32[]{:S(2)}) copy-start(f32[2,23,256]{2,0,1:T(2,128)} %param.45) | copy-start | bytes 141316
  3.6 96.6 %copy-start.14 = (f32[7,23,200]{2,1,0:T(8,128)S(1)}, f32[7,23,200]{2,1,0:T(8,128)}, u32[]{:S(2)}) copy-start(f32[7,23,200]{2,1,0:T(8,128)} %refs_18_.3) | copy-start | bytes 386404
  3.6 96.6 %copy-start.15 = (f32[7,23,200]{2,1,0:T(8,128)S(1)}, f32[7,23,200]{2,1,0:T(8,128)}, u32[]{:S(2)}) copy-start(f32[7,23,200]{2,1,0:T(8,128)} %refs_19_.3) | copy-start | bytes 386404
  3.6 96.6 %copy-start.16 = (f32[1,4639]{1,0:T(1,128)S(1)}, f32[1,4639]{1,0:T(1,128)}, u32[]{:S(2)}) copy-start(f32[1,4639]{1,0:T(1,128)} %reshape.83.refs_16_.refs_29_) | copy-start | bytes 55672
  3.6 96.6 %copy-start.18 = (f32[17,256]{1,0:T(8,128)S(1)}, f32[17,256]{1,0:T(8,128)}, u32[]{:S(2)}) copy-start(f32[17,256]{1,0:T(8,128)} %refs_14_.1) | copy-start | bytes 52228
  3.6 96.5 %copy-start.19 = (f32[256,12]{0,1:T(8,128)S(1)}, f32[256,12]{0,1:T(8,128)}, u32[]{:S(2)}) copy-start(f32[256,12]{0,1:T(8,128)} %param.57) | copy-start | bytes 36868
  3.6 96.5 %copy-start.20 = (f32[2,23,256]{2,0,1:T(2,128)S(1)}, f32[2,23,256]{2,0,1:T(2,128)}, u32[]{:S(2)}) copy-start(f32[2,23,256]{2,0,1:T(2,128)} %param.46) | copy-start | bytes 141316
  3.6 96.5 %copy-start.21 = (f32[2,23,256]{2,0,1:T(2,128)S(1)}, f32[2,23,256]{2,0,1:T(2,128)}, u32[]{:S(2)}) copy-start(f32[2,23,256]{2,0,1:T(2,128)} %param.47) | copy-start | bytes 141316
  3.6 96.5 %copy-start.22 = (f32[17,256]{1,0:T(8,128)S(1)}, f32[17,256]{1,0:T(8,128)}, u32[]{:S(2)}) copy-start(f32[17,256]{1,0:T(8,128)} %refs_15_.1) | copy-start | bytes 52228
  3.7 96.5 %copy-start.23 = (f32[17,256]{1,0:T(8,128)S(1)}, f32[17,256]{1,0:T(8,128)}, u32[]{:S(2)}) copy-start(f32[17,256]{1,0:T(8,128)} %refs_16_.1) | copy-start | bytes 52228
  3.7 96.5 %copy-start.24 = (f32[256,12]{0,1:T(8,128)S(1)}, f32[256,12]{0,1:T(8,128)}, u32[]{:S(2)}) copy-start(f32[256,12]{0,1:T(8,128)} %param.58) | copy-start | bytes 36868
  3.7 96.5 %copy-start.25 = (f32[256,12]{0,1:T(8,128)S(1)}, f32[256,12]{0,1:T(8,128)}, u32[]{:S(2)}) copy-start(f32[256,12]{0,1:T(8,128)} %param.59) | copy-start | bytes 36868
  3.7 96.5 %copy-start.28 = (f32[2,256]{1,0:T(2,128)S(1)}, f32[2,256]{1,0:T(2,128)}, u32[]{:S(2)}) copy-start(f32[2,256]{1,0:T(2,128)} %refs_21_.1) | copy-start | bytes 6148
  3.7 96.5 %copy-start.29 = (f32[2,256]{1,0:T(2,128)S(1)}, f32[2,256]{1,0:T(2,128)}, u32[]{:S(2)}) copy-start(f32[2,256]{1,0:T(2,128)} %refs_22_.1) | copy-start | bytes 6148
  100.0 0.7 copy-start.27
  100.0 0.7 copy-start.26
  100.7 1.0 copy-start.6
  101.7 1.0 copy-start.7
  102.7 1.0 copy-start.8
  103.7 0.9 copy-start.11
  104.7 0.9 copy-start.12
  105.6 0.9 copy-start.17

commit v2 on v1

--- a/solution.py
+++ b/solution.py
@@ -91,15 +91,26 @@
     return lax.broadcasted_iota(jnp.int32, shape, 0)
 
 
-def schulz(ref, steps):
+def schulz(refs, steps):
     @pl.loop(0, steps)
     def _(step):
-        matrix = ref[...]
-        parts = split(matrix)
-        gram = product(parts, parts, NT)
-        halves = split(gram)
-        blend = COEF_CUBIC * gram + COEF_QUINTIC * product(halves, halves)
-        ref[...] = COEF_LINEAR * matrix + product(split(blend), parts)
+        matrices = [ref[...] for ref in refs]
+        parts = [split(matrix) for matrix in matrices]
+        grams = [product(part, part, NT) for part in parts]
+        halves = [split(gram) for gram in grams]
+        squares = [product(half, half) for half in halves]
+        blends = [
+            split(COEF_CUBIC * gram + COEF_QUINTIC * square) for gram, square in zip(grams, squares)
+        ]
+        moved = [product(blend, part) for blend, part in zip(blends, parts)]
+        for ref, matrix, move in zip(refs, matrices, moved):
+            ref[...] = COEF_LINEAR * matrix + move
+
+
+def normalise(ref):
+    moment = ref[...]
+    norm = jnp.sqrt(jnp.sum(jnp.sum(moment * moment, axis=1, keepdims=True), axis=0, keepdims=True))
+    ref[...] = moment / (norm + 1e-7)
 
 
 class Layout:
@@ -117,10 +128,12 @@
         self.drows = HDYN // self.n_blk
         self.mat = 64 // self.n_dp
         self.sml = 32 // self.n_dp
-        self.chunk = 3 * self.mat + self.sml
-        self.split_z = self.chunk % self.n_blk == 0
-        self.part = self.chunk // self.n_blk if self.split_z else self.chunk
-        self.owners = [self.n_dp - 1 - 2 * k for k in range(3)]
+        self.chunks = (2 * self.mat, self.mat + self.sml)
+        self.split_z = all(chunk % self.n_blk == 0 for chunk in self.chunks)
+        self.owners = [self.n_dp - 5, self.n_dp - 3, self.n_dp - 1]
+
+    def part(self, group):
+        return self.chunks[group] // self.n_blk if self.split_z else self.chunks[group]
 
 
 def main_kernel(lay, *refs):
@@ -129,24 +142,29 @@
         dyn_in, crit_out, act_out, dyn_out, biases, targ_in, targ_hidden, targ_out, targ_bias,
         sac_g, sac_x, dyn_g, dyn_x, dyn_s, small, count,
         wg, asked, owned, dhg, dmg, smg, bk, xs, nz, w1f, w1t, w1n, w2t, w2h, heads, head_t, head_f,
-        rowbuf, cols, headcol, acc_h, acc_w, acc_c, acc_a, acc_m, acc_l, grid, zr, zf, mg, mat,
-        grow, xrow, dcols, dacc_h, dacc_w, dacc_o, dacc_m, dacc_b, dacc_l, xt, dmat, dpack, drow_g,
-        drow_x, *rest,
+        rowbuf, cols, headcol, acc_h, acc_w, acc_c, acc_a, acc_m, acc_l, grid_c, grid_a, zr_c, zr_a,
+        zf_c, zf_a, mg, mat, grow, dcols, dacc_h, dacc_w, dacc_o, dacc_m, dacc_b, dacc_l, xt, dmat,
+        dpack, drow_g, drow_x, bias, dhead, dhead_t, *rest,
     ) = refs
-    rs_bufs = rest[: lay.bits]
+    bits = lay.bits
+    bufs = (rest[:bits], rest[bits : 2 * bits])
     (
-        s_w, r_w, s_q, r_q, s_p, r_p, s_dh, r_dh, s_dm, r_dm, s_sm, r_sm, s_bz, r_bz, s_bp, r_bp,
-        s_rs, r_rs, s_zr, r_zr, s_za, r_za, s_pl, r_pl, s_mg, r_mg, s_ds, r_ds, s_dg, r_dg, s_dx,
-        r_dx, s_sg, r_sg, s_sx, r_sx,
-    ) = rest[lay.bits :]
-    n_dp, n_blk, bits = lay.n_dp, lay.n_blk, lay.bits
+        s_w, r_w, s_q, r_q, s_p, r_p, s_dh, r_dh, s_dm, r_dm, s_sm, r_sm, s_bz, r_bz, s_bo, r_bo,
+        s_bp, r_bp, s_rs, r_rs, s_zr, r_zr, s_za, r_za, s_pl, r_pl, s_mg, r_mg, s_ds, r_ds, s_dg,
+        r_dg, s_dx, r_dx, f_ds, f_dg, f_dx, s_sg, r_sg, s_sx, r_sx,
+    ) = rest[2 * bits :]
+    grids, zrs, zfs = (grid_c, grid_a), (zr_c, zr_a), (zf_c, zf_a)
+    n_dp, n_blk = lay.n_dp, lay.n_blk
     me = lax.axis_index("dp")
     z = lax.axis_index("blk")
+    core = lax.rem(me, 2)
+    sibling = me + 1 - 2 * core
     is_dyn = me < MEMBERS
-    owner_k = (n_dp - 1 - me) // 2
-    is_sac = jnp.logical_and(lax.rem(n_dp - 1 - me, 2) == 0, owner_k < 3)
-    sac_k = jnp.minimum(owner_k, 2)
     dyn_e = jnp.minimum(me, MEMBERS - 1)
+    is_actor = me == lay.owners[2]
+    is_critic = jnp.logical_or(me == lay.owners[0], me == lay.owners[1])
+    is_sac = jnp.logical_or(is_actor, is_critic)
+    sac_k = jnp.clip((me - lay.owners[0]) // 2, 0, 2)
 
     def on_plane(src, dst, ssem, rsem, peer):
         return pltpu.make_async_remote_copy(
@@ -165,6 +183,11 @@
         def _(off):
             body(lax.rem(me + off, n_dp))
 
+    def like_peers(body):
+        @pl.loop(1, n_dp // 2)
+        def _(off):
+            body(lax.rem(me + 2 * off, n_dp))
+
     def line_peers(body):
         @pl.loop(1, n_blk)
         def _(off):
@@ -204,13 +227,14 @@
     def sac_m_copy(owner, peer):
         return on_line(sac_m.at[sac_k], smg.at[owner], s_sm.at[peer], r_sm.at[owner], peer)
 
+    alive = live[...].astype(F32).reshape(1, lay.model)
+    bias[...] = biases[...].reshape(1, NB)
     xs[42:56, :] = jnp.zeros((14, lay.batch), F32)
     xs[0:FEAT, lay.real : lay.batch] = model[...]
-    xs[42:43, lay.real : lay.batch] = live[...].astype(F32)
+    xs[42:43, lay.real : lay.batch] = alive
     nz[...] = jnp.zeros_like(nz)
     for which in range(2):
         nz[which, 1:7, :] = noise[:, which, :]
-    bias = biases
     firsts = [
         (targ_in[:, 0, :], targ_bias[0:1, 0:HSAC]),
         (targ_in[:, 1, :], targ_bias[1:2, 0:HSAC]),
@@ -257,7 +281,7 @@
     data = replay[...]
     sums = jnp.sum(data[0:24], axis=1, keepdims=True)
     squares = jnp.sum(data[0:24] * data[0:24], axis=1, keepdims=True)
-    living = jnp.sum(live[...].astype(F32), axis=1, keepdims=True)
+    living = jnp.sum(alive, axis=1, keepdims=True)
 
     def wait_lists(peer):
         list_copy(peer, peer).wait_recv()
@@ -285,7 +309,7 @@
     hot = (rows_of((lay.replay, lay.real)) == wanted).astype(BF16)
     high, middle, low = pieces(data)
     picked = dot(high, hot) + dot(middle, hot) + dot(low, hot)
-    mine = me * n_blk + z
+    mine = me * n_blk
     bk[mine, 0:FEAT, 0 : lay.real] = picked
     bk[mine, 42:43, 0 : lay.real] = (slots >= 0.0).astype(F32)
     bk[mine, 43:44, 0 : lay.real] = in_lanes(owned)
@@ -295,14 +319,27 @@
     bk[mine, 0:24, lay.real + 1 : lay.real + 2] = squares
     bk[mine, 24:25, lay.real : lay.real + 1] = living
 
+    def slot_of(block):
+        line = lax.rem(block, n_blk)
+        return block - line + lax.rem(line - z + n_blk, n_blk)
+
     def block_line(owner, peer):
-        view = bk.at[me * n_blk + owner]
-        return on_line(view, view, s_bz.at[peer], r_bz.at[owner], peer)
+        slot = me * n_blk + lax.rem(owner - peer + n_blk, n_blk)
+        return on_line(bk.at[mine], bk.at[slot], s_bz.at[peer], r_bz.at[owner], peer)
+
+    def block_arrives(owner):
+        slot = me * n_blk + lax.rem(owner - z + n_blk, n_blk)
+        on_line(bk.at[mine], bk.at[slot], s_bz.at[owner], r_bz.at[owner], owner).wait_recv()
+
+    def block_own(owner, peer):
+        view = bk.at[owner * n_blk]
+        return on_plane(view, view, s_bo.at[peer], r_bo.at[owner], peer)
 
     def block_plane(owner, peer):
-        view = bk.at[pl.ds(owner * n_blk, n_blk)]
+        view = bk.at[pl.ds(owner * n_blk + 1, n_blk - 1)]
         return on_plane(view, view, s_bp.at[peer], r_bp.at[owner], peer)
 
+    plane_peers(lambda peer: block_own(me, peer).start())
     line_peers(lambda peer: block_line(z, peer).start())
 
     @pl.when(is_dyn)
@@ -335,86 +372,89 @@
         bias[:, CB3 + 1 : CB3 + 2],
     ]
     n_tiles = lay.batch // TILE
+    row8 = rows_of((8, TILE))
+    act_rows = jnp.logical_and(row8 >= 1, row8 < 1 + ACT)
+
+    def place_of(step):
+        return pl.ds(pl.multiple_of(lax.rem(step + 1, n_tiles) * TILE, TILE), TILE)
+
+    def ones16():
+        return jnp.ones((16, TILE), BF16)
+
+    def framed(first_row, used, where):
+        row32 = rows_of((32, TILE))
+        ones3 = jnp.logical_and(row32 >= IN, row32 < IN + 3).astype(F32)
+        return jnp.where(row32 < used, xs[first_row : first_row + 32, where], ones3)
+
+    def hidden(inputs, net):
+        first, slope1 = gate(dot(w1t[net], inputs))
+        first = first.astype(BF16)
+        second, slope2 = gate(dot(w2t[net], first) + cols[:, net : net + 1])
+        return first, slope1, second.astype(BF16), slope2
+
+    def policy(inputs, which, where):
+        first, slope1, second, slope2 = hidden(inputs, 4)
+        out = dot(heads[4], second) + headcol[0:16, 0:1]
+        bent = jnp.tanh(out[8:16])
+        log_scale = -5.0 + 3.5 * (bent + 1.0)
+        draw = nz[which, :, where]
+        moved = jnp.exp(log_scale) * draw
+        latent = out[0:8] + moved
+        terms = (
+            -0.5 * draw * draw
+            - log_scale
+            - 0.9189385
+            - 2.0 * (0.6931472 - latent - softplus(-2.0 * latent))
+        )
+        log_prob = jnp.sum(jnp.where(act_rows, terms, 0.0), axis=0, keepdims=True)
+        action = jnp.where(act_rows, jnp.tanh(latent), 0.0)
+        return action, log_prob, bent, moved, (first, slope1, second, slope2)
+
+    def with_action(inputs, action):
+        middle_rows = jnp.where(act_rows, action, inputs[16:24])
+        return jnp.concatenate([inputs[0:16], middle_rows, inputs[24:32]], 0).astype(BF16)
+
+    def critic(inputs, net):
+        kept = hidden(inputs, net)
+        value = dot(heads[net], kept[2])[0:1] + last[net]
+        return value, kept
+
+    def add_hidden(k, first, grad):
+        acc_h[k] += dot(jnp.concatenate([first, ones16()], 0), grad, NT)
 
     @pl.loop(0, n_tiles)
     def _(step):
         @pl.when(step == 1)
         def _():
-            line_peers(lambda peer: block_line(peer, peer).wait_recv())
+            line_peers(block_arrives)
             plane_peers(lambda peer: block_plane(me, peer).start())
 
         @pl.when(step == n_tiles - 1)
         def _():
-            plane_peers(lambda peer: block_plane(peer, peer).wait_recv())
+            plane_peers(lambda peer: block_own(peer, peer).wait_recv())
             lanes = lax.broadcasted_iota(jnp.int32, (48, lay.width), 1) // CAP
 
             def gather(owner, total):
                 turned = pltpu.roll(
-                    bk[owner * n_blk + z], lax.rem((owner - me) * CAP + lay.width, lay.width), axis=1
+                    bk[owner * n_blk], lax.rem((owner - me) * CAP + lay.width, lay.width), axis=1
                 )
                 return jnp.where(lanes == owner, turned, total)
 
             own = lax.fori_loop(0, n_dp, gather, jnp.zeros((48, lay.width), F32))
             xs[0:48, 0 : lay.real] = own[:, 0 : lay.real]
 
-        where = pl.ds(pl.multiple_of(lax.rem(step + 1, n_tiles) * TILE, TILE), TILE)
-        row32 = rows_of((32, TILE))
-        ones3 = jnp.logical_and(row32 >= IN, row32 < IN + 3).astype(F32)
-        now_f = jnp.where(row32 < IN, xs[0:32, where], ones3)
-        next_f = jnp.where(row32 < OBS, xs[24:56, where], ones3)
-        now_in = now_f.astype(BF16)
+        where = place_of(step)
+        now_in = framed(0, IN, where).astype(BF16)
+        next_f = framed(24, OBS, where)
         reward = xs[23:24, where]
         done = xs[41:42, where]
         weight = xs[42:43, where]
-        row8 = rows_of((8, TILE))
-        act_rows = jnp.logical_and(row8 >= 1, row8 < 1 + ACT)
         row16 = rows_of((16, TILE))
-        ones16 = jnp.ones((16, TILE), BF16)
-
-        def hidden(inputs, net):
-            first, slope1 = gate(dot(w1t[net], inputs))
-            first = first.astype(BF16)
-            second, slope2 = gate(dot(w2t[net], first) + cols[:, net : net + 1])
-            return first, slope1, second.astype(BF16), slope2
-
-        def policy(inputs, which):
-            first, slope1, second, slope2 = hidden(inputs, 4)
-            out = dot(heads[4], second) + headcol[0:16, 0:1]
-            bent = jnp.tanh(out[8:16])
-            log_scale = -5.0 + 3.5 * (bent + 1.0)
-            draw = nz[which, :, where]
-            moved = jnp.exp(log_scale) * draw
-            latent = out[0:8] + moved
-            terms = (
-                -0.5 * draw * draw
-                - log_scale
-                - 0.9189385
-                - 2.0 * (0.6931472 - latent - softplus(-2.0 * latent))
-            )
-            log_prob = jnp.sum(jnp.where(act_rows, terms, 0.0), axis=0, keepdims=True)
-            action = jnp.where(act_rows, jnp.tanh(latent), 0.0)
-            return action, log_prob, bent, moved, (first, slope1, second, slope2)
-
-        def with_action(inputs, action):
-            middle_rows = jnp.where(act_rows, action, inputs[16:24])
-            return jnp.concatenate([inputs[0:16], middle_rows, inputs[24:32]], 0).astype(BF16)
-
-        def critic(inputs, net):
-            kept = hidden(inputs, net)
-            value = dot(heads[net], kept[2])[0:1] + last[net]
-            return value, kept
-
-        def add_hidden(k, first, grad):
-            acc_h[k] += dot(jnp.concatenate([first, ones16], 0), grad, NT)
-
-        next_action, next_prob, _, _, _ = policy(next_f.astype(BF16), 1)
+        next_action, next_prob, _, _, _ = policy(next_f.astype(BF16), 1, where)
         aim_in = with_action(next_f, next_action)
         aim = jnp.minimum(critic(aim_in, 0)[0], critic(aim_in, 1)[0])
         target = reward + DISCOUNT * (1.0 - done) * (aim - alpha * next_prob)
-        action, log_prob, bent, moved, (a1, da1, a2, da2) = policy(now_in, 0)
-        judged_in = with_action(now_f, action)
-        loss = alpha * log_prob - log_alpha * (log_prob + TARGET_ENTROPY)
-        grad_action = jnp.zeros((8, TILE), F32)
+        loss = jnp.zeros((1, TILE), F32)
         heads_grad = []
         for k in range(2):
             value, (c1, dc1, c2, dc2) = critic(now_in, 2 + k)
@@ -428,6 +468,154 @@
             add_hidden(k, c1, g2)
             g1 = (dot(w2h[k], g2) * dc1).astype(BF16)
             acc_w[k] += dot(now_in, g1, NT)
+        acc_m[:, 16:48] += dot(ones16(), jnp.concatenate(heads_grad, 0), NT)
+        acc_l[0:1, :] += weight * loss
+
+    def put_matrix(group, k, at):
+        for chunk in range(n_dp):
+            tile = chunk * lay.mat
+            side, row = tile // 32, tile % 32
+            grids[group][chunk, at * lay.mat : (at + 1) * lay.mat] = acc_h[
+                k, row * 8 : (row + lay.mat) * 8, side * 128 : (side + 1) * 128
+            ].reshape(lay.mat, 8, 128)
+
+    def put(row, value):
+        for at in range(value.shape[0] // 8):
+            for side in range(value.shape[1] // 128):
+                tile = side * (R_SMALL // 8) + row // 8 + at
+                grid_a[tile // lay.sml, lay.mat + tile % lay.sml] = value[
+                    at * 8 : at * 8 + 8, side * 128 : (side + 1) * 128
+                ]
+
+    def bit(b):
+        return lax.rem(me // (1 << b), 2)
+
+    starts, faces, partners = [], [], []
+    start = 0
+    for s in range(bits):
+        if s == 0:
+            face, stride = core, 1
+        else:
+            face = (1 - core) * bit(s) + core * bit(bits - s)
+            stride = (1 - core) * (1 << s) + core * (1 << (bits - s))
+        starts.append(start)
+        faces.append(face)
+        partners.append(me + (1 - 2 * face) * stride)
+        start = start + face * (n_dp >> (s + 1))
+    place = start
+
+    def fold_copy(group, s):
+        half = n_dp >> (s + 1)
+        begin = starts[s] + (1 - faces[s]) * half
+        return on_plane(
+            grids[group].at[pl.ds(begin, half)], bufs[group][s], s_rs.at[group, s], r_rs.at[group, s],
+            partners[s],
+        )
+
+    def fold_wait(group, s):
+        half = n_dp >> (s + 1)
+        begin = starts[s] + faces[s] * half
+        fold_copy(group, s).wait_recv()
+        for at in range(half):
+            grids[group][begin + at] += bufs[group][s][at]
+
+    def line_first(group, owner, peer):
+        if lay.split_z:
+            src = grids[group].at[place, pl.ds(peer * lay.part(group), lay.part(group))]
+        else:
+            src = grids[group].at[place]
+        return on_line(src, zrs[group].at[owner], s_zr.at[group, peer], r_zr.at[group, owner], peer)
+
+    def line_second(group, owner, peer):
+        view = zfs[group].at[pl.ds(owner * lay.part(group), lay.part(group))]
+        return on_line(view, view, s_za.at[group, peer], r_za.at[group, owner], peer)
+
+    def line_start(group):
+        line_peers(lambda peer: line_first(group, z, peer).start())
+
+    def line_sum(group):
+        part, zr, zf = lay.part(group), zrs[group], zfs[group]
+        line_peers(lambda peer: line_first(group, peer, peer).wait_recv())
+        zr[z] = grids[group][place, pl.ds(z * part, part)] if lay.split_z else grids[group][place]
+        whole = zr[0]
+        for block in range(1, n_blk):
+            whole = whole + zr[block]
+        if lay.split_z:
+            zf[pl.ds(z * part, part)] = whole
+            line_peers(lambda peer: line_second(group, z, peer).start())
+        else:
+            zf[...] = whole
+
+    def line_end(group):
+        if lay.split_z:
+            line_peers(lambda peer: line_second(group, peer, peer).wait_recv())
+
+    def tile_copy(k, owner):
+        src = zfs[k // 2].at[pl.ds((k % 2) * lay.mat, lay.mat)]
+        return on_plane(src, mg.at[place], s_mg.at[k], r_mg.at[place], owner)
+
+    def send_tiles(group):
+        for k in (0, 1) if group == 0 else (2,):
+            @pl.when(me != lay.owners[k])
+            def _():
+                tile_copy(k, lay.owners[k]).start()
+
+            @pl.when(me == lay.owners[k])
+            def _():
+                mg[place] = zfs[group][(k % 2) * lay.mat : (k % 2 + 1) * lay.mat]
+
+    def small_copy(at, peer):
+        return on_plane(
+            zf_a.at[pl.ds(lay.mat, lay.sml)], small.at[pl.ds(at * lay.sml, lay.sml)],
+            s_pl.at[peer], r_pl.at[at], peer,
+        )
+
+    def chain(group):
+        steps = [functools.partial(lambda s: fold_copy(group, s).start(), 0)]
+
+        def fold(s):
+            fold_wait(group, s)
+            if s + 1 < bits:
+                fold_copy(group, s + 1).start()
+            else:
+                line_start(group)
+
+        steps += [functools.partial(fold, s) for s in range(bits)]
+        steps.append(lambda: line_sum(group))
+
+        def finish():
+            line_end(group)
+            send_tiles(group)
+            if group == 1:
+                plane_peers(lambda peer: small_copy(place, peer).start())
+                small[pl.ds(place * lay.sml, lay.sml)] = zf_a[lay.mat :]
+
+        steps.append(finish)
+        return steps
+
+    critic_chain, actor_chain = chain(0), chain(1)
+    for k in range(2):
+        put_matrix(0, k, k)
+    critic_chain[0]()
+
+    inside = min(len(critic_chain) - 1, n_tiles - 1)
+
+    @pl.loop(0, n_tiles)
+    def _(step):
+        for at in range(inside):
+            @pl.when(step == at + 1)
+            def _():
+                critic_chain[at + 1]()
+
+        where = place_of(step)
+        now_f = framed(0, IN, where)
+        now_in = now_f.astype(BF16)
+        weight = xs[42:43, where]
+        action, log_prob, bent, moved, (a1, da1, a2, da2) = policy(now_in, 0, where)
+        judged_in = with_action(now_f, action)
+        loss = alpha * log_prob - log_alpha * (log_prob + TARGET_ENTROPY)
+        grad_action = jnp.zeros((8, TILE), F32)
+        for k in range(2):
             judged, (_, df1, _, df2) = critic(judged_in, 2 + k)
             loss -= 0.5 * judged
             g2 = ((cols[:, 5 + k : 6 + k] * (-0.5 * weight)) * df2).astype(BF16)
@@ -440,7 +628,7 @@
             [jnp.where(act_rows, grad_latent, 0.0), jnp.where(act_rows, grad_bent, 0.0)], 0
         ).astype(BF16)
         acc_a[...] += dot(g3, a2, NT)
-        acc_m[...] += dot(ones16, jnp.concatenate([g3] + heads_grad, 0), NT)
+        acc_m[:, 0:16] += dot(ones16(), g3, NT)
         g2 = (dot(head_t[...], g3) * da2).astype(BF16)
         add_hidden(2, a1, g2)
         g1 = (dot(w2h[2], g2) * da1).astype(BF16)
@@ -448,22 +636,9 @@
         acc_l[0:1, :] += weight * loss
         acc_l[1:2, :] += weight * (log_prob + TARGET_ENTROPY)
 
-    for k in range(3):
-        for chunk in range(n_dp):
-            tile = chunk * lay.mat
-            side, row = tile // 32, tile % 32
-            grid[chunk, k * lay.mat : (k + 1) * lay.mat] = acc_h[
-                k, row * 8 : (row + lay.mat) * 8, side * 128 : (side + 1) * 128
-            ].reshape(lay.mat, 8, 128)
-
-    def put(row, value):
-        for at in range(value.shape[0] // 8):
-            for side in range(value.shape[1] // 128):
-                tile = side * (R_SMALL // 8) + row // 8 + at
-                grid[tile // lay.sml, 3 * lay.mat + tile % lay.sml] = value[
-                    at * 8 : at * 8 + 8, side * 128 : (side + 1) * 128
-                ]
-
+    for at in range(inside, len(critic_chain) - 1):
+        critic_chain[at + 1]()
+    put_matrix(1, 2, 0)
     for k in range(3):
         put(R_IN + 24 * k, acc_w[k, 0:24, :])
     put(R_HEAD, acc_a[...])
@@ -479,45 +654,15 @@
     rowbuf[0:1, 65:66] = folded[1:2]
     put(R_MISC, rowbuf[...])
     put(R_MISC + 8, jnp.zeros((R_SMALL - R_MISC - 8, HSAC), F32))
-
-    core = lax.rem(me, 2)
-
-    def bit(b):
-        return lax.rem(me // (1 << b), 2)
-
-    starts, faces, partners = [], [], []
-    start = 0
-    for s in range(bits):
-        if s == 0:
-            face, stride = core, 1
-        else:
-            face = (1 - core) * bit(s) + core * bit(bits - s)
-            stride = (1 - core) * (1 << s) + core * (1 << (bits - s))
-        starts.append(start)
-        faces.append(face)
-        partners.append(me + (1 - 2 * face) * stride)
-        start = start + face * (n_dp >> (s + 1))
-    place = start
-
-    def fold_copy(s):
-        half = n_dp >> (s + 1)
-        begin = starts[s] + (1 - faces[s]) * half
-        return on_plane(grid.at[pl.ds(begin, half)], rs_bufs[s], s_rs.at[s], r_rs.at[s], partners[s])
-
-    def fold_wait(s):
-        half = n_dp >> (s + 1)
-        begin = starts[s] + faces[s] * half
-        fold_copy(s).wait_recv()
-        for at in range(half):
-            grid[begin + at] += rs_bufs[s][at]
-
-    fold_copy(0).start()
-
+    actor_chain[0]()
+
+    plane_peers(lambda peer: block_plane(peer, peer).wait_recv())
     lane0 = lay.real // 128 * 128
 
     def add_block(at, carry):
         sides, fills = carry
-        return sides + bk[at, 0:32, lane0 : lane0 + 128], fills + bk[at, 40:48, 0 : lay.real]
+        slot = slot_of(at)
+        return sides + bk[slot, 0:32, lane0 : lane0 + 128], fills + bk[slot, 40:48, 0 : lay.real]
 
     sides, fills = lax.fori_loop(
         0, lay.n_dev, add_block, (jnp.zeros((32, 128), F32), jnp.zeros((8, lay.real), F32))
@@ -553,8 +698,8 @@
         dpack[...] = jnp.zeros_like(dpack)
         dpack[0:HALF, 0:HDYN] = dyn_out[dyn_e, 0:HALF, :]
         dpack[24 : 24 + HALF, 0:HDYN] = dyn_out[dyn_e, HALF:DOUT, :]
-        head = dpack[0:48, :].astype(BF16)
-        head_back = (0.5 * rounded(dpack[0:48, :])).T.astype(BF16)
+        dhead[...] = dpack[0:48, :].astype(BF16)
+        dhead_t[...] = (0.5 * rounded(dpack[0:48, :])).T.astype(BF16)
         dpack[...] = jnp.zeros_like(dpack)
 
         def wait_dyn(peer):
@@ -571,23 +716,33 @@
         w2t[0] = dmat[...].T.astype(BF16)
         for ref in (dacc_h, dacc_w, dacc_o, dacc_m, dacc_b, dacc_l):
             ref[...] = jnp.zeros_like(ref)
-        per = TILE // lay.real
-
-        @pl.loop(0, lay.n_dev // per)
-        def _(tile):
+
+    per = TILE // lay.real
+    dyn_tiles = lay.n_dev // per
+    gap = max(dyn_tiles // (bits + 1), 1)
+
+    @pl.loop(0, dyn_tiles)
+    def _(tile):
+        for s in range(bits):
+            @pl.when(tile == (s + 1) * gap)
+            def _():
+                actor_chain[s + 1]()
+
+        @pl.when(is_dyn)
+        def _():
             for at in range(per):
-                xt[:, at * lay.real : (at + 1) * lay.real] = bk[tile * per + at, :, 0 : lay.real]
+                slot = slot_of(tile * per + at)
+                xt[:, at * lay.real : (at + 1) * lay.real] = bk[slot, :, 0 : lay.real]
             now = xt[0:24, :]
             later = xt[24:48, :]
             row24 = rows_of((24, TILE))
             scaled = jnp.where(row24 < IN, (now - centre) * scale, 1.0)
-            inputs = jnp.concatenate([scaled, (rows_of((8, TILE)) < 2).astype(F32)], 0).astype(BF16)
-            ones16 = jnp.ones((16, TILE), BF16)
+            inputs = jnp.concatenate([scaled, (row8 < 2).astype(F32)], 0).astype(BF16)
             first, slope1 = gate(dot(w1t[0], inputs))
             first = first.astype(BF16)
             second, slope2 = gate(dot(w2t[0], first) + 0.5 * dcols[:, 0:1])
             second = second.astype(BF16)
-            out = dot(head, second) + dcols[0:48, 1:2]
+            out = dot(dhead[...], second) + dcols[0:48, 1:2]
             used = row24 < HALF
             upper = dcols[0:24, 2:3]
             lower = dcols[0:24, 3:4]
@@ -611,12 +766,97 @@
                 [jnp.where(used, grad_mu, 0.0), jnp.where(used, grad_lv1 * open1, 0.0)], 0
             ).astype(BF16)
             dacc_o[...] += dot(g3, second, NT)
-            dacc_m[...] += dot(ones16, g3, NT)
-            g2 = (dot(head_back, g3) * slope2).astype(BF16)
-            dacc_h[...] += dot(jnp.concatenate([first, ones16], 0), g2, NT)
+            dacc_m[...] += dot(ones16(), g3, NT)
+            g2 = (dot(dhead_t[...], g3) * slope2).astype(BF16)
+            dacc_h[...] += dot(jnp.concatenate([first, ones16()], 0), g2, NT)
             g1 = (dot(w2h[0], g2) * slope1).astype(BF16)
             dacc_w[...] += dot(inputs, g1, NT)
 
+    def pack_copy(src, owner, ssem, peer):
+        return on_plane(src, dyn_s.at[owner], ssem, r_ds.at[owner], peer)
+
+    def dyn_g_copy(src, owner, ssem, peer):
+        return on_plane(src, dyn_g.at[owner], ssem, r_dg.at[owner], peer)
+
+    def dyn_x_copy(src, owner, ssem, peer):
+        return on_plane(src, dyn_x.at[owner], ssem, r_dx.at[owner], peer)
+
+    def give(copy, src, sems):
+        like_peers(lambda peer: copy(src, dyn_e, sems.at[peer], peer).start())
+        copy(src, dyn_e, sems.at[sibling], sibling).start()
+
+    def given(copy, src, sems):
+        like_peers(lambda peer: copy(src, dyn_e, sems.at[peer], peer).wait_send())
+        copy(src, dyn_e, sems.at[sibling], sibling).wait_send()
+
+    def from_like(body):
+        def member_only(peer):
+            @pl.when(peer < MEMBERS)
+            def _():
+                body(jnp.minimum(peer, MEMBERS - 1))
+
+        like_peers(member_only)
+
+    def hand_on(copy, out, sems):
+        def body(owner):
+            copy(out.at[owner], owner, sems.at[owner], sibling).wait_recv()
+            copy(out.at[owner], owner, sems.at[owner], sibling).start()
+
+        from_like(body)
+
+    def handed_on(copy, out, sems):
+        from_like(lambda owner: copy(out.at[owner], owner, sems.at[owner], sibling).wait_send())
+
+    def from_sibling(copy, out, sems):
+        @pl.loop(0, n_dp // 2)
+        def _(off):
+            owner = lax.rem(sibling + 2 * off, n_dp)
+
+            @pl.when(owner < MEMBERS)
+            def _():
+                at = jnp.minimum(owner, MEMBERS - 1)
+                copy(out.at[at], at, sems.at[at], sibling).wait_recv()
+
+    def line_rows(ref):
+        rows = ref[0 : lay.drows, 0:HDYN]
+        for block in range(1, n_blk):
+            rows = jnp.where(z == block, ref[block * lay.drows : (block + 1) * lay.drows, 0:HDYN], rows)
+        return rows
+
+    def sac_g_copy(k, peer):
+        src = grow.at[pl.ds(pl.multiple_of(z * lay.rows, lay.rows), lay.rows)]
+        return on_plane(src, sac_g.at[k], s_sg.at[peer], r_sg.at[k], peer)
+
+    def sac_x_copy(k, peer):
+        src = mat.at[pl.ds(pl.multiple_of(z * lay.rows, lay.rows), lay.rows)]
+        return on_plane(src, sac_x.at[k], s_sx.at[peer], r_sx.at[k], peer)
+
+    mine_rows = pl.ds(pl.multiple_of(z * lay.rows, lay.rows), lay.rows)
+
+    def take_matrix():
+        line_peers(lambda peer: sac_m_copy(peer, peer).wait_recv())
+        smg[z] = sac_m[sac_k]
+
+        @pl.loop(1, n_dp)
+        def _(off):
+            at = lax.rem(place + off, n_dp)
+            on_plane(mg.at[at], mg.at[at], s_mg.at[0], r_mg.at[at], me).wait_recv()
+
+        for chunk in range(n_dp):
+            tile = chunk * lay.mat
+            side, row = tile // 32, tile % 32
+            grow[row * 8 : (row + lay.mat) * 8, side * 128 : (side + 1) * 128] = mg[chunk].reshape(
+                lay.mat * 8, 128
+            )
+        sac_g[sac_k] = grow[mine_rows, :]
+        plane_peers(lambda peer: sac_g_copy(sac_k, peer).start())
+        for block in range(n_blk):
+            at = slice(block * lay.rows, (block + 1) * lay.rows)
+            mat[at, :] = MOMENTUM * smg[block] + grow[at, :] / total
+        normalise(mat)
+
+    @pl.when(is_dyn)
+    def _():
         dpack[D_IN : D_IN + 24, :] = dacc_w[0:24, :]
         dpack[D_OUT : D_OUT + HALF, :] = dacc_o[0:HALF, :]
         dpack[D_OUT + HALF : D_OUT + DOUT, :] = dacc_o[24 : 24 + HALF, :]
@@ -633,154 +873,62 @@
             jnp.sum(dacc_l[0:1, :], axis=1, keepdims=True), (1, 128)
         )
         dyn_s[dyn_e] = dpack[...]
-
-    def pack_copy(owner, peer):
-        at = dyn_s.at[jnp.minimum(owner, MEMBERS - 1)]
-        return on_plane(dpack, at, s_ds.at[peer], r_ds.at[owner], peer)
-
-    def dyn_g_copy(owner, peer):
-        at = dyn_g.at[jnp.minimum(owner, MEMBERS - 1)]
-        return on_plane(drow_g, at, s_dg.at[peer], r_dg.at[owner], peer)
-
-    def dyn_x_copy(owner, peer):
-        at = dyn_x.at[jnp.minimum(owner, MEMBERS - 1)]
-        return on_plane(drow_x, at, s_dx.at[peer], r_dx.at[owner], peer)
-
-    def line_rows(ref):
-        rows = ref[0 : lay.drows, 0:HDYN]
-        for block in range(1, n_blk):
-            rows = jnp.where(z == block, ref[block * lay.drows : (block + 1) * lay.drows, 0:HDYN], rows)
-        return rows
-
-    fold_wait(0)
-    if bits > 1:
-        fold_copy(1).start()
-
-    @pl.when(is_dyn)
-    def _():
-        plane_peers(lambda peer: pack_copy(me, peer).start())
+        give(pack_copy, dpack, s_ds)
         rows = line_rows(dacc_h)
         drow_g[...] = rows
         dyn_g[dyn_e] = rows
-        plane_peers(lambda peer: dyn_g_copy(me, peer).start())
+        give(dyn_g_copy, drow_g, s_dg)
         dmat[...] = jnp.zeros_like(dmat)
         for block in range(n_blk):
             at = slice(block * lay.drows, (block + 1) * lay.drows)
             dmat[at, 0:HDYN] = MOMENTUM * dmg[block] + dacc_h[at, 0:HDYN] / total
-        moment = dmat[...]
-        norm = jnp.sqrt(jnp.sum(jnp.sum(moment * moment, axis=1, keepdims=True), axis=0, keepdims=True))
-        dmat[...] = moment / (norm + 1e-7)
-        schulz(dmat, 2)
-
-    for s in range(1, bits):
-        fold_wait(s)
-        if s + 1 < bits:
-            fold_copy(s + 1).start()
-
-    def line_first(owner, peer):
-        if lay.split_z:
-            src = grid.at[place, pl.ds(peer * lay.part, lay.part)]
-        else:
-            src = grid.at[place]
-        return on_line(src, zr.at[owner], s_zr.at[peer], r_zr.at[owner], peer)
-
-    def line_second(owner, peer):
-        view = zf.at[pl.ds(owner * lay.part, lay.part)]
-        return on_line(view, view, s_za.at[peer], r_za.at[owner], peer)
-
-    line_peers(lambda peer: line_first(z, peer).start())
+        normalise(dmat)
+
+    pl.when(is_critic)(take_matrix)
+    if n_dp <= MEMBERS + 1:
+        only_dyn = jnp.logical_and(is_dyn, jnp.logical_not(is_critic))
+        pairs = [(is_critic, [dmat, mat]), (only_dyn, [dmat])]
+    else:
+        pairs = [(is_critic, [mat]), (is_dyn, [dmat])]
+    for test, matrices in pairs:
+        pl.when(test)(functools.partial(schulz, matrices, 2))
+    actor_chain[bits + 1]()
+    for test, matrices in pairs:
+        pl.when(test)(functools.partial(schulz, matrices, 2))
+    actor_chain[bits + 2]()
+    for test, matrices in pairs:
+        pl.when(test)(functools.partial(schulz, matrices, NS_ITERS - 4))
+
+    def send_sac():
+        sac_x[sac_k] = mat[mine_rows, :]
+        plane_peers(lambda peer: sac_x_copy(sac_k, peer).start())
 
     @pl.when(is_dyn)
     def _():
-        schulz(dmat, NS_ITERS - 2)
         rows = line_rows(dmat)
         drow_x[...] = rows
         dyn_x[dyn_e] = rows
-        plane_peers(lambda peer: dyn_x_copy(me, peer).start())
-
-    line_peers(lambda peer: line_first(peer, peer).wait_recv())
-    if lay.split_z:
-        zr[z] = grid[place, pl.ds(z * lay.part, lay.part)]
-    else:
-        zr[z] = grid[place]
-    whole = zr[0]
-    for block in range(1, n_blk):
-        whole = whole + zr[block]
-    if lay.split_z:
-        zf[pl.ds(z * lay.part, lay.part)] = whole
-        line_peers(lambda peer: line_second(z, peer).start())
-        line_peers(lambda peer: line_second(peer, peer).wait_recv())
-    else:
-        zf[...] = whole
-
-    def tile_copy(k, owner):
-        return on_plane(zf.at[pl.ds(k * lay.mat, lay.mat)], mg.at[place], s_mg.at[k], r_mg.at[place], owner)
-
-    for k in range(3):
-        @pl.when(me != lay.owners[k])
-        def _():
-            tile_copy(k, lay.owners[k]).start()
-
-    def small_copy(at, peer):
-        return on_plane(
-            zf.at[pl.ds(3 * lay.mat, lay.sml)], small.at[pl.ds(at * lay.sml, lay.sml)],
-            s_pl.at[peer], r_pl.at[at], peer,
-        )
-
-    plane_peers(lambda peer: small_copy(place, peer).start())
-    small[pl.ds(place * lay.sml, lay.sml)] = zf[3 * lay.mat :]
-
-    def sac_g_copy(k, peer):
-        src = grow.at[pl.ds(pl.multiple_of(z * lay.rows, lay.rows), lay.rows)]
-        return on_plane(src, sac_g.at[k], s_sg.at[peer], r_sg.at[k], peer)
-
-    def sac_x_copy(k, peer):
-        src = mat.at[pl.ds(pl.multiple_of(z * lay.rows, lay.rows), lay.rows)]
-        return on_plane(src, sac_x.at[k], s_sx.at[peer], r_sx.at[k], peer)
-
-    mine_rows = pl.ds(pl.multiple_of(z * lay.rows, lay.rows), lay.rows)
-
-    @pl.when(is_sac)
+        give(dyn_x_copy, drow_x, s_dx)
+
+    pl.when(is_critic)(send_sac)
+
+    @pl.when(is_actor)
     def _():
-        line_peers(lambda peer: sac_m_copy(peer, peer).wait_recv())
-        smg[z] = sac_m[sac_k]
-        mg[place] = zf[pl.ds(sac_k * lay.mat, lay.mat)]
-
-        @pl.loop(1, n_dp)
-        def _(off):
-            at = lax.rem(place + off, n_dp)
-            on_plane(mg.at[at], mg.at[at], s_mg.at[0], r_mg.at[at], me).wait_recv()
-
-        for chunk in range(n_dp):
-            tile = chunk * lay.mat
-            side, row = tile // 32, tile % 32
-            grow[row * 8 : (row + lay.mat) * 8, side * 128 : (side + 1) * 128] = mg[chunk].reshape(
-                lay.mat * 8, 128
-            )
-        sac_g[sac_k] = grow[mine_rows, :]
-        plane_peers(lambda peer: sac_g_copy(sac_k, peer).start())
-        for block in range(n_blk):
-            at = slice(block * lay.rows, (block + 1) * lay.rows)
-            mat[at, :] = MOMENTUM * smg[block] + grow[at, :] / total
-        moment = mat[...]
-        norm = jnp.sqrt(jnp.sum(jnp.sum(moment * moment, axis=1, keepdims=True), axis=0, keepdims=True))
-        mat[...] = moment / (norm + 1e-7)
-        schulz(mat, NS_ITERS)
-        sac_x[sac_k] = mat[mine_rows, :]
-        plane_peers(lambda peer: sac_x_copy(sac_k, peer).start())
+        take_matrix()
+        schulz([mat], NS_ITERS)
+        send_sac()
+
+    hand_on(pack_copy, dyn_s, f_ds)
+    hand_on(dyn_g_copy, dyn_g, f_dg)
+    hand_on(dyn_x_copy, dyn_x, f_dx)
 
     @pl.loop(1, n_dp)
     def _(off):
         small_copy(lax.rem(place + off, n_dp), me).wait_recv()
 
-    def from_members(peer):
-        @pl.when(peer < MEMBERS)
-        def _():
-            pack_copy(peer, peer).wait_recv()
-            dyn_g_copy(peer, peer).wait_recv()
-            dyn_x_copy(peer, peer).wait_recv()
-
-    plane_peers(from_members)
+    from_sibling(pack_copy, dyn_s, f_ds)
+    from_sibling(dyn_g_copy, dyn_g, f_dg)
+    from_sibling(dyn_x_copy, dyn_x, f_dx)
     for k in range(3):
         @pl.when(me != lay.owners[k])
         def _():
@@ -791,9 +939,10 @@
         hidden_copy(z, 0, peer).wait_send()
         hidden_copy(z, 1, peer).wait_send()
         block_line(z, peer).wait_send()
-        line_first(z, peer).wait_send()
-        if lay.split_z:
-            line_second(z, peer).wait_send()
+        for group in range(2):
+            line_first(group, z, peer).wait_send()
+            if lay.split_z:
+                line_second(group, z, peer).wait_send()
 
         @pl.when(is_dyn)
         def _():
@@ -809,14 +958,9 @@
     def sent_on_plane(peer):
         list_copy(me, peer).wait_send()
         member_copy(me, peer).wait_send()
+        block_own(me, peer).wait_send()
         block_plane(me, peer).wait_send()
         small_copy(place, peer).wait_send()
-
-        @pl.when(is_dyn)
-        def _():
-            pack_copy(me, peer).wait_send()
-            dyn_g_copy(me, peer).wait_send()
-            dyn_x_copy(me, peer).wait_send()
 
         @pl.when(is_sac)
         def _():
@@ -824,8 +968,19 @@
             sac_x_copy(sac_k, peer).wait_send()
 
     plane_peers(sent_on_plane)
-    for s in range(bits):
-        fold_copy(s).wait_send()
+
+    @pl.when(is_dyn)
+    def _():
+        given(pack_copy, dpack, s_ds)
+        given(dyn_g_copy, drow_g, s_dg)
+        given(dyn_x_copy, drow_x, s_dx)
+
+    handed_on(pack_copy, dyn_s, f_ds)
+    handed_on(dyn_g_copy, dyn_g, f_dg)
+    handed_on(dyn_x_copy, dyn_x, f_dx)
+    for group in range(2):
+        for s in range(bits):
+            fold_copy(group, s).wait_send()
     for k in range(3):
         @pl.when(me != lay.owners[k])
         def _():
@@ -915,7 +1070,8 @@
         jnp.where(jnp.logical_and(lane >= MINLV, lane < LOGA), -BOUND_WEIGHT, 0.0),
     )
     grad = bg[...] / total + bounds
-    store((bi_n, bi_mn, bi_vn), ..., adamw(bi[...], bi_m[...], bi_v[...], grad))
+    flat = [ref[...].reshape(1, NB) for ref in (bi, bi_m, bi_v)]
+    store((bi_n, bi_mn, bi_vn), ..., [value.reshape(NB) for value in adamw(*flat, grad)])
     loss[...] = total_loss
     counted[...] = total
 
@@ -935,25 +1091,25 @@
     def swap(value):
         return jnp.swapaxes(value, -1, -2)
 
-    def row(value):
-        return value.reshape(1, -1)
+    def kept(value):
+        return pltpu.with_memory_space_constraint(value, pltpu.VMEM)
 
     inputs = (
-        replay, model_rows, requests, member_of, row(model_live), jnp.transpose(noise, (2, 0, 1)),
+        replay, model_rows, requests, member_of, model_live, jnp.transpose(noise, (2, 0, 1)),
         sac_hidden, sac_hidden_mom, dyn_hidden, dyn_hidden_mom, flip(crit_in), act_in, dyn_in,
-        crit_out, swap(act_out), swap(dyn_out), row(biases), flip(targ_in), targ_hidden, targ_out,
+        crit_out, swap(act_out), swap(dyn_out), biases, flip(targ_in), targ_hidden, targ_out,
         targ_bias,
     )
     shape = jax.ShapeDtypeStruct
     rows, drows = lay.rows, lay.drows
     out_shape = (
-        shape((3, rows, HSAC), F32),
-        shape((3, rows, HSAC), F32),
-        shape((MEMBERS, drows, HDYN), F32),
-        shape((MEMBERS, drows, HDYN), F32),
-        shape((MEMBERS, D_ROWS, HSAC), F32),
-        shape((32, 8, 128), F32),
-        shape((8, 128), F32),
+        pltpu.VMEM((3, rows, HSAC), F32),
+        pltpu.VMEM((3, rows, HSAC), F32),
+        pltpu.VMEM((MEMBERS, drows, HDYN), F32),
+        pltpu.VMEM((MEMBERS, drows, HDYN), F32),
+        pltpu.VMEM((MEMBERS, D_ROWS, HSAC), F32),
+        pltpu.VMEM((32, 8, 128), F32),
+        pltpu.VMEM((8, 128), F32),
     )
 
     def vm(*dims, kind=F32):
@@ -989,13 +1145,15 @@
         vm(16, HSAC),
         vm(16, 48),
         vm(8, TILE),
-        vm(n_dp, lay.chunk, 8, 128),
-        vm(n_blk, lay.part, 8, 128),
-        vm(lay.chunk, 8, 128),
+        vm(n_dp, lay.chunks[0], 8, 128),
+        vm(n_dp, lay.chunks[1], 8, 128),
+        vm(n_blk, lay.part(0), 8, 128),
+        vm(n_blk, lay.part(1), 8, 128),
+        vm(lay.chunks[0], 8, 128),
+        vm(lay.chunks[1], 8, 128),
         vm(n_dp, lay.mat, 8, 128),
         vm(HSAC, HSAC),
         vm(HSAC, HSAC),
-        vm(8, 128),
         vm(HSAC, 8),
         vm(HSAC + 16, HSAC),
         vm(32, HSAC),
@@ -1008,16 +1166,21 @@
         vm(D_ROWS, HSAC),
         vm(drows, HDYN),
         vm(drows, HDYN),
+        vm(1, NB),
+        vm(48, HSAC, kind=BF16),
+        vm(HSAC, 48, kind=BF16),
     ]
-    scratch += [vm(n_dp >> (s + 1), lay.chunk, 8, 128) for s in range(bits)]
+    scratch += [vm(n_dp >> (s + 1), chunk, 8, 128) for chunk in lay.chunks for s in range(bits)]
     scratch += sems(2, n_blk)
     scratch += sems(n_dp) + sems(n_dp)
     scratch += sems(n_blk) + sems(n_blk) + sems(n_blk)
-    scratch += sems(n_blk) + sems(n_dp)
-    scratch += sems(bits) + sems(n_blk) + sems(n_blk) + sems(n_dp)
+    scratch += sems(n_blk) + sems(n_dp) + sems(n_dp)
+    scratch += sems(2, bits) + sems(2, n_blk) + sems(2, n_blk) + sems(n_dp)
     scratch += [pltpu.SemaphoreType.DMA((3,)), pltpu.SemaphoreType.DMA((n_dp,))]
     scratch += sems(n_dp) + sems(n_dp) + sems(n_dp)
+    scratch += 3 * [pltpu.SemaphoreType.DMA((n_dp,))]
     scratch += 2 * [pltpu.SemaphoreType.DMA((n_dp,)), pltpu.SemaphoreType.DMA((3,))]
+    varying = 4 * (lay.n_dev * 48 * lay.width + 72 * lay.batch + 48 * lay.replay)
     gathered = pl.pallas_call(
         functools.partial(main_kernel, lay),
         out_shape=out_shape,
@@ -1025,19 +1188,18 @@
         out_specs=[spec] * len(out_shape),
         scratch_shapes=scratch,
         compiler_params=pltpu.CompilerParams(
-            collective_id=0, has_side_effects=True, vmem_limit_bytes=60 * 2**20
+            collective_id=0, has_side_effects=True, vmem_limit_bytes=14 * 2**20 + 2 * varying
         ),
         name="step",
-    )(*inputs)
+    )(*[pltpu.with_memory_space_constraint(value, pltpu.HBM) for value in inputs])
     params = (
         sac_hidden, sac_hidden_mom, dyn_hidden, dyn_hidden_mom,
         flip(crit_in), flip(crit_in_m), flip(crit_in_v), act_in, act_in_m, act_in_v,
         dyn_in, dyn_in_m, dyn_in_v, crit_out, crit_out_m, crit_out_v,
         swap(act_out), swap(act_out_m), swap(act_out_v),
-        swap(dyn_out), swap(dyn_out_m), swap(dyn_out_v), row(biases), row(biases_m), row(biases_v),
+        swap(dyn_out), swap(dyn_out_m), swap(dyn_out_v), biases, biases_m, biases_v,
     )
-    new_shape = [shape(params[i].shape, F32) for i in (0, 1, 2, 3)]
-    new_shape += [shape(params[i].shape, F32) for i in range(4, 25)]
+    new_shape = [shape(value.shape, F32) for value in params]
     new_shape += [shape((1, 1), F32)] * 2
     out = pl.pallas_call(
         update_kernel,
@@ -1045,16 +1207,14 @@
         in_specs=[spec] * (len(gathered) + len(params)),
         out_specs=[spec] * len(new_shape),
         scratch_shapes=[vm(1, NB)],
-        compiler_params=pltpu.CompilerParams(vmem_limit_bytes=40 * 2**20),
+        compiler_params=pltpu.CompilerParams(vmem_limit_bytes=16 * 2**20),
         name="update",
-    )(*gathered, *params)
+    )(*[kept(value) for value in gathered], *params)
     out = list(out)
     for at in (4, 5, 6):
         out[at] = flip(out[at])
     for at in (16, 17, 18, 19, 20, 21):
         out[at] = swap(out[at])
-    for at in (22, 23, 24):
-        out[at] = out[at].reshape(-1)
     for at in (25, 26):
         out[at] = out[at].reshape(())
     return tuple(out)

time: 111 us -> 94.1 us (0.85)
  local copies, waits for them, and re-layouts: 9.16 us -> 0.56 us
  Pallas kernels: 98.1 us -> 92.2 us
  other arithmetic: 1.95 us -> 0 us
    unnamed x66 -> x50, local copies, waits for them, and re-layouts: 7.21 us -> 0.56 us
    pallas_call x1, Pallas kernels: 96.3 us -> 90.1 us  [shards(): pl.pallas_call(functools.partial(main_kernel, lay), out_shape=out_shape,...]
    pallas_call x3 -> x0, other arithmetic: 1.95 us -> none  [shards(): pl.pallas_call(update_kernel, out_shape=tuple(new_shape), in_specs=[spec]...]
    reshape x4 -> x0, local copies, waits for them, and re-layouts: 1.95 us -> none  [row(): return value.reshape(1, -1)]
where the time goes in v2:
time: 94.1 us; the launch traced here: 93.8 us
  Pallas kernels  92.2 us (98%)
  between operations  1.07 us (1%)
    pallas_call x1, Pallas kernels, shards(): pl.pallas_call(functools.partial(main_kernel, lay), out_shape=out_shape,...  90.1 us
    pallas_call x1, Pallas kernels, shards(): pl.pallas_call(update_kernel, out_shape=tuple(new_shape), in_specs=[spec]...  2.12 us

profile of v2, /device:TPU:0, one launch (start us, length us, event | category | flops | bytes accessed | tf_op | source)
XLA Modules:
  0.0 93.8 jit_solution(15657497642310826102)
XLA Ops:
  0.7 0.0 copy-start
  0.7 0.0 copy-start.1
  0.7 0.0 copy-start.2
  0.7 0.0 copy-start.3
  0.7 0.0 copy-start.4
  0.7 0.0 copy-start.5
  0.7 0.0 copy-start.6
  0.7 0.0 copy-start.7
  0.8 0.0 copy-start.8
  0.8 0.0 copy-start.9
  0.8 0.0 copy-start.10
  0.8 0.0 copy-start.11
  0.8 0.0 copy-start.12
  0.8 0.0 copy-start.13
  0.8 0.0 copy-start.14
  0.8 0.0 copy-start.15
  0.8 0.0 copy-start.16
  0.8 0.0 copy-start.17
  0.9 0.0 copy-start.18
  0.9 0.0 copy-start.19
  0.9 0.0 copy-start.20
  0.9 0.0 copy-start.21
  0.9 0.0 copy-start.24
  0.9 90.1 %step.1 = (f32[3,64,256]{2,1,0:T(8,128)S(1)}, f32[3,64,256]{2,1,0:T(8,128)S(1)}, f32[7,50,200]{2,1,0:T(8,128)S(1)}, f32[7,50,200]{2,1,0:T(8,128)S(1)}, f32[7,72,...) custom-call(f32[42,3648]{1,0:T(8,128)} %refs_0_.1, f32[42,1216]{1,0:T(8,128)} %refs_1_.1, ...), custom_call_target="tpu_custom_call" | custom-call | tf_op jit(solution)/shard_map/step/pallas_call | solution.py:1184
  91.0 0.0 copy-start.23
  91.0 0.0 copy-start.22
  91.0 0.0 copy-done
  91.0 0.0 copy-done.1
  91.0 0.0 copy-done.2
  91.0 0.0 copy-done.3
  91.0 0.0 copy-done.4
  91.1 0.0 copy-done.5
  91.1 0.0 copy-done.6
  91.1 0.0 copy-done.7
  91.1 0.0 copy-done.8
  91.1 0.0 copy-done.9
  91.1 0.0 copy-done.10
  91.1 0.0 copy-done.11
  91.1 0.0 copy-done.12
  91.1 0.0 copy-done.13
  91.1 0.0 copy-done.14
  91.2 0.0 copy-done.15
  91.2 0.0 copy-done.16
  91.2 0.0 copy-done.17
  91.2 0.0 copy-done.18
  91.2 0.0 copy-done.19
  91.2 0.0 copy-done.20
  91.2 0.0 copy-done.21
  91.2 0.0 copy-done.24
  91.2 0.4 copy-done.23
  91.7 0.0 copy-done.22
  91.7 2.1 %update.1 = (f32[3,64,256]{2,1,0:T(8,128)}, f32[3,64,256]{2,1,0:T(8,128)}, f32[7,50,200]{2,1,0:T(8,128)}, f32[7,50,200]{2,1,0:T(8,128)}, f32[23,2,256]{2,1,0:T(2...) custom-call(f32[3,64,256]{2,1,0:T(8,128)S(1)} %get-tuple-element.61., ...), custom_call_target="tpu_custom_call" | custom-call | tf_op jit(solution)/shard_map/update/pallas_call | solution.py:1204
Async XLA Ops:
  0.7 90.3 %copy-start = (f32[7,50,200]{2,1,0:T(8,128)S(1)}, f32[7,50,200]{2,1,0:T(8,128)}, u32[]{:S(2)}) copy-start(f32[7,50,200]{2,1,0:T(8,128)} %refs_9_.3) | copy-start | bytes 840004
  0.7 90.3 %copy-start.1 = (f32[7,50,200]{2,1,0:T(8,128)S(1)}, f32[7,50,200]{2,1,0:T(8,128)}, u32[]{:S(2)}) copy-start(f32[7,50,200]{2,1,0:T(8,128)} %refs_10_.1) | copy-start | bytes 840004
  0.7 90.3 %copy-start.2 = (f32[7,200,36]{1,2,0:T(8,128)S(1)}, f32[7,200,36]{1,2,0:T(8,128)}, u32[]{:S(2)}) copy-start(f32[7,200,36]{1,2,0:T(8,128)} %param.60) | copy-start | bytes 604804
  0.7 90.3 %copy-start.3 = (f32[3,64,256]{2,1,0:T(8,128)S(1)}, f32[3,64,256]{2,1,0:T(8,128)}, u32[]{:S(2)}) copy-start(f32[3,64,256]{2,1,0:T(8,128)} %refs_7_.3) | copy-start | bytes 589828
  0.7 90.3 %copy-start.4 = (f32[3,64,256]{2,1,0:T(8,128)S(1)}, f32[3,64,256]{2,1,0:T(8,128)}, u32[]{:S(2)}) copy-start(f32[3,64,256]{2,1,0:T(8,128)} %refs_8_.3) | copy-start | bytes 589828
  0.7 90.3 %copy-start.5 = (f32[7,23,200]{2,1,0:T(8,128)S(1)}, f32[7,23,200]{2,1,0:T(8,128)}, u32[]{:S(2)}) copy-start(f32[7,23,200]{2,1,0:T(8,128)} %refs_17_.1) | copy-start | bytes 386404
  0.7 90.3 %copy-start.6 = (f32[7,200,36]{1,2,0:T(8,128)S(1)}, f32[7,200,36]{1,2,0:T(8,128)}, u32[]{:S(2)}) copy-start(f32[7,200,36]{1,2,0:T(8,128)} %param.61) | copy-start | bytes 604804
  0.7 90.3 %copy-start.7 = (f32[7,200,36]{1,2,0:T(8,128)S(1)}, f32[7,200,36]{1,2,0:T(8,128)}, u32[]{:S(2)}) copy-start(f32[7,200,36]{1,2,0:T(8,128)} %param.62) | copy-start | bytes 604804
  0.8 90.3 %copy-start.8 = (f32[2,23,256]{2,0,1:T(2,128)S(1)}, f32[2,23,256]{2,0,1:T(2,128)}, u32[]{:S(2)}) copy-start(f32[2,23,256]{2,0,1:T(2,128)} %param.45) | copy-start | bytes 141316
  0.8 90.3 %copy-start.9 = (f32[7,23,200]{2,1,0:T(8,128)S(1)}, f32[7,23,200]{2,1,0:T(8,128)}, u32[]{:S(2)}) copy-start(f32[7,23,200]{2,1,0:T(8,128)} %refs_18_.3) | copy-start | bytes 386404
  0.8 90.3 %copy-start.10 = (f32[7,23,200]{2,1,0:T(8,128)S(1)}, f32[7,23,200]{2,1,0:T(8,128)}, u32[]{:S(2)}) copy-start(f32[7,23,200]{2,1,0:T(8,128)} %refs_19_.3) | copy-start | bytes 386404
  0.8 90.3 %copy-start.11 = (f32[17,256]{1,0:T(8,128)S(1)}, f32[17,256]{1,0:T(8,128)}, u32[]{:S(2)}) copy-start(f32[17,256]{1,0:T(8,128)} %refs_14_.1) | copy-start | bytes 52228
  0.8 90.3 %copy-start.12 = (f32[4639]{0:T(1024)S(1)}, f32[4639]{0:T(1024)}, u32[]{:S(2)}) copy-start(f32[4639]{0:T(1024)} %refs_29_.1) | copy-start | bytes 55672
  0.8 90.3 %copy-start.13 = (f32[256,12]{0,1:T(8,128)S(1)}, f32[256,12]{0,1:T(8,128)}, u32[]{:S(2)}) copy-start(f32[256,12]{0,1:T(8,128)} %param.57) | copy-start | bytes 36868
  0.8 90.3 %copy-start.14 = (f32[2,23,256]{2,0,1:T(2,128)S(1)}, f32[2,23,256]{2,0,1:T(2,128)}, u32[]{:S(2)}) copy-start(f32[2,23,256]{2,0,1:T(2,128)} %param.46) | copy-start | bytes 141316
  0.8 90.3 %copy-start.15 = (f32[2,23,256]{2,0,1:T(2,128)S(1)}, f32[2,23,256]{2,0,1:T(2,128)}, u32[]{:S(2)}) copy-start(f32[2,23,256]{2,0,1:T(2,128)} %param.47) | copy-start | bytes 141316
  0.8 90.3 %copy-start.16 = (f32[17,256]{1,0:T(8,128)S(1)}, f32[17,256]{1,0:T(8,128)}, u32[]{:S(2)}) copy-start(f32[17,256]{1,0:T(8,128)} %refs_15_.1) | copy-start | bytes 52228
  0.8 90.3 %copy-start.17 = (f32[17,256]{1,0:T(8,128)S(1)}, f32[17,256]{1,0:T(8,128)}, u32[]{:S(2)}) copy-start(f32[17,256]{1,0:T(8,128)} %refs_16_.3) | copy-start | bytes 52228
  0.9 90.3 %copy-start.18 = (f32[4639]{0:T(1024)S(1)}, f32[4639]{0:T(1024)}, u32[]{:S(2)}) copy-start(f32[4639]{0:T(1024)} %refs_30_.1) | copy-start | bytes 55672
  0.9 90.3 %copy-start.19 = (f32[4639]{0:T(1024)S(1)}, f32[4639]{0:T(1024)}, u32[]{:S(2)}) copy-start(f32[4639]{0:T(1024)} %refs_31_.1) | copy-start | bytes 55672
  0.9 90.3 %copy-start.20 = (f32[256,12]{0,1:T(8,128)S(1)}, f32[256,12]{0,1:T(8,128)}, u32[]{:S(2)}) copy-start(f32[256,12]{0,1:T(8,128)} %param.58) | copy-start | bytes 36868
  0.9 90.3 %copy-start.21 = (f32[256,12]{0,1:T(8,128)S(1)}, f32[256,12]{0,1:T(8,128)}, u32[]{:S(2)}) copy-start(f32[256,12]{0,1:T(8,128)} %param.59) | copy-start | bytes 36868
  0.9 90.3 %copy-start.24 = (f32[2,256]{1,0:T(2,128)S(1)}, f32[2,256]{1,0:T(2,128)}, u32[]{:S(2)}) copy-start(f32[2,256]{1,0:T(2,128)} %refs_22_.1) | copy-start | bytes 6148
  91.0 0.7 copy-start.23
  91.0 0.7 copy-start.22

commit v3 on v2

--- a/solution.py
+++ b/solution.py
@@ -22,6 +22,7 @@
 STEP = 10
 CAP = 8
 TILE = 256
+ROWS = 32
 
 DISCOUNT = 0.99
 TARGET_ENTROPY = -6.0
@@ -70,7 +71,8 @@
 
 
 def product(a, b, dims=NN):
-    return dot(a[0], b[0], dims) + dot(a[0], b[1], dims) + dot(a[1], b[0], dims)
+    left = jnp.concatenate([a[0], a[0], a[1]], 1)
+    return dot(left, jnp.concatenate([b[0], b[1], b[0]], dims[0][1][0]), dims)
 
 
 def softplus(v):
@@ -85,6 +87,33 @@
     up = 1.0 + jnp.tanh(half)
     value = half * up
     return value, up + value * (2.0 - up)
+
+
+def by_rows(body, *arrays):
+    done = [
+        body(*[array[at : at + ROWS] for array in arrays]) for at in range(0, arrays[0].shape[0], ROWS)
+    ]
+    return [jnp.concatenate(parts, 0) for parts in zip(*done)]
+
+
+def twice(column):
+    return jnp.concatenate([column] * (TILE // 128), 1)
+
+
+def gated(half, column=None):
+    def body(part, *offset):
+        value, slope = gate(part + twice(offset[0]) if offset else part)
+        return value.astype(BF16), slope
+
+    return by_rows(body, half, *([] if column is None else [column]))
+
+
+def sloped(grad, slope):
+    return by_rows(lambda part, by: ((part * by).astype(BF16),), grad, slope)[0]
+
+
+def outer_sloped(column, row, slope):
+    return by_rows(lambda part, by: (((twice(part) * row) * by).astype(BF16),), column, slope)[0]
 
 
 def rows_of(shape):
@@ -142,7 +171,7 @@
         dyn_in, crit_out, act_out, dyn_out, biases, targ_in, targ_hidden, targ_out, targ_bias,
         sac_g, sac_x, dyn_g, dyn_x, dyn_s, small, count,
         wg, asked, owned, dhg, dmg, smg, bk, xs, nz, w1f, w1t, w1n, w2t, w2h, heads, head_t, head_f,
-        rowbuf, cols, headcol, acc_h, acc_w, acc_c, acc_a, acc_m, acc_l, grid_c, grid_a, zr_c, zr_a,
+        rowbuf, wide, headcol, acc_h, acc_w, acc_c, acc_a, acc_m, acc_l, grid_c, grid_a, zr_c, zr_a,
         zf_c, zf_a, mg, mat, grow, dcols, dacc_h, dacc_w, dacc_o, dacc_m, dacc_b, dacc_l, xt, dmat,
         dpack, drow_g, drow_x, bias, dhead, dhead_t, *rest,
     ) = refs
@@ -259,7 +288,9 @@
     rowbuf[3:4, :] = bias[:, CB2 + HSAC : CB2 + 2 * HSAC]
     rowbuf[4:5, :] = bias[:, AB2 : AB2 + HSAC]
     rowbuf[5:7, :] = rounded(crit_out[...])
-    cols[...] = 0.5 * rowbuf[...].T
+    columns = 0.5 * rowbuf[...].T
+    for at in range(7):
+        wide[at] = jnp.broadcast_to(columns[:, at : at + 1], (HSAC, 128))
     rowbuf[...] = jnp.zeros_like(rowbuf)
     rowbuf[0:1, 1:7] = bias[:, AB3 : AB3 + ACT]
     rowbuf[0:1, 9:15] = bias[:, AB3 + ACT : AB3 + 2 * ACT]
@@ -387,10 +418,9 @@
         return jnp.where(row32 < used, xs[first_row : first_row + 32, where], ones3)
 
     def hidden(inputs, net):
-        first, slope1 = gate(dot(w1t[net], inputs))
-        first = first.astype(BF16)
-        second, slope2 = gate(dot(w2t[net], first) + cols[:, net : net + 1])
-        return first, slope1, second.astype(BF16), slope2
+        first, slope1 = gated(dot(w1t[net], inputs))
+        second, slope2 = gated(dot(w2t[net], first), wide[net])
+        return first, slope1, second, slope2
 
     def policy(inputs, which, where):
         first, slope1, second, slope2 = hidden(inputs, 4)
@@ -464,9 +494,9 @@
             g3_rows = jnp.where(row16 == 0, g3, 0.0).astype(BF16)
             heads_grad.append(g3_rows)
             acc_c[k] += dot(g3_rows, c2, NT)
-            g2 = ((cols[:, 5 + k : 6 + k] * g3) * dc2).astype(BF16)
+            g2 = outer_sloped(wide[5 + k], g3, dc2)
             add_hidden(k, c1, g2)
-            g1 = (dot(w2h[k], g2) * dc1).astype(BF16)
+            g1 = sloped(dot(w2h[k], g2), dc1)
             acc_w[k] += dot(now_in, g1, NT)
         acc_m[:, 16:48] += dot(ones16(), jnp.concatenate(heads_grad, 0), NT)
         acc_l[0:1, :] += weight * loss
@@ -618,8 +648,8 @@
         for k in range(2):
             judged, (_, df1, _, df2) = critic(judged_in, 2 + k)
             loss -= 0.5 * judged
-            g2 = ((cols[:, 5 + k : 6 + k] * (-0.5 * weight)) * df2).astype(BF16)
-            g1 = (dot(w2h[k], g2) * df1).astype(BF16)
+            g2 = outer_sloped(wide[5 + k], -0.5 * weight, df2)
+            g1 = sloped(dot(w2h[k], g2), df1)
             grad_action += dot(w1n[k], g1)[0:8]
         grad_latent = 2.0 * alpha * weight * action + grad_action * (1.0 - action * action)
         grad_scale = grad_latent * moved - alpha * weight
@@ -629,9 +659,9 @@
         ).astype(BF16)
         acc_a[...] += dot(g3, a2, NT)
         acc_m[:, 0:16] += dot(ones16(), g3, NT)
-        g2 = (dot(head_t[...], g3) * da2).astype(BF16)
+        g2 = sloped(dot(head_t[...], g3), da2)
         add_hidden(2, a1, g2)
-        g1 = (dot(w2h[2], g2) * da1).astype(BF16)
+        g1 = sloped(dot(w2h[2], g2), da1)
         acc_w[2] += dot(now_in, g1, NT)
         acc_l[0:1, :] += weight * loss
         acc_l[1:2, :] += weight * (log_prob + TARGET_ENTROPY)
@@ -695,6 +725,7 @@
         rowbuf[2:3, 0:HALF] = bias[:, MAXLV : MAXLV + HALF]
         rowbuf[3:4, 0:HALF] = bias[:, MINLV : MINLV + HALF]
         dcols[...] = rowbuf[...].T
+        wide[0] = jnp.broadcast_to(0.5 * dcols[:, 0:1], (HSAC, 128))
         dpack[...] = jnp.zeros_like(dpack)
         dpack[0:HALF, 0:HDYN] = dyn_out[dyn_e, 0:HALF, :]
         dpack[24 : 24 + HALF, 0:HDYN] = dyn_out[dyn_e, HALF:DOUT, :]
@@ -738,10 +769,8 @@
             row24 = rows_of((24, TILE))
             scaled = jnp.where(row24 < IN, (now - centre) * scale, 1.0)
             inputs = jnp.concatenate([scaled, (row8 < 2).astype(F32)], 0).astype(BF16)
-            first, slope1 = gate(dot(w1t[0], inputs))
-            first = first.astype(BF16)
-            second, slope2 = gate(dot(w2t[0], first) + 0.5 * dcols[:, 0:1])
-            second = second.astype(BF16)
+            first, slope1 = gated(dot(w1t[0], inputs))
+            second, slope2 = gated(dot(w2t[0], first), wide[0])
             out = dot(dhead[...], second) + dcols[0:48, 1:2]
             used = row24 < HALF
             upper = dcols[0:24, 2:3]
@@ -767,9 +796,9 @@
             ).astype(BF16)
             dacc_o[...] += dot(g3, second, NT)
             dacc_m[...] += dot(ones16(), g3, NT)
-            g2 = (dot(dhead_t[...], g3) * slope2).astype(BF16)
+            g2 = sloped(dot(dhead_t[...], g3), slope2)
             dacc_h[...] += dot(jnp.concatenate([first, ones16()], 0), g2, NT)
-            g1 = (dot(w2h[0], g2) * slope1).astype(BF16)
+            g1 = sloped(dot(w2h[0], g2), slope1)
             dacc_w[...] += dot(inputs, g1, NT)
 
     def pack_copy(src, owner, ssem, peer):
@@ -912,12 +941,45 @@
 
     pl.when(is_critic)(send_sac)
 
+    def sent_on_line(peer):
+        hidden_copy(z, 0, peer).wait_send()
+        hidden_copy(z, 1, peer).wait_send()
+        block_line(z, peer).wait_send()
+        for group in range(2):
+            line_first(group, z, peer).wait_send()
+            if lay.split_z:
+                line_second(group, z, peer).wait_send()
+
+        @pl.when(is_dyn)
+        def _():
+            dyn_h_copy(z, peer).wait_send()
+            dyn_m_copy(z, peer).wait_send()
+
+        @pl.when(is_sac)
+        def _():
+            sac_m_copy(z, peer).wait_send()
+
+    def sent_on_plane(peer):
+        list_copy(me, peer).wait_send()
+        member_copy(me, peer).wait_send()
+        block_own(me, peer).wait_send()
+        block_plane(me, peer).wait_send()
+
+    def sent_early():
+        line_peers(sent_on_line)
+        plane_peers(sent_on_plane)
+        for group in range(2):
+            for s in range(bits):
+                fold_copy(group, s).wait_send()
+
     @pl.when(is_actor)
     def _():
+        sent_early()
         take_matrix()
         schulz([mat], NS_ITERS)
         send_sac()
 
+    pl.when(jnp.logical_not(is_actor))(sent_early)
     hand_on(pack_copy, dyn_s, f_ds)
     hand_on(dyn_g_copy, dyn_g, f_dg)
     hand_on(dyn_x_copy, dyn_x, f_dx)
@@ -935,31 +997,7 @@
             sac_g_copy(k, me).wait_recv()
             sac_x_copy(k, me).wait_recv()
 
-    def sent_on_line(peer):
-        hidden_copy(z, 0, peer).wait_send()
-        hidden_copy(z, 1, peer).wait_send()
-        block_line(z, peer).wait_send()
-        for group in range(2):
-            line_first(group, z, peer).wait_send()
-            if lay.split_z:
-                line_second(group, z, peer).wait_send()
-
-        @pl.when(is_dyn)
-        def _():
-            dyn_h_copy(z, peer).wait_send()
-            dyn_m_copy(z, peer).wait_send()
-
-        @pl.when(is_sac)
-        def _():
-            sac_m_copy(z, peer).wait_send()
-
-    line_peers(sent_on_line)
-
-    def sent_on_plane(peer):
-        list_copy(me, peer).wait_send()
-        member_copy(me, peer).wait_send()
-        block_own(me, peer).wait_send()
-        block_plane(me, peer).wait_send()
+    def sent_late(peer):
         small_copy(place, peer).wait_send()
 
         @pl.when(is_sac)
@@ -967,7 +1005,7 @@
             sac_g_copy(sac_k, peer).wait_send()
             sac_x_copy(sac_k, peer).wait_send()
 
-    plane_peers(sent_on_plane)
+    plane_peers(sent_late)
 
     @pl.when(is_dyn)
     def _():
@@ -978,9 +1016,6 @@
     handed_on(pack_copy, dyn_s, f_ds)
     handed_on(dyn_g_copy, dyn_g, f_dg)
     handed_on(dyn_x_copy, dyn_x, f_dx)
-    for group in range(2):
-        for s in range(bits):
-            fold_copy(group, s).wait_send()
     for k in range(3):
         @pl.when(me != lay.owners[k])
         def _():
@@ -1137,7 +1172,7 @@
         vm(HSAC, 16, kind=BF16),
         vm(16, HSAC),
         vm(8, HSAC),
-        vm(HSAC, 8),
+        vm(7, HSAC, 128),
         vm(128, 8),
         vm(3, HSAC + 16, HSAC),
         vm(3, 32, HSAC),

time: 94.1 us -> 93.8 us (level)
  no operation moved by 1% of the time
where the time goes in v3:
time: 93.8 us; the launch traced here: 93.5 us
  Pallas kernels  91.9 us (98%)
  between operations  1.07 us (1%)
    pallas_call x1, Pallas kernels, shards(): pl.pallas_call(functools.partial(main_kernel, lay), out_shape=out_shape,...  89.8 us
    pallas_call x1, Pallas kernels, shards(): pl.pallas_call(update_kernel, out_shape=tuple(new_shape), in_specs=[spec]...  2.12 us

profile of v3, /device:TPU:0, one launch (start us, length us, event | category | flops | bytes accessed | tf_op | source)
XLA Modules:
  0.0 93.5 jit_solution(13295803966781914404)
XLA Ops:
  0.7 0.0 copy-start
  0.7 0.0 copy-start.1
  0.7 0.0 copy-start.2
  0.7 0.0 copy-start.3
  0.7 0.0 copy-start.4
  0.7 0.0 copy-start.5
  0.7 0.0 copy-start.6
  0.7 0.0 copy-start.7
  0.8 0.0 copy-start.8
  0.8 0.0 copy-start.9
  0.8 0.0 copy-start.10
  0.8 0.0 copy-start.11
  0.8 0.0 copy-start.12
  0.8 0.0 copy-start.13
  0.8 0.0 copy-start.14
  0.8 0.0 copy-start.15
  0.8 0.0 copy-start.16
  0.8 0.0 copy-start.17
  0.9 0.0 copy-start.18
  0.9 0.0 copy-start.19
  0.9 0.0 copy-start.20
  0.9 0.0 copy-start.21
  0.9 0.0 copy-start.24
  0.9 89.8 %step.1 = (f32[3,64,256]{2,1,0:T(8,128)S(1)}, f32[3,64,256]{2,1,0:T(8,128)S(1)}, f32[7,50,200]{2,1,0:T(8,128)S(1)}, f32[7,50,200]{2,1,0:T(8,128)S(1)}, f32[7,72,...) custom-call(f32[42,3648]{1,0:T(8,128)} %refs_0_.1, f32[42,1216]{1,0:T(8,128)} %refs_1_.1, ...), custom_call_target="tpu_custom_call" | custom-call | tf_op jit(solution)/shard_map/step/pallas_call | solution.py:1219
  90.7 0.0 copy-start.23
  90.7 0.0 copy-start.22
  90.7 0.0 copy-done
  90.7 0.0 copy-done.1
  90.8 0.0 copy-done.2
  90.8 0.0 copy-done.3
  90.8 0.0 copy-done.4
  90.8 0.0 copy-done.5
  90.8 0.0 copy-done.6
  90.8 0.0 copy-done.7
  90.8 0.0 copy-done.8
  90.8 0.0 copy-done.9
  90.8 0.0 copy-done.10
  90.8 0.0 copy-done.11
  90.9 0.0 copy-done.12
  90.9 0.0 copy-done.13
  90.9 0.0 copy-done.14
  90.9 0.0 copy-done.15
  90.9 0.0 copy-done.16
  90.9 0.0 copy-done.17
  90.9 0.0 copy-done.18
  90.9 0.0 copy-done.19
  90.9 0.0 copy-done.20
  90.9 0.0 copy-done.21
  91.0 0.0 copy-done.24
  91.0 0.4 copy-done.23
  91.4 0.0 copy-done.22
  91.4 2.1 %update.1 = (f32[3,64,256]{2,1,0:T(8,128)}, f32[3,64,256]{2,1,0:T(8,128)}, f32[7,50,200]{2,1,0:T(8,128)}, f32[7,50,200]{2,1,0:T(8,128)}, f32[23,2,256]{2,1,0:T(2...) custom-call(f32[3,64,256]{2,1,0:T(8,128)S(1)} %get-tuple-element.61., ...), custom_call_target="tpu_custom_call" | custom-call | tf_op jit(solution)/shard_map/update/pallas_call | solution.py:1239
Async XLA Ops:
  0.7 90.1 %copy-start = (f32[7,50,200]{2,1,0:T(8,128)S(1)}, f32[7,50,200]{2,1,0:T(8,128)}, u32[]{:S(2)}) copy-start(f32[7,50,200]{2,1,0:T(8,128)} %refs_9_.3) | copy-start | bytes 840004
  0.7 90.1 %copy-start.1 = (f32[7,50,200]{2,1,0:T(8,128)S(1)}, f32[7,50,200]{2,1,0:T(8,128)}, u32[]{:S(2)}) copy-start(f32[7,50,200]{2,1,0:T(8,128)} %refs_10_.1) | copy-start | bytes 840004
  0.7 90.1 %copy-start.2 = (f32[7,200,36]{1,2,0:T(8,128)S(1)}, f32[7,200,36]{1,2,0:T(8,128)}, u32[]{:S(2)}) copy-start(f32[7,200,36]{1,2,0:T(8,128)} %param.60) | copy-start | bytes 604804
  0.7 90.1 %copy-start.3 = (f32[3,64,256]{2,1,0:T(8,128)S(1)}, f32[3,64,256]{2,1,0:T(8,128)}, u32[]{:S(2)}) copy-start(f32[3,64,256]{2,1,0:T(8,128)} %refs_7_.3) | copy-start | bytes 589828
  0.7 90.1 %copy-start.4 = (f32[3,64,256]{2,1,0:T(8,128)S(1)}, f32[3,64,256]{2,1,0:T(8,128)}, u32[]{:S(2)}) copy-start(f32[3,64,256]{2,1,0:T(8,128)} %refs_8_.3) | copy-start | bytes 589828
  0.7 90.1 %copy-start.5 = (f32[7,23,200]{2,1,0:T(8,128)S(1)}, f32[7,23,200]{2,1,0:T(8,128)}, u32[]{:S(2)}) copy-start(f32[7,23,200]{2,1,0:T(8,128)} %refs_17_.1) | copy-start | bytes 386404
  0.7 90.1 %copy-start.6 = (f32[7,200,36]{1,2,0:T(8,128)S(1)}, f32[7,200,36]{1,2,0:T(8,128)}, u32[]{:S(2)}) copy-start(f32[7,200,36]{1,2,0:T(8,128)} %param.61) | copy-start | bytes 604804
  0.7 90.1 %copy-start.7 = (f32[7,200,36]{1,2,0:T(8,128)S(1)}, f32[7,200,36]{1,2,0:T(8,128)}, u32[]{:S(2)}) copy-start(f32[7,200,36]{1,2,0:T(8,128)} %param.62) | copy-start | bytes 604804
  0.8 90.1 %copy-start.8 = (f32[2,23,256]{2,0,1:T(2,128)S(1)}, f32[2,23,256]{2,0,1:T(2,128)}, u32[]{:S(2)}) copy-start(f32[2,23,256]{2,0,1:T(2,128)} %param.45) | copy-start | bytes 141316
  0.8 90.1 %copy-start.9 = (f32[7,23,200]{2,1,0:T(8,128)S(1)}, f32[7,23,200]{2,1,0:T(8,128)}, u32[]{:S(2)}) copy-start(f32[7,23,200]{2,1,0:T(8,128)} %refs_18_.3) | copy-start | bytes 386404
  0.8 90.1 %copy-start.10 = (f32[7,23,200]{2,1,0:T(8,128)S(1)}, f32[7,23,200]{2,1,0:T(8,128)}, u32[]{:S(2)}) copy-start(f32[7,23,200]{2,1,0:T(8,128)} %refs_19_.3) | copy-start | bytes 386404
  0.8 90.1 %copy-start.11 = (f32[17,256]{1,0:T(8,128)S(1)}, f32[17,256]{1,0:T(8,128)}, u32[]{:S(2)}) copy-start(f32[17,256]{1,0:T(8,128)} %refs_14_.1) | copy-start | bytes 52228
  0.8 90.1 %copy-start.12 = (f32[4639]{0:T(1024)S(1)}, f32[4639]{0:T(1024)}, u32[]{:S(2)}) copy-start(f32[4639]{0:T(1024)} %refs_29_.1) | copy-start | bytes 55672
  0.8 90.1 %copy-start.13 = (f32[256,12]{0,1:T(8,128)S(1)}, f32[256,12]{0,1:T(8,128)}, u32[]{:S(2)}) copy-start(f32[256,12]{0,1:T(8,128)} %param.57) | copy-start | bytes 36868
  0.8 90.1 %copy-start.14 = (f32[2,23,256]{2,0,1:T(2,128)S(1)}, f32[2,23,256]{2,0,1:T(2,128)}, u32[]{:S(2)}) copy-start(f32[2,23,256]{2,0,1:T(2,128)} %param.46) | copy-start | bytes 141316
  0.8 90.1 %copy-start.15 = (f32[2,23,256]{2,0,1:T(2,128)S(1)}, f32[2,23,256]{2,0,1:T(2,128)}, u32[]{:S(2)}) copy-start(f32[2,23,256]{2,0,1:T(2,128)} %param.47) | copy-start | bytes 141316
  0.8 90.1 %copy-start.16 = (f32[17,256]{1,0:T(8,128)S(1)}, f32[17,256]{1,0:T(8,128)}, u32[]{:S(2)}) copy-start(f32[17,256]{1,0:T(8,128)} %refs_15_.1) | copy-start | bytes 52228
  0.8 90.1 %copy-start.17 = (f32[17,256]{1,0:T(8,128)S(1)}, f32[17,256]{1,0:T(8,128)}, u32[]{:S(2)}) copy-start(f32[17,256]{1,0:T(8,128)} %refs_16_.3) | copy-start | bytes 52228
  0.9 90.1 %copy-start.18 = (f32[4639]{0:T(1024)S(1)}, f32[4639]{0:T(1024)}, u32[]{:S(2)}) copy-start(f32[4639]{0:T(1024)} %refs_30_.1) | copy-start | bytes 55672
  0.9 90.1 %copy-start.19 = (f32[4639]{0:T(1024)S(1)}, f32[4639]{0:T(1024)}, u32[]{:S(2)}) copy-start(f32[4639]{0:T(1024)} %refs_31_.1) | copy-start | bytes 55672
  0.9 90.1 %copy-start.20 = (f32[256,12]{0,1:T(8,128)S(1)}, f32[256,12]{0,1:T(8,128)}, u32[]{:S(2)}) copy-start(f32[256,12]{0,1:T(8,128)} %param.58) | copy-start | bytes 36868
  0.9 90.1 %copy-start.21 = (f32[256,12]{0,1:T(8,128)S(1)}, f32[256,12]{0,1:T(8,128)}, u32[]{:S(2)}) copy-start(f32[256,12]{0,1:T(8,128)} %param.59) | copy-start | bytes 36868
  0.9 90.1 %copy-start.24 = (f32[2,256]{1,0:T(2,128)S(1)}, f32[2,256]{1,0:T(2,128)}, u32[]{:S(2)}) copy-start(f32[2,256]{1,0:T(2,128)} %refs_22_.1) | copy-start | bytes 6148
  90.7 0.7 copy-start.23
  90.7 0.7 copy-start.22

commit v4 on v3

--- a/solution.py
+++ b/solution.py
@@ -42,7 +42,7 @@
 DB1, DB2, DB3, MAXLV, MINLV, LOGA = 1550, 2950, 4350, 4602, 4620, 4638
 
 R_IN, R_HEAD, R_OUT, R_MISC, R_SMALL = 0, 72, 88, 96, 128
-D_IN, D_OUT, D_B2, D_B3, D_UP, D_LOW, D_LOSS, D_ROWS = 0, 24, 60, 61, 62, 63, 64, 72
+D_IN, D_OUT, D_B2, D_B3, D_UP, D_LOW, D_LOSS, D_HID, D_ROWS = 0, 24, 60, 61, 62, 63, 64, 72, 128
 
 F32, BF16 = jnp.float32, jnp.bfloat16
 MESH = pl.DeviceIdType.MESH
@@ -161,6 +161,24 @@
         self.split_z = all(chunk % self.n_blk == 0 for chunk in self.chunks)
         self.owners = [self.n_dp - 5, self.n_dp - 3, self.n_dp - 1]
 
+        groups = [("fold", g, s) for g in range(2) for s in range(self.bits)]
+        groups += [(name, g) for name in ("first", "second") for g in range(2)]
+        common = ["hidden", "hidden on", "lists", "own", "line", "plane", "dyn h", "dyn m", "sac m", "small"]
+        common += groups
+        kinds = [(name, kind) for name in ("pack", "x") for kind in ("own", "on")]
+        sent = common + [("tiles", k) for k in range(3)] + kinds
+        self.sent = {name: at for at, name in enumerate(sent)}
+        self.sent["sac g"] = len(sent)
+        self.sent["sac x"] = len(sent) + self.n_dp
+        self.departures = len(sent) + 2 * self.n_dp
+        self.here, self.arrivals = {}, 0
+        for name in common + ["tiles", ("pack", "sibling"), ("x", "sibling")]:
+            self.here[name] = self.arrivals
+            self.arrivals += 1
+        for name, number in (("sac g", 3), ("sac x", 3), (("pack", "like"), MEMBERS), (("x", "like"), MEMBERS)):
+            self.here[name] = self.arrivals
+            self.arrivals += number
+
     def part(self, group):
         return self.chunks[group] // self.n_blk if self.split_z else self.chunks[group]
 
@@ -169,19 +187,16 @@
     (
         replay, model, requests, member, live, noise, sac_h, sac_m, dyn_h, dyn_m, crit_in, act_in,
         dyn_in, crit_out, act_out, dyn_out, biases, targ_in, targ_hidden, targ_out, targ_bias,
-        sac_g, sac_x, dyn_g, dyn_x, dyn_s, small, count,
-        wg, asked, owned, dhg, dmg, smg, bk, xs, nz, w1f, w1t, w1n, w2t, w2h, heads, head_t, head_f,
+        sac_g, sac_x, dyn_x, dyn_s, small, count,
+        wg, lists, asked, dhg, dmg, smg, bk, xs, nz, w1f, w1t, w1n, w2t, w2h, heads, head_t, head_f,
         rowbuf, wide, headcol, acc_h, acc_w, acc_c, acc_a, acc_m, acc_l, grid_c, grid_a, zr_c, zr_a,
         zf_c, zf_a, mg, mat, grow, dcols, dacc_h, dacc_w, dacc_o, dacc_m, dacc_b, dacc_l, xt, dmat,
-        dpack, drow_g, drow_x, bias, dhead, dhead_t, *rest,
+        dpack, drow_x, bias, dhead, dhead_t, *rest,
     ) = refs
     bits = lay.bits
     bufs = (rest[:bits], rest[bits : 2 * bits])
-    (
-        s_w, r_w, s_q, r_q, s_p, r_p, s_dh, r_dh, s_dm, r_dm, s_sm, r_sm, s_bz, r_bz, s_bo, r_bo,
-        s_bp, r_bp, s_rs, r_rs, s_zr, r_zr, s_za, r_za, s_pl, r_pl, s_mg, r_mg, s_ds, r_ds, s_dg,
-        r_dg, s_dx, r_dx, f_ds, f_dg, f_dx, s_sg, r_sg, s_sx, r_sx,
-    ) = rest[2 * bits :]
+    send, recv = rest[2 * bits :]
+    sent, here_at = lay.sent, lay.here
     grids, zrs, zfs = (grid_c, grid_a), (zr_c, zr_a), (zf_c, zf_a)
     n_dp, n_blk = lay.n_dp, lay.n_blk
     me = lax.axis_index("dp")
@@ -207,54 +222,67 @@
             device_id={"blk": peer}, device_id_type=MESH,
         )
 
+    def over(number, body):
+        if number <= 8:
+            for off in range(1, number):
+                body(off)
+        else:
+            pl.loop(1, number)(body)
+
     def plane_peers(body):
-        @pl.loop(1, n_dp)
-        def _(off):
-            body(lax.rem(me + off, n_dp))
+        over(n_dp, lambda off: body(lax.rem(me + off, n_dp)))
 
     def like_peers(body):
-        @pl.loop(1, n_dp // 2)
-        def _(off):
-            body(lax.rem(me + 2 * off, n_dp))
+        over(n_dp // 2, lambda off: body(lax.rem(me + 2 * off, n_dp)))
 
     def line_peers(body):
-        @pl.loop(1, n_blk)
-        def _(off):
-            body(lax.rem(z + off, n_blk))
+        over(n_blk, lambda off: body(lax.rem(z + off, n_blk)))
+
+    def has_sent(view, name):
+        at = send.at[sent[name]]
+        on_plane(view, view, at, at, sibling).wait_send()
+
+    def has_come(view, name):
+        at = recv.at[here_at[name]]
+        on_plane(view, view, at, at, sibling).wait_recv()
 
     barrier = pltpu.get_barrier_semaphore()
     plane_peers(lambda peer: pl.semaphore_signal(barrier, inc=1, device_id={"dp": peer}, device_id_type=MESH))
     line_peers(lambda peer: pl.semaphore_signal(barrier, inc=1, device_id={"blk": peer}, device_id_type=MESH))
-    wg[z] = sac_h[...].astype(BF16)
+    wg[0] = sac_h[...].astype(BF16)
+    lists[0] = requests[...]
+    lists[1] = member[...]
     pl.semaphore_wait(barrier, n_dp - 1 + n_blk - 1)
 
-    def hidden_copy(owner, part, peer):
-        at = (2, 1) if part == 0 else (0, 2)
-        view = wg.at[owner, pl.ds(*at)]
-        return on_line(view, view, s_w.at[part, peer], r_w.at[part, owner], peer)
-
-    line_peers(lambda peer: hidden_copy(z, 0, peer).start())
-
-    def list_copy(owner, peer):
-        return on_plane(requests, asked.at[owner], s_q.at[peer], r_q.at[owner], peer)
-
-    def member_copy(owner, peer):
-        return on_plane(member, owned.at[owner], s_p.at[peer], r_p.at[owner], peer)
-
-    plane_peers(lambda peer: list_copy(me, peer).start())
-    plane_peers(lambda peer: member_copy(me, peer).start())
-    line_peers(lambda peer: hidden_copy(z, 1, peer).start())
-    asked[me] = requests[...]
-    owned[me] = member[...]
-
-    def dyn_h_copy(owner, peer):
-        return on_line(dyn_h.at[dyn_e], dhg.at[owner], s_dh.at[peer], r_dh.at[owner], peer)
-
-    def dyn_m_copy(owner, peer):
-        return on_line(dyn_m.at[dyn_e], dmg.at[owner], s_dm.at[peer], r_dm.at[owner], peer)
-
-    def sac_m_copy(owner, peer):
-        return on_line(sac_m.at[sac_k], smg.at[owner], s_sm.at[peer], r_sm.at[owner], peer)
+    half_rows = pl.ds(pl.multiple_of(core * (lay.rows // 2), lay.rows // 2), lay.rows // 2)
+
+    def slot_from(owner, at):
+        return lax.rem(owner - at + n_blk, n_blk)
+
+    def hidden_copy(peer):
+        src = wg.at[0, :, half_rows]
+        dst = wg.at[slot_from(z, peer), :, half_rows]
+        return on_line(src, dst, send.at[sent["hidden"]], recv.at[here_at["hidden"]], peer)
+
+    def hidden_on():
+        view = wg.at[pl.ds(1, n_blk - 1), :, half_rows]
+        return on_plane(view, view, send.at[sent["hidden on"]], recv.at[here_at["hidden on"]], sibling)
+
+    def list_copy(peer):
+        return on_plane(lists, asked.at[me], send.at[sent["lists"]], recv.at[here_at["lists"]], peer)
+
+    line_peers(lambda peer: hidden_copy(peer).start())
+    plane_peers(lambda peer: list_copy(peer).start())
+    asked[me] = lists[...]
+
+    def dyn_h_copy(peer):
+        return on_line(dyn_h.at[dyn_e], dhg.at[z], send.at[sent["dyn h"]], recv.at[here_at["dyn h"]], peer)
+
+    def dyn_m_copy(peer):
+        return on_line(dyn_m.at[dyn_e], dmg.at[z], send.at[sent["dyn m"]], recv.at[here_at["dyn m"]], peer)
+
+    def sac_m_copy(peer):
+        return on_line(sac_m.at[sac_k], smg.at[z], send.at[sent["sac m"]], recv.at[here_at["sac m"]], peer)
 
     alive = live[...].astype(F32).reshape(1, lay.model)
     bias[...] = biases[...].reshape(1, NB)
@@ -314,11 +342,7 @@
     squares = jnp.sum(data[0:24] * data[0:24], axis=1, keepdims=True)
     living = jnp.sum(alive, axis=1, keepdims=True)
 
-    def wait_lists(peer):
-        list_copy(peer, peer).wait_recv()
-        member_copy(peer, peer).wait_recv()
-
-    plane_peers(wait_lists)
+    has_come(asked.at[pl.ds(0, n_dp - 1)], "lists")
     spread = (
         lax.rem(lax.broadcasted_iota(jnp.int32, (CAP, lay.real), 1), CAP)
         == lax.broadcasted_iota(jnp.int32, (CAP, lay.real), 0)
@@ -328,14 +352,14 @@
         == lax.broadcasted_iota(jnp.int32, (n_dp, lay.real), 0)
     )
 
-    def in_lanes(ref):
-        lists = ref[:, me, :].astype(F32)
+    def in_lanes(which):
+        values = asked[:, which, me, :].astype(F32)
         wide = lax.dot_general(
-            lists, spread, NN, precision=lax.Precision.HIGHEST, preferred_element_type=F32
+            values, spread, NN, precision=lax.Precision.HIGHEST, preferred_element_type=F32
         )
         return jnp.sum(jnp.where(here, wide, 0.0), axis=0, keepdims=True)
 
-    slots = in_lanes(asked)
+    slots = in_lanes(0)
     wanted = jnp.maximum(slots, 0.0).astype(jnp.int32)
     hot = (rows_of((lay.replay, lay.real)) == wanted).astype(BF16)
     high, middle, low = pieces(data)
@@ -343,7 +367,7 @@
     mine = me * n_blk
     bk[mine, 0:FEAT, 0 : lay.real] = picked
     bk[mine, 42:43, 0 : lay.real] = (slots >= 0.0).astype(F32)
-    bk[mine, 43:44, 0 : lay.real] = in_lanes(owned)
+    bk[mine, 43:44, 0 : lay.real] = in_lanes(1)
     bk[mine, 44:48, 0 : lay.real] = jnp.zeros((4, lay.real), F32)
     bk[mine, :, lay.real : lay.width] = jnp.zeros((48, lay.width - lay.real), F32)
     bk[mine, 0:24, lay.real : lay.real + 1] = sums
@@ -352,45 +376,39 @@
 
     def slot_of(block):
         line = lax.rem(block, n_blk)
-        return block - line + lax.rem(line - z + n_blk, n_blk)
-
-    def block_line(owner, peer):
-        slot = me * n_blk + lax.rem(owner - peer + n_blk, n_blk)
-        return on_line(bk.at[mine], bk.at[slot], s_bz.at[peer], r_bz.at[owner], peer)
-
-    def block_arrives(owner):
-        slot = me * n_blk + lax.rem(owner - z + n_blk, n_blk)
-        on_line(bk.at[mine], bk.at[slot], s_bz.at[owner], r_bz.at[owner], owner).wait_recv()
-
-    def block_own(owner, peer):
-        view = bk.at[owner * n_blk]
-        return on_plane(view, view, s_bo.at[peer], r_bo.at[owner], peer)
-
-    def block_plane(owner, peer):
-        view = bk.at[pl.ds(owner * n_blk + 1, n_blk - 1)]
-        return on_plane(view, view, s_bp.at[peer], r_bp.at[owner], peer)
-
-    plane_peers(lambda peer: block_own(me, peer).start())
-    line_peers(lambda peer: block_line(z, peer).start())
+        return block - line + slot_from(line, z)
+
+    def block_line(peer):
+        dst = bk.at[me * n_blk + slot_from(z, peer)]
+        return on_line(bk.at[mine], dst, send.at[sent["line"]], recv.at[here_at["line"]], peer)
+
+    def block_own(peer):
+        view = bk.at[mine]
+        return on_plane(view, view, send.at[sent["own"]], recv.at[here_at["own"]], peer)
+
+    def block_plane(peer):
+        view = bk.at[pl.ds(mine + 1, n_blk - 1)]
+        return on_plane(view, view, send.at[sent["plane"]], recv.at[here_at["plane"]], peer)
+
+    plane_peers(lambda peer: block_own(peer).start())
+    line_peers(lambda peer: block_line(peer).start())
+    has_come(wg.at[pl.ds(0, n_blk - 1), :, half_rows], "hidden")
+    hidden_on().start()
 
     @pl.when(is_dyn)
     def _():
-        line_peers(lambda peer: dyn_h_copy(z, peer).start())
-        line_peers(lambda peer: dyn_m_copy(z, peer).start())
+        line_peers(lambda peer: dyn_h_copy(peer).start())
+        line_peers(lambda peer: dyn_m_copy(peer).start())
 
     @pl.when(is_sac)
     def _():
-        line_peers(lambda peer: sac_m_copy(z, peer).start())
-
-    def wait_hidden(peer):
-        hidden_copy(peer, 0, peer).wait_recv()
-        hidden_copy(peer, 1, peer).wait_recv()
-
-    line_peers(wait_hidden)
+        line_peers(lambda peer: sac_m_copy(peer).start())
+
+    has_come(wg.at[pl.ds(0, n_blk - 1), :, half_rows], "hidden on")
     for k in range(3):
         for block in range(n_blk):
             w2h[k, block * lay.rows : (block + 1) * lay.rows, :] = (
-                0.5 * wg[block, k].astype(F32)
+                0.5 * wg[slot_from(block, z), k].astype(F32)
             ).astype(BF16)
         w2t[2 + k] = w2h[k].astype(F32).T.astype(BF16)
 
@@ -456,12 +474,12 @@
     def _(step):
         @pl.when(step == 1)
         def _():
-            line_peers(block_arrives)
-            plane_peers(lambda peer: block_plane(me, peer).start())
+            has_come(bk.at[pl.ds(0, n_blk - 1)], "line")
+            plane_peers(lambda peer: block_plane(peer).start())
 
         @pl.when(step == n_tiles - 1)
         def _():
-            plane_peers(lambda peer: block_own(peer, peer).wait_recv())
+            has_come(bk.at[pl.ds(0, n_dp - 1)], "own")
             lanes = lax.broadcasted_iota(jnp.int32, (48, lay.width), 1) // CAP
 
             def gather(owner, total):
@@ -538,8 +556,8 @@
         half = n_dp >> (s + 1)
         begin = starts[s] + (1 - faces[s]) * half
         return on_plane(
-            grids[group].at[pl.ds(begin, half)], bufs[group][s], s_rs.at[group, s], r_rs.at[group, s],
-            partners[s],
+            grids[group].at[pl.ds(begin, half)], bufs[group][s], send.at[sent["fold", group, s]],
+            recv.at[here_at["fold", group, s]], partners[s],
         )
 
     def fold_wait(group, s):
@@ -549,40 +567,48 @@
         for at in range(half):
             grids[group][begin + at] += bufs[group][s][at]
 
-    def line_first(group, owner, peer):
+    def line_first(group, peer):
         if lay.split_z:
             src = grids[group].at[place, pl.ds(peer * lay.part(group), lay.part(group))]
         else:
             src = grids[group].at[place]
-        return on_line(src, zrs[group].at[owner], s_zr.at[group, peer], r_zr.at[group, owner], peer)
-
-    def line_second(group, owner, peer):
-        view = zfs[group].at[pl.ds(owner * lay.part(group), lay.part(group))]
-        return on_line(view, view, s_za.at[group, peer], r_za.at[group, owner], peer)
+        name = ("first", group)
+        return on_line(src, zrs[group].at[z], send.at[sent[name]], recv.at[here_at[name]], peer)
+
+    def line_second(group, peer):
+        view = zfs[group].at[pl.ds(z * lay.part(group), lay.part(group))]
+        name = ("second", group)
+        return on_line(view, view, send.at[sent[name]], recv.at[here_at[name]], peer)
+
+    def firsts_of(group):
+        return zrs[group].at[pl.ds(0, n_blk - 1)]
+
+    def seconds_of(group):
+        return zfs[group].at[pl.ds(0, (n_blk - 1) * lay.part(group))]
 
     def line_start(group):
-        line_peers(lambda peer: line_first(group, z, peer).start())
+        line_peers(lambda peer: line_first(group, peer).start())
 
     def line_sum(group):
         part, zr, zf = lay.part(group), zrs[group], zfs[group]
-        line_peers(lambda peer: line_first(group, peer, peer).wait_recv())
+        has_come(firsts_of(group), ("first", group))
         zr[z] = grids[group][place, pl.ds(z * part, part)] if lay.split_z else grids[group][place]
         whole = zr[0]
         for block in range(1, n_blk):
             whole = whole + zr[block]
         if lay.split_z:
             zf[pl.ds(z * part, part)] = whole
-            line_peers(lambda peer: line_second(group, z, peer).start())
+            line_peers(lambda peer: line_second(group, peer).start())
         else:
             zf[...] = whole
 
     def line_end(group):
         if lay.split_z:
-            line_peers(lambda peer: line_second(group, peer, peer).wait_recv())
+            has_come(seconds_of(group), ("second", group))
 
     def tile_copy(k, owner):
         src = zfs[k // 2].at[pl.ds((k % 2) * lay.mat, lay.mat)]
-        return on_plane(src, mg.at[place], s_mg.at[k], r_mg.at[place], owner)
+        return on_plane(src, mg.at[place], send.at[sent["tiles", k]], recv.at[here_at["tiles"]], owner)
 
     def send_tiles(group):
         for k in (0, 1) if group == 0 else (2,):
@@ -594,10 +620,10 @@
             def _():
                 mg[place] = zfs[group][(k % 2) * lay.mat : (k % 2 + 1) * lay.mat]
 
-    def small_copy(at, peer):
+    def small_copy(peer):
         return on_plane(
-            zf_a.at[pl.ds(lay.mat, lay.sml)], small.at[pl.ds(at * lay.sml, lay.sml)],
-            s_pl.at[peer], r_pl.at[at], peer,
+            zf_a.at[pl.ds(lay.mat, lay.sml)], small.at[pl.ds(place * lay.sml, lay.sml)],
+            send.at[sent["small"]], recv.at[here_at["small"]], peer,
         )
 
     def chain(group):
@@ -617,7 +643,7 @@
             line_end(group)
             send_tiles(group)
             if group == 1:
-                plane_peers(lambda peer: small_copy(place, peer).start())
+                plane_peers(lambda peer: small_copy(peer).start())
                 small[pl.ds(place * lay.sml, lay.sml)] = zf_a[lay.mat :]
 
         steps.append(finish)
@@ -686,7 +712,7 @@
     put(R_MISC + 8, jnp.zeros((R_SMALL - R_MISC - 8, HSAC), F32))
     actor_chain[0]()
 
-    plane_peers(lambda peer: block_plane(peer, peer).wait_recv())
+    has_come(bk.at[pl.ds(0, (n_dp - 1) * (n_blk - 1))], "plane")
     lane0 = lay.real // 128 * 128
 
     def add_block(at, carry):
@@ -733,11 +759,8 @@
         dhead_t[...] = (0.5 * rounded(dpack[0:48, :])).T.astype(BF16)
         dpack[...] = jnp.zeros_like(dpack)
 
-        def wait_dyn(peer):
-            dyn_h_copy(peer, peer).wait_recv()
-            dyn_m_copy(peer, peer).wait_recv()
-
-        line_peers(wait_dyn)
+        has_come(dhg.at[pl.ds(0, n_blk - 1)], "dyn h")
+        has_come(dmg.at[pl.ds(0, n_blk - 1)], "dyn m")
         dhg[z] = dyn_h[dyn_e]
         dmg[z] = dyn_m[dyn_e]
         dmat[...] = jnp.zeros_like(dmat)
@@ -801,50 +824,48 @@
             g1 = sloped(dot(w2h[0], g2), slope1)
             dacc_w[...] += dot(inputs, g1, NT)
 
-    def pack_copy(src, owner, ssem, peer):
-        return on_plane(src, dyn_s.at[owner], ssem, r_ds.at[owner], peer)
-
-    def dyn_g_copy(src, owner, ssem, peer):
-        return on_plane(src, dyn_g.at[owner], ssem, r_dg.at[owner], peer)
-
-    def dyn_x_copy(src, owner, ssem, peer):
-        return on_plane(src, dyn_x.at[owner], ssem, r_dx.at[owner], peer)
-
-    def give(copy, src, sems):
-        like_peers(lambda peer: copy(src, dyn_e, sems.at[peer], peer).start())
-        copy(src, dyn_e, sems.at[sibling], sibling).start()
-
-    def given(copy, src, sems):
-        like_peers(lambda peer: copy(src, dyn_e, sems.at[peer], peer).wait_send())
-        copy(src, dyn_e, sems.at[sibling], sibling).wait_send()
-
-    def from_like(body):
-        def member_only(peer):
+    out_of = {"pack": dyn_s, "x": dyn_x}
+
+    def member_copy(name, src, owner, kind, sem, peer):
+        return on_plane(src, out_of[name].at[owner], send.at[sent[name, kind]], recv.at[sem], peer)
+
+    def give(name, src):
+        like_peers(
+            lambda peer: member_copy(name, src, dyn_e, "own", here_at[name, "like"] + dyn_e, peer).start()
+        )
+        member_copy(name, src, dyn_e, "own", here_at[name, "sibling"], sibling).start()
+
+    def hand_on(name):
+        def body(peer):
             @pl.when(peer < MEMBERS)
             def _():
-                body(jnp.minimum(peer, MEMBERS - 1))
-
-        like_peers(member_only)
-
-    def hand_on(copy, out, sems):
-        def body(owner):
-            copy(out.at[owner], owner, sems.at[owner], sibling).wait_recv()
-            copy(out.at[owner], owner, sems.at[owner], sibling).start()
-
-        from_like(body)
-
-    def handed_on(copy, out, sems):
-        from_like(lambda owner: copy(out.at[owner], owner, sems.at[owner], sibling).wait_send())
-
-    def from_sibling(copy, out, sems):
-        @pl.loop(0, n_dp // 2)
-        def _(off):
-            owner = lax.rem(sibling + 2 * off, n_dp)
-
-            @pl.when(owner < MEMBERS)
+                owner = jnp.minimum(peer, MEMBERS - 1)
+                view = out_of[name].at[owner]
+                member_copy(name, view, owner, "on", here_at[name, "like"] + owner, sibling).wait_recv()
+                member_copy(name, view, owner, "on", here_at[name, "sibling"], sibling).start()
+
+        like_peers(body)
+
+    even, odd = (MEMBERS + 1) // 2, MEMBERS // 2
+    handed = even - core * (even - odd) - jnp.where(is_dyn, 1, 0)
+
+    def from_sibling(name):
+        for side, number in ((0, odd), (1, even)):
+            @pl.when(core == side)
             def _():
-                at = jnp.minimum(owner, MEMBERS - 1)
-                copy(out.at[at], at, sems.at[at], sibling).wait_recv()
+                has_come(out_of[name].at[pl.ds(0, number)], (name, "sibling"))
+
+    def gave(name):
+        @pl.when(is_dyn)
+        def _():
+            for begin in range(0, n_dp // 2, MEMBERS):
+                number = min(MEMBERS, n_dp // 2 - begin)
+                has_sent(out_of[name].at[pl.ds(0, number)], (name, "own"))
+
+        for number in (even, even - 1, even - 2):
+            @pl.when(handed == number)
+            def _():
+                has_sent(out_of[name].at[pl.ds(0, number)], (name, "on"))
 
     def line_rows(ref):
         rows = ref[0 : lay.drows, 0:HDYN]
@@ -854,23 +875,18 @@
 
     def sac_g_copy(k, peer):
         src = grow.at[pl.ds(pl.multiple_of(z * lay.rows, lay.rows), lay.rows)]
-        return on_plane(src, sac_g.at[k], s_sg.at[peer], r_sg.at[k], peer)
+        return on_plane(src, sac_g.at[k], send.at[sent["sac g"] + peer], recv.at[here_at["sac g"] + k], peer)
 
     def sac_x_copy(k, peer):
         src = mat.at[pl.ds(pl.multiple_of(z * lay.rows, lay.rows), lay.rows)]
-        return on_plane(src, sac_x.at[k], s_sx.at[peer], r_sx.at[k], peer)
+        return on_plane(src, sac_x.at[k], send.at[sent["sac x"] + peer], recv.at[here_at["sac x"] + k], peer)
 
     mine_rows = pl.ds(pl.multiple_of(z * lay.rows, lay.rows), lay.rows)
 
     def take_matrix():
-        line_peers(lambda peer: sac_m_copy(peer, peer).wait_recv())
+        has_come(smg.at[pl.ds(0, n_blk - 1)], "sac m")
         smg[z] = sac_m[sac_k]
-
-        @pl.loop(1, n_dp)
-        def _(off):
-            at = lax.rem(place + off, n_dp)
-            on_plane(mg.at[at], mg.at[at], s_mg.at[0], r_mg.at[at], me).wait_recv()
-
+        has_come(mg.at[pl.ds(0, n_dp - 1)], "tiles")
         for chunk in range(n_dp):
             tile = chunk * lay.mat
             side, row = tile // 32, tile % 32
@@ -901,12 +917,9 @@
         dpack[D_LOSS : D_LOSS + 1, 0:128] = jnp.broadcast_to(
             jnp.sum(dacc_l[0:1, :], axis=1, keepdims=True), (1, 128)
         )
+        dpack[D_HID : D_HID + lay.drows, 0:HDYN] = line_rows(dacc_h)
         dyn_s[dyn_e] = dpack[...]
-        give(pack_copy, dpack, s_ds)
-        rows = line_rows(dacc_h)
-        drow_g[...] = rows
-        dyn_g[dyn_e] = rows
-        give(dyn_g_copy, drow_g, s_dg)
+        give("pack", dpack)
         dmat[...] = jnp.zeros_like(dmat)
         for block in range(n_blk):
             at = slice(block * lay.drows, (block + 1) * lay.drows)
@@ -937,40 +950,33 @@
         rows = line_rows(dmat)
         drow_x[...] = rows
         dyn_x[dyn_e] = rows
-        give(dyn_x_copy, drow_x, s_dx)
+        give("x", drow_x)
 
     pl.when(is_critic)(send_sac)
 
-    def sent_on_line(peer):
-        hidden_copy(z, 0, peer).wait_send()
-        hidden_copy(z, 1, peer).wait_send()
-        block_line(z, peer).wait_send()
-        for group in range(2):
-            line_first(group, z, peer).wait_send()
-            if lay.split_z:
-                line_second(group, z, peer).wait_send()
+    def sent_early():
+        has_sent(wg.at[pl.ds(0, n_blk - 1), :, half_rows], "hidden")
+        has_sent(wg.at[pl.ds(0, n_blk - 1), :, half_rows], "hidden on")
+        has_sent(asked.at[pl.ds(0, n_dp - 1)], "lists")
+        has_sent(bk.at[pl.ds(0, n_dp - 1)], "own")
+        has_sent(bk.at[pl.ds(0, n_blk - 1)], "line")
+        has_sent(bk.at[pl.ds(0, (n_dp - 1) * (n_blk - 1))], "plane")
 
         @pl.when(is_dyn)
         def _():
-            dyn_h_copy(z, peer).wait_send()
-            dyn_m_copy(z, peer).wait_send()
+            has_sent(dhg.at[pl.ds(0, n_blk - 1)], "dyn h")
+            has_sent(dmg.at[pl.ds(0, n_blk - 1)], "dyn m")
 
         @pl.when(is_sac)
         def _():
-            sac_m_copy(z, peer).wait_send()
-
-    def sent_on_plane(peer):
-        list_copy(me, peer).wait_send()
-        member_copy(me, peer).wait_send()
-        block_own(me, peer).wait_send()
-        block_plane(me, peer).wait_send()
-
-    def sent_early():
-        line_peers(sent_on_line)
-        plane_peers(sent_on_plane)
+            has_sent(smg.at[pl.ds(0, n_blk - 1)], "sac m")
+
         for group in range(2):
             for s in range(bits):
                 fold_copy(group, s).wait_send()
+            has_sent(firsts_of(group), ("first", group))
+            if lay.split_z:
+                has_sent(seconds_of(group), ("second", group))
 
     @pl.when(is_actor)
     def _():
@@ -980,46 +986,29 @@
         send_sac()
 
     pl.when(jnp.logical_not(is_actor))(sent_early)
-    hand_on(pack_copy, dyn_s, f_ds)
-    hand_on(dyn_g_copy, dyn_g, f_dg)
-    hand_on(dyn_x_copy, dyn_x, f_dx)
-
-    @pl.loop(1, n_dp)
-    def _(off):
-        small_copy(lax.rem(place + off, n_dp), me).wait_recv()
-
-    from_sibling(pack_copy, dyn_s, f_ds)
-    from_sibling(dyn_g_copy, dyn_g, f_dg)
-    from_sibling(dyn_x_copy, dyn_x, f_dx)
+    hand_on("pack")
+    hand_on("x")
+    has_come(small.at[pl.ds(0, (n_dp - 1) * lay.sml)], "small")
+    from_sibling("pack")
+    from_sibling("x")
     for k in range(3):
         @pl.when(me != lay.owners[k])
         def _():
             sac_g_copy(k, me).wait_recv()
             sac_x_copy(k, me).wait_recv()
 
-    def sent_late(peer):
-        small_copy(place, peer).wait_send()
-
-        @pl.when(is_sac)
-        def _():
-            sac_g_copy(sac_k, peer).wait_send()
-            sac_x_copy(sac_k, peer).wait_send()
-
-    plane_peers(sent_late)
-
-    @pl.when(is_dyn)
-    def _():
-        given(pack_copy, dpack, s_ds)
-        given(dyn_g_copy, drow_g, s_dg)
-        given(dyn_x_copy, drow_x, s_dx)
-
-    handed_on(pack_copy, dyn_s, f_ds)
-    handed_on(dyn_g_copy, dyn_g, f_dg)
-    handed_on(dyn_x_copy, dyn_x, f_dx)
+    has_sent(small.at[pl.ds(0, (n_dp - 1) * lay.sml)], "small")
+    gave("pack")
+    gave("x")
     for k in range(3):
         @pl.when(me != lay.owners[k])
         def _():
             tile_copy(k, lay.owners[k]).wait_send()
+
+    @pl.when(is_sac)
+    def _():
+        plane_peers(lambda peer: sac_g_copy(sac_k, peer).wait_send())
+        plane_peers(lambda peer: sac_x_copy(sac_k, peer).wait_send())
 
 
 def adamw(weights, first, second, gradient):
@@ -1033,7 +1022,7 @@
 
 def update_kernel(*refs):
     (
-        sac_g, sac_x, dyn_g, dyn_x, dyn_s, small, count, sac_h, sac_m, dyn_h, dyn_m,
+        sac_g, sac_x, dyn_x, dyn_s, small, count, sac_h, sac_m, dyn_h, dyn_m,
         ci, ci_m, ci_v, ai, ai_m, ai_v, di, di_m, di_v, co, co_m, co_v, ao, ao_m, ao_v,
         do, do_m, do_v, bi, bi_m, bi_v,
         sac_new, sac_mom, dyn_new, dyn_mom, ci_n, ci_mn, ci_vn, ai_n, ai_mn, ai_vn, di_n, di_mn,
@@ -1043,7 +1032,8 @@
     total = count[0:1, 0:1]
     sac_mom[...] = MOMENTUM * sac_m[...] + sac_g[...] / total.reshape(1, 1, 1)
     sac_new[...] = sac_h[...] * (1.0 - MUON_RATE * MUON_DECAY) - MUON_RATE * sac_x[...]
-    dyn_mom[...] = MOMENTUM * dyn_m[...] + dyn_g[...] / total.reshape(1, 1, 1)
+    dyn_rows = dyn_s[:, D_HID : D_HID + dyn_m.shape[1], 0:HDYN]
+    dyn_mom[...] = MOMENTUM * dyn_m[...] + dyn_rows / total.reshape(1, 1, 1)
     dyn_new[...] = dyn_h[...] * (1.0 - MUON_RATE * MUON_DECAY) - MUON_RATE * dyn_x[...]
 
     def rows(row, number):
@@ -1141,7 +1131,6 @@
         pltpu.VMEM((3, rows, HSAC), F32),
         pltpu.VMEM((3, rows, HSAC), F32),
         pltpu.VMEM((MEMBERS, drows, HDYN), F32),
-        pltpu.VMEM((MEMBERS, drows, HDYN), F32),
         pltpu.VMEM((MEMBERS, D_ROWS, HSAC), F32),
         pltpu.VMEM((32, 8, 128), F32),
         pltpu.VMEM((8, 128), F32),
@@ -1150,13 +1139,10 @@
     def vm(*dims, kind=F32):
         return pltpu.VMEM(dims, kind)
 
-    def sems(*dims):
-        return [pltpu.SemaphoreType.DMA(dims), pltpu.SemaphoreType.DMA(dims)]
-
     scratch = [
         vm(n_blk, 3, rows, HSAC, kind=BF16),
-        vm(n_dp, n_dp, CAP, kind=jnp.int32),
-        vm(n_dp, n_dp, CAP, kind=jnp.int32),
+        vm(2, n_dp, CAP, kind=jnp.int32),
+        vm(n_dp, 2, n_dp, CAP, kind=jnp.int32),
         vm(n_blk, drows, HDYN),
         vm(n_blk, drows, HDYN),
         vm(n_blk, rows, HSAC),
@@ -1200,21 +1186,12 @@
         vm(HSAC, HSAC),
         vm(D_ROWS, HSAC),
         vm(drows, HDYN),
-        vm(drows, HDYN),
         vm(1, NB),
         vm(48, HSAC, kind=BF16),
         vm(HSAC, 48, kind=BF16),
     ]
     scratch += [vm(n_dp >> (s + 1), chunk, 8, 128) for chunk in lay.chunks for s in range(bits)]
-    scratch += sems(2, n_blk)
-    scratch += sems(n_dp) + sems(n_dp)
-    scratch += sems(n_blk) + sems(n_blk) + sems(n_blk)
-    scratch += sems(n_blk) + sems(n_dp) + sems(n_dp)
-    scratch += sems(2, bits) + sems(2, n_blk) + sems(2, n_blk) + sems(n_dp)
-    scratch += [pltpu.SemaphoreType.DMA((3,)), pltpu.SemaphoreType.DMA((n_dp,))]
-    scratch += sems(n_dp) + sems(n_dp) + sems(n_dp)
-    scratch += 3 * [pltpu.SemaphoreType.DMA((n_dp,))]
-    scratch += 2 * [pltpu.SemaphoreType.DMA((n_dp,)), pltpu.SemaphoreType.DMA((3,))]
+    scratch += [pltpu.SemaphoreType.DMA((lay.departures,)), pltpu.SemaphoreType.DMA((lay.arrivals,))]
     varying = 4 * (lay.n_dev * 48 * lay.width + 72 * lay.batch + 48 * lay.replay)
     gathered = pl.pallas_call(
         functools.partial(main_kernel, lay),

time: 93.8 us -> 84 us (0.90)
  Pallas kernels: 91.9 us -> 82.1 us
    pallas_call x1, Pallas kernels: 89.8 us -> 80 us  [shards(): pl.pallas_call(functools.partial(main_kernel, lay), out_shape=out_shape,...]
where the time goes in v4:
time: 84 us; the launch traced here: 83.7 us
  Pallas kernels  82.1 us (98%)
  between operations  1.07 us (1%)
    pallas_call x1, Pallas kernels, shards(): pl.pallas_call(functools.partial(main_kernel, lay), out_shape=out_shape,...  80 us
    pallas_call x1, Pallas kernels, shards(): pl.pallas_call(update_kernel, out_shape=tuple(new_shape), in_specs=[spec]...  2.13 us

profile of v4, /device:TPU:0, one launch (start us, length us, event | category | flops | bytes accessed | tf_op | source)
XLA Modules:
  0.0 83.7 jit_solution(2032781285778952108)
XLA Ops:
  0.7 0.0 copy-start
  0.7 0.0 copy-start.1
  0.7 0.0 copy-start.2
  0.7 0.0 copy-start.3
  0.7 0.0 copy-start.4
  0.7 0.0 copy-start.5
  0.7 0.0 copy-start.6
  0.7 0.0 copy-start.7
  0.8 0.0 copy-start.8
  0.8 0.0 copy-start.9
  0.8 0.0 copy-start.10
  0.8 0.0 copy-start.11
  0.8 0.0 copy-start.12
  0.8 0.0 copy-start.13
  0.8 0.0 copy-start.14
  0.8 0.0 copy-start.15
  0.8 0.0 copy-start.16
  0.8 0.0 copy-start.17
  0.9 0.0 copy-start.18
  0.9 0.0 copy-start.19
  0.9 0.0 copy-start.20
  0.9 0.0 copy-start.21
  0.9 0.0 copy-start.24
  0.9 80.0 %step.1 = (f32[3,64,256]{2,1,0:T(8,128)S(1)}, f32[3,64,256]{2,1,0:T(8,128)S(1)}, f32[7,50,200]{2,1,0:T(8,128)S(1)}, f32[7,128,256]{2,1,0:T(8,128)S(1)}, f32[32,8,128]{2,1,0:T(8,128)S(1)}, /*index=5*/f32[8,128]{1,0:T(8,128)S(1)}) custom-call(f32[42,3648]{1,0:T(8,128)} %refs_0_.1, f32[42,1216]{1,0:T(8,128)} %refs_1_.1, s32[8,8]{1,0:T(8,128)} %refs_2_.1, ...), custom_call_target="tpu_custom_call" | custom-call | tf_op jit(solution)/shard_map/step/pallas_call | solution.py:1196
  80.9 0.0 copy-start.23
  80.9 0.0 copy-start.22
  80.9 0.0 copy-done
  80.9 0.0 copy-done.1
  80.9 0.0 copy-done.2
  80.9 0.0 copy-done.3
  81.0 0.0 copy-done.4
  81.0 0.0 copy-done.5
  81.0 0.0 copy-done.6
  81.0 0.0 copy-done.7
  81.0 0.0 copy-done.8
  81.0 0.0 copy-done.9
  81.0 0.0 copy-done.10
  81.0 0.0 copy-done.11
  81.0 0.0 copy-done.12
  81.0 0.0 copy-done.13
  81.1 0.0 copy-done.14
  81.1 0.0 copy-done.15
  81.1 0.0 copy-done.16
  81.1 0.0 copy-done.17
  81.1 0.0 copy-done.18
  81.1 0.0 copy-done.19
  81.1 0.0 copy-done.20
  81.1 0.0 copy-done.21
  81.1 0.0 copy-done.24
  81.1 0.4 copy-done.23
  81.6 0.0 copy-done.22
  81.6 2.1 %update.1 = (f32[3,64,256]{2,1,0:T(8,128)}, f32[3,64,256]{2,1,0:T(8,128)}, f32[7,50,200]{2,1,0:T(8,128)}, f32[7,50,200]{2,1,0:T(8,128)}, f32[23,2,256]{2,1,0:T(2...) custom-call(f32[3,64,256]{2,1,0:T(8,128)S(1)} %get-tuple-element.60., ...), custom_call_target="tpu_custom_call" | custom-call | tf_op jit(solution)/shard_map/update/pallas_call | solution.py:1216
Async XLA Ops:
  0.7 80.2 %copy-start = (f32[7,50,200]{2,1,0:T(8,128)S(1)}, f32[7,50,200]{2,1,0:T(8,128)}, u32[]{:S(2)}) copy-start(f32[7,50,200]{2,1,0:T(8,128)} %refs_8_.3) | copy-start | bytes 840004
  0.7 80.2 %copy-start.1 = (f32[7,50,200]{2,1,0:T(8,128)S(1)}, f32[7,50,200]{2,1,0:T(8,128)}, u32[]{:S(2)}) copy-start(f32[7,50,200]{2,1,0:T(8,128)} %refs_9_.3) | copy-start | bytes 840004
  0.7 80.2 %copy-start.2 = (f32[7,200,36]{1,2,0:T(8,128)S(1)}, f32[7,200,36]{1,2,0:T(8,128)}, u32[]{:S(2)}) copy-start(f32[7,200,36]{1,2,0:T(8,128)} %param.60) | copy-start | bytes 604804
  0.7 80.2 %copy-start.3 = (f32[3,64,256]{2,1,0:T(8,128)S(1)}, f32[3,64,256]{2,1,0:T(8,128)}, u32[]{:S(2)}) copy-start(f32[3,64,256]{2,1,0:T(8,128)} %refs_6_.3) | copy-start | bytes 589828
  0.7 80.2 %copy-start.4 = (f32[3,64,256]{2,1,0:T(8,128)S(1)}, f32[3,64,256]{2,1,0:T(8,128)}, u32[]{:S(2)}) copy-start(f32[3,64,256]{2,1,0:T(8,128)} %refs_7_.3) | copy-start | bytes 589828
  0.7 80.2 %copy-start.5 = (f32[7,23,200]{2,1,0:T(8,128)S(1)}, f32[7,23,200]{2,1,0:T(8,128)}, u32[]{:S(2)}) copy-start(f32[7,23,200]{2,1,0:T(8,128)} %refs_16_.3) | copy-start | bytes 386404
  0.7 80.2 %copy-start.6 = (f32[7,200,36]{1,2,0:T(8,128)S(1)}, f32[7,200,36]{1,2,0:T(8,128)}, u32[]{:S(2)}) copy-start(f32[7,200,36]{1,2,0:T(8,128)} %param.61) | copy-start | bytes 604804
  0.7 80.2 %copy-start.7 = (f32[7,200,36]{1,2,0:T(8,128)S(1)}, f32[7,200,36]{1,2,0:T(8,128)}, u32[]{:S(2)}) copy-start(f32[7,200,36]{1,2,0:T(8,128)} %param.62) | copy-start | bytes 604804
  0.8 80.2 %copy-start.8 = (f32[2,23,256]{2,0,1:T(2,128)S(1)}, f32[2,23,256]{2,0,1:T(2,128)}, u32[]{:S(2)}) copy-start(f32[2,23,256]{2,0,1:T(2,128)} %param.45) | copy-start | bytes 141316
  0.8 80.2 %copy-start.9 = (f32[7,23,200]{2,1,0:T(8,128)S(1)}, f32[7,23,200]{2,1,0:T(8,128)}, u32[]{:S(2)}) copy-start(f32[7,23,200]{2,1,0:T(8,128)} %refs_17_.1) | copy-start | bytes 386404
  0.8 80.2 %copy-start.10 = (f32[7,23,200]{2,1,0:T(8,128)S(1)}, f32[7,23,200]{2,1,0:T(8,128)}, u32[]{:S(2)}) copy-start(f32[7,23,200]{2,1,0:T(8,128)} %refs_18_.3) | copy-start | bytes 386404
  0.8 80.2 %copy-start.11 = (f32[17,256]{1,0:T(8,128)S(1)}, f32[17,256]{1,0:T(8,128)}, u32[]{:S(2)}) copy-start(f32[17,256]{1,0:T(8,128)} %refs_13_.3) | copy-start | bytes 52228
  0.8 80.2 %copy-start.12 = (f32[4639]{0:T(1024)S(1)}, f32[4639]{0:T(1024)}, u32[]{:S(2)}) copy-start(f32[4639]{0:T(1024)} %refs_28_.1) | copy-start | bytes 55672
  0.8 80.2 %copy-start.13 = (f32[256,12]{0,1:T(8,128)S(1)}, f32[256,12]{0,1:T(8,128)}, u32[]{:S(2)}) copy-start(f32[256,12]{0,1:T(8,128)} %param.57) | copy-start | bytes 36868
  0.8 80.2 %copy-start.14 = (f32[2,23,256]{2,0,1:T(2,128)S(1)}, f32[2,23,256]{2,0,1:T(2,128)}, u32[]{:S(2)}) copy-start(f32[2,23,256]{2,0,1:T(2,128)} %param.46) | copy-start | bytes 141316
  0.8 80.2 %copy-start.15 = (f32[2,23,256]{2,0,1:T(2,128)S(1)}, f32[2,23,256]{2,0,1:T(2,128)}, u32[]{:S(2)}) copy-start(f32[2,23,256]{2,0,1:T(2,128)} %param.47) | copy-start | bytes 141316
  0.8 80.2 %copy-start.16 = (f32[17,256]{1,0:T(8,128)S(1)}, f32[17,256]{1,0:T(8,128)}, u32[]{:S(2)}) copy-start(f32[17,256]{1,0:T(8,128)} %refs_14_.1) | copy-start | bytes 52228
  0.8 80.2 %copy-start.17 = (f32[17,256]{1,0:T(8,128)S(1)}, f32[17,256]{1,0:T(8,128)}, u32[]{:S(2)}) copy-start(f32[17,256]{1,0:T(8,128)} %refs_15_.1) | copy-start | bytes 52228
  0.9 80.2 %copy-start.18 = (f32[4639]{0:T(1024)S(1)}, f32[4639]{0:T(1024)}, u32[]{:S(2)}) copy-start(f32[4639]{0:T(1024)} %refs_29_.1) | copy-start | bytes 55672
  0.9 80.2 %copy-start.19 = (f32[4639]{0:T(1024)S(1)}, f32[4639]{0:T(1024)}, u32[]{:S(2)}) copy-start(f32[4639]{0:T(1024)} %refs_30_.1) | copy-start | bytes 55672
  0.9 80.2 %copy-start.20 = (f32[256,12]{0,1:T(8,128)S(1)}, f32[256,12]{0,1:T(8,128)}, u32[]{:S(2)}) copy-start(f32[256,12]{0,1:T(8,128)} %param.58) | copy-start | bytes 36868
  0.9 80.2 %copy-start.21 = (f32[256,12]{0,1:T(8,128)S(1)}, f32[256,12]{0,1:T(8,128)}, u32[]{:S(2)}) copy-start(f32[256,12]{0,1:T(8,128)} %param.59) | copy-start | bytes 36868
  0.9 80.2 %copy-start.24 = (f32[2,256]{1,0:T(2,128)S(1)}, f32[2,256]{1,0:T(2,128)}, u32[]{:S(2)}) copy-start(f32[2,256]{1,0:T(2,128)} %refs_21_.1) | copy-start | bytes 6148
  80.9 0.7 copy-start.23
  80.9 0.7 copy-start.22

commit v5 on v4

--- a/solution.py
+++ b/solution.py
@@ -21,7 +21,8 @@
 NS_ITERS = 5
 STEP = 10
 CAP = 8
-TILE = 256
+TILE = 640
+DYN_TILE = 512
 ROWS = 32
 
 DISCOUNT = 0.99
@@ -72,7 +73,9 @@
 
 def product(a, b, dims=NN):
     left = jnp.concatenate([a[0], a[0], a[1]], 1)
-    return dot(left, jnp.concatenate([b[0], b[1], b[0]], dims[0][1][0]), dims)
+    right = jnp.concatenate([b[0], b[1], b[0]], dims[0][1][0])
+    half = left.shape[0] // 2
+    return jnp.concatenate([dot(left[:half], right, dims), dot(left[half:], right, dims)], 0)
 
 
 def softplus(v):
@@ -96,13 +99,13 @@
     return [jnp.concatenate(parts, 0) for parts in zip(*done)]
 
 
-def twice(column):
-    return jnp.concatenate([column] * (TILE // 128), 1)
+def spread_to(column, width):
+    return jnp.concatenate([column] * (width // 128), 1)
 
 
 def gated(half, column=None):
     def body(part, *offset):
-        value, slope = gate(part + twice(offset[0]) if offset else part)
+        value, slope = gate(part + spread_to(offset[0], part.shape[1]) if offset else part)
         return value.astype(BF16), slope
 
     return by_rows(body, half, *([] if column is None else [column]))
@@ -113,16 +116,18 @@
 
 
 def outer_sloped(column, row, slope):
-    return by_rows(lambda part, by: (((twice(part) * row) * by).astype(BF16),), column, slope)[0]
+    return by_rows(lambda part, by: (((spread_to(part, by.shape[1]) * row) * by).astype(BF16),), column, slope)[0]
 
 
 def rows_of(shape):
     return lax.broadcasted_iota(jnp.int32, shape, 0)
 
 
-def schulz(refs, steps):
+def schulz(refs, steps, before=None):
     @pl.loop(0, steps)
     def _(step):
+        if before is not None:
+            before(step)
         matrices = [ref[...] for ref in refs]
         parts = [split(matrix) for matrix in matrices]
         grams = [product(part, part, NT) for part in parts]
@@ -309,6 +314,9 @@
         w1n[k] = w1f[2 + k, 16:32, :].astype(BF16)
     for net in range(2):
         w2t[net] = (0.5 * rounded(targ_hidden[net])).T.astype(BF16)
+    has_come(wg.at[pl.ds(0, n_blk - 1), :, half_rows], "hidden")
+    hidden_on().start()
+
     rowbuf[...] = jnp.zeros_like(rowbuf)
     rowbuf[0:1, :] = targ_bias[0:1, HSAC : 2 * HSAC]
     rowbuf[1:2, :] = targ_bias[1:2, HSAC : 2 * HSAC]
@@ -392,8 +400,6 @@
 
     plane_peers(lambda peer: block_own(peer).start())
     line_peers(lambda peer: block_line(peer).start())
-    has_come(wg.at[pl.ds(0, n_blk - 1), :, half_rows], "hidden")
-    hidden_on().start()
 
     @pl.when(is_dyn)
     def _():
@@ -427,8 +433,8 @@
     def place_of(step):
         return pl.ds(pl.multiple_of(lax.rem(step + 1, n_tiles) * TILE, TILE), TILE)
 
-    def ones16():
-        return jnp.ones((16, TILE), BF16)
+    def ones16(width=TILE):
+        return jnp.ones((16, width), BF16)
 
     def framed(first_row, used, where):
         row32 = rows_of((32, TILE))
@@ -650,19 +656,30 @@
         return steps
 
     critic_chain, actor_chain = chain(0), chain(1)
+    per = DYN_TILE // lay.real
+    dyn_tiles = lay.n_dev // per
+    inside = min(bits + 2, n_tiles - 1)
+    in_actor = {step: [critic_chain[step]] for step in range(1, inside + 1)}
+    in_dyn = {}
+    for at, event in enumerate(critic_chain[inside + 1 :]):
+        in_dyn.setdefault(min(at, dyn_tiles - 1), []).append(event)
+    for at in range(1, bits + 1):
+        in_dyn.setdefault(min(at, dyn_tiles - 1), []).append(actor_chain[at])
+
+    def take(slots, step):
+        for at, events in slots.items():
+            @pl.when(step == at)
+            def _():
+                for event in events:
+                    event()
+
     for k in range(2):
         put_matrix(0, k, k)
     critic_chain[0]()
 
-    inside = min(len(critic_chain) - 1, n_tiles - 1)
-
     @pl.loop(0, n_tiles)
     def _(step):
-        for at in range(inside):
-            @pl.when(step == at + 1)
-            def _():
-                critic_chain[at + 1]()
-
+        take(in_actor, step)
         where = place_of(step)
         now_f = framed(0, IN, where)
         now_in = now_f.astype(BF16)
@@ -692,8 +709,6 @@
         acc_l[0:1, :] += weight * loss
         acc_l[1:2, :] += weight * (log_prob + TARGET_ENTROPY)
 
-    for at in range(inside, len(critic_chain) - 1):
-        critic_chain[at + 1]()
     put_matrix(1, 2, 0)
     for k in range(3):
         put(R_IN + 24 * k, acc_w[k, 0:24, :])
@@ -771,16 +786,9 @@
         for ref in (dacc_h, dacc_w, dacc_o, dacc_m, dacc_b, dacc_l):
             ref[...] = jnp.zeros_like(ref)
 
-    per = TILE // lay.real
-    dyn_tiles = lay.n_dev // per
-    gap = max(dyn_tiles // (bits + 1), 1)
-
     @pl.loop(0, dyn_tiles)
     def _(tile):
-        for s in range(bits):
-            @pl.when(tile == (s + 1) * gap)
-            def _():
-                actor_chain[s + 1]()
+        take(in_dyn, tile)
 
         @pl.when(is_dyn)
         def _():
@@ -789,9 +797,9 @@
                 xt[:, at * lay.real : (at + 1) * lay.real] = bk[slot, :, 0 : lay.real]
             now = xt[0:24, :]
             later = xt[24:48, :]
-            row24 = rows_of((24, TILE))
+            row24 = rows_of((24, DYN_TILE))
             scaled = jnp.where(row24 < IN, (now - centre) * scale, 1.0)
-            inputs = jnp.concatenate([scaled, (row8 < 2).astype(F32)], 0).astype(BF16)
+            inputs = jnp.concatenate([scaled, (rows_of((8, DYN_TILE)) < 2).astype(F32)], 0).astype(BF16)
             first, slope1 = gated(dot(w1t[0], inputs))
             second, slope2 = gated(dot(w2t[0], first), wide[0])
             out = dot(dhead[...], second) + dcols[0:48, 1:2]
@@ -818,9 +826,9 @@
                 [jnp.where(used, grad_mu, 0.0), jnp.where(used, grad_lv1 * open1, 0.0)], 0
             ).astype(BF16)
             dacc_o[...] += dot(g3, second, NT)
-            dacc_m[...] += dot(ones16(), g3, NT)
+            dacc_m[...] += dot(ones16(DYN_TILE), g3, NT)
             g2 = sloped(dot(dhead_t[...], g3), slope2)
-            dacc_h[...] += dot(jnp.concatenate([first, ones16()], 0), g2, NT)
+            dacc_h[...] += dot(jnp.concatenate([first, ones16(DYN_TILE)], 0), g2, NT)
             g1 = sloped(dot(w2h[0], g2), slope1)
             dacc_w[...] += dot(inputs, g1, NT)
 
@@ -899,6 +907,8 @@
             at = slice(block * lay.rows, (block + 1) * lay.rows)
             mat[at, :] = MOMENTUM * smg[block] + grow[at, :] / total
         normalise(mat)
+
+    actor_chain[bits + 1]()
 
     @pl.when(is_dyn)
     def _():
@@ -932,14 +942,15 @@
         pairs = [(is_critic, [dmat, mat]), (only_dyn, [dmat])]
     else:
         pairs = [(is_critic, [mat]), (is_dyn, [dmat])]
+    def sum_end(step):
+        pl.when(step == 2)(actor_chain[bits + 2])
+
     for test, matrices in pairs:
-        pl.when(test)(functools.partial(schulz, matrices, 2))
-    actor_chain[bits + 1]()
-    for test, matrices in pairs:
-        pl.when(test)(functools.partial(schulz, matrices, 2))
-    actor_chain[bits + 2]()
-    for test, matrices in pairs:
-        pl.when(test)(functools.partial(schulz, matrices, NS_ITERS - 4))
+        pl.when(test)(functools.partial(schulz, matrices, NS_ITERS, sum_end))
+    if n_dp <= MEMBERS + 1:
+        pl.when(is_actor)(actor_chain[bits + 2])
+    else:
+        pl.when(jnp.logical_not(jnp.logical_or(is_critic, is_dyn)))(actor_chain[bits + 2])
 
     def send_sac():
         sac_x[sac_k] = mat[mine_rows, :]
@@ -1180,9 +1191,9 @@
         vm(32, HSAC),
         vm(48, HSAC),
         vm(16, 48),
-        vm(2, 24, TILE),
-        vm(8, TILE),
-        vm(48, TILE),
+        vm(2, 24, DYN_TILE),
+        vm(8, DYN_TILE),
+        vm(48, DYN_TILE),
         vm(HSAC, HSAC),
         vm(D_ROWS, HSAC),
         vm(drows, HDYN),
@@ -1200,7 +1211,7 @@
         out_specs=[spec] * len(out_shape),
         scratch_shapes=scratch,
         compiler_params=pltpu.CompilerParams(
-            collective_id=0, has_side_effects=True, vmem_limit_bytes=14 * 2**20 + 2 * varying
+            collective_id=0, has_side_effects=True, vmem_limit_bytes=26 * 2**20 + varying
         ),
         name="step",
     )(*[pltpu.with_memory_space_constraint(value, pltpu.HBM) for value in inputs])

time: 84 us -> 69.6 us (0.83)
  Pallas kernels: 82.1 us -> 67.7 us
    pallas_call x1, Pallas kernels: 80 us -> 65.6 us  [shards(): pl.pallas_call(functools.partial(main_kernel, lay), out_shape=out_shape,...]
where the time goes in v5:
time: 69.6 us; the launch traced here: 69.3 us
  Pallas kernels  67.7 us (97%)
  between operations  1.07 us (2%)
    pallas_call x1, Pallas kernels, shards(): pl.pallas_call(functools.partial(main_kernel, lay), out_shape=out_shape,...  65.6 us
    pallas_call x1, Pallas kernels, shards(): pl.pallas_call(update_kernel, out_shape=tuple(new_shape), in_specs=[spec]...  2.13 us

profile of v5, /device:TPU:0, one launch (start us, length us, event | category | flops | bytes accessed | tf_op | source)
XLA Modules:
  0.0 69.3 jit_solution(2821479863546152831)
XLA Ops:
  0.7 0.0 copy-start
  0.7 0.0 copy-start.1
  0.7 0.0 copy-start.2
  0.7 0.0 copy-start.3
  0.7 0.0 copy-start.4
  0.7 0.0 copy-start.5
  0.7 0.0 copy-start.6
  0.7 0.0 copy-start.7
  0.8 0.0 copy-start.8
  0.8 0.0 copy-start.9
  0.8 0.0 copy-start.10
  0.8 0.0 copy-start.11
  0.8 0.0 copy-start.12
  0.8 0.0 copy-start.13
  0.8 0.0 copy-start.14
  0.8 0.0 copy-start.15
  0.8 0.0 copy-start.16
  0.8 0.0 copy-start.17
  0.9 0.0 copy-start.18
  0.9 0.0 copy-start.19
  0.9 0.0 copy-start.20
  0.9 0.0 copy-start.21
  0.9 0.0 copy-start.24
  0.9 65.6 %step.1 = (f32[3,64,256]{2,1,0:T(8,128)S(1)}, f32[3,64,256]{2,1,0:T(8,128)S(1)}, f32[7,50,200]{2,1,0:T(8,128)S(1)}, f32[7,128,256]{2,1,0:T(8,128)S(1)}, f32[32,8,128]{2,1,0:T(8,128)S(1)}, /*index=5*/f32[8,128]{1,0:T(8,128)S(1)}) custom-call(f32[42,3648]{1,0:T(8,128)} %refs_0_.1, f32[42,1216]{1,0:T(8,128)} %refs_1_.1, s32[8,8]{1,0:T(8,128)} %refs_2_.1, ...), custom_call_target="tpu_custom_call" | custom-call | tf_op jit(solution)/shard_map/step/pallas_call | solution.py:1207
  66.5 0.0 copy-start.23
  66.5 0.0 copy-start.22
  66.5 0.0 copy-done
  66.5 0.0 copy-done.1
  66.6 0.0 copy-done.2
  66.6 0.0 copy-done.3
  66.6 0.0 copy-done.4
  66.6 0.0 copy-done.5
  66.6 0.0 copy-done.6
  66.6 0.0 copy-done.7
  66.6 0.0 copy-done.8
  66.6 0.0 copy-done.9
  66.6 0.0 copy-done.10
  66.6 0.0 copy-done.11
  66.7 0.0 copy-done.12
  66.7 0.0 copy-done.13
  66.7 0.0 copy-done.14
  66.7 0.0 copy-done.15
  66.7 0.0 copy-done.16
  66.7 0.0 copy-done.17
  66.7 0.0 copy-done.18
  66.7 0.0 copy-done.19
  66.7 0.0 copy-done.20
  66.7 0.0 copy-done.21
  66.8 0.0 copy-done.24
  66.8 0.4 copy-done.23
  67.2 0.0 copy-done.22
  67.2 2.1 %update.1 = (f32[3,64,256]{2,1,0:T(8,128)}, f32[3,64,256]{2,1,0:T(8,128)}, f32[7,50,200]{2,1,0:T(8,128)}, f32[7,50,200]{2,1,0:T(8,128)}, f32[23,2,256]{2,1,0:T(2...) custom-call(f32[3,64,256]{2,1,0:T(8,128)S(1)} %get-tuple-element.60., ...), custom_call_target="tpu_custom_call" | custom-call | tf_op jit(solution)/shard_map/update/pallas_call | solution.py:1227
Async XLA Ops:
  0.7 65.9 %copy-start = (f32[7,50,200]{2,1,0:T(8,128)S(1)}, f32[7,50,200]{2,1,0:T(8,128)}, u32[]{:S(2)}) copy-start(f32[7,50,200]{2,1,0:T(8,128)} %refs_8_.3) | copy-start | bytes 840004
  0.7 65.9 %copy-start.1 = (f32[7,50,200]{2,1,0:T(8,128)S(1)}, f32[7,50,200]{2,1,0:T(8,128)}, u32[]{:S(2)}) copy-start(f32[7,50,200]{2,1,0:T(8,128)} %refs_9_.3) | copy-start | bytes 840004
  0.7 65.9 %copy-start.2 = (f32[7,200,36]{1,2,0:T(8,128)S(1)}, f32[7,200,36]{1,2,0:T(8,128)}, u32[]{:S(2)}) copy-start(f32[7,200,36]{1,2,0:T(8,128)} %param.60) | copy-start | bytes 604804
  0.7 65.9 %copy-start.3 = (f32[3,64,256]{2,1,0:T(8,128)S(1)}, f32[3,64,256]{2,1,0:T(8,128)}, u32[]{:S(2)}) copy-start(f32[3,64,256]{2,1,0:T(8,128)} %refs_6_.3) | copy-start | bytes 589828
  0.7 65.9 %copy-start.4 = (f32[3,64,256]{2,1,0:T(8,128)S(1)}, f32[3,64,256]{2,1,0:T(8,128)}, u32[]{:S(2)}) copy-start(f32[3,64,256]{2,1,0:T(8,128)} %refs_7_.3) | copy-start | bytes 589828
  0.7 65.9 %copy-start.5 = (f32[7,23,200]{2,1,0:T(8,128)S(1)}, f32[7,23,200]{2,1,0:T(8,128)}, u32[]{:S(2)}) copy-start(f32[7,23,200]{2,1,0:T(8,128)} %refs_16_.3) | copy-start | bytes 386404
  0.7 65.9 %copy-start.6 = (f32[7,200,36]{1,2,0:T(8,128)S(1)}, f32[7,200,36]{1,2,0:T(8,128)}, u32[]{:S(2)}) copy-start(f32[7,200,36]{1,2,0:T(8,128)} %param.61) | copy-start | bytes 604804
  0.7 65.9 %copy-start.7 = (f32[7,200,36]{1,2,0:T(8,128)S(1)}, f32[7,200,36]{1,2,0:T(8,128)}, u32[]{:S(2)}) copy-start(f32[7,200,36]{1,2,0:T(8,128)} %param.62) | copy-start | bytes 604804
  0.8 65.9 %copy-start.8 = (f32[2,23,256]{2,0,1:T(2,128)S(1)}, f32[2,23,256]{2,0,1:T(2,128)}, u32[]{:S(2)}) copy-start(f32[2,23,256]{2,0,1:T(2,128)} %param.45) | copy-start | bytes 141316
  0.8 65.9 %copy-start.9 = (f32[7,23,200]{2,1,0:T(8,128)S(1)}, f32[7,23,200]{2,1,0:T(8,128)}, u32[]{:S(2)}) copy-start(f32[7,23,200]{2,1,0:T(8,128)} %refs_17_.1) | copy-start | bytes 386404
  0.8 65.9 %copy-start.10 = (f32[7,23,200]{2,1,0:T(8,128)S(1)}, f32[7,23,200]{2,1,0:T(8,128)}, u32[]{:S(2)}) copy-start(f32[7,23,200]{2,1,0:T(8,128)} %refs_18_.3) | copy-start | bytes 386404
  0.8 65.9 %copy-start.11 = (f32[17,256]{1,0:T(8,128)S(1)}, f32[17,256]{1,0:T(8,128)}, u32[]{:S(2)}) copy-start(f32[17,256]{1,0:T(8,128)} %refs_13_.3) | copy-start | bytes 52228
  0.8 65.9 %copy-start.12 = (f32[4639]{0:T(1024)S(1)}, f32[4639]{0:T(1024)}, u32[]{:S(2)}) copy-start(f32[4639]{0:T(1024)} %refs_28_.1) | copy-start | bytes 55672
  0.8 65.9 %copy-start.13 = (f32[256,12]{0,1:T(8,128)S(1)}, f32[256,12]{0,1:T(8,128)}, u32[]{:S(2)}) copy-start(f32[256,12]{0,1:T(8,128)} %param.57) | copy-start | bytes 36868
  0.8 65.9 %copy-start.14 = (f32[2,23,256]{2,0,1:T(2,128)S(1)}, f32[2,23,256]{2,0,1:T(2,128)}, u32[]{:S(2)}) copy-start(f32[2,23,256]{2,0,1:T(2,128)} %param.46) | copy-start | bytes 141316
  0.8 65.9 %copy-start.15 = (f32[2,23,256]{2,0,1:T(2,128)S(1)}, f32[2,23,256]{2,0,1:T(2,128)}, u32[]{:S(2)}) copy-start(f32[2,23,256]{2,0,1:T(2,128)} %param.47) | copy-start | bytes 141316
  0.8 65.9 %copy-start.16 = (f32[17,256]{1,0:T(8,128)S(1)}, f32[17,256]{1,0:T(8,128)}, u32[]{:S(2)}) copy-start(f32[17,256]{1,0:T(8,128)} %refs_14_.1) | copy-start | bytes 52228
  0.8 65.9 %copy-start.17 = (f32[17,256]{1,0:T(8,128)S(1)}, f32[17,256]{1,0:T(8,128)}, u32[]{:S(2)}) copy-start(f32[17,256]{1,0:T(8,128)} %refs_15_.1) | copy-start | bytes 52228
  0.9 65.9 %copy-start.18 = (f32[4639]{0:T(1024)S(1)}, f32[4639]{0:T(1024)}, u32[]{:S(2)}) copy-start(f32[4639]{0:T(1024)} %refs_29_.1) | copy-start | bytes 55672
  0.9 65.9 %copy-start.19 = (f32[4639]{0:T(1024)S(1)}, f32[4639]{0:T(1024)}, u32[]{:S(2)}) copy-start(f32[4639]{0:T(1024)} %refs_30_.1) | copy-start | bytes 55672
  0.9 65.9 %copy-start.20 = (f32[256,12]{0,1:T(8,128)S(1)}, f32[256,12]{0,1:T(8,128)}, u32[]{:S(2)}) copy-start(f32[256,12]{0,1:T(8,128)} %param.58) | copy-start | bytes 36868
  0.9 65.9 %copy-start.21 = (f32[256,12]{0,1:T(8,128)S(1)}, f32[256,12]{0,1:T(8,128)}, u32[]{:S(2)}) copy-start(f32[256,12]{0,1:T(8,128)} %param.59) | copy-start | bytes 36868
  0.9 65.9 %copy-start.24 = (f32[2,256]{1,0:T(2,128)S(1)}, f32[2,256]{1,0:T(2,128)}, u32[]{:S(2)}) copy-start(f32[2,256]{1,0:T(2,128)} %refs_21_.1) | copy-start | bytes 6148
  66.5 0.7 copy-start.23
  66.5 0.7 copy-start.22

commit v6 on v5

--- a/solution.py
+++ b/solution.py
@@ -1,5 +1,4 @@
 import functools
-import math
 
 import jax
 import jax.numpy as jnp
@@ -151,7 +150,6 @@
     def __init__(self, mesh, replay, model):
         self.n_dp = mesh.shape["dp"]
         self.n_blk = mesh.shape["blk"]
-        self.bits = int(math.log2(self.n_dp))
         self.n_dev = self.n_dp * self.n_blk
         self.replay = replay
         self.model = model
@@ -163,29 +161,27 @@
         self.mat = 64 // self.n_dp
         self.sml = 32 // self.n_dp
         self.chunks = (2 * self.mat, self.mat + self.sml)
-        self.split_z = all(chunk % self.n_blk == 0 for chunk in self.chunks)
-        self.owners = [self.n_dp - 5, self.n_dp - 3, self.n_dp - 1]
-
-        groups = [("fold", g, s) for g in range(2) for s in range(self.bits)]
-        groups += [(name, g) for name in ("first", "second") for g in range(2)]
+        self.owner = self.n_dp - 1
+
+        groups = [("plane sum", g) for g in range(2)] + [("line sum", g) for g in range(3)]
         common = ["hidden", "hidden on", "lists", "own", "line", "plane", "dyn h", "dyn m", "sac m", "small"]
         common += groups
         kinds = [(name, kind) for name in ("pack", "x") for kind in ("own", "on")]
         sent = common + [("tiles", k) for k in range(3)] + kinds
         self.sent = {name: at for at, name in enumerate(sent)}
-        self.sent["sac g"] = len(sent)
-        self.sent["sac x"] = len(sent) + self.n_dp
-        self.departures = len(sent) + 2 * self.n_dp
+        self.departures = len(sent)
+        for k in range(3):
+            for name in ("sac g", "sac x"):
+                self.sent[name, k] = self.departures
+                self.departures += self.n_dp
         self.here, self.arrivals = {}, 0
-        for name in common + ["tiles", ("pack", "sibling"), ("x", "sibling")]:
+        tiles = [("tiles", k) for k in range(3)]
+        for name in common + tiles + [("pack", "sibling"), ("x", "sibling")]:
             self.here[name] = self.arrivals
             self.arrivals += 1
         for name, number in (("sac g", 3), ("sac x", 3), (("pack", "like"), MEMBERS), (("x", "like"), MEMBERS)):
             self.here[name] = self.arrivals
             self.arrivals += number
-
-    def part(self, group):
-        return self.chunks[group] // self.n_blk if self.split_z else self.chunks[group]
 
 
 def main_kernel(lay, *refs):
@@ -194,15 +190,13 @@
         dyn_in, crit_out, act_out, dyn_out, biases, targ_in, targ_hidden, targ_out, targ_bias,
         sac_g, sac_x, dyn_x, dyn_s, small, count,
         wg, lists, asked, dhg, dmg, smg, bk, xs, nz, w1f, w1t, w1n, w2t, w2h, heads, head_t, head_f,
-        rowbuf, wide, headcol, acc_h, acc_w, acc_c, acc_a, acc_m, acc_l, grid_c, grid_a, zr_c, zr_a,
-        zf_c, zf_a, mg, mat, grow, dcols, dacc_h, dacc_w, dacc_o, dacc_m, dacc_b, dacc_l, xt, dmat,
+        rowbuf, wide, headcol, acc_h, acc_w, acc_c, acc_a, acc_m, acc_l, grid_c, grid_a, from_c, from_a,
+        zr_c, zr_a, zf_c, zf_a, sum_c, sum_a, mg, mat, grow, dcols, dacc_h, dacc_w, dacc_o, dacc_m, dacc_b, dacc_l, xt, dmat,
         dpack, drow_x, bias, dhead, dhead_t, *rest,
     ) = refs
-    bits = lay.bits
-    bufs = (rest[:bits], rest[bits : 2 * bits])
-    send, recv = rest[2 * bits :]
+    send, recv = rest
     sent, here_at = lay.sent, lay.here
-    grids, zrs, zfs = (grid_c, grid_a), (zr_c, zr_a), (zf_c, zf_a)
+    grids, froms, zrs, zfs = (grid_c, grid_a), (from_c, from_a), (zr_c, zr_a), (zf_c, zf_a)
     n_dp, n_blk = lay.n_dp, lay.n_blk
     me = lax.axis_index("dp")
     z = lax.axis_index("blk")
@@ -210,10 +204,7 @@
     sibling = me + 1 - 2 * core
     is_dyn = me < MEMBERS
     dyn_e = jnp.minimum(me, MEMBERS - 1)
-    is_actor = me == lay.owners[2]
-    is_critic = jnp.logical_or(me == lay.owners[0], me == lay.owners[1])
-    is_sac = jnp.logical_or(is_actor, is_critic)
-    sac_k = jnp.clip((me - lay.owners[0]) // 2, 0, 2)
+    is_owner = me == lay.owner
 
     def on_plane(src, dst, ssem, rsem, peer):
         return pltpu.make_async_remote_copy(
@@ -287,7 +278,7 @@
         return on_line(dyn_m.at[dyn_e], dmg.at[z], send.at[sent["dyn m"]], recv.at[here_at["dyn m"]], peer)
 
     def sac_m_copy(peer):
-        return on_line(sac_m.at[sac_k], smg.at[z], send.at[sent["sac m"]], recv.at[here_at["sac m"]], peer)
+        return on_line(sac_m, smg.at[z], send.at[sent["sac m"]], recv.at[here_at["sac m"]], peer)
 
     alive = live[...].astype(F32).reshape(1, lay.model)
     bias[...] = biases[...].reshape(1, NB)
@@ -406,7 +397,7 @@
         line_peers(lambda peer: dyn_h_copy(peer).start())
         line_peers(lambda peer: dyn_m_copy(peer).start())
 
-    @pl.when(is_sac)
+    @pl.when(is_owner)
     def _():
         line_peers(lambda peer: sac_m_copy(peer).start())
 
@@ -541,130 +532,88 @@
                     at * 8 : at * 8 + 8, side * 128 : (side + 1) * 128
                 ]
 
-    def bit(b):
-        return lax.rem(me // (1 << b), 2)
-
-    starts, faces, partners = [], [], []
-    start = 0
-    for s in range(bits):
-        if s == 0:
-            face, stride = core, 1
-        else:
-            face = (1 - core) * bit(s) + core * bit(bits - s)
-            stride = (1 - core) * (1 << s) + core * (1 << (bits - s))
-        starts.append(start)
-        faces.append(face)
-        partners.append(me + (1 - 2 * face) * stride)
-        start = start + face * (n_dp >> (s + 1))
-    place = start
-
-    def fold_copy(group, s):
-        half = n_dp >> (s + 1)
-        begin = starts[s] + (1 - faces[s]) * half
+    def plane_sum(group, peer):
+        name = ("plane sum", group)
         return on_plane(
-            grids[group].at[pl.ds(begin, half)], bufs[group][s], send.at[sent["fold", group, s]],
-            recv.at[here_at["fold", group, s]], partners[s],
+            grids[group].at[peer], froms[group].at[me], send.at[sent[name]], recv.at[here_at[name]], peer
         )
 
-    def fold_wait(group, s):
-        half = n_dp >> (s + 1)
-        begin = starts[s] + faces[s] * half
-        fold_copy(group, s).wait_recv()
-        for at in range(half):
-            grids[group][begin + at] += bufs[group][s][at]
-
-    def line_first(group, peer):
-        if lay.split_z:
-            src = grids[group].at[place, pl.ds(peer * lay.part(group), lay.part(group))]
-        else:
-            src = grids[group].at[place]
-        name = ("first", group)
-        return on_line(src, zrs[group].at[z], send.at[sent[name]], recv.at[here_at[name]], peer)
-
-    def line_second(group, peer):
-        view = zfs[group].at[pl.ds(z * lay.part(group), lay.part(group))]
-        name = ("second", group)
-        return on_line(view, view, send.at[sent[name]], recv.at[here_at[name]], peer)
-
-    def firsts_of(group):
-        return zrs[group].at[pl.ds(0, n_blk - 1)]
-
-    def seconds_of(group):
-        return zfs[group].at[pl.ds(0, (n_blk - 1) * lay.part(group))]
-
-    def line_start(group):
-        line_peers(lambda peer: line_first(group, peer).start())
-
-    def line_sum(group):
-        part, zr, zf = lay.part(group), zrs[group], zfs[group]
-        has_come(firsts_of(group), ("first", group))
-        zr[z] = grids[group][place, pl.ds(z * part, part)] if lay.split_z else grids[group][place]
-        whole = zr[0]
-        for block in range(1, n_blk):
-            whole = whole + zr[block]
-        if lay.split_z:
-            zf[pl.ds(z * part, part)] = whole
-            line_peers(lambda peer: line_second(group, peer).start())
-        else:
-            zf[...] = whole
-
-    def line_end(group):
-        if lay.split_z:
-            has_come(seconds_of(group), ("second", group))
-
-    def tile_copy(k, owner):
-        src = zfs[k // 2].at[pl.ds((k % 2) * lay.mat, lay.mat)]
-        return on_plane(src, mg.at[place], send.at[sent["tiles", k]], recv.at[here_at["tiles"]], owner)
-
-    def send_tiles(group):
-        for k in (0, 1) if group == 0 else (2,):
-            @pl.when(me != lay.owners[k])
-            def _():
-                tile_copy(k, lay.owners[k]).start()
-
-            @pl.when(me == lay.owners[k])
-            def _():
-                mg[place] = zfs[group][(k % 2) * lay.mat : (k % 2 + 1) * lay.mat]
+    def line_part(part):
+        group = min(part, 1)
+        tiles = (pl.ds(0, 2 * lay.mat), pl.ds(0, lay.mat), pl.ds(lay.mat, lay.sml))[part]
+        return group, tiles
+
+    def line_sum(part, peer):
+        group, tiles = line_part(part)
+        name = ("line sum", part)
+        src, dst = zfs[group].at[tiles], zrs[group].at[z, tiles]
+        return on_line(src, dst, send.at[sent[name]], recv.at[here_at[name]], peer)
+
+    def line_bytes(part):
+        group, tiles = line_part(part)
+        return zrs[group].at[pl.ds(0, n_blk - 1), tiles]
+
+    def fold_plane(group):
+        has_come(froms[group].at[pl.ds(0, n_dp - 1)], ("plane sum", group))
+        froms[group][me] = grids[group][me]
+        whole = froms[group][0]
+        for at in range(1, n_dp):
+            whole = whole + froms[group][at]
+        zfs[group][...] = whole
+        for part in (0,) if group == 0 else (1, 2):
+            line_peers(lambda peer: line_sum(part, peer).start())
+
+    def tile_copy(k):
+        src = (sum_c, sum_a)[k // 2].at[pl.ds((k % 2) * lay.mat, lay.mat)]
+        return on_plane(src, mg.at[k, me], send.at[sent["tiles", k]], recv.at[here_at["tiles", k]], lay.owner)
 
     def small_copy(peer):
         return on_plane(
-            zf_a.at[pl.ds(lay.mat, lay.sml)], small.at[pl.ds(place * lay.sml, lay.sml)],
+            sum_a.at[pl.ds(lay.mat, lay.sml)], small.at[pl.ds(me * lay.sml, lay.sml)],
             send.at[sent["small"]], recv.at[here_at["small"]], peer,
         )
 
+    def fold_end(part):
+        group, tiles = line_part(part)
+        has_come(line_bytes(part), ("line sum", part))
+        zrs[group][z, tiles] = zfs[group][tiles]
+        whole = zrs[group][0, tiles]
+        for block in range(1, n_blk):
+            whole = whole + zrs[group][block, tiles]
+        (sum_c, sum_a)[group][tiles] = whole
+        for k in ((0, 1), (2,), ())[part]:
+            pl.when(jnp.logical_not(is_owner))(tile_copy(k).start)
+
+            @pl.when(is_owner)
+            def _():
+                mg[k, me] = (sum_c, sum_a)[group][(k % 2) * lay.mat : (k % 2 + 1) * lay.mat]
+
+        if part == 2:
+            plane_peers(lambda peer: small_copy(peer).start())
+            small[pl.ds(me * lay.sml, lay.sml)] = sum_a[lay.mat :]
+
     def chain(group):
-        steps = [functools.partial(lambda s: fold_copy(group, s).start(), 0)]
-
-        def fold(s):
-            fold_wait(group, s)
-            if s + 1 < bits:
-                fold_copy(group, s + 1).start()
-            else:
-                line_start(group)
-
-        steps += [functools.partial(fold, s) for s in range(bits)]
-        steps.append(lambda: line_sum(group))
-
-        def finish():
-            line_end(group)
-            send_tiles(group)
-            if group == 1:
-                plane_peers(lambda peer: small_copy(peer).start())
-                small[pl.ds(place * lay.sml, lay.sml)] = zf_a[lay.mat :]
-
-        steps.append(finish)
-        return steps
+        def end():
+            for part in (0,) if group == 0 else (1, 2):
+                fold_end(part)
+
+        return [
+            lambda: plane_peers(lambda peer: plane_sum(group, peer).start()),
+            lambda: fold_plane(group),
+            end,
+        ]
 
     critic_chain, actor_chain = chain(0), chain(1)
     per = DYN_TILE // lay.real
     dyn_tiles = lay.n_dev // per
-    inside = min(bits + 2, n_tiles - 1)
-    in_actor = {step: [critic_chain[step]] for step in range(1, inside + 1)}
-    in_dyn = {}
-    for at, event in enumerate(critic_chain[inside + 1 :]):
-        in_dyn.setdefault(min(at, dyn_tiles - 1), []).append(event)
-    for at in range(1, bits + 1):
-        in_dyn.setdefault(min(at, dyn_tiles - 1), []).append(actor_chain[at])
+    in_actor, in_dyn = {}, {}
+    if n_tiles > 1:
+        in_actor[1] = [critic_chain[1]]
+        in_dyn[0] = [critic_chain[2]]
+    else:
+        in_dyn[0] = [critic_chain[1]]
+        in_dyn[min(1, dyn_tiles - 1)] = [critic_chain[2]]
+    in_dyn.setdefault(dyn_tiles - 1, []).append(actor_chain[1])
 
     def take(slots, step):
         for at, events in slots.items():
@@ -882,33 +831,26 @@
         return rows
 
     def sac_g_copy(k, peer):
-        src = grow.at[pl.ds(pl.multiple_of(z * lay.rows, lay.rows), lay.rows)]
-        return on_plane(src, sac_g.at[k], send.at[sent["sac g"] + peer], recv.at[here_at["sac g"] + k], peer)
+        return on_plane(grow.at[k, mine_rows], sac_g.at[k], send.at[sent["sac g", k] + peer], recv.at[here_at["sac g"] + k], peer)
 
     def sac_x_copy(k, peer):
-        src = mat.at[pl.ds(pl.multiple_of(z * lay.rows, lay.rows), lay.rows)]
-        return on_plane(src, sac_x.at[k], send.at[sent["sac x"] + peer], recv.at[here_at["sac x"] + k], peer)
+        return on_plane(mat.at[k, mine_rows], sac_x.at[k], send.at[sent["sac x", k] + peer], recv.at[here_at["sac x"] + k], peer)
 
     mine_rows = pl.ds(pl.multiple_of(z * lay.rows, lay.rows), lay.rows)
 
-    def take_matrix():
-        has_come(smg.at[pl.ds(0, n_blk - 1)], "sac m")
-        smg[z] = sac_m[sac_k]
-        has_come(mg.at[pl.ds(0, n_dp - 1)], "tiles")
+    def take_matrix(k):
+        has_come(mg.at[k, pl.ds(0, n_dp - 1)], ("tiles", k))
         for chunk in range(n_dp):
             tile = chunk * lay.mat
             side, row = tile // 32, tile % 32
-            grow[row * 8 : (row + lay.mat) * 8, side * 128 : (side + 1) * 128] = mg[chunk].reshape(
-                lay.mat * 8, 128
-            )
-        sac_g[sac_k] = grow[mine_rows, :]
-        plane_peers(lambda peer: sac_g_copy(sac_k, peer).start())
+            at = slice(row * 8, (row + lay.mat) * 8)
+            grow[k, at, side * 128 : (side + 1) * 128] = mg[k, chunk].reshape(lay.mat * 8, 128)
+        sac_g[k] = grow[k, mine_rows, :]
+        plane_peers(lambda peer: sac_g_copy(k, peer).start())
         for block in range(n_blk):
             at = slice(block * lay.rows, (block + 1) * lay.rows)
-            mat[at, :] = MOMENTUM * smg[block] + grow[at, :] / total
-        normalise(mat)
-
-    actor_chain[bits + 1]()
+            mat[k, at, :] = MOMENTUM * smg[block, k] + grow[k, at, :] / total
+        normalise(mat.at[k])
 
     @pl.when(is_dyn)
     def _():
@@ -936,34 +878,33 @@
             dmat[at, 0:HDYN] = MOMENTUM * dmg[block] + dacc_h[at, 0:HDYN] / total
         normalise(dmat)
 
-    pl.when(is_critic)(take_matrix)
-    if n_dp <= MEMBERS + 1:
-        only_dyn = jnp.logical_and(is_dyn, jnp.logical_not(is_critic))
-        pairs = [(is_critic, [dmat, mat]), (only_dyn, [dmat])]
-    else:
-        pairs = [(is_critic, [mat]), (is_dyn, [dmat])]
+    def send_sac(k):
+        sac_x[k] = mat[k, mine_rows, :]
+        plane_peers(lambda peer: sac_x_copy(k, peer).start())
+
     def sum_end(step):
-        pl.when(step == 2)(actor_chain[bits + 2])
-
-    for test, matrices in pairs:
-        pl.when(test)(functools.partial(schulz, matrices, NS_ITERS, sum_end))
-    if n_dp <= MEMBERS + 1:
-        pl.when(is_actor)(actor_chain[bits + 2])
-    else:
-        pl.when(jnp.logical_not(jnp.logical_or(is_critic, is_dyn)))(actor_chain[bits + 2])
-
-    def send_sac():
-        sac_x[sac_k] = mat[mine_rows, :]
-        plane_peers(lambda peer: sac_x_copy(sac_k, peer).start())
+        pl.when(step == NS_ITERS - 2)(actor_chain[2])
 
     @pl.when(is_dyn)
     def _():
+        schulz([dmat], NS_ITERS, sum_end)
         rows = line_rows(dmat)
         drow_x[...] = rows
         dyn_x[dyn_e] = rows
         give("x", drow_x)
 
-    pl.when(is_critic)(send_sac)
+    @pl.when(is_owner)
+    def _():
+        has_come(smg.at[pl.ds(0, n_blk - 1)], "sac m")
+        smg[z] = sac_m[...]
+        for k in range(2):
+            take_matrix(k)
+        schulz([mat.at[0], mat.at[1]], NS_ITERS, sum_end)
+        for k in range(2):
+            send_sac(k)
+
+    if n_dp > MEMBERS + 1:
+        pl.when(jnp.logical_not(jnp.logical_or(is_dyn, is_owner)))(actor_chain[2])
 
     def sent_early():
         has_sent(wg.at[pl.ds(0, n_blk - 1), :, half_rows], "hidden")
@@ -978,48 +919,48 @@
             has_sent(dhg.at[pl.ds(0, n_blk - 1)], "dyn h")
             has_sent(dmg.at[pl.ds(0, n_blk - 1)], "dyn m")
 
-        @pl.when(is_sac)
+        @pl.when(is_owner)
         def _():
             has_sent(smg.at[pl.ds(0, n_blk - 1)], "sac m")
 
         for group in range(2):
-            for s in range(bits):
-                fold_copy(group, s).wait_send()
-            has_sent(firsts_of(group), ("first", group))
-            if lay.split_z:
-                has_sent(seconds_of(group), ("second", group))
-
-    @pl.when(is_actor)
+            has_sent(froms[group].at[pl.ds(0, n_dp - 1)], ("plane sum", group))
+        for part in range(3):
+            has_sent(line_bytes(part), ("line sum", part))
+
+    @pl.when(is_owner)
     def _():
-        sent_early()
-        take_matrix()
-        schulz([mat], NS_ITERS)
-        send_sac()
-
-    pl.when(jnp.logical_not(is_actor))(sent_early)
+        take_matrix(2)
+        schulz([mat.at[2]], NS_ITERS)
+        send_sac(2)
+
+    sent_early()
     hand_on("pack")
     hand_on("x")
     has_come(small.at[pl.ds(0, (n_dp - 1) * lay.sml)], "small")
     from_sibling("pack")
     from_sibling("x")
-    for k in range(3):
-        @pl.when(me != lay.owners[k])
-        def _():
-            sac_g_copy(k, me).wait_recv()
-            sac_x_copy(k, me).wait_recv()
+
+    @pl.when(jnp.logical_not(is_owner))
+    def _():
+        for k in range(3):
+            sac_g_copy(k, sibling).wait_recv()
+            sac_x_copy(k, sibling).wait_recv()
 
     has_sent(small.at[pl.ds(0, (n_dp - 1) * lay.sml)], "small")
     gave("pack")
     gave("x")
-    for k in range(3):
-        @pl.when(me != lay.owners[k])
-        def _():
-            tile_copy(k, lay.owners[k]).wait_send()
-
-    @pl.when(is_sac)
+
+    @pl.when(jnp.logical_not(is_owner))
     def _():
-        plane_peers(lambda peer: sac_g_copy(sac_k, peer).wait_send())
-        plane_peers(lambda peer: sac_x_copy(sac_k, peer).wait_send())
+        for k in range(3):
+            tile_copy(k).wait_send()
+
+    @pl.when(is_owner)
+    def _():
+        for k in range(3):
+            plane_peers(lambda peer: sac_g_copy(k, peer).wait_send())
+            plane_peers(lambda peer: sac_x_copy(k, peer).wait_send())
 
 
 def adamw(weights, first, second, gradient):
@@ -1118,7 +1059,7 @@
     dyn_in_m, dyn_in_v, crit_out, crit_out_m, crit_out_v, act_out, act_out_m, act_out_v, dyn_out,
     dyn_out_m, dyn_out_v, biases, biases_m, biases_v, targ_in, targ_hidden, targ_out, targ_bias,
 ):
-    n_dp, n_blk, bits = lay.n_dp, lay.n_blk, lay.bits
+    n_dp, n_blk = lay.n_dp, lay.n_blk
     spec = pl.BlockSpec(memory_space=pltpu.VMEM)
 
     def flip(value):
@@ -1156,7 +1097,7 @@
         vm(n_dp, 2, n_dp, CAP, kind=jnp.int32),
         vm(n_blk, drows, HDYN),
         vm(n_blk, drows, HDYN),
-        vm(n_blk, rows, HSAC),
+        vm(n_blk, 3, rows, HSAC),
         vm(lay.n_dev, 48, lay.width),
         vm(56, lay.batch),
         vm(2, 8, lay.batch),
@@ -1179,13 +1120,17 @@
         vm(8, TILE),
         vm(n_dp, lay.chunks[0], 8, 128),
         vm(n_dp, lay.chunks[1], 8, 128),
-        vm(n_blk, lay.part(0), 8, 128),
-        vm(n_blk, lay.part(1), 8, 128),
+        vm(n_dp, lay.chunks[0], 8, 128),
+        vm(n_dp, lay.chunks[1], 8, 128),
+        vm(n_blk, lay.chunks[0], 8, 128),
+        vm(n_blk, lay.chunks[1], 8, 128),
         vm(lay.chunks[0], 8, 128),
         vm(lay.chunks[1], 8, 128),
-        vm(n_dp, lay.mat, 8, 128),
-        vm(HSAC, HSAC),
-        vm(HSAC, HSAC),
+        vm(lay.chunks[0], 8, 128),
+        vm(lay.chunks[1], 8, 128),
+        vm(3, n_dp, lay.mat, 8, 128),
+        vm(3, HSAC, HSAC),
+        vm(3, HSAC, HSAC),
         vm(HSAC, 8),
         vm(HSAC + 16, HSAC),
         vm(32, HSAC),
@@ -1201,7 +1146,6 @@
         vm(48, HSAC, kind=BF16),
         vm(HSAC, 48, kind=BF16),
     ]
-    scratch += [vm(n_dp >> (s + 1), chunk, 8, 128) for chunk in lay.chunks for s in range(bits)]
     scratch += [pltpu.SemaphoreType.DMA((lay.departures,)), pltpu.SemaphoreType.DMA((lay.arrivals,))]
     varying = 4 * (lay.n_dev * 48 * lay.width + 72 * lay.batch + 48 * lay.replay)
     gathered = pl.pallas_call(

time: 69.6 us -> 72.6 us (1.043)
  Pallas kernels: 67.7 us -> 70.7 us
    pallas_call x1, Pallas kernels: 65.6 us -> 68.6 us  [shards(): pl.pallas_call(functools.partial(main_kernel, lay), out_shape=out_shape,...]
where the time goes in v6:
time: 72.6 us; the launch traced here: 72.3 us
  Pallas kernels  70.7 us (97%)
  between operations  1.07 us (1%)
    pallas_call x1, Pallas kernels, shards(): pl.pallas_call(functools.partial(main_kernel, lay), out_shape=out_shape,...  68.6 us
    pallas_call x1, Pallas kernels, shards(): pl.pallas_call(update_kernel, out_shape=tuple(new_shape), in_specs=[spec]...  2.13 us

profile of v6, /device:TPU:0, one launch (start us, length us, event | category | flops | bytes accessed | tf_op | source)
XLA Modules:
  0.0 72.3 jit_solution(3968269499263298495)
XLA Ops:
  0.7 0.0 copy-start
  0.7 0.0 copy-start.1
  0.7 0.0 copy-start.2
  0.7 0.0 copy-start.3
  0.7 0.0 copy-start.4
  0.7 0.0 copy-start.5
  0.7 0.0 copy-start.6
  0.7 0.0 copy-start.7
  0.8 0.0 copy-start.8
  0.8 0.0 copy-start.9
  0.8 0.0 copy-start.10
  0.8 0.0 copy-start.11
  0.8 0.0 copy-start.12
  0.8 0.0 copy-start.13
  0.8 0.0 copy-start.14
  0.8 0.0 copy-start.15
  0.8 0.0 copy-start.16
  0.8 0.0 copy-start.17
  0.9 0.0 copy-start.18
  0.9 0.0 copy-start.19
  0.9 0.0 copy-start.20
  0.9 0.0 copy-start.21
  0.9 0.0 copy-start.24
  0.9 68.6 %step.1 = (f32[3,64,256]{2,1,0:T(8,128)S(1)}, f32[3,64,256]{2,1,0:T(8,128)S(1)}, f32[7,50,200]{2,1,0:T(8,128)S(1)}, f32[7,128,256]{2,1,0:T(8,128)S(1)}, f32[32,8,128]{2,1,0:T(8,128)S(1)}, /*index=5*/f32[8,128]{1,0:T(8,128)S(1)}) custom-call(f32[42,3648]{1,0:T(8,128)} %refs_0_.1, f32[42,1216]{1,0:T(8,128)} %refs_1_.1, s32[8,8]{1,0:T(8,128)} %refs_2_.1, ...), custom_call_target="tpu_custom_call" | custom-call | tf_op jit(solution)/shard_map/step/pallas_call | solution.py:1151
  69.5 0.0 copy-start.23
  69.5 0.0 copy-start.22
  69.5 0.0 copy-done
  69.5 0.0 copy-done.1
  69.6 0.0 copy-done.2
  69.6 0.0 copy-done.3
  69.6 0.0 copy-done.4
  69.6 0.0 copy-done.5
  69.6 0.0 copy-done.6
  69.6 0.0 copy-done.7
  69.6 0.0 copy-done.8
  69.6 0.0 copy-done.9
  69.6 0.0 copy-done.10
  69.6 0.0 copy-done.11
  69.7 0.0 copy-done.12
  69.7 0.0 copy-done.13
  69.7 0.0 copy-done.14
  69.7 0.0 copy-done.15
  69.7 0.0 copy-done.16
  69.7 0.0 copy-done.17
  69.7 0.0 copy-done.18
  69.7 0.0 copy-done.19
  69.7 0.0 copy-done.20
  69.7 0.0 copy-done.21
  69.8 0.0 copy-done.24
  69.8 0.4 copy-done.23
  70.2 0.0 copy-done.22
  70.2 2.1 %update.1 = (f32[3,64,256]{2,1,0:T(8,128)}, f32[3,64,256]{2,1,0:T(8,128)}, f32[7,50,200]{2,1,0:T(8,128)}, f32[7,50,200]{2,1,0:T(8,128)}, f32[23,2,256]{2,1,0:T(2...) custom-call(f32[3,64,256]{2,1,0:T(8,128)S(1)} %get-tuple-element.60., ...), custom_call_target="tpu_custom_call" | custom-call | tf_op jit(solution)/shard_map/update/pallas_call | solution.py:1171
Async XLA Ops:
  0.7 68.9 %copy-start = (f32[7,50,200]{2,1,0:T(8,128)S(1)}, f32[7,50,200]{2,1,0:T(8,128)}, u32[]{:S(2)}) copy-start(f32[7,50,200]{2,1,0:T(8,128)} %refs_8_.3) | copy-start | bytes 840004
  0.7 68.9 %copy-start.1 = (f32[7,50,200]{2,1,0:T(8,128)S(1)}, f32[7,50,200]{2,1,0:T(8,128)}, u32[]{:S(2)}) copy-start(f32[7,50,200]{2,1,0:T(8,128)} %refs_9_.3) | copy-start | bytes 840004
  0.7 68.9 %copy-start.2 = (f32[7,200,36]{1,2,0:T(8,128)S(1)}, f32[7,200,36]{1,2,0:T(8,128)}, u32[]{:S(2)}) copy-start(f32[7,200,36]{1,2,0:T(8,128)} %param.60) | copy-start | bytes 604804
  0.7 68.9 %copy-start.3 = (f32[3,64,256]{2,1,0:T(8,128)S(1)}, f32[3,64,256]{2,1,0:T(8,128)}, u32[]{:S(2)}) copy-start(f32[3,64,256]{2,1,0:T(8,128)} %refs_6_.3) | copy-start | bytes 589828
  0.7 68.9 %copy-start.4 = (f32[3,64,256]{2,1,0:T(8,128)S(1)}, f32[3,64,256]{2,1,0:T(8,128)}, u32[]{:S(2)}) copy-start(f32[3,64,256]{2,1,0:T(8,128)} %refs_7_.3) | copy-start | bytes 589828
  0.7 68.9 %copy-start.5 = (f32[7,23,200]{2,1,0:T(8,128)S(1)}, f32[7,23,200]{2,1,0:T(8,128)}, u32[]{:S(2)}) copy-start(f32[7,23,200]{2,1,0:T(8,128)} %refs_16_.3) | copy-start | bytes 386404
  0.7 68.9 %copy-start.6 = (f32[7,200,36]{1,2,0:T(8,128)S(1)}, f32[7,200,36]{1,2,0:T(8,128)}, u32[]{:S(2)}) copy-start(f32[7,200,36]{1,2,0:T(8,128)} %param.61) | copy-start | bytes 604804
  0.7 68.9 %copy-start.7 = (f32[7,200,36]{1,2,0:T(8,128)S(1)}, f32[7,200,36]{1,2,0:T(8,128)}, u32[]{:S(2)}) copy-start(f32[7,200,36]{1,2,0:T(8,128)} %param.62) | copy-start | bytes 604804
  0.8 68.9 %copy-start.8 = (f32[2,23,256]{2,0,1:T(2,128)S(1)}, f32[2,23,256]{2,0,1:T(2,128)}, u32[]{:S(2)}) copy-start(f32[2,23,256]{2,0,1:T(2,128)} %param.45) | copy-start | bytes 141316
  0.8 68.9 %copy-start.9 = (f32[7,23,200]{2,1,0:T(8,128)S(1)}, f32[7,23,200]{2,1,0:T(8,128)}, u32[]{:S(2)}) copy-start(f32[7,23,200]{2,1,0:T(8,128)} %refs_17_.1) | copy-start | bytes 386404
  0.8 68.9 %copy-start.10 = (f32[7,23,200]{2,1,0:T(8,128)S(1)}, f32[7,23,200]{2,1,0:T(8,128)}, u32[]{:S(2)}) copy-start(f32[7,23,200]{2,1,0:T(8,128)} %refs_18_.3) | copy-start | bytes 386404
  0.8 68.9 %copy-start.11 = (f32[17,256]{1,0:T(8,128)S(1)}, f32[17,256]{1,0:T(8,128)}, u32[]{:S(2)}) copy-start(f32[17,256]{1,0:T(8,128)} %refs_13_.3) | copy-start | bytes 52228
  0.8 68.9 %copy-start.12 = (f32[4639]{0:T(1024)S(1)}, f32[4639]{0:T(1024)}, u32[]{:S(2)}) copy-start(f32[4639]{0:T(1024)} %refs_28_.1) | copy-start | bytes 55672
  0.8 68.9 %copy-start.13 = (f32[256,12]{0,1:T(8,128)S(1)}, f32[256,12]{0,1:T(8,128)}, u32[]{:S(2)}) copy-start(f32[256,12]{0,1:T(8,128)} %param.57) | copy-start | bytes 36868
  0.8 68.9 %copy-start.14 = (f32[2,23,256]{2,0,1:T(2,128)S(1)}, f32[2,23,256]{2,0,1:T(2,128)}, u32[]{:S(2)}) copy-start(f32[2,23,256]{2,0,1:T(2,128)} %param.46) | copy-start | bytes 141316
  0.8 68.9 %copy-start.15 = (f32[2,23,256]{2,0,1:T(2,128)S(1)}, f32[2,23,256]{2,0,1:T(2,128)}, u32[]{:S(2)}) copy-start(f32[2,23,256]{2,0,1:T(2,128)} %param.47) | copy-start | bytes 141316
  0.8 68.9 %copy-start.16 = (f32[17,256]{1,0:T(8,128)S(1)}, f32[17,256]{1,0:T(8,128)}, u32[]{:S(2)}) copy-start(f32[17,256]{1,0:T(8,128)} %refs_14_.1) | copy-start | bytes 52228
  0.8 68.9 %copy-start.17 = (f32[17,256]{1,0:T(8,128)S(1)}, f32[17,256]{1,0:T(8,128)}, u32[]{:S(2)}) copy-start(f32[17,256]{1,0:T(8,128)} %refs_15_.1) | copy-start | bytes 52228
  0.9 68.9 %copy-start.18 = (f32[4639]{0:T(1024)S(1)}, f32[4639]{0:T(1024)}, u32[]{:S(2)}) copy-start(f32[4639]{0:T(1024)} %refs_29_.1) | copy-start | bytes 55672
  0.9 68.9 %copy-start.19 = (f32[4639]{0:T(1024)S(1)}, f32[4639]{0:T(1024)}, u32[]{:S(2)}) copy-start(f32[4639]{0:T(1024)} %refs_30_.1) | copy-start | bytes 55672
  0.9 68.9 %copy-start.20 = (f32[256,12]{0,1:T(8,128)S(1)}, f32[256,12]{0,1:T(8,128)}, u32[]{:S(2)}) copy-start(f32[256,12]{0,1:T(8,128)} %param.58) | copy-start | bytes 36868
  0.9 68.9 %copy-start.21 = (f32[256,12]{0,1:T(8,128)S(1)}, f32[256,12]{0,1:T(8,128)}, u32[]{:S(2)}) copy-start(f32[256,12]{0,1:T(8,128)} %param.59) | copy-start | bytes 36868
  0.9 68.9 %copy-start.24 = (f32[2,256]{1,0:T(2,128)S(1)}, f32[2,256]{1,0:T(2,128)}, u32[]{:S(2)}) copy-start(f32[2,256]{1,0:T(2,128)} %refs_21_.1) | copy-start | bytes 6148
  69.5 0.7 copy-start.23
  69.5 0.7 copy-start.22

commit v7 on v6

--- a/solution.py
+++ b/solution.py
@@ -164,24 +164,25 @@
         self.owner = self.n_dp - 1
 
         groups = [("plane sum", g) for g in range(2)] + [("line sum", g) for g in range(3)]
-        common = ["hidden", "hidden on", "lists", "own", "line", "plane", "dyn h", "dyn m", "sac m", "small"]
-        common += groups
+        common = ["hidden", "hidden on", "lists", "own", "line", "plane", "dyn h", "dyn m", "small"]
+        common += groups + ["sac g c", "sac g a"]
         kinds = [(name, kind) for name in ("pack", "x") for kind in ("own", "on")]
         sent = common + [("tiles", k) for k in range(3)] + kinds
         self.sent = {name: at for at, name in enumerate(sent)}
         self.departures = len(sent)
-        for k in range(3):
-            for name in ("sac g", "sac x"):
-                self.sent[name, k] = self.departures
-                self.departures += self.n_dp
+        for name in ("sac x c", "sac x a"):
+            self.sent[name] = self.departures
+            self.departures += self.n_dp
         self.here, self.arrivals = {}, 0
         tiles = [("tiles", k) for k in range(3)]
-        for name in common + tiles + [("pack", "sibling"), ("x", "sibling")]:
+        tiles += ["sac x c", "sac x a", ("pack", "sibling"), ("x", "sibling")]
+        for name in common + tiles:
             self.here[name] = self.arrivals
             self.arrivals += 1
-        for name, number in (("sac g", 3), ("sac x", 3), (("pack", "like"), MEMBERS), (("x", "like"), MEMBERS)):
-            self.here[name] = self.arrivals
-            self.arrivals += number
+        for name in ("pack", "x"):
+            self.here[name, "like"] = self.arrivals
+            self.arrivals += MEMBERS
+        self.keepers = 2 * (self.rows // 8) // self.mat
 
 
 def main_kernel(lay, *refs):
@@ -189,9 +190,9 @@
         replay, model, requests, member, live, noise, sac_h, sac_m, dyn_h, dyn_m, crit_in, act_in,
         dyn_in, crit_out, act_out, dyn_out, biases, targ_in, targ_hidden, targ_out, targ_bias,
         sac_g, sac_x, dyn_x, dyn_s, small, count,
-        wg, lists, asked, dhg, dmg, smg, bk, xs, nz, w1f, w1t, w1n, w2t, w2h, heads, head_t, head_f,
+        wg, lists, asked, dhg, dmg, bk, xs, nz, w1f, w1t, w1n, w2t, w2h, heads, head_t, head_f,
         rowbuf, wide, headcol, acc_h, acc_w, acc_c, acc_a, acc_m, acc_l, grid_c, grid_a, from_c, from_a,
-        zr_c, zr_a, zf_c, zf_a, sum_c, sum_a, mg, mat, grow, dcols, dacc_h, dacc_w, dacc_o, dacc_m, dacc_b, dacc_l, xt, dmat,
+        zr_c, zr_a, zf_c, zf_a, sum_c, sum_a, mg, mat, dcols, dacc_h, dacc_w, dacc_o, dacc_m, dacc_b, dacc_l, xt, dmat,
         dpack, drow_x, bias, dhead, dhead_t, *rest,
     ) = refs
     send, recv = rest
@@ -276,9 +277,6 @@
 
     def dyn_m_copy(peer):
         return on_line(dyn_m.at[dyn_e], dmg.at[z], send.at[sent["dyn m"]], recv.at[here_at["dyn m"]], peer)
-
-    def sac_m_copy(peer):
-        return on_line(sac_m, smg.at[z], send.at[sent["sac m"]], recv.at[here_at["sac m"]], peer)
 
     alive = live[...].astype(F32).reshape(1, lay.model)
     bias[...] = biases[...].reshape(1, NB)
@@ -397,10 +395,6 @@
         line_peers(lambda peer: dyn_h_copy(peer).start())
         line_peers(lambda peer: dyn_m_copy(peer).start())
 
-    @pl.when(is_owner)
-    def _():
-        line_peers(lambda peer: sac_m_copy(peer).start())
-
     has_come(wg.at[pl.ds(0, n_blk - 1), :, half_rows], "hidden on")
     for k in range(3):
         for block in range(n_blk):
@@ -467,13 +461,11 @@
     def add_hidden(k, first, grad):
         acc_h[k] += dot(jnp.concatenate([first, ones16()], 0), grad, NT)
 
+    has_come(bk.at[pl.ds(0, n_blk - 1)], "line")
+    plane_peers(lambda peer: block_plane(peer).start())
+
     @pl.loop(0, n_tiles)
     def _(step):
-        @pl.when(step == 1)
-        def _():
-            has_come(bk.at[pl.ds(0, n_blk - 1)], "line")
-            plane_peers(lambda peer: block_plane(peer).start())
-
         @pl.when(step == n_tiles - 1)
         def _():
             has_come(bk.at[pl.ds(0, n_dp - 1)], "own")
@@ -553,6 +545,13 @@
         group, tiles = line_part(part)
         return zrs[group].at[pl.ds(0, n_blk - 1), tiles]
 
+    first_tile = me * lay.mat
+    side = first_tile // 32
+    row_tile = lax.rem(first_tile, 32)
+    keeper_z = row_tile * 8 // lay.rows
+    local_tile = row_tile - keeper_z * (lay.rows // 8)
+    is_keeper = z == keeper_z
+
     def fold_plane(group):
         has_come(froms[group].at[pl.ds(0, n_dp - 1)], ("plane sum", group))
         froms[group][me] = grids[group][me]
@@ -560,6 +559,15 @@
         for at in range(1, n_dp):
             whole = whole + froms[group][at]
         zfs[group][...] = whole
+
+        @pl.when(is_keeper)
+        def _():
+            held_rows = pl.ds(pl.multiple_of(local_tile * 8, 8), lay.mat * 8)
+            held_lanes = pl.ds(pl.multiple_of(side * 128, 128), 128)
+            for at, k in enumerate(((0, 1), (2,))[group]):
+                old = sac_m[k, held_rows, held_lanes].reshape(lay.mat, 8, 128)
+                zfs[group][at * lay.mat : (at + 1) * lay.mat] += (MOMENTUM * total).reshape(1, 1, 1) * old
+
         for part in (0,) if group == 0 else (1, 2):
             line_peers(lambda peer: line_sum(part, peer).start())
 
@@ -572,6 +580,15 @@
             sum_a.at[pl.ds(lay.mat, lay.sml)], small.at[pl.ds(me * lay.sml, lay.sml)],
             send.at[sent["small"]], recv.at[here_at["small"]], peer,
         )
+
+    def keep_copy(part, peer):
+        ks = pl.ds(2 * part, 2 - part)
+        view = sac_g.at[side, ks, pl.ds(local_tile, lay.mat)]
+        name = ("sac g c", "sac g a")[part]
+        return on_plane(view, view, send.at[sent[name]], recv.at[here_at[name]], peer)
+
+    def kept_bytes(part, number):
+        return froms[0].at[pl.ds(0, number)] if part == 0 else mg.at[0, pl.ds(0, number)]
 
     def fold_end(part):
         group, tiles = line_part(part)
@@ -587,6 +604,13 @@
             @pl.when(is_owner)
             def _():
                 mg[k, me] = (sum_c, sum_a)[group][(k % 2) * lay.mat : (k % 2 + 1) * lay.mat]
+
+        if part < 2:
+            @pl.when(is_keeper)
+            def _():
+                for at, k in enumerate(((0, 1), (2,))[part]):
+                    sac_g[side, k, pl.ds(local_tile, lay.mat)] = whole[at * lay.mat : (at + 1) * lay.mat]
+                plane_peers(lambda peer: keep_copy(part, peer).start())
 
         if part == 2:
             plane_peers(lambda peer: small_copy(peer).start())
@@ -625,6 +649,24 @@
     for k in range(2):
         put_matrix(0, k, k)
     critic_chain[0]()
+
+    has_come(bk.at[pl.ds(0, (n_dp - 1) * (n_blk - 1))], "plane")
+    lane0 = lay.real // 128 * 128
+
+    def add_block(at, carry):
+        sides, fills = carry
+        slot = slot_of(at)
+        return sides + bk[slot, 0:32, lane0 : lane0 + 128], fills + bk[slot, 40:48, 0 : lay.real]
+
+    sides, fills = lax.fori_loop(
+        0, lay.n_dev, add_block, (jnp.zeros((32, 128), F32), jnp.zeros((8, lay.real), F32))
+    )
+    at = lay.real - lane0
+    rows_all = float(lay.replay * lay.n_dev)
+    centre = sides[0:24, at : at + 1] / rows_all
+    scale = lax.rsqrt(sides[0:24, at + 1 : at + 2] / rows_all - centre * centre + 1e-6)
+    total = sides[24:25, at : at + 1] + jnp.sum(fills[2:3, :], axis=1, keepdims=True)
+    count[...] = jnp.broadcast_to(total, (8, 128))
 
     @pl.loop(0, n_tiles)
     def _(step):
@@ -675,24 +717,6 @@
     put(R_MISC, rowbuf[...])
     put(R_MISC + 8, jnp.zeros((R_SMALL - R_MISC - 8, HSAC), F32))
     actor_chain[0]()
-
-    has_come(bk.at[pl.ds(0, (n_dp - 1) * (n_blk - 1))], "plane")
-    lane0 = lay.real // 128 * 128
-
-    def add_block(at, carry):
-        sides, fills = carry
-        slot = slot_of(at)
-        return sides + bk[slot, 0:32, lane0 : lane0 + 128], fills + bk[slot, 40:48, 0 : lay.real]
-
-    sides, fills = lax.fori_loop(
-        0, lay.n_dev, add_block, (jnp.zeros((32, 128), F32), jnp.zeros((8, lay.real), F32))
-    )
-    at = lay.real - lane0
-    rows_all = float(lay.replay * lay.n_dev)
-    centre = sides[0:24, at : at + 1] / rows_all
-    scale = lax.rsqrt(sides[0:24, at + 1 : at + 2] / rows_all - centre * centre + 1e-6)
-    total = sides[24:25, at : at + 1] + jnp.sum(fills[2:3, :], axis=1, keepdims=True)
-    count[...] = jnp.broadcast_to(total, (8, 128))
 
     def dyn_bias(start, width):
         row = jnp.zeros((1, width), F32)
@@ -830,11 +854,10 @@
             rows = jnp.where(z == block, ref[block * lay.drows : (block + 1) * lay.drows, 0:HDYN], rows)
         return rows
 
-    def sac_g_copy(k, peer):
-        return on_plane(grow.at[k, mine_rows], sac_g.at[k], send.at[sent["sac g", k] + peer], recv.at[here_at["sac g"] + k], peer)
-
-    def sac_x_copy(k, peer):
-        return on_plane(mat.at[k, mine_rows], sac_x.at[k], send.at[sent["sac x", k] + peer], recv.at[here_at["sac x"] + k], peer)
+    def sac_x_copy(part, src, peer):
+        name = ("sac x c", "sac x a")[part]
+        dst = sac_x.at[pl.ds(2 * part, 2 - part)]
+        return on_plane(src, dst, send.at[sent[name] + peer], recv.at[here_at[name]], peer)
 
     mine_rows = pl.ds(pl.multiple_of(z * lay.rows, lay.rows), lay.rows)
 
@@ -842,14 +865,10 @@
         has_come(mg.at[k, pl.ds(0, n_dp - 1)], ("tiles", k))
         for chunk in range(n_dp):
             tile = chunk * lay.mat
-            side, row = tile // 32, tile % 32
+            half, row = tile // 32, tile % 32
             at = slice(row * 8, (row + lay.mat) * 8)
-            grow[k, at, side * 128 : (side + 1) * 128] = mg[k, chunk].reshape(lay.mat * 8, 128)
-        sac_g[k] = grow[k, mine_rows, :]
-        plane_peers(lambda peer: sac_g_copy(k, peer).start())
-        for block in range(n_blk):
-            at = slice(block * lay.rows, (block + 1) * lay.rows)
-            mat[k, at, :] = MOMENTUM * smg[block, k] + grow[k, at, :] / total
+            piece = mg[k, chunk].reshape(lay.mat * 8, 128)
+            mat[k, at, half * 128 : (half + 1) * 128] = piece / total
         normalise(mat.at[k])
 
     @pl.when(is_dyn)
@@ -878,9 +897,23 @@
             dmat[at, 0:HDYN] = MOMENTUM * dmg[block] + dacc_h[at, 0:HDYN] / total
         normalise(dmat)
 
-    def send_sac(k):
-        sac_x[k] = mat[k, mine_rows, :]
-        plane_peers(lambda peer: sac_x_copy(k, peer).start())
+    def own_x(part):
+        return mat.at[pl.ds(2 * part, 2 - part), mine_rows]
+
+    def passed_x(part):
+        return sac_x.at[pl.ds(2 * part, 2 - part)]
+
+    def send_sac(part):
+        for k in ((0, 1), (2,))[part]:
+            sac_x[k] = mat[k, mine_rows, :]
+        like_peers(lambda peer: sac_x_copy(part, own_x(part), peer).start())
+        sac_x_copy(part, own_x(part), sibling).start()
+
+    passes_x = jnp.logical_and(core == lay.owner % 2, jnp.logical_not(is_owner))
+
+    def receive_sac(part):
+        pl.when(jnp.logical_not(is_owner))(sac_x_copy(part, passed_x(part), sibling).wait_recv)
+        pl.when(passes_x)(sac_x_copy(part, passed_x(part), sibling).start)
 
     def sum_end(step):
         pl.when(step == NS_ITERS - 2)(actor_chain[2])
@@ -895,13 +928,10 @@
 
     @pl.when(is_owner)
     def _():
-        has_come(smg.at[pl.ds(0, n_blk - 1)], "sac m")
-        smg[z] = sac_m[...]
         for k in range(2):
             take_matrix(k)
         schulz([mat.at[0], mat.at[1]], NS_ITERS, sum_end)
-        for k in range(2):
-            send_sac(k)
+        send_sac(0)
 
     if n_dp > MEMBERS + 1:
         pl.when(jnp.logical_not(jnp.logical_or(is_dyn, is_owner)))(actor_chain[2])
@@ -919,10 +949,6 @@
             has_sent(dhg.at[pl.ds(0, n_blk - 1)], "dyn h")
             has_sent(dmg.at[pl.ds(0, n_blk - 1)], "dyn m")
 
-        @pl.when(is_owner)
-        def _():
-            has_sent(smg.at[pl.ds(0, n_blk - 1)], "sac m")
-
         for group in range(2):
             has_sent(froms[group].at[pl.ds(0, n_dp - 1)], ("plane sum", group))
         for part in range(3):
@@ -932,20 +958,21 @@
     def _():
         take_matrix(2)
         schulz([mat.at[2]], NS_ITERS)
-        send_sac(2)
+        send_sac(1)
 
     sent_early()
     hand_on("pack")
+    receive_sac(0)
     hand_on("x")
     has_come(small.at[pl.ds(0, (n_dp - 1) * lay.sml)], "small")
+    for part in range(2):
+        for number, test in ((lay.keepers - 1, is_keeper), (lay.keepers, jnp.logical_not(is_keeper))):
+            pl.when(test)(
+                functools.partial(has_come, kept_bytes(part, number), ("sac g c", "sac g a")[part])
+            )
     from_sibling("pack")
     from_sibling("x")
-
-    @pl.when(jnp.logical_not(is_owner))
-    def _():
-        for k in range(3):
-            sac_g_copy(k, sibling).wait_recv()
-            sac_x_copy(k, sibling).wait_recv()
+    receive_sac(1)
 
     has_sent(small.at[pl.ds(0, (n_dp - 1) * lay.sml)], "small")
     gave("pack")
@@ -956,11 +983,18 @@
         for k in range(3):
             tile_copy(k).wait_send()
 
-    @pl.when(is_owner)
+    @pl.when(is_keeper)
     def _():
-        for k in range(3):
-            plane_peers(lambda peer: sac_g_copy(k, peer).wait_send())
-            plane_peers(lambda peer: sac_x_copy(k, peer).wait_send())
+        for part in range(2):
+            has_sent(kept_bytes(part, n_dp - 1), ("sac g c", "sac g a")[part])
+
+    for part in range(2):
+        @pl.when(is_owner)
+        def _():
+            like_peers(lambda peer: sac_x_copy(part, own_x(part), peer).wait_send())
+
+        pl.when(is_owner)(sac_x_copy(part, own_x(part), sibling).wait_send)
+        pl.when(passes_x)(sac_x_copy(part, passed_x(part), sibling).wait_send)
 
 
 def adamw(weights, first, second, gradient):
@@ -974,7 +1008,7 @@
 
 def update_kernel(*refs):
     (
-        sac_g, sac_x, dyn_x, dyn_s, small, count, sac_h, sac_m, dyn_h, dyn_m,
+        sac_g, sac_x, dyn_x, dyn_s, small, count, sac_h, dyn_h, dyn_m,
         ci, ci_m, ci_v, ai, ai_m, ai_v, di, di_m, di_v, co, co_m, co_v, ao, ao_m, ao_v,
         do, do_m, do_v, bi, bi_m, bi_v,
         sac_new, sac_mom, dyn_new, dyn_mom, ci_n, ci_mn, ci_vn, ai_n, ai_mn, ai_vn, di_n, di_mn,
@@ -982,7 +1016,10 @@
         loss, counted, bg,
     ) = refs
     total = count[0:1, 0:1]
-    sac_mom[...] = MOMENTUM * sac_m[...] + sac_g[...] / total.reshape(1, 1, 1)
+    for k in range(3):
+        for side in range(2):
+            tiles = sac_g[side, k].reshape(sac_mom.shape[1], 128)
+            sac_mom[k, :, side * 128 : (side + 1) * 128] = tiles / total
     sac_new[...] = sac_h[...] * (1.0 - MUON_RATE * MUON_DECAY) - MUON_RATE * sac_x[...]
     dyn_rows = dyn_s[:, D_HID : D_HID + dyn_m.shape[1], 0:HDYN]
     dyn_mom[...] = MOMENTUM * dyn_m[...] + dyn_rows / total.reshape(1, 1, 1)
@@ -1080,7 +1117,7 @@
     shape = jax.ShapeDtypeStruct
     rows, drows = lay.rows, lay.drows
     out_shape = (
-        pltpu.VMEM((3, rows, HSAC), F32),
+        pltpu.VMEM((2, 3, rows // 8, 8, 128), F32),
         pltpu.VMEM((3, rows, HSAC), F32),
         pltpu.VMEM((MEMBERS, drows, HDYN), F32),
         pltpu.VMEM((MEMBERS, D_ROWS, HSAC), F32),
@@ -1097,7 +1134,6 @@
         vm(n_dp, 2, n_dp, CAP, kind=jnp.int32),
         vm(n_blk, drows, HDYN),
         vm(n_blk, drows, HDYN),
-        vm(n_blk, 3, rows, HSAC),
         vm(lay.n_dev, 48, lay.width),
         vm(56, lay.batch),
         vm(2, 8, lay.batch),
@@ -1130,7 +1166,6 @@
         vm(lay.chunks[1], 8, 128),
         vm(3, n_dp, lay.mat, 8, 128),
         vm(3, HSAC, HSAC),
-        vm(3, HSAC, HSAC),
         vm(HSAC, 8),
         vm(HSAC + 16, HSAC),
         vm(32, HSAC),
@@ -1160,13 +1195,13 @@
         name="step",
     )(*[pltpu.with_memory_space_constraint(value, pltpu.HBM) for value in inputs])
     params = (
-        sac_hidden, sac_hidden_mom, dyn_hidden, dyn_hidden_mom,
+        sac_hidden, dyn_hidden, dyn_hidden_mom,
         flip(crit_in), flip(crit_in_m), flip(crit_in_v), act_in, act_in_m, act_in_v,
         dyn_in, dyn_in_m, dyn_in_v, crit_out, crit_out_m, crit_out_v,
         swap(act_out), swap(act_out_m), swap(act_out_v),
         swap(dyn_out), swap(dyn_out_m), swap(dyn_out_v), biases, biases_m, biases_v,
     )
-    new_shape = [shape(value.shape, F32) for value in params]
+    new_shape = [shape(sac_hidden.shape, F32)] + [shape(value.shape, F32) for value in params]
     new_shape += [shape((1, 1), F32)] * 2
     out = pl.pallas_call(
         update_kernel,

time: 72.6 us -> 68.3 us (0.941)
  Pallas kernels: 70.7 us -> 66.3 us
    pallas_call x1, Pallas kernels: 68.6 us -> 64.2 us  [shards(): pl.pallas_call(functools.partial(main_kernel, lay), out_shape=out_shape,...]
where the time goes in v7:
time: 68.3 us; the launch traced here: 67.9 us
  Pallas kernels  66.3 us (97%)
  between operations  1.05 us (2%)
    pallas_call x1, Pallas kernels, shards(): pl.pallas_call(functools.partial(main_kernel, lay), out_shape=out_shape,...  64.2 us
    pallas_call x1, Pallas kernels, shards(): pl.pallas_call(update_kernel, out_shape=tuple(new_shape), in_specs=[spec]...  2.11 us

profile of v7, /device:TPU:0, one launch (start us, length us, event | category | flops | bytes accessed | tf_op | source)
XLA Modules:
  0.0 67.9 jit_solution(5844177269683895206)
XLA Ops:
  0.7 0.0 copy-start
  0.7 0.0 copy-start.1
  0.7 0.0 copy-start.2
  0.7 0.0 copy-start.3
  0.7 0.0 copy-start.4
  0.7 0.0 copy-start.5
  0.7 0.0 copy-start.6
  0.7 0.0 copy-start.7
  0.8 0.0 copy-start.8
  0.8 0.0 copy-start.9
  0.8 0.0 copy-start.10
  0.8 0.0 copy-start.11
  0.8 0.0 copy-start.12
  0.8 0.0 copy-start.13
  0.8 0.0 copy-start.14
  0.8 0.0 copy-start.15
  0.8 0.0 copy-start.16
  0.8 0.0 copy-start.17
  0.9 0.0 copy-start.18
  0.9 0.0 copy-start.19
  0.9 0.0 copy-start.20
  0.9 0.0 copy-start.23
  0.9 64.2 %step.1 = (f32[2,3,8,8,128]{4,3,2,1,0:T(8,128)S(1)}, f32[3,64,256]{2,1,0:T(8,128)S(1)}, f32[7,50,200]{2,1,0:T(8,128)S(1)}, f32[7,128,256]{2,1,0:T(8,128)S(1)}, f...) custom-call(f32[42,3648]{1,0:T(8,128)} %refs_0_.1, f32[42,1216]{1,0:T(8,128)} %refs_1_.1, s32[8,8]{1,0:T(8,128)} %refs_2_.1, ...), custom_call_target="tpu_custom_call" | custom-call | tf_op jit(solution)/shard_map/step/pallas_call | solution.py:1186
  65.1 0.0 copy-start.22
  65.1 0.0 copy-start.21
  65.1 0.0 copy-done
  65.1 0.0 copy-done.1
  65.1 0.0 copy-done.2
  65.2 0.0 copy-done.3
  65.2 0.0 copy-done.4
  65.2 0.0 copy-done.5
  65.2 0.0 copy-done.6
  65.2 0.0 copy-done.7
  65.2 0.0 copy-done.8
  65.2 0.0 copy-done.9
  65.2 0.0 copy-done.10
  65.2 0.0 copy-done.11
  65.2 0.0 copy-done.12
  65.3 0.0 copy-done.13
  65.3 0.0 copy-done.14
  65.3 0.0 copy-done.15
  65.3 0.0 copy-done.16
  65.3 0.0 copy-done.17
  65.3 0.0 copy-done.18
  65.3 0.0 copy-done.19
  65.3 0.0 copy-done.20
  65.3 0.0 copy-done.23
  65.3 0.4 copy-done.22
  65.8 0.0 copy-done.21
  65.8 2.1 %update.1 = (f32[3,64,256]{2,1,0:T(8,128)}, f32[3,64,256]{2,1,0:T(8,128)}, f32[7,50,200]{2,1,0:T(8,128)}, f32[7,50,200]{2,1,0:T(8,128)}, f32[23,2,256]{2,1,0:T(2...) custom-call(f32[2,3,8,8,128]{4,3,2,1,0:T(8,128)S(1)} %get-tuple-elem, ...), custom_call_target="tpu_custom_call" | custom-call | tf_op jit(solution)/shard_map/update/pallas_call | solution.py:1206
Async XLA Ops:
  0.7 64.5 %copy-start = (f32[7,50,200]{2,1,0:T(8,128)S(1)}, f32[7,50,200]{2,1,0:T(8,128)}, u32[]{:S(2)}) copy-start(f32[7,50,200]{2,1,0:T(8,128)} %refs_7_.3) | copy-start | bytes 840004
  0.7 64.5 %copy-start.1 = (f32[7,50,200]{2,1,0:T(8,128)S(1)}, f32[7,50,200]{2,1,0:T(8,128)}, u32[]{:S(2)}) copy-start(f32[7,50,200]{2,1,0:T(8,128)} %refs_8_.3) | copy-start | bytes 840004
  0.7 64.5 %copy-start.2 = (f32[7,200,36]{1,2,0:T(8,128)S(1)}, f32[7,200,36]{1,2,0:T(8,128)}, u32[]{:S(2)}) copy-start(f32[7,200,36]{1,2,0:T(8,128)} %param.60) | copy-start | bytes 604804
  0.7 64.5 %copy-start.3 = (f32[3,64,256]{2,1,0:T(8,128)S(1)}, f32[3,64,256]{2,1,0:T(8,128)}, u32[]{:S(2)}) copy-start(f32[3,64,256]{2,1,0:T(8,128)} %refs_6_.3) | copy-start | bytes 589828
  0.7 64.5 %copy-start.4 = (f32[7,23,200]{2,1,0:T(8,128)S(1)}, f32[7,23,200]{2,1,0:T(8,128)}, u32[]{:S(2)}) copy-start(f32[7,23,200]{2,1,0:T(8,128)} %refs_15_.1) | copy-start | bytes 386404
  0.7 64.5 %copy-start.5 = (f32[7,200,36]{1,2,0:T(8,128)S(1)}, f32[7,200,36]{1,2,0:T(8,128)}, u32[]{:S(2)}) copy-start(f32[7,200,36]{1,2,0:T(8,128)} %param.61) | copy-start | bytes 604804
  0.7 64.5 %copy-start.6 = (f32[7,200,36]{1,2,0:T(8,128)S(1)}, f32[7,200,36]{1,2,0:T(8,128)}, u32[]{:S(2)}) copy-start(f32[7,200,36]{1,2,0:T(8,128)} %param.62) | copy-start | bytes 604804
  0.7 64.5 %copy-start.7 = (f32[2,23,256]{2,0,1:T(2,128)S(1)}, f32[2,23,256]{2,0,1:T(2,128)}, u32[]{:S(2)}) copy-start(f32[2,23,256]{2,0,1:T(2,128)} %param.45) | copy-start | bytes 141316
  0.8 64.5 %copy-start.8 = (f32[7,23,200]{2,1,0:T(8,128)S(1)}, f32[7,23,200]{2,1,0:T(8,128)}, u32[]{:S(2)}) copy-start(f32[7,23,200]{2,1,0:T(8,128)} %refs_16_.3) | copy-start | bytes 386404
  0.8 64.5 %copy-start.9 = (f32[7,23,200]{2,1,0:T(8,128)S(1)}, f32[7,23,200]{2,1,0:T(8,128)}, u32[]{:S(2)}) copy-start(f32[7,23,200]{2,1,0:T(8,128)} %refs_17_.1) | copy-start | bytes 386404
  0.8 64.5 %copy-start.10 = (f32[17,256]{1,0:T(8,128)S(1)}, f32[17,256]{1,0:T(8,128)}, u32[]{:S(2)}) copy-start(f32[17,256]{1,0:T(8,128)} %refs_12_.3) | copy-start | bytes 52228
  0.8 64.5 %copy-start.11 = (f32[4639]{0:T(1024)S(1)}, f32[4639]{0:T(1024)}, u32[]{:S(2)}) copy-start(f32[4639]{0:T(1024)} %refs_27_.1) | copy-start | bytes 55672
  0.8 64.5 %copy-start.12 = (f32[256,12]{0,1:T(8,128)S(1)}, f32[256,12]{0,1:T(8,128)}, u32[]{:S(2)}) copy-start(f32[256,12]{0,1:T(8,128)} %param.57) | copy-start | bytes 36868
  0.8 64.5 %copy-start.13 = (f32[2,23,256]{2,0,1:T(2,128)S(1)}, f32[2,23,256]{2,0,1:T(2,128)}, u32[]{:S(2)}) copy-start(f32[2,23,256]{2,0,1:T(2,128)} %param.46) | copy-start | bytes 141316
  0.8 64.5 %copy-start.14 = (f32[2,23,256]{2,0,1:T(2,128)S(1)}, f32[2,23,256]{2,0,1:T(2,128)}, u32[]{:S(2)}) copy-start(f32[2,23,256]{2,0,1:T(2,128)} %param.47) | copy-start | bytes 141316
  0.8 64.5 %copy-start.15 = (f32[17,256]{1,0:T(8,128)S(1)}, f32[17,256]{1,0:T(8,128)}, u32[]{:S(2)}) copy-start(f32[17,256]{1,0:T(8,128)} %refs_13_.3) | copy-start | bytes 52228
  0.8 64.5 %copy-start.16 = (f32[17,256]{1,0:T(8,128)S(1)}, f32[17,256]{1,0:T(8,128)}, u32[]{:S(2)}) copy-start(f32[17,256]{1,0:T(8,128)} %refs_14_.1) | copy-start | bytes 52228
  0.8 64.5 %copy-start.17 = (f32[4639]{0:T(1024)S(1)}, f32[4639]{0:T(1024)}, u32[]{:S(2)}) copy-start(f32[4639]{0:T(1024)} %refs_28_.1) | copy-start | bytes 55672
  0.9 64.5 %copy-start.18 = (f32[4639]{0:T(1024)S(1)}, f32[4639]{0:T(1024)}, u32[]{:S(2)}) copy-start(f32[4639]{0:T(1024)} %refs_29_.1) | copy-start | bytes 55672
  0.9 64.5 %copy-start.19 = (f32[256,12]{0,1:T(8,128)S(1)}, f32[256,12]{0,1:T(8,128)}, u32[]{:S(2)}) copy-start(f32[256,12]{0,1:T(8,128)} %param.58) | copy-start | bytes 36868
  0.9 64.5 %copy-start.20 = (f32[256,12]{0,1:T(8,128)S(1)}, f32[256,12]{0,1:T(8,128)}, u32[]{:S(2)}) copy-start(f32[256,12]{0,1:T(8,128)} %param.59) | copy-start | bytes 36868
  0.9 64.5 %copy-start.23 = (f32[2,256]{1,0:T(2,128)S(1)}, f32[2,256]{1,0:T(2,128)}, u32[]{:S(2)}) copy-start(f32[2,256]{1,0:T(2,128)} %refs_20_.3) | copy-start | bytes 6148
  65.1 0.7 %copy-start.22 = (f32[2,256]{1,0:T(2,128)S(1)}, f32[2,256]{1,0:T(2,128)}, u32[]{:S(2)}) copy-start(f32[2,256]{1,0:T(2,128)} %refs_19_.3) | copy-start | bytes 6148
  65.1 0.7 %copy-start.21 = (f32[2,256]{1,0:T(2,128)S(1)}, f32[2,256]{1,0:T(2,128)}, u32[]{:S(2)}) copy-start(f32[2,256]{1,0:T(2,128)} %refs_18_.3) | copy-start | bytes 6148

commit v8 on v7

--- a/solution.py
+++ b/solution.py
@@ -20,7 +20,8 @@
 NS_ITERS = 5
 STEP = 10
 CAP = 8
-TILE = 640
+CRITIC_TILE = 1280
+ACTOR_TILE = 640
 DYN_TILE = 512
 ROWS = 32
 
@@ -165,17 +166,16 @@
 
         groups = [("plane sum", g) for g in range(2)] + [("line sum", g) for g in range(3)]
         common = ["hidden", "hidden on", "lists", "own", "line", "plane", "dyn h", "dyn m", "small"]
-        common += groups + ["sac g c", "sac g a"]
+        common += groups + ["sac g"]
         kinds = [(name, kind) for name in ("pack", "x") for kind in ("own", "on")]
         sent = common + [("tiles", k) for k in range(3)] + kinds
         self.sent = {name: at for at, name in enumerate(sent)}
         self.departures = len(sent)
-        for name in ("sac x c", "sac x a"):
-            self.sent[name] = self.departures
-            self.departures += self.n_dp
+        self.sent["sac x"] = self.departures
+        self.departures += self.n_dp
         self.here, self.arrivals = {}, 0
         tiles = [("tiles", k) for k in range(3)]
-        tiles += ["sac x c", "sac x a", ("pack", "sibling"), ("x", "sibling")]
+        tiles += ["sac x", ("pack", "sibling"), ("x", "sibling")]
         for name in common + tiles:
             self.here[name] = self.arrivals
             self.arrivals += 1
@@ -411,18 +411,21 @@
         bias[:, CB3 : CB3 + 1],
         bias[:, CB3 + 1 : CB3 + 2],
     ]
-    n_tiles = lay.batch // TILE
-    row8 = rows_of((8, TILE))
-    act_rows = jnp.logical_and(row8 >= 1, row8 < 1 + ACT)
-
-    def place_of(step):
-        return pl.ds(pl.multiple_of(lax.rem(step + 1, n_tiles) * TILE, TILE), TILE)
-
-    def ones16(width=TILE):
+    critic_tiles = lay.batch // CRITIC_TILE
+    actor_tiles = lay.batch // ACTOR_TILE
+
+    def act_rows(width):
+        row8 = rows_of((8, width))
+        return jnp.logical_and(row8 >= 1, row8 < 1 + ACT)
+
+    def place_of(step, width):
+        return pl.ds(pl.multiple_of(lax.rem(step + 1, lay.batch // width) * width, width), width)
+
+    def ones16(width):
         return jnp.ones((16, width), BF16)
 
     def framed(first_row, used, where):
-        row32 = rows_of((32, TILE))
+        row32 = rows_of((32, where.size))
         ones3 = jnp.logical_and(row32 >= IN, row32 < IN + 3).astype(F32)
         return jnp.where(row32 < used, xs[first_row : first_row + 32, where], ones3)
 
@@ -445,12 +448,13 @@
             - 0.9189385
             - 2.0 * (0.6931472 - latent - softplus(-2.0 * latent))
         )
-        log_prob = jnp.sum(jnp.where(act_rows, terms, 0.0), axis=0, keepdims=True)
-        action = jnp.where(act_rows, jnp.tanh(latent), 0.0)
+        used = act_rows(where.size)
+        log_prob = jnp.sum(jnp.where(used, terms, 0.0), axis=0, keepdims=True)
+        action = jnp.where(used, jnp.tanh(latent), 0.0)
         return action, log_prob, bent, moved, (first, slope1, second, slope2)
 
     def with_action(inputs, action):
-        middle_rows = jnp.where(act_rows, action, inputs[16:24])
+        middle_rows = jnp.where(act_rows(action.shape[1]), action, inputs[16:24])
         return jnp.concatenate([inputs[0:16], middle_rows, inputs[24:32]], 0).astype(BF16)
 
     def critic(inputs, net):
@@ -459,14 +463,14 @@
         return value, kept
 
     def add_hidden(k, first, grad):
-        acc_h[k] += dot(jnp.concatenate([first, ones16()], 0), grad, NT)
+        acc_h[k] += dot(jnp.concatenate([first, ones16(grad.shape[1])], 0), grad, NT)
 
     has_come(bk.at[pl.ds(0, n_blk - 1)], "line")
     plane_peers(lambda peer: block_plane(peer).start())
 
-    @pl.loop(0, n_tiles)
+    @pl.loop(0, critic_tiles)
     def _(step):
-        @pl.when(step == n_tiles - 1)
+        @pl.when(step == critic_tiles - 1)
         def _():
             has_come(bk.at[pl.ds(0, n_dp - 1)], "own")
             lanes = lax.broadcasted_iota(jnp.int32, (48, lay.width), 1) // CAP
@@ -480,18 +484,18 @@
             own = lax.fori_loop(0, n_dp, gather, jnp.zeros((48, lay.width), F32))
             xs[0:48, 0 : lay.real] = own[:, 0 : lay.real]
 
-        where = place_of(step)
+        where = place_of(step, CRITIC_TILE)
         now_in = framed(0, IN, where).astype(BF16)
         next_f = framed(24, OBS, where)
         reward = xs[23:24, where]
         done = xs[41:42, where]
         weight = xs[42:43, where]
-        row16 = rows_of((16, TILE))
+        row16 = rows_of((16, CRITIC_TILE))
         next_action, next_prob, _, _, _ = policy(next_f.astype(BF16), 1, where)
         aim_in = with_action(next_f, next_action)
         aim = jnp.minimum(critic(aim_in, 0)[0], critic(aim_in, 1)[0])
         target = reward + DISCOUNT * (1.0 - done) * (aim - alpha * next_prob)
-        loss = jnp.zeros((1, TILE), F32)
+        loss = jnp.zeros((1, CRITIC_TILE), F32)
         heads_grad = []
         for k in range(2):
             value, (c1, dc1, c2, dc2) = critic(now_in, 2 + k)
@@ -505,8 +509,8 @@
             add_hidden(k, c1, g2)
             g1 = sloped(dot(w2h[k], g2), dc1)
             acc_w[k] += dot(now_in, g1, NT)
-        acc_m[:, 16:48] += dot(ones16(), jnp.concatenate(heads_grad, 0), NT)
-        acc_l[0:1, :] += weight * loss
+        acc_m[:, 16:48] += dot(ones16(CRITIC_TILE), jnp.concatenate(heads_grad, 0), NT)
+        acc_l[0:1, 0:CRITIC_TILE] += weight * loss
 
     def put_matrix(group, k, at):
         for chunk in range(n_dp):
@@ -571,9 +575,9 @@
         for part in (0,) if group == 0 else (1, 2):
             line_peers(lambda peer: line_sum(part, peer).start())
 
-    def tile_copy(k):
+    def tile_copy(k, peer):
         src = (sum_c, sum_a)[k // 2].at[pl.ds((k % 2) * lay.mat, lay.mat)]
-        return on_plane(src, mg.at[k, me], send.at[sent["tiles", k]], recv.at[here_at["tiles", k]], lay.owner)
+        return on_plane(src, mg.at[k, me], send.at[sent["tiles", k]], recv.at[here_at["tiles", k]], peer)
 
     def small_copy(peer):
         return on_plane(
@@ -581,14 +585,12 @@
             send.at[sent["small"]], recv.at[here_at["small"]], peer,
         )
 
-    def keep_copy(part, peer):
-        ks = pl.ds(2 * part, 2 - part)
-        view = sac_g.at[side, ks, pl.ds(local_tile, lay.mat)]
-        name = ("sac g c", "sac g a")[part]
-        return on_plane(view, view, send.at[sent[name]], recv.at[here_at[name]], peer)
-
-    def kept_bytes(part, number):
-        return froms[0].at[pl.ds(0, number)] if part == 0 else mg.at[0, pl.ds(0, number)]
+    def keep_copy(peer):
+        view = sac_g.at[side, pl.ds(0, 2), pl.ds(local_tile, lay.mat)]
+        return on_plane(view, view, send.at[sent["sac g"]], recv.at[here_at["sac g"]], peer)
+
+    def kept_bytes(number):
+        return froms[0].at[pl.ds(0, number)]
 
     def fold_end(part):
         group, tiles = line_part(part)
@@ -598,19 +600,23 @@
         for block in range(1, n_blk):
             whole = whole + zrs[group][block, tiles]
         (sum_c, sum_a)[group][tiles] = whole
-        for k in ((0, 1), (2,), ())[part]:
-            pl.when(jnp.logical_not(is_owner))(tile_copy(k).start)
-
-            @pl.when(is_owner)
-            def _():
-                mg[k, me] = (sum_c, sum_a)[group][(k % 2) * lay.mat : (k % 2 + 1) * lay.mat]
-
-        if part < 2:
+        if part == 0:
+            for k in range(2):
+                pl.when(jnp.logical_not(is_owner))(tile_copy(k, lay.owner).start)
+
+                @pl.when(is_owner)
+                def _():
+                    mg[k, me] = whole[k * lay.mat : (k + 1) * lay.mat]
+
             @pl.when(is_keeper)
             def _():
-                for at, k in enumerate(((0, 1), (2,))[part]):
-                    sac_g[side, k, pl.ds(local_tile, lay.mat)] = whole[at * lay.mat : (at + 1) * lay.mat]
-                plane_peers(lambda peer: keep_copy(part, peer).start())
+                for k in range(2):
+                    sac_g[side, k, pl.ds(local_tile, lay.mat)] = whole[k * lay.mat : (k + 1) * lay.mat]
+                plane_peers(lambda peer: keep_copy(peer).start())
+
+        if part == 1:
+            plane_peers(lambda peer: tile_copy(2, peer).start())
+            mg[2, me] = whole
 
         if part == 2:
             plane_peers(lambda peer: small_copy(peer).start())
@@ -631,7 +637,7 @@
     per = DYN_TILE // lay.real
     dyn_tiles = lay.n_dev // per
     in_actor, in_dyn = {}, {}
-    if n_tiles > 1:
+    if actor_tiles > 1:
         in_actor[1] = [critic_chain[1]]
         in_dyn[0] = [critic_chain[2]]
     else:
@@ -668,17 +674,18 @@
     total = sides[24:25, at : at + 1] + jnp.sum(fills[2:3, :], axis=1, keepdims=True)
     count[...] = jnp.broadcast_to(total, (8, 128))
 
-    @pl.loop(0, n_tiles)
+    @pl.loop(0, actor_tiles)
     def _(step):
         take(in_actor, step)
-        where = place_of(step)
+        where = place_of(step, ACTOR_TILE)
         now_f = framed(0, IN, where)
         now_in = now_f.astype(BF16)
         weight = xs[42:43, where]
         action, log_prob, bent, moved, (a1, da1, a2, da2) = policy(now_in, 0, where)
         judged_in = with_action(now_f, action)
         loss = alpha * log_prob - log_alpha * (log_prob + TARGET_ENTROPY)
-        grad_action = jnp.zeros((8, TILE), F32)
+        grad_action = jnp.zeros((8, ACTOR_TILE), F32)
+        used = act_rows(ACTOR_TILE)
         for k in range(2):
             judged, (_, df1, _, df2) = critic(judged_in, 2 + k)
             loss -= 0.5 * judged
@@ -689,16 +696,16 @@
         grad_scale = grad_latent * moved - alpha * weight
         grad_bent = grad_scale * 3.5 * (1.0 - bent * bent)
         g3 = jnp.concatenate(
-            [jnp.where(act_rows, grad_latent, 0.0), jnp.where(act_rows, grad_bent, 0.0)], 0
+            [jnp.where(used, grad_latent, 0.0), jnp.where(used, grad_bent, 0.0)], 0
         ).astype(BF16)
         acc_a[...] += dot(g3, a2, NT)
-        acc_m[:, 0:16] += dot(ones16(), g3, NT)
+        acc_m[:, 0:16] += dot(ones16(ACTOR_TILE), g3, NT)
         g2 = sloped(dot(head_t[...], g3), da2)
         add_hidden(2, a1, g2)
         g1 = sloped(dot(w2h[2], g2), da1)
         acc_w[2] += dot(now_in, g1, NT)
-        acc_l[0:1, :] += weight * loss
-        acc_l[1:2, :] += weight * (log_prob + TARGET_ENTROPY)
+        acc_l[1:2, 0:ACTOR_TILE] += weight * loss
+        acc_l[2:3, 0:ACTOR_TILE] += weight * (log_prob + TARGET_ENTROPY)
 
     put_matrix(1, 2, 0)
     for k in range(3):
@@ -712,8 +719,8 @@
     folded = jnp.sum(acc_l[...], axis=1, keepdims=True)
     rowbuf[...] = jnp.zeros_like(rowbuf)
     rowbuf[0:1, 0:48] = acc_m[0:1, :]
-    rowbuf[0:1, 64:65] = folded[0:1]
-    rowbuf[0:1, 65:66] = folded[1:2]
+    rowbuf[0:1, 64:65] = folded[0:1] + folded[1:2]
+    rowbuf[0:1, 65:66] = folded[2:3]
     put(R_MISC, rowbuf[...])
     put(R_MISC + 8, jnp.zeros((R_SMALL - R_MISC - 8, HSAC), F32))
     actor_chain[0]()
@@ -854,10 +861,9 @@
             rows = jnp.where(z == block, ref[block * lay.drows : (block + 1) * lay.drows, 0:HDYN], rows)
         return rows
 
-    def sac_x_copy(part, src, peer):
-        name = ("sac x c", "sac x a")[part]
-        dst = sac_x.at[pl.ds(2 * part, 2 - part)]
-        return on_plane(src, dst, send.at[sent[name] + peer], recv.at[here_at[name]], peer)
+    def sac_x_copy(src, peer):
+        dst = sac_x.at[pl.ds(0, 2)]
+        return on_plane(src, dst, send.at[sent["sac x"] + peer], recv.at[here_at["sac x"]], peer)
 
     mine_rows = pl.ds(pl.multiple_of(z * lay.rows, lay.rows), lay.rows)
 
@@ -897,23 +903,8 @@
             dmat[at, 0:HDYN] = MOMENTUM * dmg[block] + dacc_h[at, 0:HDYN] / total
         normalise(dmat)
 
-    def own_x(part):
-        return mat.at[pl.ds(2 * part, 2 - part), mine_rows]
-
-    def passed_x(part):
-        return sac_x.at[pl.ds(2 * part, 2 - part)]
-
-    def send_sac(part):
-        for k in ((0, 1), (2,))[part]:
-            sac_x[k] = mat[k, mine_rows, :]
-        like_peers(lambda peer: sac_x_copy(part, own_x(part), peer).start())
-        sac_x_copy(part, own_x(part), sibling).start()
-
+    own_x, passed_x = mat.at[pl.ds(0, 2), mine_rows], sac_x.at[pl.ds(0, 2)]
     passes_x = jnp.logical_and(core == lay.owner % 2, jnp.logical_not(is_owner))
-
-    def receive_sac(part):
-        pl.when(jnp.logical_not(is_owner))(sac_x_copy(part, passed_x(part), sibling).wait_recv)
-        pl.when(passes_x)(sac_x_copy(part, passed_x(part), sibling).start)
 
     def sum_end(step):
         pl.when(step == NS_ITERS - 2)(actor_chain[2])
@@ -931,7 +922,10 @@
         for k in range(2):
             take_matrix(k)
         schulz([mat.at[0], mat.at[1]], NS_ITERS, sum_end)
-        send_sac(0)
+        for k in range(2):
+            sac_x[k] = mat[k, mine_rows, :]
+        like_peers(lambda peer: sac_x_copy(own_x, peer).start())
+        sac_x_copy(own_x, sibling).start()
 
     if n_dp > MEMBERS + 1:
         pl.when(jnp.logical_not(jnp.logical_or(is_dyn, is_owner)))(actor_chain[2])
@@ -954,47 +948,48 @@
         for part in range(3):
             has_sent(line_bytes(part), ("line sum", part))
 
-    @pl.when(is_owner)
-    def _():
-        take_matrix(2)
-        schulz([mat.at[2]], NS_ITERS)
-        send_sac(1)
+    def pass_on(step):
+        @pl.when(step == 2)
+        def _():
+            hand_on("pack")
+            hand_on("x")
+            pl.when(jnp.logical_not(is_owner))(sac_x_copy(passed_x, sibling).wait_recv)
+            pl.when(passes_x)(sac_x_copy(passed_x, sibling).start)
+
+    take_matrix(2)
+    for half in range(2):
+        for piece in range(lay.rows // 8 // lay.mat):
+            chunk = (half * 32 + z * (lay.rows // 8)) // lay.mat + piece
+            sac_g[half, 2, piece * lay.mat : (piece + 1) * lay.mat] = mg[2, chunk]
+    schulz([mat.at[2]], NS_ITERS, pass_on)
+    sac_x[2] = mat[2, mine_rows, :]
 
     sent_early()
-    hand_on("pack")
-    receive_sac(0)
-    hand_on("x")
     has_come(small.at[pl.ds(0, (n_dp - 1) * lay.sml)], "small")
-    for part in range(2):
-        for number, test in ((lay.keepers - 1, is_keeper), (lay.keepers, jnp.logical_not(is_keeper))):
-            pl.when(test)(
-                functools.partial(has_come, kept_bytes(part, number), ("sac g c", "sac g a")[part])
-            )
+    for number, test in ((lay.keepers - 1, is_keeper), (lay.keepers, jnp.logical_not(is_keeper))):
+        pl.when(test)(functools.partial(has_come, kept_bytes(number), "sac g"))
     from_sibling("pack")
     from_sibling("x")
-    receive_sac(1)
 
     has_sent(small.at[pl.ds(0, (n_dp - 1) * lay.sml)], "small")
     gave("pack")
     gave("x")
 
+    has_sent(mg.at[2, pl.ds(0, n_dp - 1)], ("tiles", 2))
+
     @pl.when(jnp.logical_not(is_owner))
     def _():
-        for k in range(3):
-            tile_copy(k).wait_send()
-
-    @pl.when(is_keeper)
+        for k in range(2):
+            tile_copy(k, sibling).wait_send()
+
+    pl.when(is_keeper)(functools.partial(has_sent, kept_bytes(n_dp - 1), "sac g"))
+
+    @pl.when(is_owner)
     def _():
-        for part in range(2):
-            has_sent(kept_bytes(part, n_dp - 1), ("sac g c", "sac g a")[part])
-
-    for part in range(2):
-        @pl.when(is_owner)
-        def _():
-            like_peers(lambda peer: sac_x_copy(part, own_x(part), peer).wait_send())
-
-        pl.when(is_owner)(sac_x_copy(part, own_x(part), sibling).wait_send)
-        pl.when(passes_x)(sac_x_copy(part, passed_x(part), sibling).wait_send)
+        like_peers(lambda peer: sac_x_copy(own_x, peer).wait_send())
+        sac_x_copy(own_x, sibling).wait_send()
+
+    pl.when(passes_x)(sac_x_copy(passed_x, sibling).wait_send)
 
 
 def adamw(weights, first, second, gradient):
@@ -1153,7 +1148,7 @@
         vm(2, 16, HSAC),
         vm(16, HSAC),
         vm(16, 48),
-        vm(8, TILE),
+        vm(8, max(CRITIC_TILE, ACTOR_TILE)),
         vm(n_dp, lay.chunks[0], 8, 128),
         vm(n_dp, lay.chunks[1], 8, 128),
         vm(n_dp, lay.chunks[0], 8, 128),

time: 68.3 us -> 66.1 us (0.968)
  Pallas kernels: 66.3 us -> 64.2 us
    pallas_call x1, Pallas kernels: 64.2 us -> 62.1 us  [shards(): pl.pallas_call(functools.partial(main_kernel, lay), out_shape=out_shape,...]
where the time goes in v8:
time: 66.1 us; the launch traced here: 66 us
  Pallas kernels  64.2 us (97%)
  between operations  1.21 us (2%)
    pallas_call x1, Pallas kernels, shards(): pl.pallas_call(functools.partial(main_kernel, lay), out_shape=out_shape,...  62.1 us
    pallas_call x1, Pallas kernels, shards(): pl.pallas_call(update_kernel, out_shape=tuple(new_shape), in_specs=[spec]...  2.11 us

profile of v8, /device:TPU:0, one launch (start us, length us, event | category | flops | bytes accessed | tf_op | source)
XLA Modules:
  0.0 66.0 jit_solution(12936978529568533860)
XLA Ops:
  0.7 0.0 copy-start
  0.7 0.0 copy-start.1
  0.7 0.0 copy-start.2
  0.7 0.0 copy-start.3
  0.7 0.0 copy-start.4
  0.7 0.0 copy-start.5
  0.7 0.0 copy-start.6
  0.7 0.0 copy-start.7
  0.8 0.0 copy-start.8
  0.8 0.0 copy-start.9
  0.8 0.0 copy-start.10
  0.8 0.0 copy-start.11
  0.8 0.0 copy-start.12
  0.8 0.0 copy-start.13
  0.8 0.0 copy-start.14
  0.8 0.0 copy-start.15
  0.8 0.0 copy-start.16
  0.8 0.0 copy-start.17
  0.9 0.0 copy-start.18
  0.9 0.0 copy-start.19
  0.9 0.0 copy-start.20
  0.9 0.0 copy-start.23
  0.9 62.1 %step.1 = (f32[2,3,8,8,128]{4,3,2,1,0:T(8,128)S(1)}, f32[3,64,256]{2,1,0:T(8,128)S(1)}, f32[7,50,200]{2,1,0:T(8,128)S(1)}, f32[7,128,256]{2,1,0:T(8,128)S(1)}, f...) custom-call(f32[42,3648]{1,0:T(8,128)} %refs_0_.1, f32[42,1216]{1,0:T(8,128)} %refs_1_.1, s32[8,8]{1,0:T(8,128)} %refs_2_.1, ...), custom_call_target="tpu_custom_call" | custom-call | tf_op jit(solution)/shard_map/step/pallas_call | solution.py:1181
  63.0 0.0 copy-start.22
  63.0 0.0 copy-start.21
  63.0 0.0 copy-done
  63.0 0.0 copy-done.1
  63.0 0.0 copy-done.2
  63.0 0.0 copy-done.3
  63.0 0.0 copy-done.4
  63.1 0.0 copy-done.5
  63.1 0.0 copy-done.6
  63.1 0.0 copy-done.7
  63.1 0.0 copy-done.8
  63.1 0.0 copy-done.9
  63.1 0.0 copy-done.10
  63.1 0.0 copy-done.11
  63.1 0.0 copy-done.12
  63.1 0.0 copy-done.13
  63.1 0.0 copy-done.14
  63.2 0.0 copy-done.15
  63.2 0.0 copy-done.16
  63.2 0.0 copy-done.17
  63.2 0.0 copy-done.18
  63.2 0.0 copy-done.19
  63.2 0.0 copy-done.20
  63.2 0.0 copy-done.23
  63.2 0.4 copy-done.22
  63.7 0.0 copy-done.21
  63.7 2.1 %update.1 = (f32[3,64,256]{2,1,0:T(8,128)}, f32[3,64,256]{2,1,0:T(8,128)}, f32[7,50,200]{2,1,0:T(8,128)}, f32[7,50,200]{2,1,0:T(8,128)}, f32[23,2,256]{2,1,0:T(2...) custom-call(f32[2,3,8,8,128]{4,3,2,1,0:T(8,128)S(1)} %get-tuple-elem, ...), custom_call_target="tpu_custom_call" | custom-call | tf_op jit(solution)/shard_map/update/pallas_call | solution.py:1201
Async XLA Ops:
  0.7 62.3 %copy-start = (f32[7,50,200]{2,1,0:T(8,128)S(1)}, f32[7,50,200]{2,1,0:T(8,128)}, u32[]{:S(2)}) copy-start(f32[7,50,200]{2,1,0:T(8,128)} %refs_7_.3) | copy-start | bytes 840004
  0.7 62.3 %copy-start.1 = (f32[7,50,200]{2,1,0:T(8,128)S(1)}, f32[7,50,200]{2,1,0:T(8,128)}, u32[]{:S(2)}) copy-start(f32[7,50,200]{2,1,0:T(8,128)} %refs_8_.3) | copy-start | bytes 840004
  0.7 62.3 %copy-start.2 = (f32[7,200,36]{1,2,0:T(8,128)S(1)}, f32[7,200,36]{1,2,0:T(8,128)}, u32[]{:S(2)}) copy-start(f32[7,200,36]{1,2,0:T(8,128)} %param.60) | copy-start | bytes 604804
  0.7 62.3 %copy-start.3 = (f32[3,64,256]{2,1,0:T(8,128)S(1)}, f32[3,64,256]{2,1,0:T(8,128)}, u32[]{:S(2)}) copy-start(f32[3,64,256]{2,1,0:T(8,128)} %refs_6_.3) | copy-start | bytes 589828
  0.7 62.3 %copy-start.4 = (f32[7,23,200]{2,1,0:T(8,128)S(1)}, f32[7,23,200]{2,1,0:T(8,128)}, u32[]{:S(2)}) copy-start(f32[7,23,200]{2,1,0:T(8,128)} %refs_15_.1) | copy-start | bytes 386404
  0.7 62.3 %copy-start.5 = (f32[7,200,36]{1,2,0:T(8,128)S(1)}, f32[7,200,36]{1,2,0:T(8,128)}, u32[]{:S(2)}) copy-start(f32[7,200,36]{1,2,0:T(8,128)} %param.61) | copy-start | bytes 604804
  0.7 62.3 %copy-start.6 = (f32[7,200,36]{1,2,0:T(8,128)S(1)}, f32[7,200,36]{1,2,0:T(8,128)}, u32[]{:S(2)}) copy-start(f32[7,200,36]{1,2,0:T(8,128)} %param.62) | copy-start | bytes 604804
  0.7 62.3 %copy-start.7 = (f32[2,23,256]{2,0,1:T(2,128)S(1)}, f32[2,23,256]{2,0,1:T(2,128)}, u32[]{:S(2)}) copy-start(f32[2,23,256]{2,0,1:T(2,128)} %param.45) | copy-start | bytes 141316
  0.8 62.3 %copy-start.8 = (f32[7,23,200]{2,1,0:T(8,128)S(1)}, f32[7,23,200]{2,1,0:T(8,128)}, u32[]{:S(2)}) copy-start(f32[7,23,200]{2,1,0:T(8,128)} %refs_16_.3) | copy-start | bytes 386404
  0.8 62.3 %copy-start.9 = (f32[7,23,200]{2,1,0:T(8,128)S(1)}, f32[7,23,200]{2,1,0:T(8,128)}, u32[]{:S(2)}) copy-start(f32[7,23,200]{2,1,0:T(8,128)} %refs_17_.1) | copy-start | bytes 386404
  0.8 62.3 %copy-start.10 = (f32[17,256]{1,0:T(8,128)S(1)}, f32[17,256]{1,0:T(8,128)}, u32[]{:S(2)}) copy-start(f32[17,256]{1,0:T(8,128)} %refs_12_.3) | copy-start | bytes 52228
  0.8 62.3 %copy-start.11 = (f32[4639]{0:T(1024)S(1)}, f32[4639]{0:T(1024)}, u32[]{:S(2)}) copy-start(f32[4639]{0:T(1024)} %refs_27_.1) | copy-start | bytes 55672
  0.8 62.3 %copy-start.12 = (f32[256,12]{0,1:T(8,128)S(1)}, f32[256,12]{0,1:T(8,128)}, u32[]{:S(2)}) copy-start(f32[256,12]{0,1:T(8,128)} %param.57) | copy-start | bytes 36868
  0.8 62.3 %copy-start.13 = (f32[2,23,256]{2,0,1:T(2,128)S(1)}, f32[2,23,256]{2,0,1:T(2,128)}, u32[]{:S(2)}) copy-start(f32[2,23,256]{2,0,1:T(2,128)} %param.46) | copy-start | bytes 141316
  0.8 62.3 %copy-start.14 = (f32[2,23,256]{2,0,1:T(2,128)S(1)}, f32[2,23,256]{2,0,1:T(2,128)}, u32[]{:S(2)}) copy-start(f32[2,23,256]{2,0,1:T(2,128)} %param.47) | copy-start | bytes 141316
  0.8 62.3 %copy-start.15 = (f32[17,256]{1,0:T(8,128)S(1)}, f32[17,256]{1,0:T(8,128)}, u32[]{:S(2)}) copy-start(f32[17,256]{1,0:T(8,128)} %refs_13_.3) | copy-start | bytes 52228
  0.8 62.3 %copy-start.16 = (f32[17,256]{1,0:T(8,128)S(1)}, f32[17,256]{1,0:T(8,128)}, u32[]{:S(2)}) copy-start(f32[17,256]{1,0:T(8,128)} %refs_14_.1) | copy-start | bytes 52228
  0.8 62.3 %copy-start.17 = (f32[4639]{0:T(1024)S(1)}, f32[4639]{0:T(1024)}, u32[]{:S(2)}) copy-start(f32[4639]{0:T(1024)} %refs_28_.1) | copy-start | bytes 55672
  0.9 62.3 %copy-start.18 = (f32[4639]{0:T(1024)S(1)}, f32[4639]{0:T(1024)}, u32[]{:S(2)}) copy-start(f32[4639]{0:T(1024)} %refs_29_.1) | copy-start | bytes 55672
  0.9 62.3 %copy-start.19 = (f32[256,12]{0,1:T(8,128)S(1)}, f32[256,12]{0,1:T(8,128)}, u32[]{:S(2)}) copy-start(f32[256,12]{0,1:T(8,128)} %param.58) | copy-start | bytes 36868
  0.9 62.3 %copy-start.20 = (f32[256,12]{0,1:T(8,128)S(1)}, f32[256,12]{0,1:T(8,128)}, u32[]{:S(2)}) copy-start(f32[256,12]{0,1:T(8,128)} %param.59) | copy-start | bytes 36868
  0.9 62.3 %copy-start.23 = (f32[2,256]{1,0:T(2,128)S(1)}, f32[2,256]{1,0:T(2,128)}, u32[]{:S(2)}) copy-start(f32[2,256]{1,0:T(2,128)} %refs_20_.3) | copy-start | bytes 6148
  63.0 0.7 %copy-start.22 = (f32[2,256]{1,0:T(2,128)S(1)}, f32[2,256]{1,0:T(2,128)}, u32[]{:S(2)}) copy-start(f32[2,256]{1,0:T(2,128)} %refs_19_.3) | copy-start | bytes 6148
  63.0 0.7 %copy-start.21 = (f32[2,256]{1,0:T(2,128)S(1)}, f32[2,256]{1,0:T(2,128)}, u32[]{:S(2)}) copy-start(f32[2,256]{1,0:T(2,128)} %refs_18_.3) | copy-start | bytes 6148

commit v9 on v8

--- a/solution.py
+++ b/solution.py
@@ -161,21 +161,22 @@
         self.drows = HDYN // self.n_blk
         self.mat = 64 // self.n_dp
         self.sml = 32 // self.n_dp
-        self.chunks = (2 * self.mat, self.mat + self.sml)
+        self.chunks = (self.mat, self.mat, self.mat + self.sml)
         self.owner = self.n_dp - 1
 
-        groups = [("plane sum", g) for g in range(2)] + [("line sum", g) for g in range(3)]
+        groups = [("plane sum", g) for g in range(3)] + [("line sum", g) for g in range(4)]
         common = ["hidden", "hidden on", "lists", "own", "line", "plane", "dyn h", "dyn m", "small"]
-        common += groups + ["sac g"]
+        common += groups + [("sac g", k) for k in range(2)]
         kinds = [(name, kind) for name in ("pack", "x") for kind in ("own", "on")]
         sent = common + [("tiles", k) for k in range(3)] + kinds
         self.sent = {name: at for at, name in enumerate(sent)}
         self.departures = len(sent)
-        self.sent["sac x"] = self.departures
-        self.departures += self.n_dp
+        for k in range(2):
+            self.sent["sac x", k] = self.departures
+            self.departures += self.n_dp
         self.here, self.arrivals = {}, 0
         tiles = [("tiles", k) for k in range(3)]
-        tiles += ["sac x", ("pack", "sibling"), ("x", "sibling")]
+        tiles += [("sac x", 0), ("sac x", 1), ("pack", "sibling"), ("x", "sibling")]
         for name in common + tiles:
             self.here[name] = self.arrivals
             self.arrivals += 1
@@ -191,13 +192,14 @@
         dyn_in, crit_out, act_out, dyn_out, biases, targ_in, targ_hidden, targ_out, targ_bias,
         sac_g, sac_x, dyn_x, dyn_s, small, count,
         wg, lists, asked, dhg, dmg, bk, xs, nz, w1f, w1t, w1n, w2t, w2h, heads, head_t, head_f,
-        rowbuf, wide, headcol, acc_h, acc_w, acc_c, acc_a, acc_m, acc_l, grid_c, grid_a, from_c, from_a,
-        zr_c, zr_a, zf_c, zf_a, sum_c, sum_a, mg, mat, dcols, dacc_h, dacc_w, dacc_o, dacc_m, dacc_b, dacc_l, xt, dmat,
+        rowbuf, wide, headcol, acc_h, acc_w, acc_c, acc_a, acc_m, acc_l, grid_0, grid_1, grid_a, from_0, from_1,
+        from_a, zr_0, zr_1, zr_a, zf_0, zf_1, zf_a, sum_0, sum_1, sum_a, ys, mg, mat, dcols, dacc_h, dacc_w, dacc_o, dacc_m, dacc_b, dacc_l, xt, dmat,
         dpack, drow_x, bias, dhead, dhead_t, *rest,
     ) = refs
     send, recv = rest
     sent, here_at = lay.sent, lay.here
-    grids, froms, zrs, zfs = (grid_c, grid_a), (from_c, from_a), (zr_c, zr_a), (zf_c, zf_a)
+    grids, froms = (grid_0, grid_1, grid_a), (from_0, from_1, from_a)
+    zrs, zfs, totals = (zr_0, zr_1, zr_a), (zf_0, zf_1, zf_a), (sum_0, sum_1, sum_a)
     n_dp, n_blk = lay.n_dp, lay.n_blk
     me = lax.axis_index("dp")
     z = lax.axis_index("blk")
@@ -359,10 +361,14 @@
     slots = in_lanes(0)
     wanted = jnp.maximum(slots, 0.0).astype(jnp.int32)
     hot = (rows_of((lay.replay, lay.real)) == wanted).astype(BF16)
-    high, middle, low = pieces(data)
-    picked = dot(high, hot) + dot(middle, hot) + dot(low, hot)
+    padded = jnp.concatenate([data[0:40], jnp.zeros((8, lay.replay), F32)], 0)
+    tail = jnp.concatenate([data[40:FEAT], jnp.zeros((14, lay.replay), F32)], 0)
+    parts = [jnp.concatenate(pair, 0) for pair in zip(pieces(padded), pieces(tail))]
+    chosen = dot(jnp.concatenate(parts, 0), hot)
+    chosen = chosen[0:64] + chosen[64:128] + chosen[128:192]
     mine = me * n_blk
-    bk[mine, 0:FEAT, 0 : lay.real] = picked
+    bk[mine, 0:40, 0 : lay.real] = chosen[0:40]
+    bk[mine, 40:FEAT, 0 : lay.real] = chosen[48:50]
     bk[mine, 42:43, 0 : lay.real] = (slots >= 0.0).astype(F32)
     bk[mine, 43:44, 0 : lay.real] = in_lanes(1)
     bk[mine, 44:48, 0 : lay.real] = jnp.zeros((4, lay.real), F32)
@@ -468,6 +474,20 @@
     has_come(bk.at[pl.ds(0, n_blk - 1)], "line")
     plane_peers(lambda peer: block_plane(peer).start())
 
+    def critic_pass(k, now_in, where, target):
+        weight = xs[42:43, where]
+        value, (c1, dc1, c2, dc2) = critic(now_in, 2 + k)
+        miss = value - target
+        g3 = rounded(weight * miss)
+        g3_rows = jnp.where(rows_of((16, CRITIC_TILE)) == 0, g3, 0.0).astype(BF16)
+        acc_c[k] += dot(g3_rows, c2, NT)
+        acc_m[:, 16 + 16 * k : 32 + 16 * k] += dot(ones16(CRITIC_TILE), g3_rows, NT)
+        g2 = outer_sloped(wide[5 + k], g3, dc2)
+        add_hidden(k, c1, g2)
+        g1 = sloped(dot(w2h[k], g2), dc1)
+        acc_w[k] += dot(now_in, g1, NT)
+        acc_l[0:1, 0:CRITIC_TILE] += weight * (0.5 * miss * miss)
+
     @pl.loop(0, critic_tiles)
     def _(step):
         @pl.when(step == critic_tiles - 1)
@@ -489,34 +509,18 @@
         next_f = framed(24, OBS, where)
         reward = xs[23:24, where]
         done = xs[41:42, where]
-        weight = xs[42:43, where]
-        row16 = rows_of((16, CRITIC_TILE))
         next_action, next_prob, _, _, _ = policy(next_f.astype(BF16), 1, where)
         aim_in = with_action(next_f, next_action)
         aim = jnp.minimum(critic(aim_in, 0)[0], critic(aim_in, 1)[0])
         target = reward + DISCOUNT * (1.0 - done) * (aim - alpha * next_prob)
-        loss = jnp.zeros((1, CRITIC_TILE), F32)
-        heads_grad = []
-        for k in range(2):
-            value, (c1, dc1, c2, dc2) = critic(now_in, 2 + k)
-            miss = value - target
-            loss += 0.5 * miss * miss
-            g3 = rounded(weight * miss)
-            g3_rows = jnp.where(row16 == 0, g3, 0.0).astype(BF16)
-            heads_grad.append(g3_rows)
-            acc_c[k] += dot(g3_rows, c2, NT)
-            g2 = outer_sloped(wide[5 + k], g3, dc2)
-            add_hidden(k, c1, g2)
-            g1 = sloped(dot(w2h[k], g2), dc1)
-            acc_w[k] += dot(now_in, g1, NT)
-        acc_m[:, 16:48] += dot(ones16(CRITIC_TILE), jnp.concatenate(heads_grad, 0), NT)
-        acc_l[0:1, 0:CRITIC_TILE] += weight * loss
-
-    def put_matrix(group, k, at):
+        ys[0:1, where] = target
+        critic_pass(0, now_in, where, target)
+
+    def put_matrix(k):
         for chunk in range(n_dp):
             tile = chunk * lay.mat
             side, row = tile // 32, tile % 32
-            grids[group][chunk, at * lay.mat : (at + 1) * lay.mat] = acc_h[
+            grids[k][chunk, 0 : lay.mat] = acc_h[
                 k, row * 8 : (row + lay.mat) * 8, side * 128 : (side + 1) * 128
             ].reshape(lay.mat, 8, 128)
 
@@ -535,9 +539,7 @@
         )
 
     def line_part(part):
-        group = min(part, 1)
-        tiles = (pl.ds(0, 2 * lay.mat), pl.ds(0, lay.mat), pl.ds(lay.mat, lay.sml))[part]
-        return group, tiles
+        return min(part, 2), pl.ds(lay.mat, lay.sml) if part == 3 else pl.ds(0, lay.mat)
 
     def line_sum(part, peer):
         group, tiles = line_part(part)
@@ -568,16 +570,14 @@
         def _():
             held_rows = pl.ds(pl.multiple_of(local_tile * 8, 8), lay.mat * 8)
             held_lanes = pl.ds(pl.multiple_of(side * 128, 128), 128)
-            for at, k in enumerate(((0, 1), (2,))[group]):
-                old = sac_m[k, held_rows, held_lanes].reshape(lay.mat, 8, 128)
-                zfs[group][at * lay.mat : (at + 1) * lay.mat] += (MOMENTUM * total).reshape(1, 1, 1) * old
-
-        for part in (0,) if group == 0 else (1, 2):
+            old = sac_m[group, held_rows, held_lanes].reshape(lay.mat, 8, 128)
+            zfs[group][0 : lay.mat] += (MOMENTUM * total).reshape(1, 1, 1) * old
+
+        for part in (2, 3) if group == 2 else (group,):
             line_peers(lambda peer: line_sum(part, peer).start())
 
     def tile_copy(k, peer):
-        src = (sum_c, sum_a)[k // 2].at[pl.ds((k % 2) * lay.mat, lay.mat)]
-        return on_plane(src, mg.at[k, me], send.at[sent["tiles", k]], recv.at[here_at["tiles", k]], peer)
+        return on_plane(totals[k].at[pl.ds(0, lay.mat)], mg.at[k, me], send.at[sent["tiles", k]], recv.at[here_at["tiles", k]], peer)
 
     def small_copy(peer):
         return on_plane(
@@ -585,9 +585,9 @@
             send.at[sent["small"]], recv.at[here_at["small"]], peer,
         )
 
-    def keep_copy(peer):
-        view = sac_g.at[side, pl.ds(0, 2), pl.ds(local_tile, lay.mat)]
-        return on_plane(view, view, send.at[sent["sac g"]], recv.at[here_at["sac g"]], peer)
+    def keep_copy(k, peer):
+        view = sac_g.at[side, k, pl.ds(local_tile, lay.mat)]
+        return on_plane(view, view, send.at[sent["sac g", k]], recv.at[here_at["sac g", k]], peer)
 
     def kept_bytes(number):
         return froms[0].at[pl.ds(0, number)]
@@ -599,32 +599,30 @@
         whole = zrs[group][0, tiles]
         for block in range(1, n_blk):
             whole = whole + zrs[group][block, tiles]
-        (sum_c, sum_a)[group][tiles] = whole
-        if part == 0:
-            for k in range(2):
-                pl.when(jnp.logical_not(is_owner))(tile_copy(k, lay.owner).start)
-
-                @pl.when(is_owner)
-                def _():
-                    mg[k, me] = whole[k * lay.mat : (k + 1) * lay.mat]
+        totals[group][tiles] = whole
+        if part < 2:
+            pl.when(jnp.logical_not(is_owner))(tile_copy(part, lay.owner).start)
+
+            @pl.when(is_owner)
+            def _():
+                mg[part, me] = whole
 
             @pl.when(is_keeper)
             def _():
-                for k in range(2):
-                    sac_g[side, k, pl.ds(local_tile, lay.mat)] = whole[k * lay.mat : (k + 1) * lay.mat]
-                plane_peers(lambda peer: keep_copy(peer).start())
-
-        if part == 1:
+                sac_g[side, part, pl.ds(local_tile, lay.mat)] = whole
+                plane_peers(lambda peer: keep_copy(part, peer).start())
+
+        if part == 2:
             plane_peers(lambda peer: tile_copy(2, peer).start())
             mg[2, me] = whole
 
-        if part == 2:
+        if part == 3:
             plane_peers(lambda peer: small_copy(peer).start())
             small[pl.ds(me * lay.sml, lay.sml)] = sum_a[lay.mat :]
 
     def chain(group):
         def end():
-            for part in (0,) if group == 0 else (1, 2):
+            for part in (2, 3) if group == 2 else (group,):
                 fold_end(part)
 
         return [
@@ -633,17 +631,14 @@
             end,
         ]
 
-    critic_chain, actor_chain = chain(0), chain(1)
+    chains = [chain(group) for group in range(3)]
     per = DYN_TILE // lay.real
     dyn_tiles = lay.n_dev // per
-    in_actor, in_dyn = {}, {}
-    if actor_tiles > 1:
-        in_actor[1] = [critic_chain[1]]
-        in_dyn[0] = [critic_chain[2]]
-    else:
-        in_dyn[0] = [critic_chain[1]]
-        in_dyn[min(1, dyn_tiles - 1)] = [critic_chain[2]]
-    in_dyn.setdefault(dyn_tiles - 1, []).append(actor_chain[1])
+    in_actor = {actor_tiles - 1: [chains[0][1]]} if actor_tiles > 1 else {}
+    after_actor = [chains[1][1]] if actor_tiles > 1 else [chains[0][1], chains[1][1]]
+    in_dyn = {}
+    in_dyn.setdefault(min(1, dyn_tiles - 1), []).append(chains[0][2])
+    in_dyn.setdefault(dyn_tiles - 1, []).append(chains[1][2])
 
     def take(slots, step):
         for at, events in slots.items():
@@ -652,9 +647,16 @@
                 for event in events:
                     event()
 
-    for k in range(2):
-        put_matrix(0, k, k)
-    critic_chain[0]()
+    put_matrix(0)
+    chains[0][0]()
+
+    @pl.loop(0, critic_tiles)
+    def _(step):
+        where = place_of(step, CRITIC_TILE)
+        critic_pass(1, framed(0, IN, where).astype(BF16), where, ys[0:1, where])
+
+    put_matrix(1)
+    chains[1][0]()
 
     has_come(bk.at[pl.ds(0, (n_dp - 1) * (n_blk - 1))], "plane")
     lane0 = lay.real // 128 * 128
@@ -707,7 +709,7 @@
         acc_l[1:2, 0:ACTOR_TILE] += weight * loss
         acc_l[2:3, 0:ACTOR_TILE] += weight * (log_prob + TARGET_ENTROPY)
 
-    put_matrix(1, 2, 0)
+    put_matrix(2)
     for k in range(3):
         put(R_IN + 24 * k, acc_w[k, 0:24, :])
     put(R_HEAD, acc_a[...])
@@ -723,7 +725,9 @@
     rowbuf[0:1, 65:66] = folded[2:3]
     put(R_MISC, rowbuf[...])
     put(R_MISC + 8, jnp.zeros((R_SMALL - R_MISC - 8, HSAC), F32))
-    actor_chain[0]()
+    chains[2][0]()
+    for event in after_actor:
+        event()
 
     def dyn_bias(start, width):
         row = jnp.zeros((1, width), F32)
@@ -861,9 +865,9 @@
             rows = jnp.where(z == block, ref[block * lay.drows : (block + 1) * lay.drows, 0:HDYN], rows)
         return rows
 
-    def sac_x_copy(src, peer):
-        dst = sac_x.at[pl.ds(0, 2)]
-        return on_plane(src, dst, send.at[sent["sac x"] + peer], recv.at[here_at["sac x"]], peer)
+    def sac_x_copy(k, src, peer):
+        name = ("sac x", k)
+        return on_plane(src, sac_x.at[k], send.at[sent[name] + peer], recv.at[here_at[name]], peer)
 
     mine_rows = pl.ds(pl.multiple_of(z * lay.rows, lay.rows), lay.rows)
 
@@ -876,6 +880,8 @@
             piece = mg[k, chunk].reshape(lay.mat * 8, 128)
             mat[k, at, half * 128 : (half + 1) * 128] = piece / total
         normalise(mat.at[k])
+
+    chains[2][1]()
 
     @pl.when(is_dyn)
     def _():
@@ -903,11 +909,13 @@
             dmat[at, 0:HDYN] = MOMENTUM * dmg[block] + dacc_h[at, 0:HDYN] / total
         normalise(dmat)
 
-    own_x, passed_x = mat.at[pl.ds(0, 2), mine_rows], sac_x.at[pl.ds(0, 2)]
+    def own_x(k):
+        return mat.at[k, mine_rows]
+
     passes_x = jnp.logical_and(core == lay.owner % 2, jnp.logical_not(is_owner))
 
     def sum_end(step):
-        pl.when(step == NS_ITERS - 2)(actor_chain[2])
+        pl.when(step == NS_ITERS - 1)(chains[2][2])
 
     @pl.when(is_dyn)
     def _():
@@ -921,14 +929,13 @@
     def _():
         for k in range(2):
             take_matrix(k)
-        schulz([mat.at[0], mat.at[1]], NS_ITERS, sum_end)
-        for k in range(2):
+            schulz([mat.at[k]], NS_ITERS, sum_end if k == 1 else None)
             sac_x[k] = mat[k, mine_rows, :]
-        like_peers(lambda peer: sac_x_copy(own_x, peer).start())
-        sac_x_copy(own_x, sibling).start()
+            like_peers(lambda peer: sac_x_copy(k, own_x(k), peer).start())
+            sac_x_copy(k, own_x(k), sibling).start()
 
     if n_dp > MEMBERS + 1:
-        pl.when(jnp.logical_not(jnp.logical_or(is_dyn, is_owner)))(actor_chain[2])
+        pl.when(jnp.logical_not(jnp.logical_or(is_dyn, is_owner)))(chains[2][2])
 
     def sent_early():
         has_sent(wg.at[pl.ds(0, n_blk - 1), :, half_rows], "hidden")
@@ -943,9 +950,9 @@
             has_sent(dhg.at[pl.ds(0, n_blk - 1)], "dyn h")
             has_sent(dmg.at[pl.ds(0, n_blk - 1)], "dyn m")
 
-        for group in range(2):
+        for group in range(3):
             has_sent(froms[group].at[pl.ds(0, n_dp - 1)], ("plane sum", group))
-        for part in range(3):
+        for part in range(4):
             has_sent(line_bytes(part), ("line sum", part))
 
     def pass_on(step):
@@ -953,8 +960,9 @@
         def _():
             hand_on("pack")
             hand_on("x")
-            pl.when(jnp.logical_not(is_owner))(sac_x_copy(passed_x, sibling).wait_recv)
-            pl.when(passes_x)(sac_x_copy(passed_x, sibling).start)
+            for k in range(2):
+                pl.when(jnp.logical_not(is_owner))(sac_x_copy(k, sac_x.at[k], sibling).wait_recv)
+                pl.when(passes_x)(sac_x_copy(k, sac_x.at[k], sibling).start)
 
     take_matrix(2)
     for half in range(2):
@@ -967,7 +975,8 @@
     sent_early()
     has_come(small.at[pl.ds(0, (n_dp - 1) * lay.sml)], "small")
     for number, test in ((lay.keepers - 1, is_keeper), (lay.keepers, jnp.logical_not(is_keeper))):
-        pl.when(test)(functools.partial(has_come, kept_bytes(number), "sac g"))
+        for k in range(2):
+            pl.when(test)(functools.partial(has_come, kept_bytes(number), ("sac g", k)))
     from_sibling("pack")
     from_sibling("x")
 
@@ -982,14 +991,16 @@
         for k in range(2):
             tile_copy(k, sibling).wait_send()
 
-    pl.when(is_keeper)(functools.partial(has_sent, kept_bytes(n_dp - 1), "sac g"))
-
-    @pl.when(is_owner)
-    def _():
-        like_peers(lambda peer: sac_x_copy(own_x, peer).wait_send())
-        sac_x_copy(own_x, sibling).wait_send()
-
-    pl.when(passes_x)(sac_x_copy(passed_x, sibling).wait_send)
+    for k in range(2):
+        pl.when(is_keeper)(functools.partial(has_sent, kept_bytes(n_dp - 1), ("sac g", k)))
+
+    for k in range(2):
+        @pl.when(is_owner)
+        def _():
+            like_peers(lambda peer: sac_x_copy(k, own_x(k), peer).wait_send())
+            sac_x_copy(k, own_x(k), sibling).wait_send()
+
+        pl.when(passes_x)(sac_x_copy(k, sac_x.at[k], sibling).wait_send)
 
 
 def adamw(weights, first, second, gradient):
@@ -1149,16 +1160,12 @@
         vm(16, HSAC),
         vm(16, 48),
         vm(8, max(CRITIC_TILE, ACTOR_TILE)),
-        vm(n_dp, lay.chunks[0], 8, 128),
-        vm(n_dp, lay.chunks[1], 8, 128),
-        vm(n_dp, lay.chunks[0], 8, 128),
-        vm(n_dp, lay.chunks[1], 8, 128),
-        vm(n_blk, lay.chunks[0], 8, 128),
-        vm(n_blk, lay.chunks[1], 8, 128),
-        vm(lay.chunks[0], 8, 128),
-        vm(lay.chunks[1], 8, 128),
-        vm(lay.chunks[0], 8, 128),
-        vm(lay.chunks[1], 8, 128),
+        *[vm(n_dp, chunk, 8, 128) for chunk in lay.chunks],
+        *[vm(n_dp, chunk, 8, 128) for chunk in lay.chunks],
+        *[vm(n_blk, chunk, 8, 128) for chunk in lay.chunks],
+        *[vm(chunk, 8, 128) for chunk in lay.chunks],
+        *[vm(chunk, 8, 128) for chunk in lay.chunks],
+        vm(8, lay.batch),
         vm(3, n_dp, lay.mat, 8, 128),
         vm(3, HSAC, HSAC),
         vm(HSAC, 8),

time: 66.1 us -> 65.3 us (0.988)
  the two profiles are of different devices: /device:TPU:0 before, /device:TPU:10 now
where the time goes in v9:
time: 65.3 us; the launch traced here: 65.1 us
  Pallas kernels  63.3 us (97%)
  between operations  1.21 us (2%)
    pallas_call x1, Pallas kernels, shards(): pl.pallas_call(functools.partial(main_kernel, lay), out_shape=out_shape,...  61.2 us
    pallas_call x1, Pallas kernels, shards(): pl.pallas_call(update_kernel, out_shape=tuple(new_shape), in_specs=[spec]...  2.11 us

profile of v9, /device:TPU:10, one launch (start us, length us, event | category | flops | bytes accessed | tf_op | source)
XLA Modules:
  0.0 65.1 jit_solution(5865918097306707945)
XLA Ops:
  0.7 0.0 copy-start
  0.7 0.0 copy-start.1
  0.7 0.0 copy-start.2
  0.7 0.0 copy-start.3
  0.7 0.0 copy-start.4
  0.7 0.0 copy-start.5
  0.7 0.0 copy-start.6
  0.7 0.0 copy-start.7
  0.8 0.0 copy-start.8
  0.8 0.0 copy-start.9
  0.8 0.0 copy-start.10
  0.8 0.0 copy-start.11
  0.8 0.0 copy-start.12
  0.8 0.0 copy-start.13
  0.8 0.0 copy-start.14
  0.8 0.0 copy-start.15
  0.8 0.0 copy-start.16
  0.8 0.0 copy-start.17
  0.9 0.0 copy-start.18
  0.9 0.0 copy-start.19
  0.9 0.0 copy-start.20
  0.9 0.0 copy-start.23
  0.9 61.2 %step.1 = (f32[2,3,8,8,128]{4,3,2,1,0:T(8,128)S(1)}, f32[3,64,256]{2,1,0:T(8,128)S(1)}, f32[7,50,200]{2,1,0:T(8,128)S(1)}, f32[7,128,256]{2,1,0:T(8,128)S(1)}, f...) custom-call(f32[42,3648]{1,0:T(8,128)} %refs_0_.1, f32[42,1216]{1,0:T(8,128)} %refs_1_.1, s32[8,8]{1,0:T(8,128)} %refs_2_.1, ...), custom_call_target="tpu_custom_call" | custom-call | tf_op jit(solution)/shard_map/step/pallas_call | solution.py:1188
  62.1 0.0 copy-start.22
  62.1 0.0 copy-start.21
  62.1 0.0 copy-done
  62.2 0.0 copy-done.1
  62.2 0.0 copy-done.2
  62.2 0.0 copy-done.3
  62.2 0.0 copy-done.4
  62.2 0.0 copy-done.5
  62.2 0.0 copy-done.6
  62.2 0.0 copy-done.7
  62.2 0.0 copy-done.8
  62.2 0.0 copy-done.9
  62.2 0.0 copy-done.10
  62.3 0.0 copy-done.11
  62.3 0.0 copy-done.12
  62.3 0.0 copy-done.13
  62.3 0.0 copy-done.14
  62.3 0.0 copy-done.15
  62.3 0.0 copy-done.16
  62.3 0.0 copy-done.17
  62.3 0.0 copy-done.18
  62.3 0.0 copy-done.19
  62.3 0.0 copy-done.20
  62.4 0.0 copy-done.23
  62.4 0.4 copy-done.22
  62.8 0.0 copy-done.21
  62.8 2.1 %update.1 = (f32[3,64,256]{2,1,0:T(8,128)}, f32[3,64,256]{2,1,0:T(8,128)}, f32[7,50,200]{2,1,0:T(8,128)}, f32[7,50,200]{2,1,0:T(8,128)}, f32[23,2,256]{2,1,0:T(2...) custom-call(f32[2,3,8,8,128]{4,3,2,1,0:T(8,128)S(1)} %get-tuple-elem, ...), custom_call_target="tpu_custom_call" | custom-call | tf_op jit(solution)/shard_map/update/pallas_call | solution.py:1208
Async XLA Ops:
  0.7 61.5 %copy-start = (f32[7,50,200]{2,1,0:T(8,128)S(1)}, f32[7,50,200]{2,1,0:T(8,128)}, u32[]{:S(2)}) copy-start(f32[7,50,200]{2,1,0:T(8,128)} %refs_7_.3) | copy-start | bytes 840004
  0.7 61.5 %copy-start.1 = (f32[7,50,200]{2,1,0:T(8,128)S(1)}, f32[7,50,200]{2,1,0:T(8,128)}, u32[]{:S(2)}) copy-start(f32[7,50,200]{2,1,0:T(8,128)} %refs_8_.3) | copy-start | bytes 840004
  0.7 61.5 %copy-start.2 = (f32[7,200,36]{1,2,0:T(8,128)S(1)}, f32[7,200,36]{1,2,0:T(8,128)}, u32[]{:S(2)}) copy-start(f32[7,200,36]{1,2,0:T(8,128)} %param.60) | copy-start | bytes 604804
  0.7 61.5 %copy-start.3 = (f32[3,64,256]{2,1,0:T(8,128)S(1)}, f32[3,64,256]{2,1,0:T(8,128)}, u32[]{:S(2)}) copy-start(f32[3,64,256]{2,1,0:T(8,128)} %refs_6_.3) | copy-start | bytes 589828
  0.7 61.5 %copy-start.4 = (f32[7,23,200]{2,1,0:T(8,128)S(1)}, f32[7,23,200]{2,1,0:T(8,128)}, u32[]{:S(2)}) copy-start(f32[7,23,200]{2,1,0:T(8,128)} %refs_15_.1) | copy-start | bytes 386404
  0.7 61.5 %copy-start.5 = (f32[7,200,36]{1,2,0:T(8,128)S(1)}, f32[7,200,36]{1,2,0:T(8,128)}, u32[]{:S(2)}) copy-start(f32[7,200,36]{1,2,0:T(8,128)} %param.61) | copy-start | bytes 604804
  0.7 61.5 %copy-start.6 = (f32[7,200,36]{1,2,0:T(8,128)S(1)}, f32[7,200,36]{1,2,0:T(8,128)}, u32[]{:S(2)}) copy-start(f32[7,200,36]{1,2,0:T(8,128)} %param.62) | copy-start | bytes 604804
  0.7 61.5 %copy-start.7 = (f32[2,23,256]{2,0,1:T(2,128)S(1)}, f32[2,23,256]{2,0,1:T(2,128)}, u32[]{:S(2)}) copy-start(f32[2,23,256]{2,0,1:T(2,128)} %param.45) | copy-start | bytes 141316
  0.8 61.5 %copy-start.8 = (f32[7,23,200]{2,1,0:T(8,128)S(1)}, f32[7,23,200]{2,1,0:T(8,128)}, u32[]{:S(2)}) copy-start(f32[7,23,200]{2,1,0:T(8,128)} %refs_16_.3) | copy-start | bytes 386404
  0.8 61.5 %copy-start.9 = (f32[7,23,200]{2,1,0:T(8,128)S(1)}, f32[7,23,200]{2,1,0:T(8,128)}, u32[]{:S(2)}) copy-start(f32[7,23,200]{2,1,0:T(8,128)} %refs_17_.1) | copy-start | bytes 386404
  0.8 61.5 %copy-start.10 = (f32[17,256]{1,0:T(8,128)S(1)}, f32[17,256]{1,0:T(8,128)}, u32[]{:S(2)}) copy-start(f32[17,256]{1,0:T(8,128)} %refs_12_.3) | copy-start | bytes 52228
  0.8 61.5 %copy-start.11 = (f32[4639]{0:T(1024)S(1)}, f32[4639]{0:T(1024)}, u32[]{:S(2)}) copy-start(f32[4639]{0:T(1024)} %refs_27_.1) | copy-start | bytes 55672
  0.8 61.5 %copy-start.12 = (f32[256,12]{0,1:T(8,128)S(1)}, f32[256,12]{0,1:T(8,128)}, u32[]{:S(2)}) copy-start(f32[256,12]{0,1:T(8,128)} %param.57) | copy-start | bytes 36868
  0.8 61.5 %copy-start.13 = (f32[2,23,256]{2,0,1:T(2,128)S(1)}, f32[2,23,256]{2,0,1:T(2,128)}, u32[]{:S(2)}) copy-start(f32[2,23,256]{2,0,1:T(2,128)} %param.46) | copy-start | bytes 141316
  0.8 61.5 %copy-start.14 = (f32[2,23,256]{2,0,1:T(2,128)S(1)}, f32[2,23,256]{2,0,1:T(2,128)}, u32[]{:S(2)}) copy-start(f32[2,23,256]{2,0,1:T(2,128)} %param.47) | copy-start | bytes 141316
  0.8 61.5 %copy-start.15 = (f32[17,256]{1,0:T(8,128)S(1)}, f32[17,256]{1,0:T(8,128)}, u32[]{:S(2)}) copy-start(f32[17,256]{1,0:T(8,128)} %refs_13_.3) | copy-start | bytes 52228
  0.8 61.5 %copy-start.16 = (f32[17,256]{1,0:T(8,128)S(1)}, f32[17,256]{1,0:T(8,128)}, u32[]{:S(2)}) copy-start(f32[17,256]{1,0:T(8,128)} %refs_14_.1) | copy-start | bytes 52228
  0.8 61.5 %copy-start.17 = (f32[4639]{0:T(1024)S(1)}, f32[4639]{0:T(1024)}, u32[]{:S(2)}) copy-start(f32[4639]{0:T(1024)} %refs_28_.1) | copy-start | bytes 55672
  0.9 61.5 %copy-start.18 = (f32[4639]{0:T(1024)S(1)}, f32[4639]{0:T(1024)}, u32[]{:S(2)}) copy-start(f32[4639]{0:T(1024)} %refs_29_.1) | copy-start | bytes 55672
  0.9 61.5 %copy-start.19 = (f32[256,12]{0,1:T(8,128)S(1)}, f32[256,12]{0,1:T(8,128)}, u32[]{:S(2)}) copy-start(f32[256,12]{0,1:T(8,128)} %param.58) | copy-start | bytes 36868
  0.9 61.5 %copy-start.20 = (f32[256,12]{0,1:T(8,128)S(1)}, f32[256,12]{0,1:T(8,128)}, u32[]{:S(2)}) copy-start(f32[256,12]{0,1:T(8,128)} %param.59) | copy-start | bytes 36868
  0.9 61.5 %copy-start.23 = (f32[2,256]{1,0:T(2,128)S(1)}, f32[2,256]{1,0:T(2,128)}, u32[]{:S(2)}) copy-start(f32[2,256]{1,0:T(2,128)} %refs_20_.3) | copy-start | bytes 6148
  62.1 0.7 %copy-start.22 = (f32[2,256]{1,0:T(2,128)S(1)}, f32[2,256]{1,0:T(2,128)}, u32[]{:S(2)}) copy-start(f32[2,256]{1,0:T(2,128)} %refs_19_.3) | copy-start | bytes 6148
  62.1 0.7 %copy-start.21 = (f32[2,256]{1,0:T(2,128)S(1)}, f32[2,256]{1,0:T(2,128)}, u32[]{:S(2)}) copy-start(f32[2,256]{1,0:T(2,128)} %refs_18_.3) | copy-start | bytes 6148

commit v10 on v9

--- a/solution.py
+++ b/solution.py
@@ -161,29 +161,23 @@
         self.drows = HDYN // self.n_blk
         self.mat = 64 // self.n_dp
         self.sml = 32 // self.n_dp
-        self.chunks = (self.mat, self.mat, self.mat + self.sml)
-        self.owner = self.n_dp - 1
-
+        self.chunks = (self.mat, self.mat + self.sml, self.mat)
         groups = [("plane sum", g) for g in range(3)] + [("line sum", g) for g in range(4)]
         common = ["hidden", "hidden on", "lists", "own", "line", "plane", "dyn h", "dyn m", "small"]
-        common += groups + [("sac g", k) for k in range(2)]
+        common += groups
         kinds = [(name, kind) for name in ("pack", "x") for kind in ("own", "on")]
         sent = common + [("tiles", k) for k in range(3)] + kinds
         self.sent = {name: at for at, name in enumerate(sent)}
         self.departures = len(sent)
-        for k in range(2):
-            self.sent["sac x", k] = self.departures
-            self.departures += self.n_dp
         self.here, self.arrivals = {}, 0
         tiles = [("tiles", k) for k in range(3)]
-        tiles += [("sac x", 0), ("sac x", 1), ("pack", "sibling"), ("x", "sibling")]
+        tiles += [("pack", "sibling"), ("x", "sibling")]
         for name in common + tiles:
             self.here[name] = self.arrivals
             self.arrivals += 1
         for name in ("pack", "x"):
             self.here[name, "like"] = self.arrivals
             self.arrivals += MEMBERS
-        self.keepers = 2 * (self.rows // 8) // self.mat
 
 
 def main_kernel(lay, *refs):
@@ -191,15 +185,15 @@
         replay, model, requests, member, live, noise, sac_h, sac_m, dyn_h, dyn_m, crit_in, act_in,
         dyn_in, crit_out, act_out, dyn_out, biases, targ_in, targ_hidden, targ_out, targ_bias,
         sac_g, sac_x, dyn_x, dyn_s, small, count,
-        wg, lists, asked, dhg, dmg, bk, xs, nz, w1f, w1t, w1n, w2t, w2h, heads, head_t, head_f,
-        rowbuf, wide, headcol, acc_h, acc_w, acc_c, acc_a, acc_m, acc_l, grid_0, grid_1, grid_a, from_0, from_1,
-        from_a, zr_0, zr_1, zr_a, zf_0, zf_1, zf_a, sum_0, sum_1, sum_a, ys, mg, mat, dcols, dacc_h, dacc_w, dacc_o, dacc_m, dacc_b, dacc_l, xt, dmat,
+        wg, lists, asked, dhg, dmg, bk, xs, nz, ys, w1f, w1t, w1n, w2t, w2h, heads, head_t, head_f,
+        rowbuf, wide, headcol, acc_h, acc_w, acc_c, acc_a, acc_m, acc_l, grid_0, grid_1, grid_2, from_0, from_1,
+        from_2, zr_0, zr_1, zr_2, zf_0, zf_1, zf_2, sum_0, sum_1, sum_2, mg, mat, dcols, dacc_h, dacc_w, dacc_o, dacc_m, dacc_b, dacc_l, xt, dmat,
         dpack, drow_x, bias, dhead, dhead_t, *rest,
     ) = refs
     send, recv = rest
     sent, here_at = lay.sent, lay.here
-    grids, froms = (grid_0, grid_1, grid_a), (from_0, from_1, from_a)
-    zrs, zfs, totals = (zr_0, zr_1, zr_a), (zf_0, zf_1, zf_a), (sum_0, sum_1, sum_a)
+    grids, froms = (grid_0, grid_1, grid_2), (from_0, from_1, from_2)
+    zrs, zfs, totals = (zr_0, zr_1, zr_2), (zf_0, zf_1, zf_2), (sum_0, sum_1, sum_2)
     n_dp, n_blk = lay.n_dp, lay.n_blk
     me = lax.axis_index("dp")
     z = lax.axis_index("blk")
@@ -207,7 +201,6 @@
     sibling = me + 1 - 2 * core
     is_dyn = me < MEMBERS
     dyn_e = jnp.minimum(me, MEMBERS - 1)
-    is_owner = me == lay.owner
 
     def on_plane(src, dst, ssem, rsem, peer):
         return pltpu.make_async_remote_copy(
@@ -281,6 +274,71 @@
         return on_line(dyn_m.at[dyn_e], dmg.at[z], send.at[sent["dyn m"]], recv.at[here_at["dyn m"]], peer)
 
     alive = live[...].astype(F32).reshape(1, lay.model)
+    data = replay[...]
+    sums = jnp.sum(data[0:24], axis=1, keepdims=True)
+    squares = jnp.sum(data[0:24] * data[0:24], axis=1, keepdims=True)
+    living = jnp.sum(alive, axis=1, keepdims=True)
+
+    has_come(asked.at[pl.ds(0, n_dp - 1)], "lists")
+    spread = (
+        lax.rem(lax.broadcasted_iota(jnp.int32, (CAP, lay.real), 1), CAP)
+        == lax.broadcasted_iota(jnp.int32, (CAP, lay.real), 0)
+    ).astype(F32)
+    here = (
+        lax.broadcasted_iota(jnp.int32, (n_dp, lay.real), 1) // CAP
+        == lax.broadcasted_iota(jnp.int32, (n_dp, lay.real), 0)
+    )
+
+    def in_lanes(which):
+        values = asked[:, which, me, :].astype(F32)
+        wide = lax.dot_general(
+            values, spread, NN, precision=lax.Precision.HIGHEST, preferred_element_type=F32
+        )
+        return jnp.sum(jnp.where(here, wide, 0.0), axis=0, keepdims=True)
+
+    slots = in_lanes(0)
+    wanted = jnp.maximum(slots, 0.0).astype(jnp.int32)
+    hot = (rows_of((lay.replay, lay.real)) == wanted).astype(BF16)
+    padded = jnp.concatenate([data[0:40], jnp.zeros((8, lay.replay), F32)], 0)
+    tail = jnp.concatenate([data[40:FEAT], jnp.zeros((14, lay.replay), F32)], 0)
+    parts = [jnp.concatenate(pair, 0) for pair in zip(pieces(padded), pieces(tail))]
+    chosen = dot(jnp.concatenate(parts, 0), hot)
+    chosen = chosen[0:64] + chosen[64:128] + chosen[128:192]
+    mine = me * n_blk
+    bk[mine, 0:40, 0 : lay.real] = chosen[0:40]
+    bk[mine, 40:FEAT, 0 : lay.real] = chosen[48:50]
+    bk[mine, 42:43, 0 : lay.real] = (slots >= 0.0).astype(F32)
+    bk[mine, 43:44, 0 : lay.real] = in_lanes(1)
+    bk[mine, 44:48, 0 : lay.real] = jnp.zeros((4, lay.real), F32)
+    bk[mine, :, lay.real : lay.width] = jnp.zeros((48, lay.width - lay.real), F32)
+    bk[mine, 0:24, lay.real : lay.real + 1] = sums
+    bk[mine, 0:24, lay.real + 1 : lay.real + 2] = squares
+    bk[mine, 24:25, lay.real : lay.real + 1] = living
+
+    def slot_of(block):
+        line = lax.rem(block, n_blk)
+        return block - line + slot_from(line, z)
+
+    def block_line(peer):
+        dst = bk.at[me * n_blk + slot_from(z, peer)]
+        return on_line(bk.at[mine], dst, send.at[sent["line"]], recv.at[here_at["line"]], peer)
+
+    def block_own(peer):
+        view = bk.at[mine]
+        return on_plane(view, view, send.at[sent["own"]], recv.at[here_at["own"]], peer)
+
+    def block_plane(peer):
+        view = bk.at[pl.ds(mine + 1, n_blk - 1)]
+        return on_plane(view, view, send.at[sent["plane"]], recv.at[here_at["plane"]], peer)
+
+    plane_peers(lambda peer: block_own(peer).start())
+    line_peers(lambda peer: block_line(peer).start())
+
+    @pl.when(is_dyn)
+    def _():
+        line_peers(lambda peer: dyn_h_copy(peer).start())
+        line_peers(lambda peer: dyn_m_copy(peer).start())
+
     bias[...] = biases[...].reshape(1, NB)
     xs[42:56, :] = jnp.zeros((14, lay.batch), F32)
     xs[0:FEAT, lay.real : lay.batch] = model[...]
@@ -336,71 +394,6 @@
     for ref in (acc_h, acc_w, acc_c, acc_a, acc_m, acc_l):
         ref[...] = jnp.zeros_like(ref)
 
-    data = replay[...]
-    sums = jnp.sum(data[0:24], axis=1, keepdims=True)
-    squares = jnp.sum(data[0:24] * data[0:24], axis=1, keepdims=True)
-    living = jnp.sum(alive, axis=1, keepdims=True)
-
-    has_come(asked.at[pl.ds(0, n_dp - 1)], "lists")
-    spread = (
-        lax.rem(lax.broadcasted_iota(jnp.int32, (CAP, lay.real), 1), CAP)
-        == lax.broadcasted_iota(jnp.int32, (CAP, lay.real), 0)
-    ).astype(F32)
-    here = (
-        lax.broadcasted_iota(jnp.int32, (n_dp, lay.real), 1) // CAP
-        == lax.broadcasted_iota(jnp.int32, (n_dp, lay.real), 0)
-    )
-
-    def in_lanes(which):
-        values = asked[:, which, me, :].astype(F32)
-        wide = lax.dot_general(
-            values, spread, NN, precision=lax.Precision.HIGHEST, preferred_element_type=F32
-        )
-        return jnp.sum(jnp.where(here, wide, 0.0), axis=0, keepdims=True)
-
-    slots = in_lanes(0)
-    wanted = jnp.maximum(slots, 0.0).astype(jnp.int32)
-    hot = (rows_of((lay.replay, lay.real)) == wanted).astype(BF16)
-    padded = jnp.concatenate([data[0:40], jnp.zeros((8, lay.replay), F32)], 0)
-    tail = jnp.concatenate([data[40:FEAT], jnp.zeros((14, lay.replay), F32)], 0)
-    parts = [jnp.concatenate(pair, 0) for pair in zip(pieces(padded), pieces(tail))]
-    chosen = dot(jnp.concatenate(parts, 0), hot)
-    chosen = chosen[0:64] + chosen[64:128] + chosen[128:192]
-    mine = me * n_blk
-    bk[mine, 0:40, 0 : lay.real] = chosen[0:40]
-    bk[mine, 40:FEAT, 0 : lay.real] = chosen[48:50]
-    bk[mine, 42:43, 0 : lay.real] = (slots >= 0.0).astype(F32)
-    bk[mine, 43:44, 0 : lay.real] = in_lanes(1)
-    bk[mine, 44:48, 0 : lay.real] = jnp.zeros((4, lay.real), F32)
-    bk[mine, :, lay.real : lay.width] = jnp.zeros((48, lay.width - lay.real), F32)
-    bk[mine, 0:24, lay.real : lay.real + 1] = sums
-    bk[mine, 0:24, lay.real + 1 : lay.real + 2] = squares
-    bk[mine, 24:25, lay.real : lay.real + 1] = living
-
-    def slot_of(block):
-        line = lax.rem(block, n_blk)
-        return block - line + slot_from(line, z)
-
-    def block_line(peer):
-        dst = bk.at[me * n_blk + slot_from(z, peer)]
-        return on_line(bk.at[mine], dst, send.at[sent["line"]], recv.at[here_at["line"]], peer)
-
-    def block_own(peer):
-        view = bk.at[mine]
-        return on_plane(view, view, send.at[sent["own"]], recv.at[here_at["own"]], peer)
-
-    def block_plane(peer):
-        view = bk.at[pl.ds(mine + 1, n_blk - 1)]
-        return on_plane(view, view, send.at[sent["plane"]], recv.at[here_at["plane"]], peer)
-
-    plane_peers(lambda peer: block_own(peer).start())
-    line_peers(lambda peer: block_line(peer).start())
-
-    @pl.when(is_dyn)
-    def _():
-        line_peers(lambda peer: dyn_h_copy(peer).start())
-        line_peers(lambda peer: dyn_m_copy(peer).start())
-
     has_come(wg.at[pl.ds(0, n_blk - 1), :, half_rows], "hidden on")
     for k in range(3):
         for block in range(n_blk):
@@ -488,34 +481,6 @@
         acc_w[k] += dot(now_in, g1, NT)
         acc_l[0:1, 0:CRITIC_TILE] += weight * (0.5 * miss * miss)
 
-    @pl.loop(0, critic_tiles)
-    def _(step):
-        @pl.when(step == critic_tiles - 1)
-        def _():
-            has_come(bk.at[pl.ds(0, n_dp - 1)], "own")
-            lanes = lax.broadcasted_iota(jnp.int32, (48, lay.width), 1) // CAP
-
-            def gather(owner, total):
-                turned = pltpu.roll(
-                    bk[owner * n_blk], lax.rem((owner - me) * CAP + lay.width, lay.width), axis=1
-                )
-                return jnp.where(lanes == owner, turned, total)
-
-            own = lax.fori_loop(0, n_dp, gather, jnp.zeros((48, lay.width), F32))
-            xs[0:48, 0 : lay.real] = own[:, 0 : lay.real]
-
-        where = place_of(step, CRITIC_TILE)
-        now_in = framed(0, IN, where).astype(BF16)
-        next_f = framed(24, OBS, where)
-        reward = xs[23:24, where]
-        done = xs[41:42, where]
-        next_action, next_prob, _, _, _ = policy(next_f.astype(BF16), 1, where)
-        aim_in = with_action(next_f, next_action)
-        aim = jnp.minimum(critic(aim_in, 0)[0], critic(aim_in, 1)[0])
-        target = reward + DISCOUNT * (1.0 - done) * (aim - alpha * next_prob)
-        ys[0:1, where] = target
-        critic_pass(0, now_in, where, target)
-
     def put_matrix(k):
         for chunk in range(n_dp):
             tile = chunk * lay.mat
@@ -528,7 +493,7 @@
         for at in range(value.shape[0] // 8):
             for side in range(value.shape[1] // 128):
                 tile = side * (R_SMALL // 8) + row // 8 + at
-                grid_a[tile // lay.sml, lay.mat + tile % lay.sml] = value[
+                grid_1[tile // lay.sml, lay.mat + tile % lay.sml] = value[
                     at * 8 : at * 8 + 8, side * 128 : (side + 1) * 128
                 ]
 
@@ -539,7 +504,7 @@
         )
 
     def line_part(part):
-        return min(part, 2), pl.ds(lay.mat, lay.sml) if part == 3 else pl.ds(0, lay.mat)
+        return (1, pl.ds(lay.mat, lay.sml)) if part == 3 else (part, pl.ds(0, lay.mat))
 
     def line_sum(part, peer):
         group, tiles = line_part(part)
@@ -556,7 +521,6 @@
     row_tile = lax.rem(first_tile, 32)
     keeper_z = row_tile * 8 // lay.rows
     local_tile = row_tile - keeper_z * (lay.rows // 8)
-    is_keeper = z == keeper_z
 
     def fold_plane(group):
         has_come(froms[group].at[pl.ds(0, n_dp - 1)], ("plane sum", group))
@@ -566,31 +530,26 @@
             whole = whole + froms[group][at]
         zfs[group][...] = whole
 
-        @pl.when(is_keeper)
+        @pl.when(z == keeper_z)
         def _():
             held_rows = pl.ds(pl.multiple_of(local_tile * 8, 8), lay.mat * 8)
             held_lanes = pl.ds(pl.multiple_of(side * 128, 128), 128)
             old = sac_m[group, held_rows, held_lanes].reshape(lay.mat, 8, 128)
-            zfs[group][0 : lay.mat] += (MOMENTUM * total).reshape(1, 1, 1) * old
-
-        for part in (2, 3) if group == 2 else (group,):
+            zfs[group][0 : lay.mat] += (MOMENTUM * count[0:1, 0:1]).reshape(1, 1, 1) * old
+
+        for part in (1, 3) if group == 1 else (group,):
             line_peers(lambda peer: line_sum(part, peer).start())
 
     def tile_copy(k, peer):
-        return on_plane(totals[k].at[pl.ds(0, lay.mat)], mg.at[k, me], send.at[sent["tiles", k]], recv.at[here_at["tiles", k]], peer)
+        name = ("tiles", k)
+        src = totals[k].at[pl.ds(0, lay.mat)]
+        return on_plane(src, mg.at[k, me], send.at[sent[name]], recv.at[here_at[name]], peer)
 
     def small_copy(peer):
         return on_plane(
-            sum_a.at[pl.ds(lay.mat, lay.sml)], small.at[pl.ds(me * lay.sml, lay.sml)],
+            sum_1.at[pl.ds(lay.mat, lay.sml)], small.at[pl.ds(me * lay.sml, lay.sml)],
             send.at[sent["small"]], recv.at[here_at["small"]], peer,
         )
-
-    def keep_copy(k, peer):
-        view = sac_g.at[side, k, pl.ds(local_tile, lay.mat)]
-        return on_plane(view, view, send.at[sent["sac g", k]], recv.at[here_at["sac g", k]], peer)
-
-    def kept_bytes(number):
-        return froms[0].at[pl.ds(0, number)]
 
     def fold_end(part):
         group, tiles = line_part(part)
@@ -600,29 +559,16 @@
         for block in range(1, n_blk):
             whole = whole + zrs[group][block, tiles]
         totals[group][tiles] = whole
-        if part < 2:
-            pl.when(jnp.logical_not(is_owner))(tile_copy(part, lay.owner).start)
-
-            @pl.when(is_owner)
-            def _():
-                mg[part, me] = whole
-
-            @pl.when(is_keeper)
-            def _():
-                sac_g[side, part, pl.ds(local_tile, lay.mat)] = whole
-                plane_peers(lambda peer: keep_copy(part, peer).start())
-
-        if part == 2:
-            plane_peers(lambda peer: tile_copy(2, peer).start())
-            mg[2, me] = whole
-
         if part == 3:
             plane_peers(lambda peer: small_copy(peer).start())
-            small[pl.ds(me * lay.sml, lay.sml)] = sum_a[lay.mat :]
+            small[pl.ds(me * lay.sml, lay.sml)] = whole
+        else:
+            plane_peers(lambda peer: tile_copy(part, peer).start())
+            mg[part, me] = whole
 
     def chain(group):
         def end():
-            for part in (2, 3) if group == 2 else (group,):
+            for part in (1, 3) if group == 1 else (group,):
                 fold_end(part)
 
         return [
@@ -634,11 +580,6 @@
     chains = [chain(group) for group in range(3)]
     per = DYN_TILE // lay.real
     dyn_tiles = lay.n_dev // per
-    in_actor = {actor_tiles - 1: [chains[0][1]]} if actor_tiles > 1 else {}
-    after_actor = [chains[1][1]] if actor_tiles > 1 else [chains[0][1], chains[1][1]]
-    in_dyn = {}
-    in_dyn.setdefault(min(1, dyn_tiles - 1), []).append(chains[0][2])
-    in_dyn.setdefault(dyn_tiles - 1, []).append(chains[1][2])
 
     def take(slots, step):
         for at, events in slots.items():
@@ -647,38 +588,22 @@
                 for event in events:
                     event()
 
-    put_matrix(0)
-    chains[0][0]()
-
-    @pl.loop(0, critic_tiles)
-    def _(step):
-        where = place_of(step, CRITIC_TILE)
-        critic_pass(1, framed(0, IN, where).astype(BF16), where, ys[0:1, where])
-
-    put_matrix(1)
-    chains[1][0]()
-
-    has_come(bk.at[pl.ds(0, (n_dp - 1) * (n_blk - 1))], "plane")
-    lane0 = lay.real // 128 * 128
-
-    def add_block(at, carry):
-        sides, fills = carry
-        slot = slot_of(at)
-        return sides + bk[slot, 0:32, lane0 : lane0 + 128], fills + bk[slot, 40:48, 0 : lay.real]
-
-    sides, fills = lax.fori_loop(
-        0, lay.n_dev, add_block, (jnp.zeros((32, 128), F32), jnp.zeros((8, lay.real), F32))
-    )
-    at = lay.real - lane0
-    rows_all = float(lay.replay * lay.n_dev)
-    centre = sides[0:24, at : at + 1] / rows_all
-    scale = lax.rsqrt(sides[0:24, at + 1 : at + 2] / rows_all - centre * centre + 1e-6)
-    total = sides[24:25, at : at + 1] + jnp.sum(fills[2:3, :], axis=1, keepdims=True)
-    count[...] = jnp.broadcast_to(total, (8, 128))
-
     @pl.loop(0, actor_tiles)
     def _(step):
-        take(in_actor, step)
+        @pl.when(step == actor_tiles - 1)
+        def _():
+            has_come(bk.at[pl.ds(0, n_dp - 1)], "own")
+            lanes = lax.broadcasted_iota(jnp.int32, (48, lay.width), 1) // CAP
+
+            def gather(owner, total):
+                turned = pltpu.roll(
+                    bk[owner * n_blk], lax.rem((owner - me) * CAP + lay.width, lay.width), axis=1
+                )
+                return jnp.where(lanes == owner, turned, total)
+
+            own = lax.fori_loop(0, n_dp, gather, jnp.zeros((48, lay.width), F32))
+            xs[0:48, 0 : lay.real] = own[:, 0 : lay.real]
+
         where = place_of(step, ACTOR_TILE)
         now_f = framed(0, IN, where)
         now_in = now_f.astype(BF16)
@@ -710,6 +635,51 @@
         acc_l[2:3, 0:ACTOR_TILE] += weight * (log_prob + TARGET_ENTROPY)
 
     put_matrix(2)
+    chains[2][0]()
+
+    @pl.loop(0, critic_tiles)
+    def _(step):
+        where = place_of(step, CRITIC_TILE)
+        now_in = framed(0, IN, where).astype(BF16)
+        next_f = framed(24, OBS, where)
+        reward = xs[23:24, where]
+        done = xs[41:42, where]
+        next_action, next_prob, _, _, _ = policy(next_f.astype(BF16), 1, where)
+        aim_in = with_action(next_f, next_action)
+        aim = jnp.minimum(critic(aim_in, 0)[0], critic(aim_in, 1)[0])
+        target = reward + DISCOUNT * (1.0 - done) * (aim - alpha * next_prob)
+        ys[0:1, where] = target
+        critic_pass(0, now_in, where, target)
+
+    put_matrix(0)
+    chains[0][0]()
+
+    has_come(bk.at[pl.ds(0, (n_dp - 1) * (n_blk - 1))], "plane")
+    lane0 = lay.real // 128 * 128
+
+    def add_block(at, carry):
+        sides, fills = carry
+        slot = slot_of(at)
+        return sides + bk[slot, 0:32, lane0 : lane0 + 128], fills + bk[slot, 40:48, 0 : lay.real]
+
+    sides, fills = lax.fori_loop(
+        0, lay.n_dev, add_block, (jnp.zeros((32, 128), F32), jnp.zeros((8, lay.real), F32))
+    )
+    at = lay.real - lane0
+    rows_all = float(lay.replay * lay.n_dev)
+    centre = sides[0:24, at : at + 1] / rows_all
+    scale = lax.rsqrt(sides[0:24, at + 1 : at + 2] / rows_all - centre * centre + 1e-6)
+    total = sides[24:25, at : at + 1] + jnp.sum(fills[2:3, :], axis=1, keepdims=True)
+    count[...] = jnp.broadcast_to(total, (8, 128))
+
+    chains[2][1]()
+
+    @pl.loop(0, critic_tiles)
+    def _(step):
+        where = place_of(step, CRITIC_TILE)
+        critic_pass(1, framed(0, IN, where).astype(BF16), where, ys[0:1, where])
+
+    put_matrix(1)
     for k in range(3):
         put(R_IN + 24 * k, acc_w[k, 0:24, :])
     put(R_HEAD, acc_a[...])
@@ -725,9 +695,7 @@
     rowbuf[0:1, 65:66] = folded[2:3]
     put(R_MISC, rowbuf[...])
     put(R_MISC + 8, jnp.zeros((R_SMALL - R_MISC - 8, HSAC), F32))
-    chains[2][0]()
-    for event in after_actor:
-        event()
+    chains[1][0]()
 
     def dyn_bias(start, width):
         row = jnp.zeros((1, width), F32)
@@ -769,6 +737,10 @@
         w2t[0] = dmat[...].T.astype(BF16)
         for ref in (dacc_h, dacc_w, dacc_o, dacc_m, dacc_b, dacc_l):
             ref[...] = jnp.zeros_like(ref)
+
+    in_dyn = {}
+    for at, event in ((1, chains[2][2]), (1, chains[0][1]), (dyn_tiles - 1, chains[1][1])):
+        in_dyn.setdefault(min(at, dyn_tiles - 1), []).append(event)
 
     @pl.loop(0, dyn_tiles)
     def _(tile):
@@ -865,10 +837,6 @@
             rows = jnp.where(z == block, ref[block * lay.drows : (block + 1) * lay.drows, 0:HDYN], rows)
         return rows
 
-    def sac_x_copy(k, src, peer):
-        name = ("sac x", k)
-        return on_plane(src, sac_x.at[k], send.at[sent[name] + peer], recv.at[here_at[name]], peer)
-
     mine_rows = pl.ds(pl.multiple_of(z * lay.rows, lay.rows), lay.rows)
 
     def take_matrix(k):
@@ -881,7 +849,7 @@
             mat[k, at, half * 128 : (half + 1) * 128] = piece / total
         normalise(mat.at[k])
 
-    chains[2][1]()
+    chains[0][2]()
 
     @pl.when(is_dyn)
     def _():
@@ -909,33 +877,22 @@
             dmat[at, 0:HDYN] = MOMENTUM * dmg[block] + dacc_h[at, 0:HDYN] / total
         normalise(dmat)
 
-    def own_x(k):
-        return mat.at[k, mine_rows]
-
-    passes_x = jnp.logical_and(core == lay.owner % 2, jnp.logical_not(is_owner))
-
     def sum_end(step):
-        pl.when(step == NS_ITERS - 1)(chains[2][2])
+        pl.when(step == 2)(chains[1][2])
+
+    take_matrix(2)
 
     @pl.when(is_dyn)
     def _():
-        schulz([dmat], NS_ITERS, sum_end)
+        schulz([dmat, mat.at[2]], NS_ITERS, sum_end)
         rows = line_rows(dmat)
         drow_x[...] = rows
         dyn_x[dyn_e] = rows
         give("x", drow_x)
 
-    @pl.when(is_owner)
+    @pl.when(jnp.logical_not(is_dyn))
     def _():
-        for k in range(2):
-            take_matrix(k)
-            schulz([mat.at[k]], NS_ITERS, sum_end if k == 1 else None)
-            sac_x[k] = mat[k, mine_rows, :]
-            like_peers(lambda peer: sac_x_copy(k, own_x(k), peer).start())
-            sac_x_copy(k, own_x(k), sibling).start()
-
-    if n_dp > MEMBERS + 1:
-        pl.when(jnp.logical_not(jnp.logical_or(is_dyn, is_owner)))(chains[2][2])
+        schulz([mat.at[2]], NS_ITERS, sum_end)
 
     def sent_early():
         has_sent(wg.at[pl.ds(0, n_blk - 1), :, half_rows], "hidden")
@@ -956,27 +913,21 @@
             has_sent(line_bytes(part), ("line sum", part))
 
     def pass_on(step):
-        @pl.when(step == 2)
-        def _():
-            hand_on("pack")
-            hand_on("x")
-            for k in range(2):
-                pl.when(jnp.logical_not(is_owner))(sac_x_copy(k, sac_x.at[k], sibling).wait_recv)
-                pl.when(passes_x)(sac_x_copy(k, sac_x.at[k], sibling).start)
-
-    take_matrix(2)
-    for half in range(2):
-        for piece in range(lay.rows // 8 // lay.mat):
-            chunk = (half * 32 + z * (lay.rows // 8)) // lay.mat + piece
-            sac_g[half, 2, piece * lay.mat : (piece + 1) * lay.mat] = mg[2, chunk]
-    schulz([mat.at[2]], NS_ITERS, pass_on)
-    sac_x[2] = mat[2, mine_rows, :]
+        pl.when(step == 2)(functools.partial(hand_on, "pack"))
+        pl.when(step == NS_ITERS - 1)(functools.partial(hand_on, "x"))
+
+    for k in range(2):
+        take_matrix(k)
+    schulz([mat.at[0], mat.at[1]], NS_ITERS, pass_on)
+    for k in range(3):
+        sac_x[k] = mat[k, mine_rows, :]
+        for half in range(2):
+            for piece in range(lay.rows // 8 // lay.mat):
+                chunk = (half * 32 + z * (lay.rows // 8)) // lay.mat + piece
+                sac_g[half, k, piece * lay.mat : (piece + 1) * lay.mat] = mg[k, chunk]
 
     sent_early()
     has_come(small.at[pl.ds(0, (n_dp - 1) * lay.sml)], "small")
-    for number, test in ((lay.keepers - 1, is_keeper), (lay.keepers, jnp.logical_not(is_keeper))):
-        for k in range(2):
-            pl.when(test)(functools.partial(has_come, kept_bytes(number), ("sac g", k)))
     from_sibling("pack")
     from_sibling("x")
 
@@ -984,23 +935,8 @@
     gave("pack")
     gave("x")
 
-    has_sent(mg.at[2, pl.ds(0, n_dp - 1)], ("tiles", 2))
-
-    @pl.when(jnp.logical_not(is_owner))
-    def _():
-        for k in range(2):
-            tile_copy(k, sibling).wait_send()
-
-    for k in range(2):
-        pl.when(is_keeper)(functools.partial(has_sent, kept_bytes(n_dp - 1), ("sac g", k)))
-
-    for k in range(2):
-        @pl.when(is_owner)
-        def _():
-            like_peers(lambda peer: sac_x_copy(k, own_x(k), peer).wait_send())
-            sac_x_copy(k, own_x(k), sibling).wait_send()
-
-        pl.when(passes_x)(sac_x_copy(k, sac_x.at[k], sibling).wait_send)
+    for k in range(3):
+        has_sent(mg.at[k, pl.ds(0, n_dp - 1)], ("tiles", k))
 
 
 def adamw(weights, first, second, gradient):
@@ -1143,6 +1079,7 @@
         vm(lay.n_dev, 48, lay.width),
         vm(56, lay.batch),
         vm(2, 8, lay.batch),
+        vm(8, lay.batch),
         vm(5, 32, HSAC),
         vm(5, HSAC, 32, kind=BF16),
         vm(2, 16, HSAC, kind=BF16),
@@ -1165,7 +1102,6 @@
         *[vm(n_blk, chunk, 8, 128) for chunk in lay.chunks],
         *[vm(chunk, 8, 128) for chunk in lay.chunks],
         *[vm(chunk, 8, 128) for chunk in lay.chunks],
-        vm(8, lay.batch),
         vm(3, n_dp, lay.mat, 8, 128),
         vm(3, HSAC, HSAC),
         vm(HSAC, 8),

time: 65.3 us -> 63.4 us (0.971)
  the two profiles are of different devices: /device:TPU:10 before, /device:TPU:0 now
where the time goes in v10:
time: 63.4 us; the launch traced here: 63.2 us
  Pallas kernels  61.4 us (97%)
  between operations  1.21 us (2%)
    pallas_call x1, Pallas kernels, shards(): pl.pallas_call(functools.partial(main_kernel, lay), out_shape=out_shape,...  59.3 us
    pallas_call x1, Pallas kernels, shards(): pl.pallas_call(update_kernel, out_shape=tuple(new_shape), in_specs=[spec]...  2.11 us

profile of v10, /device:TPU:0, one launch (start us, length us, event | category | flops | bytes accessed | tf_op | source)
XLA Modules:
  0.0 63.2 jit_solution(3646943915176132510)
XLA Ops:
  0.7 0.0 copy-start
  0.7 0.0 copy-start.1
  0.7 0.0 copy-start.2
  0.7 0.0 copy-start.3
  0.7 0.0 copy-start.4
  0.7 0.0 copy-start.5
  0.7 0.0 copy-start.6
  0.7 0.0 copy-start.7
  0.8 0.0 copy-start.8
  0.8 0.0 copy-start.9
  0.8 0.0 copy-start.10
  0.8 0.0 copy-start.11
  0.8 0.0 copy-start.12
  0.8 0.0 copy-start.13
  0.8 0.0 copy-start.14
  0.8 0.0 copy-start.15
  0.8 0.0 copy-start.16
  0.8 0.0 copy-start.17
  0.9 0.0 copy-start.18
  0.9 0.0 copy-start.19
  0.9 0.0 copy-start.20
  0.9 0.0 copy-start.23
  0.9 59.3 %step.1 = (f32[2,3,8,8,128]{4,3,2,1,0:T(8,128)S(1)}, f32[3,64,256]{2,1,0:T(8,128)S(1)}, f32[7,50,200]{2,1,0:T(8,128)S(1)}, f32[7,128,256]{2,1,0:T(8,128)S(1)}, f...) custom-call(f32[42,3648]{1,0:T(8,128)} %refs_0_.1, f32[42,1216]{1,0:T(8,128)} %refs_1_.1, s32[8,8]{1,0:T(8,128)} %refs_2_.1, ...), custom_call_target="tpu_custom_call" | custom-call | tf_op jit(solution)/shard_map/step/pallas_call | solution.py:1124
  60.2 0.0 copy-start.22
  60.2 0.0 copy-start.21
  60.2 0.0 copy-done
  60.2 0.0 copy-done.1
  60.3 0.0 copy-done.2
  60.3 0.0 copy-done.3
  60.3 0.0 copy-done.4
  60.3 0.0 copy-done.5
  60.3 0.0 copy-done.6
  60.3 0.0 copy-done.7
  60.3 0.0 copy-done.8
  60.3 0.0 copy-done.9
  60.3 0.0 copy-done.10
  60.3 0.0 copy-done.11
  60.4 0.0 copy-done.12
  60.4 0.0 copy-done.13
  60.4 0.0 copy-done.14
  60.4 0.0 copy-done.15
  60.4 0.0 copy-done.16
  60.4 0.0 copy-done.17
  60.4 0.0 copy-done.18
  60.4 0.0 copy-done.19
  60.4 0.0 copy-done.20
  60.4 0.0 copy-done.23
  60.5 0.4 copy-done.22
  60.9 0.0 copy-done.21
  60.9 2.1 %update.1 = (f32[3,64,256]{2,1,0:T(8,128)}, f32[3,64,256]{2,1,0:T(8,128)}, f32[7,50,200]{2,1,0:T(8,128)}, f32[7,50,200]{2,1,0:T(8,128)}, f32[23,2,256]{2,1,0:T(2...) custom-call(f32[2,3,8,8,128]{4,3,2,1,0:T(8,128)S(1)} %get-tuple-elem, ...), custom_call_target="tpu_custom_call" | custom-call | tf_op jit(solution)/shard_map/update/pallas_call | solution.py:1144
Async XLA Ops:
  0.7 59.6 %copy-start = (f32[7,50,200]{2,1,0:T(8,128)S(1)}, f32[7,50,200]{2,1,0:T(8,128)}, u32[]{:S(2)}) copy-start(f32[7,50,200]{2,1,0:T(8,128)} %refs_7_.3) | copy-start | bytes 840004
  0.7 59.6 %copy-start.1 = (f32[7,50,200]{2,1,0:T(8,128)S(1)}, f32[7,50,200]{2,1,0:T(8,128)}, u32[]{:S(2)}) copy-start(f32[7,50,200]{2,1,0:T(8,128)} %refs_8_.3) | copy-start | bytes 840004
  0.7 59.6 %copy-start.2 = (f32[7,200,36]{1,2,0:T(8,128)S(1)}, f32[7,200,36]{1,2,0:T(8,128)}, u32[]{:S(2)}) copy-start(f32[7,200,36]{1,2,0:T(8,128)} %param.60) | copy-start | bytes 604804
  0.7 59.6 %copy-start.3 = (f32[3,64,256]{2,1,0:T(8,128)S(1)}, f32[3,64,256]{2,1,0:T(8,128)}, u32[]{:S(2)}) copy-start(f32[3,64,256]{2,1,0:T(8,128)} %refs_6_.3) | copy-start | bytes 589828
  0.7 59.6 %copy-start.4 = (f32[7,23,200]{2,1,0:T(8,128)S(1)}, f32[7,23,200]{2,1,0:T(8,128)}, u32[]{:S(2)}) copy-start(f32[7,23,200]{2,1,0:T(8,128)} %refs_15_.1) | copy-start | bytes 386404
  0.7 59.6 %copy-start.5 = (f32[7,200,36]{1,2,0:T(8,128)S(1)}, f32[7,200,36]{1,2,0:T(8,128)}, u32[]{:S(2)}) copy-start(f32[7,200,36]{1,2,0:T(8,128)} %param.61) | copy-start | bytes 604804
  0.7 59.6 %copy-start.6 = (f32[7,200,36]{1,2,0:T(8,128)S(1)}, f32[7,200,36]{1,2,0:T(8,128)}, u32[]{:S(2)}) copy-start(f32[7,200,36]{1,2,0:T(8,128)} %param.62) | copy-start | bytes 604804
  0.7 59.6 %copy-start.7 = (f32[2,23,256]{2,0,1:T(2,128)S(1)}, f32[2,23,256]{2,0,1:T(2,128)}, u32[]{:S(2)}) copy-start(f32[2,23,256]{2,0,1:T(2,128)} %param.45) | copy-start | bytes 141316
  0.8 59.6 %copy-start.8 = (f32[7,23,200]{2,1,0:T(8,128)S(1)}, f32[7,23,200]{2,1,0:T(8,128)}, u32[]{:S(2)}) copy-start(f32[7,23,200]{2,1,0:T(8,128)} %refs_16_.3) | copy-start | bytes 386404
  0.8 59.6 %copy-start.9 = (f32[7,23,200]{2,1,0:T(8,128)S(1)}, f32[7,23,200]{2,1,0:T(8,128)}, u32[]{:S(2)}) copy-start(f32[7,23,200]{2,1,0:T(8,128)} %refs_17_.1) | copy-start | bytes 386404
  0.8 59.6 %copy-start.10 = (f32[17,256]{1,0:T(8,128)S(1)}, f32[17,256]{1,0:T(8,128)}, u32[]{:S(2)}) copy-start(f32[17,256]{1,0:T(8,128)} %refs_12_.3) | copy-start | bytes 52228
  0.8 59.6 %copy-start.11 = (f32[4639]{0:T(1024)S(1)}, f32[4639]{0:T(1024)}, u32[]{:S(2)}) copy-start(f32[4639]{0:T(1024)} %refs_27_.1) | copy-start | bytes 55672
  0.8 59.6 %copy-start.12 = (f32[256,12]{0,1:T(8,128)S(1)}, f32[256,12]{0,1:T(8,128)}, u32[]{:S(2)}) copy-start(f32[256,12]{0,1:T(8,128)} %param.57) | copy-start | bytes 36868
  0.8 59.6 %copy-start.13 = (f32[2,23,256]{2,0,1:T(2,128)S(1)}, f32[2,23,256]{2,0,1:T(2,128)}, u32[]{:S(2)}) copy-start(f32[2,23,256]{2,0,1:T(2,128)} %param.46) | copy-start | bytes 141316
  0.8 59.6 %copy-start.14 = (f32[2,23,256]{2,0,1:T(2,128)S(1)}, f32[2,23,256]{2,0,1:T(2,128)}, u32[]{:S(2)}) copy-start(f32[2,23,256]{2,0,1:T(2,128)} %param.47) | copy-start | bytes 141316
  0.8 59.6 %copy-start.15 = (f32[17,256]{1,0:T(8,128)S(1)}, f32[17,256]{1,0:T(8,128)}, u32[]{:S(2)}) copy-start(f32[17,256]{1,0:T(8,128)} %refs_13_.3) | copy-start | bytes 52228
  0.8 59.6 %copy-start.16 = (f32[17,256]{1,0:T(8,128)S(1)}, f32[17,256]{1,0:T(8,128)}, u32[]{:S(2)}) copy-start(f32[17,256]{1,0:T(8,128)} %refs_14_.1) | copy-start | bytes 52228
  0.8 59.6 %copy-start.17 = (f32[4639]{0:T(1024)S(1)}, f32[4639]{0:T(1024)}, u32[]{:S(2)}) copy-start(f32[4639]{0:T(1024)} %refs_28_.1) | copy-start | bytes 55672
  0.9 59.6 %copy-start.18 = (f32[4639]{0:T(1024)S(1)}, f32[4639]{0:T(1024)}, u32[]{:S(2)}) copy-start(f32[4639]{0:T(1024)} %refs_29_.1) | copy-start | bytes 55672
  0.9 59.6 %copy-start.19 = (f32[256,12]{0,1:T(8,128)S(1)}, f32[256,12]{0,1:T(8,128)}, u32[]{:S(2)}) copy-start(f32[256,12]{0,1:T(8,128)} %param.58) | copy-start | bytes 36868
  0.9 59.6 %copy-start.20 = (f32[256,12]{0,1:T(8,128)S(1)}, f32[256,12]{0,1:T(8,128)}, u32[]{:S(2)}) copy-start(f32[256,12]{0,1:T(8,128)} %param.59) | copy-start | bytes 36868
  0.9 59.6 %copy-start.23 = (f32[2,256]{1,0:T(2,128)S(1)}, f32[2,256]{1,0:T(2,128)}, u32[]{:S(2)}) copy-start(f32[2,256]{1,0:T(2,128)} %refs_20_.3) | copy-start | bytes 6148
  60.2 0.7 %copy-start.22 = (f32[2,256]{1,0:T(2,128)S(1)}, f32[2,256]{1,0:T(2,128)}, u32[]{:S(2)}) copy-start(f32[2,256]{1,0:T(2,128)} %refs_19_.3) | copy-start | bytes 6148
  60.2 0.7 %copy-start.21 = (f32[2,256]{1,0:T(2,128)S(1)}, f32[2,256]{1,0:T(2,128)}, u32[]{:S(2)}) copy-start(f32[2,256]{1,0:T(2,128)} %refs_18_.3) | copy-start | bytes 6148

commit v11 on v10

--- a/solution.py
+++ b/solution.py
@@ -20,7 +20,7 @@
 NS_ITERS = 5
 STEP = 10
 CAP = 8
-CRITIC_TILE = 1280
+CRITIC_TILE = 640
 ACTOR_TILE = 640
 DYN_TILE = 512
 ROWS = 32
@@ -150,6 +150,7 @@
 class Layout:
     def __init__(self, mesh, replay, model):
         self.n_dp = mesh.shape["dp"]
+        self.half = self.n_dp // 2
         self.n_blk = mesh.shape["blk"]
         self.n_dev = self.n_dp * self.n_blk
         self.replay = replay
@@ -162,15 +163,16 @@
         self.mat = 64 // self.n_dp
         self.sml = 32 // self.n_dp
         self.chunks = (self.mat, self.mat + self.sml, self.mat)
-        groups = [("plane sum", g) for g in range(3)] + [("line sum", g) for g in range(4)]
-        common = ["hidden", "hidden on", "lists", "own", "line", "plane", "dyn h", "dyn m", "small"]
+        groups = [(name, g) for name in ("core sum", "plane sum") for g in range(3)]
+        groups += [("line sum", g) for g in range(4)]
+        common = ["hidden", "hidden on", "lists", "own", "line", "plane", "dyn h", "dyn m", "small", "small on"]
         common += groups
         kinds = [(name, kind) for name in ("pack", "x") for kind in ("own", "on")]
-        sent = common + [("tiles", k) for k in range(3)] + kinds
+        tiles = [(name, k) for name in ("tiles", "tiles on") for k in range(3)]
+        sent = common + tiles + kinds
         self.sent = {name: at for at, name in enumerate(sent)}
         self.departures = len(sent)
         self.here, self.arrivals = {}, 0
-        tiles = [("tiles", k) for k in range(3)]
         tiles += [("pack", "sibling"), ("x", "sibling")]
         for name in common + tiles:
             self.here[name] = self.arrivals
@@ -186,18 +188,18 @@
         dyn_in, crit_out, act_out, dyn_out, biases, targ_in, targ_hidden, targ_out, targ_bias,
         sac_g, sac_x, dyn_x, dyn_s, small, count,
         wg, lists, asked, dhg, dmg, bk, xs, nz, ys, w1f, w1t, w1n, w2t, w2h, heads, head_t, head_f,
-        rowbuf, wide, headcol, acc_h, acc_w, acc_c, acc_a, acc_m, acc_l, grid_0, grid_1, grid_2, from_0, from_1,
-        from_2, zr_0, zr_1, zr_2, zf_0, zf_1, zf_2, sum_0, sum_1, sum_2, mg, mat, dcols, dacc_h, dacc_w, dacc_o, dacc_m, dacc_b, dacc_l, xt, dmat,
+        rowbuf, wide, headcol, acc_h, acc_w, acc_c, acc_a, acc_m, acc_l, grid_0, grid_1, grid_2, core_0, core_1,
+        core_2, from_0, from_1, from_2, zr_0, zr_1, zr_2, zf_0, zf_1, zf_2, sum_0, sum_1, sum_2, mg, mat, dcols, dacc_h, dacc_w, dacc_o, dacc_m, dacc_b, dacc_l, xt, dmat,
         dpack, drow_x, bias, dhead, dhead_t, *rest,
     ) = refs
     send, recv = rest
     sent, here_at = lay.sent, lay.here
-    grids, froms = (grid_0, grid_1, grid_2), (from_0, from_1, from_2)
+    grids, cores, froms = (grid_0, grid_1, grid_2), (core_0, core_1, core_2), (from_0, from_1, from_2)
     zrs, zfs, totals = (zr_0, zr_1, zr_2), (zf_0, zf_1, zf_2), (sum_0, sum_1, sum_2)
     n_dp, n_blk = lay.n_dp, lay.n_blk
     me = lax.axis_index("dp")
     z = lax.axis_index("blk")
-    core = lax.rem(me, 2)
+    core, like = lax.rem(me, 2), me // 2
     sibling = me + 1 - 2 * core
     is_dyn = me < MEMBERS
     dyn_e = jnp.minimum(me, MEMBERS - 1)
@@ -485,7 +487,7 @@
         for chunk in range(n_dp):
             tile = chunk * lay.mat
             side, row = tile // 32, tile % 32
-            grids[k][chunk, 0 : lay.mat] = acc_h[
+            grids[k][chunk % 2, chunk // 2, 0 : lay.mat] = acc_h[
                 k, row * 8 : (row + lay.mat) * 8, side * 128 : (side + 1) * 128
             ].reshape(lay.mat, 8, 128)
 
@@ -493,15 +495,27 @@
         for at in range(value.shape[0] // 8):
             for side in range(value.shape[1] // 128):
                 tile = side * (R_SMALL // 8) + row // 8 + at
-                grid_1[tile // lay.sml, lay.mat + tile % lay.sml] = value[
+                chunk = tile // lay.sml
+                grid_1[chunk % 2, chunk // 2, lay.mat + tile % lay.sml] = value[
                     at * 8 : at * 8 + 8, side * 128 : (side + 1) * 128
                 ]
+
+    def core_sum(group):
+        name = ("core sum", group)
+        return on_plane(
+            grids[group].at[1 - core], cores[group], send.at[sent[name]], recv.at[here_at[name]], sibling
+        )
 
     def plane_sum(group, peer):
         name = ("plane sum", group)
         return on_plane(
-            grids[group].at[peer], froms[group].at[me], send.at[sent[name]], recv.at[here_at[name]], peer
+            cores[group].at[peer // 2], froms[group].at[like], send.at[sent[name]], recv.at[here_at[name]], peer
         )
+
+    def fold_core(group):
+        core_sum(group).wait_recv()
+        cores[group][...] += grids[group][core]
+        like_peers(lambda peer: plane_sum(group, peer).start())
 
     def line_part(part):
         return (1, pl.ds(lay.mat, lay.sml)) if part == 3 else (part, pl.ds(0, lay.mat))
@@ -523,10 +537,10 @@
     local_tile = row_tile - keeper_z * (lay.rows // 8)
 
     def fold_plane(group):
-        has_come(froms[group].at[pl.ds(0, n_dp - 1)], ("plane sum", group))
-        froms[group][me] = grids[group][me]
+        has_come(froms[group].at[pl.ds(0, lay.half - 1)], ("plane sum", group))
+        froms[group][like] = cores[group][like]
         whole = froms[group][0]
-        for at in range(1, n_dp):
+        for at in range(1, lay.half):
             whole = whole + froms[group][at]
         zfs[group][...] = whole
 
@@ -543,13 +557,24 @@
     def tile_copy(k, peer):
         name = ("tiles", k)
         src = totals[k].at[pl.ds(0, lay.mat)]
-        return on_plane(src, mg.at[k, me], send.at[sent[name]], recv.at[here_at[name]], peer)
+        return on_plane(src, mg.at[k, core, like], send.at[sent[name]], recv.at[here_at[name]], peer)
+
+    def tiles_on(k):
+        name = ("tiles on", k)
+        view = mg.at[k, core]
+        return on_plane(view, view, send.at[sent[name]], recv.at[here_at[name]], sibling)
+
+    small_at = (core * lay.half + like) * lay.sml
 
     def small_copy(peer):
         return on_plane(
-            sum_1.at[pl.ds(lay.mat, lay.sml)], small.at[pl.ds(me * lay.sml, lay.sml)],
+            sum_1.at[pl.ds(lay.mat, lay.sml)], small.at[pl.ds(small_at, lay.sml)],
             send.at[sent["small"]], recv.at[here_at["small"]], peer,
         )
+
+    def small_on():
+        view = small.at[pl.ds(core * lay.half * lay.sml, lay.half * lay.sml)]
+        return on_plane(view, view, send.at[sent["small on"]], recv.at[here_at["small on"]], sibling)
 
     def fold_end(part):
         group, tiles = line_part(part)
@@ -560,21 +585,30 @@
             whole = whole + zrs[group][block, tiles]
         totals[group][tiles] = whole
         if part == 3:
-            plane_peers(lambda peer: small_copy(peer).start())
-            small[pl.ds(me * lay.sml, lay.sml)] = whole
+            like_peers(lambda peer: small_copy(peer).start())
+            small[pl.ds(small_at, lay.sml)] = whole
         else:
-            plane_peers(lambda peer: tile_copy(part, peer).start())
-            mg[part, me] = whole
+            like_peers(lambda peer: tile_copy(part, peer).start())
+            mg[part, core, like] = whole
 
     def chain(group):
         def end():
             for part in (1, 3) if group == 1 else (group,):
                 fold_end(part)
 
+        def turn():
+            has_come(mg.at[group, 0, pl.ds(0, lay.half - 1)], ("tiles", group))
+            tiles_on(group).start()
+            if group == 1:
+                has_come(small.at[pl.ds(0, (lay.half - 1) * lay.sml)], "small")
+                small_on().start()
+
         return [
-            lambda: plane_peers(lambda peer: plane_sum(group, peer).start()),
+            lambda: core_sum(group).start(),
+            lambda: fold_core(group),
             lambda: fold_plane(group),
             end,
+            turn,
         ]
 
     chains = [chain(group) for group in range(3)]
@@ -639,6 +673,9 @@
 
     @pl.loop(0, critic_tiles)
     def _(step):
+        if critic_tiles > 1:
+            take({1: [chains[2][1]]}, step)
+
         where = place_of(step, CRITIC_TILE)
         now_in = framed(0, IN, where).astype(BF16)
         next_f = framed(24, OBS, where)
@@ -653,6 +690,8 @@
 
     put_matrix(0)
     chains[0][0]()
+    if critic_tiles == 1:
+        chains[2][1]()
 
     has_come(bk.at[pl.ds(0, (n_dp - 1) * (n_blk - 1))], "plane")
     lane0 = lay.real // 128 * 128
@@ -672,10 +711,9 @@
     total = sides[24:25, at : at + 1] + jnp.sum(fills[2:3, :], axis=1, keepdims=True)
     count[...] = jnp.broadcast_to(total, (8, 128))
 
-    chains[2][1]()
-
     @pl.loop(0, critic_tiles)
     def _(step):
+        take({critic_tiles - 1: [chains[0][1], chains[2][2]]}, step)
         where = place_of(step, CRITIC_TILE)
         critic_pass(1, framed(0, IN, where).astype(BF16), where, ys[0:1, where])
 
@@ -739,7 +777,9 @@
             ref[...] = jnp.zeros_like(ref)
 
     in_dyn = {}
-    for at, event in ((1, chains[2][2]), (1, chains[0][1]), (dyn_tiles - 1, chains[1][1])):
+    for at, event in (
+        (1, chains[0][2]), (1, chains[1][1]), (2, chains[2][3]), (dyn_tiles - 1, chains[1][2]),
+    ):
         in_dyn.setdefault(min(at, dyn_tiles - 1), []).append(event)
 
     @pl.loop(0, dyn_tiles)
@@ -840,16 +880,17 @@
     mine_rows = pl.ds(pl.multiple_of(z * lay.rows, lay.rows), lay.rows)
 
     def take_matrix(k):
-        has_come(mg.at[k, pl.ds(0, n_dp - 1)], ("tiles", k))
+        tiles_on(k).wait_recv()
         for chunk in range(n_dp):
             tile = chunk * lay.mat
             half, row = tile // 32, tile % 32
             at = slice(row * 8, (row + lay.mat) * 8)
-            piece = mg[k, chunk].reshape(lay.mat * 8, 128)
+            piece = mg[k, chunk % 2, chunk // 2].reshape(lay.mat * 8, 128)
             mat[k, at, half * 128 : (half + 1) * 128] = piece / total
         normalise(mat.at[k])
 
-    chains[0][2]()
+    chains[2][4]()
+    chains[0][3]()
 
     @pl.when(is_dyn)
     def _():
@@ -878,7 +919,10 @@
         normalise(dmat)
 
     def sum_end(step):
-        pl.when(step == 2)(chains[1][2])
+        @pl.when(step == 3)
+        def _():
+            chains[0][4]()
+            chains[1][3]()
 
     take_matrix(2)
 
@@ -908,7 +952,8 @@
             has_sent(dmg.at[pl.ds(0, n_blk - 1)], "dyn m")
 
         for group in range(3):
-            has_sent(froms[group].at[pl.ds(0, n_dp - 1)], ("plane sum", group))
+            core_sum(group).wait_send()
+            has_sent(froms[group].at[pl.ds(0, lay.half - 1)], ("plane sum", group))
         for part in range(4):
             has_sent(line_bytes(part), ("line sum", part))
 
@@ -916,6 +961,7 @@
         pl.when(step == 2)(functools.partial(hand_on, "pack"))
         pl.when(step == NS_ITERS - 1)(functools.partial(hand_on, "x"))
 
+    chains[1][4]()
     for k in range(2):
         take_matrix(k)
     schulz([mat.at[0], mat.at[1]], NS_ITERS, pass_on)
@@ -924,19 +970,22 @@
         for half in range(2):
             for piece in range(lay.rows // 8 // lay.mat):
                 chunk = (half * 32 + z * (lay.rows // 8)) // lay.mat + piece
-                sac_g[half, k, piece * lay.mat : (piece + 1) * lay.mat] = mg[k, chunk]
+                kept = mg[k, lax.rem(chunk, 2), chunk // 2]
+                sac_g[half, k, piece * lay.mat : (piece + 1) * lay.mat] = kept
 
     sent_early()
-    has_come(small.at[pl.ds(0, (n_dp - 1) * lay.sml)], "small")
+    small_on().wait_recv()
     from_sibling("pack")
     from_sibling("x")
 
-    has_sent(small.at[pl.ds(0, (n_dp - 1) * lay.sml)], "small")
+    has_sent(small.at[pl.ds(0, (lay.half - 1) * lay.sml)], "small")
+    small_on().wait_send()
     gave("pack")
     gave("x")
 
     for k in range(3):
-        has_sent(mg.at[k, pl.ds(0, n_dp - 1)], ("tiles", k))
+        has_sent(mg.at[k, 0, pl.ds(0, lay.half - 1)], ("tiles", k))
+        tiles_on(k).wait_send()
 
 
 def adamw(weights, first, second, gradient):
@@ -948,7 +997,7 @@
     return weights - ADAM_RATE * step, first, second
 
 
-def update_kernel(*refs):
+def update_kernel(lay, *refs):
     (
         sac_g, sac_x, dyn_x, dyn_s, small, count, sac_h, dyn_h, dyn_m,
         ci, ci_m, ci_v, ai, ai_m, ai_v, di, di_m, di_v, co, co_m, co_v, ao, ao_m, ao_v,
@@ -968,10 +1017,14 @@
     dyn_new[...] = dyn_h[...] * (1.0 - MUON_RATE * MUON_DECAY) - MUON_RATE * dyn_x[...]
 
     def rows(row, number):
+        def tile(at):
+            chunk = at // lay.sml
+            return small[(chunk % 2 * lay.half + chunk // 2) * lay.sml + at % lay.sml]
+
         sides = []
         for side in range(2):
             at = side * (R_SMALL // 8) + row // 8
-            sides.append(small[at : at + -(-number // 8)].reshape(-1, 128))
+            sides.append(jnp.concatenate([tile(at + more) for more in range(-(-number // 8))], 0))
         return jnp.concatenate(sides, 1)
 
     def store(outs, at, values):
@@ -1097,12 +1150,13 @@
         vm(16, HSAC),
         vm(16, 48),
         vm(8, max(CRITIC_TILE, ACTOR_TILE)),
-        *[vm(n_dp, chunk, 8, 128) for chunk in lay.chunks],
-        *[vm(n_dp, chunk, 8, 128) for chunk in lay.chunks],
+        *[vm(2, lay.half, chunk, 8, 128) for chunk in lay.chunks],
+        *[vm(lay.half, chunk, 8, 128) for chunk in lay.chunks],
+        *[vm(lay.half, chunk, 8, 128) for chunk in lay.chunks],
         *[vm(n_blk, chunk, 8, 128) for chunk in lay.chunks],
         *[vm(chunk, 8, 128) for chunk in lay.chunks],
         *[vm(chunk, 8, 128) for chunk in lay.chunks],
-        vm(3, n_dp, lay.mat, 8, 128),
+        vm(3, 2, lay.half, lay.mat, 8, 128),
         vm(3, HSAC, HSAC),
         vm(HSAC, 8),
         vm(HSAC + 16, HSAC),
@@ -1142,7 +1196,7 @@
     new_shape = [shape(sac_hidden.shape, F32)] + [shape(value.shape, F32) for value in params]
     new_shape += [shape((1, 1), F32)] * 2
     out = pl.pallas_call(
-        update_kernel,
+        functools.partial(update_kernel, lay),
         out_shape=tuple(new_shape),
         in_specs=[spec] * (len(gathered) + len(params)),
         out_specs=[spec] * len(new_shape),

time: 63.4 us -> 61.7 us (0.973)
  Pallas kernels: 61.4 us -> 59.7 us
    pallas_call x1, Pallas kernels: 59.3 us -> 57.6 us  [shards(): pl.pallas_call(functools.partial(main_kernel, lay), out_shape=out_shape,...]
where the time goes in v11:
time: 61.7 us; the launch traced here: 61.5 us
  Pallas kernels  59.7 us (97%)
  between operations  1.21 us (2%)
    pallas_call x1, Pallas kernels, shards(): pl.pallas_call(functools.partial(main_kernel, lay), out_shape=out_shape,...  57.6 us
    pallas_call x1, Pallas kernels, shards(): pl.pallas_call(functools.partial(update_kernel, lay), out_shape=tuple(new...  2.11 us

profile of v11, /device:TPU:0, one launch (start us, length us, event | category | flops | bytes accessed | tf_op | source)
XLA Modules:
  0.0 61.5 jit_solution(8943169925133059091)
XLA Ops:
  0.7 0.0 copy-start
  0.7 0.0 copy-start.1
  0.7 0.0 copy-start.2
  0.7 0.0 copy-start.3
  0.7 0.0 copy-start.4
  0.7 0.0 copy-start.5
  0.7 0.0 copy-start.6
  0.7 0.0 copy-start.7
  0.8 0.0 copy-start.8
  0.8 0.0 copy-start.9
  0.8 0.0 copy-start.10
  0.8 0.0 copy-start.11
  0.8 0.0 copy-start.12
  0.8 0.0 copy-start.13
  0.8 0.0 copy-start.14
  0.8 0.0 copy-start.15
  0.8 0.0 copy-start.16
  0.8 0.0 copy-start.17
  0.9 0.0 copy-start.18
  0.9 0.0 copy-start.19
  0.9 0.0 copy-start.20
  0.9 0.0 copy-start.23
  0.9 57.6 %step.1 = (f32[2,3,8,8,128]{4,3,2,1,0:T(8,128)S(1)}, f32[3,64,256]{2,1,0:T(8,128)S(1)}, f32[7,50,200]{2,1,0:T(8,128)S(1)}, f32[7,128,256]{2,1,0:T(8,128)S(1)}, f...) custom-call(f32[42,3648]{1,0:T(8,128)} %refs_0_.1, f32[42,1216]{1,0:T(8,128)} %refs_1_.1, s32[8,8]{1,0:T(8,128)} %refs_2_.1, ...), custom_call_target="tpu_custom_call" | custom-call | tf_op jit(solution)/shard_map/step/pallas_call | solution.py:1178
  58.5 0.0 copy-start.22
  58.6 0.0 copy-start.21
  58.6 0.0 copy-done
  58.6 0.0 copy-done.1
  58.6 0.0 copy-done.2
  58.6 0.0 copy-done.3
  58.6 0.0 copy-done.4
  58.6 0.0 copy-done.5
  58.6 0.0 copy-done.6
  58.6 0.0 copy-done.7
  58.6 0.0 copy-done.8
  58.7 0.0 copy-done.9
  58.7 0.0 copy-done.10
  58.7 0.0 copy-done.11
  58.7 0.0 copy-done.12
  58.7 0.0 copy-done.13
  58.7 0.0 copy-done.14
  58.7 0.0 copy-done.15
  58.7 0.0 copy-done.16
  58.7 0.0 copy-done.17
  58.7 0.0 copy-done.18
  58.8 0.0 copy-done.19
  58.8 0.0 copy-done.20
  58.8 0.0 copy-done.23
  58.8 0.4 copy-done.22
  59.2 0.0 copy-done.21
  59.2 2.1 %update.1 = (f32[3,64,256]{2,1,0:T(8,128)}, f32[3,64,256]{2,1,0:T(8,128)}, f32[7,50,200]{2,1,0:T(8,128)}, f32[7,50,200]{2,1,0:T(8,128)}, f32[23,2,256]{2,1,0:T(2...) custom-call(f32[2,3,8,8,128]{4,3,2,1,0:T(8,128)S(1)} %get-tuple-elem, ...), custom_call_target="tpu_custom_call" | custom-call | tf_op jit(solution)/shard_map/update/pallas_call | solution.py:1198
Async XLA Ops:
  0.7 57.9 %copy-start = (f32[7,50,200]{2,1,0:T(8,128)S(1)}, f32[7,50,200]{2,1,0:T(8,128)}, u32[]{:S(2)}) copy-start(f32[7,50,200]{2,1,0:T(8,128)} %refs_7_.3) | copy-start | bytes 840004
  0.7 57.9 %copy-start.1 = (f32[7,50,200]{2,1,0:T(8,128)S(1)}, f32[7,50,200]{2,1,0:T(8,128)}, u32[]{:S(2)}) copy-start(f32[7,50,200]{2,1,0:T(8,128)} %refs_8_.3) | copy-start | bytes 840004
  0.7 57.9 %copy-start.2 = (f32[7,200,36]{1,2,0:T(8,128)S(1)}, f32[7,200,36]{1,2,0:T(8,128)}, u32[]{:S(2)}) copy-start(f32[7,200,36]{1,2,0:T(8,128)} %param.60) | copy-start | bytes 604804
  0.7 57.9 %copy-start.3 = (f32[3,64,256]{2,1,0:T(8,128)S(1)}, f32[3,64,256]{2,1,0:T(8,128)}, u32[]{:S(2)}) copy-start(f32[3,64,256]{2,1,0:T(8,128)} %refs_6_.3) | copy-start | bytes 589828
  0.7 57.9 %copy-start.4 = (f32[7,23,200]{2,1,0:T(8,128)S(1)}, f32[7,23,200]{2,1,0:T(8,128)}, u32[]{:S(2)}) copy-start(f32[7,23,200]{2,1,0:T(8,128)} %refs_15_.1) | copy-start | bytes 386404
  0.7 57.9 %copy-start.5 = (f32[7,200,36]{1,2,0:T(8,128)S(1)}, f32[7,200,36]{1,2,0:T(8,128)}, u32[]{:S(2)}) copy-start(f32[7,200,36]{1,2,0:T(8,128)} %param.61) | copy-start | bytes 604804
  0.7 57.9 %copy-start.6 = (f32[7,200,36]{1,2,0:T(8,128)S(1)}, f32[7,200,36]{1,2,0:T(8,128)}, u32[]{:S(2)}) copy-start(f32[7,200,36]{1,2,0:T(8,128)} %param.62) | copy-start | bytes 604804
  0.7 57.9 %copy-start.7 = (f32[2,23,256]{2,0,1:T(2,128)S(1)}, f32[2,23,256]{2,0,1:T(2,128)}, u32[]{:S(2)}) copy-start(f32[2,23,256]{2,0,1:T(2,128)} %param.45) | copy-start | bytes 141316
  0.8 57.9 %copy-start.8 = (f32[7,23,200]{2,1,0:T(8,128)S(1)}, f32[7,23,200]{2,1,0:T(8,128)}, u32[]{:S(2)}) copy-start(f32[7,23,200]{2,1,0:T(8,128)} %refs_16_.3) | copy-start | bytes 386404
  0.8 57.9 %copy-start.9 = (f32[7,23,200]{2,1,0:T(8,128)S(1)}, f32[7,23,200]{2,1,0:T(8,128)}, u32[]{:S(2)}) copy-start(f32[7,23,200]{2,1,0:T(8,128)} %refs_17_.1) | copy-start | bytes 386404
  0.8 57.9 %copy-start.10 = (f32[17,256]{1,0:T(8,128)S(1)}, f32[17,256]{1,0:T(8,128)}, u32[]{:S(2)}) copy-start(f32[17,256]{1,0:T(8,128)} %refs_12_.3) | copy-start | bytes 52228
  0.8 57.9 %copy-start.11 = (f32[4639]{0:T(1024)S(1)}, f32[4639]{0:T(1024)}, u32[]{:S(2)}) copy-start(f32[4639]{0:T(1024)} %refs_27_.1) | copy-start | bytes 55672
  0.8 57.9 %copy-start.12 = (f32[256,12]{0,1:T(8,128)S(1)}, f32[256,12]{0,1:T(8,128)}, u32[]{:S(2)}) copy-start(f32[256,12]{0,1:T(8,128)} %param.57) | copy-start | bytes 36868
  0.8 57.9 %copy-start.13 = (f32[2,23,256]{2,0,1:T(2,128)S(1)}, f32[2,23,256]{2,0,1:T(2,128)}, u32[]{:S(2)}) copy-start(f32[2,23,256]{2,0,1:T(2,128)} %param.46) | copy-start | bytes 141316
  0.8 57.9 %copy-start.14 = (f32[2,23,256]{2,0,1:T(2,128)S(1)}, f32[2,23,256]{2,0,1:T(2,128)}, u32[]{:S(2)}) copy-start(f32[2,23,256]{2,0,1:T(2,128)} %param.47) | copy-start | bytes 141316
  0.8 57.9 %copy-start.15 = (f32[17,256]{1,0:T(8,128)S(1)}, f32[17,256]{1,0:T(8,128)}, u32[]{:S(2)}) copy-start(f32[17,256]{1,0:T(8,128)} %refs_13_.3) | copy-start | bytes 52228
  0.8 57.9 %copy-start.16 = (f32[17,256]{1,0:T(8,128)S(1)}, f32[17,256]{1,0:T(8,128)}, u32[]{:S(2)}) copy-start(f32[17,256]{1,0:T(8,128)} %refs_14_.1) | copy-start | bytes 52228
  0.8 57.9 %copy-start.17 = (f32[4639]{0:T(1024)S(1)}, f32[4639]{0:T(1024)}, u32[]{:S(2)}) copy-start(f32[4639]{0:T(1024)} %refs_28_.1) | copy-start | bytes 55672
  0.9 57.9 %copy-start.18 = (f32[4639]{0:T(1024)S(1)}, f32[4639]{0:T(1024)}, u32[]{:S(2)}) copy-start(f32[4639]{0:T(1024)} %refs_29_.1) | copy-start | bytes 55672
  0.9 57.9 %copy-start.19 = (f32[256,12]{0,1:T(8,128)S(1)}, f32[256,12]{0,1:T(8,128)}, u32[]{:S(2)}) copy-start(f32[256,12]{0,1:T(8,128)} %param.58) | copy-start | bytes 36868
  0.9 57.9 %copy-start.20 = (f32[256,12]{0,1:T(8,128)S(1)}, f32[256,12]{0,1:T(8,128)}, u32[]{:S(2)}) copy-start(f32[256,12]{0,1:T(8,128)} %param.59) | copy-start | bytes 36868
  0.9 57.9 %copy-start.23 = (f32[2,256]{1,0:T(2,128)S(1)}, f32[2,256]{1,0:T(2,128)}, u32[]{:S(2)}) copy-start(f32[2,256]{1,0:T(2,128)} %refs_20_.3) | copy-start | bytes 6148
  58.5 0.7 %copy-start.22 = (f32[2,256]{1,0:T(2,128)S(1)}, f32[2,256]{1,0:T(2,128)}, u32[]{:S(2)}) copy-start(f32[2,256]{1,0:T(2,128)} %refs_19_.3) | copy-start | bytes 6148
  58.6 0.7 %copy-start.21 = (f32[2,256]{1,0:T(2,128)S(1)}, f32[2,256]{1,0:T(2,128)}, u32[]{:S(2)}) copy-start(f32[2,256]{1,0:T(2,128)} %refs_18_.3) | copy-start | bytes 6148

commit v12 on v11

--- a/solution.py
+++ b/solution.py
@@ -163,16 +163,22 @@
         self.mat = 64 // self.n_dp
         self.sml = 32 // self.n_dp
         self.chunks = (self.mat, self.mat + self.sml, self.mat)
+        self.owners = (self.n_dp - 3, self.n_dp - 1, self.n_dp - 1)
+        self.keepers = 2 * (self.rows // 8) // self.mat
         groups = [(name, g) for name in ("core sum", "plane sum") for g in range(3)]
         groups += [("line sum", g) for g in range(4)]
         common = ["hidden", "hidden on", "lists", "own", "line", "plane", "dyn h", "dyn m", "small", "small on"]
         common += groups
         kinds = [(name, kind) for name in ("pack", "x") for kind in ("own", "on")]
-        tiles = [(name, k) for name in ("tiles", "tiles on") for k in range(3)]
+        tiles = [(name, k) for name in ("tiles", "sac g") for k in range(3)]
         sent = common + tiles + kinds
         self.sent = {name: at for at, name in enumerate(sent)}
         self.departures = len(sent)
+        for k in range(3):
+            self.sent["sac x", k] = self.departures
+            self.departures += self.n_dp
         self.here, self.arrivals = {}, 0
+        tiles += [("sac x", k) for k in range(3)]
         tiles += [("pack", "sibling"), ("x", "sibling")]
         for name in common + tiles:
             self.here[name] = self.arrivals
@@ -554,15 +560,18 @@
         for part in (1, 3) if group == 1 else (group,):
             line_peers(lambda peer: line_sum(part, peer).start())
 
-    def tile_copy(k, peer):
-        name = ("tiles", k)
+    def tile_copy(k):
+        name, owner = ("tiles", k), lay.owners[k]
         src = totals[k].at[pl.ds(0, lay.mat)]
-        return on_plane(src, mg.at[k, core, like], send.at[sent[name]], recv.at[here_at[name]], peer)
-
-    def tiles_on(k):
-        name = ("tiles on", k)
-        view = mg.at[k, core]
-        return on_plane(view, view, send.at[sent[name]], recv.at[here_at[name]], sibling)
+        return on_plane(src, mg.at[k, me], send.at[sent[name]], recv.at[here_at[name]], owner)
+
+    def keep_copy(k, peer):
+        name = ("sac g", k)
+        view = sac_g.at[side, k, pl.ds(local_tile, lay.mat)]
+        return on_plane(view, view, send.at[sent[name]], recv.at[here_at[name]], peer)
+
+    def kept_bytes(number):
+        return mg.at[0, pl.ds(0, number)]
 
     small_at = (core * lay.half + like) * lay.sml
 
@@ -588,8 +597,16 @@
             like_peers(lambda peer: small_copy(peer).start())
             small[pl.ds(small_at, lay.sml)] = whole
         else:
-            like_peers(lambda peer: tile_copy(part, peer).start())
-            mg[part, core, like] = whole
+            pl.when(me != lay.owners[part])(tile_copy(part).start)
+
+            @pl.when(me == lay.owners[part])
+            def _():
+                mg[part, me] = whole
+
+            @pl.when(z == keeper_z)
+            def _():
+                sac_g[side, part, pl.ds(local_tile, lay.mat)] = whole
+                plane_peers(lambda peer: keep_copy(part, peer).start())
 
     def chain(group):
         def end():
@@ -597,11 +614,8 @@
                 fold_end(part)
 
         def turn():
-            has_come(mg.at[group, 0, pl.ds(0, lay.half - 1)], ("tiles", group))
-            tiles_on(group).start()
-            if group == 1:
-                has_come(small.at[pl.ds(0, (lay.half - 1) * lay.sml)], "small")
-                small_on().start()
+            has_come(small.at[pl.ds(0, (lay.half - 1) * lay.sml)], "small")
+            small_on().start()
 
         return [
             lambda: core_sum(group).start(),
@@ -880,16 +894,15 @@
     mine_rows = pl.ds(pl.multiple_of(z * lay.rows, lay.rows), lay.rows)
 
     def take_matrix(k):
-        tiles_on(k).wait_recv()
+        has_come(mg.at[k, pl.ds(0, n_dp - 1)], ("tiles", k))
         for chunk in range(n_dp):
             tile = chunk * lay.mat
             half, row = tile // 32, tile % 32
             at = slice(row * 8, (row + lay.mat) * 8)
-            piece = mg[k, chunk % 2, chunk // 2].reshape(lay.mat * 8, 128)
+            piece = mg[k, chunk].reshape(lay.mat * 8, 128)
             mat[k, at, half * 128 : (half + 1) * 128] = piece / total
         normalise(mat.at[k])
 
-    chains[2][4]()
     chains[0][3]()
 
     @pl.when(is_dyn)
@@ -918,25 +931,60 @@
             dmat[at, 0:HDYN] = MOMENTUM * dmg[block] + dacc_h[at, 0:HDYN] / total
         normalise(dmat)
 
+    def sac_x_copy(k, src, peer):
+        name = ("sac x", k)
+        return on_plane(src, sac_x.at[k], send.at[sent[name] + peer], recv.at[here_at[name]], peer)
+
+    def own_x(k):
+        return mat.at[k, mine_rows]
+
+    def passes_x(k):
+        return jnp.logical_and(core == lay.owners[k] % 2, me != lay.owners[k])
+
+    def receive_sac(k):
+        pl.when(me != lay.owners[k])(sac_x_copy(k, sac_x.at[k], sibling).wait_recv)
+        pl.when(passes_x(k))(sac_x_copy(k, sac_x.at[k], sibling).start)
+
+    def own_matrix(k, before):
+        take_matrix(k)
+        schulz([mat.at[k]], NS_ITERS, before)
+        sac_x[k] = mat[k, mine_rows, :]
+        like_peers(lambda peer: sac_x_copy(k, own_x(k), peer).start())
+        sac_x_copy(k, own_x(k), sibling).start()
+
     def sum_end(step):
-        @pl.when(step == 3)
-        def _():
-            chains[0][4]()
-            chains[1][3]()
-
-    take_matrix(2)
+        pl.when(step == 2)(chains[1][3])
+        pl.when(step == NS_ITERS - 1)(chains[1][4])
+
+    def pass_on(step):
+        pl.when(step == 2)(functools.partial(hand_on, "pack"))
+        pl.when(step == NS_ITERS - 1)(functools.partial(hand_on, "x"))
 
     @pl.when(is_dyn)
     def _():
-        schulz([dmat, mat.at[2]], NS_ITERS, sum_end)
+        schulz([dmat], NS_ITERS, sum_end)
         rows = line_rows(dmat)
         drow_x[...] = rows
         dyn_x[dyn_e] = rows
         give("x", drow_x)
 
-    @pl.when(jnp.logical_not(is_dyn))
+    if lay.owners[0] >= MEMBERS:
+        @pl.when(jnp.logical_not(jnp.logical_or(is_dyn, me == lay.owners[1])))
+        def _():
+            chains[1][3]()
+            chains[1][4]()
+
+    pl.when(me == lay.owners[0])(functools.partial(own_matrix, 0, pass_on))
+
+    @pl.when(me == lay.owners[1])
     def _():
-        schulz([mat.at[2]], NS_ITERS, sum_end)
+        own_matrix(2, sum_end)
+        own_matrix(1, pass_on)
+
+    @pl.when(jnp.logical_and(me != lay.owners[0], me != lay.owners[1]))
+    def _():
+        hand_on("pack")
+        hand_on("x")
 
     def sent_early():
         has_sent(wg.at[pl.ds(0, n_blk - 1), :, half_rows], "hidden")
@@ -957,24 +1005,15 @@
         for part in range(4):
             has_sent(line_bytes(part), ("line sum", part))
 
-    def pass_on(step):
-        pl.when(step == 2)(functools.partial(hand_on, "pack"))
-        pl.when(step == NS_ITERS - 1)(functools.partial(hand_on, "x"))
-
-    chains[1][4]()
-    for k in range(2):
-        take_matrix(k)
-    schulz([mat.at[0], mat.at[1]], NS_ITERS, pass_on)
-    for k in range(3):
-        sac_x[k] = mat[k, mine_rows, :]
-        for half in range(2):
-            for piece in range(lay.rows // 8 // lay.mat):
-                chunk = (half * 32 + z * (lay.rows // 8)) // lay.mat + piece
-                kept = mg[k, lax.rem(chunk, 2), chunk // 2]
-                sac_g[half, k, piece * lay.mat : (piece + 1) * lay.mat] = kept
-
     sent_early()
+    for k in (2, 0, 1):
+        receive_sac(k)
+
     small_on().wait_recv()
+    for number, test in ((lay.keepers - 1, z == keeper_z), (lay.keepers, z != keeper_z)):
+        for k in range(3):
+            pl.when(test)(functools.partial(has_come, kept_bytes(number), ("sac g", k)))
+
     from_sibling("pack")
     from_sibling("x")
 
@@ -984,8 +1023,14 @@
     gave("x")
 
     for k in range(3):
-        has_sent(mg.at[k, 0, pl.ds(0, lay.half - 1)], ("tiles", k))
-        tiles_on(k).wait_send()
+        pl.when(me != lay.owners[k])(tile_copy(k).wait_send)
+        pl.when(z == keeper_z)(functools.partial(has_sent, kept_bytes(n_dp - 1), ("sac g", k)))
+        pl.when(passes_x(k))(sac_x_copy(k, sac_x.at[k], sibling).wait_send)
+
+        @pl.when(me == lay.owners[k])
+        def _():
+            like_peers(lambda peer: sac_x_copy(k, own_x(k), peer).wait_send())
+            sac_x_copy(k, own_x(k), sibling).wait_send()
 
 
 def adamw(weights, first, second, gradient):
@@ -1156,7 +1201,7 @@
         *[vm(n_blk, chunk, 8, 128) for chunk in lay.chunks],
         *[vm(chunk, 8, 128) for chunk in lay.chunks],
         *[vm(chunk, 8, 128) for chunk in lay.chunks],
-        vm(3, 2, lay.half, lay.mat, 8, 128),
+        vm(3, n_dp, lay.mat, 8, 128),
         vm(3, HSAC, HSAC),
         vm(HSAC, 8),
         vm(HSAC + 16, HSAC),

time: 61.7 us -> 64.3 us (1.042)
  Pallas kernels: 59.7 us -> 62.2 us
    pallas_call x1, Pallas kernels: 57.6 us -> 60.1 us  [shards(): pl.pallas_call(functools.partial(main_kernel, lay), out_shape=out_shape,...]
where the time goes in v12:
time: 64.3 us; the launch traced here: 63.9 us
  Pallas kernels  62.2 us (97%)
  between operations  1.05 us (2%)
    pallas_call x1, Pallas kernels, shards(): pl.pallas_call(functools.partial(main_kernel, lay), out_shape=out_shape,...  60.1 us
    pallas_call x1, Pallas kernels, shards(): pl.pallas_call(functools.partial(update_kernel, lay), out_shape=tuple(new...  2.11 us

profile of v12, /device:TPU:0, one launch (start us, length us, event | category | flops | bytes accessed | tf_op | source)
XLA Modules:
  0.0 63.9 jit_solution(2715905685003560273)
XLA Ops:
  0.7 0.0 copy-start
  0.7 0.0 copy-start.1
  0.7 0.0 copy-start.2
  0.7 0.0 copy-start.3
  0.7 0.0 copy-start.4
  0.7 0.0 copy-start.5
  0.7 0.0 copy-start.6
  0.7 0.0 copy-start.7
  0.8 0.0 copy-start.8
  0.8 0.0 copy-start.9
  0.8 0.0 copy-start.10
  0.8 0.0 copy-start.11
  0.8 0.0 copy-start.12
  0.8 0.0 copy-start.13
  0.8 0.0 copy-start.14
  0.8 0.0 copy-start.15
  0.8 0.0 copy-start.16
  0.8 0.0 copy-start.17
  0.9 0.0 copy-start.18
  0.9 0.0 copy-start.19
  0.9 0.0 copy-start.20
  0.9 0.0 copy-start.23
  0.9 60.1 %step.1 = (f32[2,3,8,8,128]{4,3,2,1,0:T(8,128)S(1)}, f32[3,64,256]{2,1,0:T(8,128)S(1)}, f32[7,50,200]{2,1,0:T(8,128)S(1)}, f32[7,128,256]{2,1,0:T(8,128)S(1)}, f...) custom-call(f32[42,3648]{1,0:T(8,128)} %refs_0_.1, f32[42,1216]{1,0:T(8,128)} %refs_1_.1, s32[8,8]{1,0:T(8,128)} %refs_2_.1, ...), custom_call_target="tpu_custom_call" | custom-call | tf_op jit(solution)/shard_map/step/pallas_call | solution.py:1223
  61.0 0.0 copy-start.22
  61.1 0.0 copy-start.21
  61.1 0.0 copy-done
  61.1 0.0 copy-done.1
  61.1 0.0 copy-done.2
  61.1 0.0 copy-done.3
  61.1 0.0 copy-done.4
  61.1 0.0 copy-done.5
  61.1 0.0 copy-done.6
  61.1 0.0 copy-done.7
  61.1 0.0 copy-done.8
  61.2 0.0 copy-done.9
  61.2 0.0 copy-done.10
  61.2 0.0 copy-done.11
  61.2 0.0 copy-done.12
  61.2 0.0 copy-done.13
  61.2 0.0 copy-done.14
  61.2 0.0 copy-done.15
  61.2 0.0 copy-done.16
  61.2 0.0 copy-done.17
  61.2 0.0 copy-done.18
  61.3 0.0 copy-done.19
  61.3 0.0 copy-done.20
  61.3 0.0 copy-done.23
  61.3 0.4 copy-done.22
  61.7 0.0 copy-done.21
  61.7 2.1 %update.1 = (f32[3,64,256]{2,1,0:T(8,128)}, f32[3,64,256]{2,1,0:T(8,128)}, f32[7,50,200]{2,1,0:T(8,128)}, f32[7,50,200]{2,1,0:T(8,128)}, f32[23,2,256]{2,1,0:T(2...) custom-call(f32[2,3,8,8,128]{4,3,2,1,0:T(8,128)S(1)} %get-tuple-elem, ...), custom_call_target="tpu_custom_call" | custom-call | tf_op jit(solution)/shard_map/update/pallas_call | solution.py:1243
Async XLA Ops:
  0.7 60.4 %copy-start = (f32[7,50,200]{2,1,0:T(8,128)S(1)}, f32[7,50,200]{2,1,0:T(8,128)}, u32[]{:S(2)}) copy-start(f32[7,50,200]{2,1,0:T(8,128)} %refs_7_.3) | copy-start | bytes 840004
  0.7 60.4 %copy-start.1 = (f32[7,50,200]{2,1,0:T(8,128)S(1)}, f32[7,50,200]{2,1,0:T(8,128)}, u32[]{:S(2)}) copy-start(f32[7,50,200]{2,1,0:T(8,128)} %refs_8_.3) | copy-start | bytes 840004
  0.7 60.4 %copy-start.2 = (f32[7,200,36]{1,2,0:T(8,128)S(1)}, f32[7,200,36]{1,2,0:T(8,128)}, u32[]{:S(2)}) copy-start(f32[7,200,36]{1,2,0:T(8,128)} %param.60) | copy-start | bytes 604804
  0.7 60.4 %copy-start.3 = (f32[3,64,256]{2,1,0:T(8,128)S(1)}, f32[3,64,256]{2,1,0:T(8,128)}, u32[]{:S(2)}) copy-start(f32[3,64,256]{2,1,0:T(8,128)} %refs_6_.3) | copy-start | bytes 589828
  0.7 60.4 %copy-start.4 = (f32[7,23,200]{2,1,0:T(8,128)S(1)}, f32[7,23,200]{2,1,0:T(8,128)}, u32[]{:S(2)}) copy-start(f32[7,23,200]{2,1,0:T(8,128)} %refs_15_.1) | copy-start | bytes 386404
  0.7 60.4 %copy-start.5 = (f32[7,200,36]{1,2,0:T(8,128)S(1)}, f32[7,200,36]{1,2,0:T(8,128)}, u32[]{:S(2)}) copy-start(f32[7,200,36]{1,2,0:T(8,128)} %param.61) | copy-start | bytes 604804
  0.7 60.4 %copy-start.6 = (f32[7,200,36]{1,2,0:T(8,128)S(1)}, f32[7,200,36]{1,2,0:T(8,128)}, u32[]{:S(2)}) copy-start(f32[7,200,36]{1,2,0:T(8,128)} %param.62) | copy-start | bytes 604804
  0.7 60.4 %copy-start.7 = (f32[2,23,256]{2,0,1:T(2,128)S(1)}, f32[2,23,256]{2,0,1:T(2,128)}, u32[]{:S(2)}) copy-start(f32[2,23,256]{2,0,1:T(2,128)} %param.45) | copy-start | bytes 141316
  0.8 60.4 %copy-start.8 = (f32[7,23,200]{2,1,0:T(8,128)S(1)}, f32[7,23,200]{2,1,0:T(8,128)}, u32[]{:S(2)}) copy-start(f32[7,23,200]{2,1,0:T(8,128)} %refs_16_.3) | copy-start | bytes 386404
  0.8 60.4 %copy-start.9 = (f32[7,23,200]{2,1,0:T(8,128)S(1)}, f32[7,23,200]{2,1,0:T(8,128)}, u32[]{:S(2)}) copy-start(f32[7,23,200]{2,1,0:T(8,128)} %refs_17_.1) | copy-start | bytes 386404
  0.8 60.4 %copy-start.10 = (f32[17,256]{1,0:T(8,128)S(1)}, f32[17,256]{1,0:T(8,128)}, u32[]{:S(2)}) copy-start(f32[17,256]{1,0:T(8,128)} %refs_12_.3) | copy-start | bytes 52228
  0.8 60.4 %copy-start.11 = (f32[4639]{0:T(1024)S(1)}, f32[4639]{0:T(1024)}, u32[]{:S(2)}) copy-start(f32[4639]{0:T(1024)} %refs_27_.1) | copy-start | bytes 55672
  0.8 60.4 %copy-start.12 = (f32[256,12]{0,1:T(8,128)S(1)}, f32[256,12]{0,1:T(8,128)}, u32[]{:S(2)}) copy-start(f32[256,12]{0,1:T(8,128)} %param.57) | copy-start | bytes 36868
  0.8 60.4 %copy-start.13 = (f32[2,23,256]{2,0,1:T(2,128)S(1)}, f32[2,23,256]{2,0,1:T(2,128)}, u32[]{:S(2)}) copy-start(f32[2,23,256]{2,0,1:T(2,128)} %param.46) | copy-start | bytes 141316
  0.8 60.4 %copy-start.14 = (f32[2,23,256]{2,0,1:T(2,128)S(1)}, f32[2,23,256]{2,0,1:T(2,128)}, u32[]{:S(2)}) copy-start(f32[2,23,256]{2,0,1:T(2,128)} %param.47) | copy-start | bytes 141316
  0.8 60.4 %copy-start.15 = (f32[17,256]{1,0:T(8,128)S(1)}, f32[17,256]{1,0:T(8,128)}, u32[]{:S(2)}) copy-start(f32[17,256]{1,0:T(8,128)} %refs_13_.3) | copy-start | bytes 52228
  0.8 60.4 %copy-start.16 = (f32[17,256]{1,0:T(8,128)S(1)}, f32[17,256]{1,0:T(8,128)}, u32[]{:S(2)}) copy-start(f32[17,256]{1,0:T(8,128)} %refs_14_.1) | copy-start | bytes 52228
  0.8 60.4 %copy-start.17 = (f32[4639]{0:T(1024)S(1)}, f32[4639]{0:T(1024)}, u32[]{:S(2)}) copy-start(f32[4639]{0:T(1024)} %refs_28_.1) | copy-start | bytes 55672
  0.9 60.4 %copy-start.18 = (f32[4639]{0:T(1024)S(1)}, f32[4639]{0:T(1024)}, u32[]{:S(2)}) copy-start(f32[4639]{0:T(1024)} %refs_29_.1) | copy-start | bytes 55672
  0.9 60.4 %copy-start.19 = (f32[256,12]{0,1:T(8,128)S(1)}, f32[256,12]{0,1:T(8,128)}, u32[]{:S(2)}) copy-start(f32[256,12]{0,1:T(8,128)} %param.58) | copy-start | bytes 36868
  0.9 60.4 %copy-start.20 = (f32[256,12]{0,1:T(8,128)S(1)}, f32[256,12]{0,1:T(8,128)}, u32[]{:S(2)}) copy-start(f32[256,12]{0,1:T(8,128)} %param.59) | copy-start | bytes 36868
  0.9 60.4 %copy-start.23 = (f32[2,256]{1,0:T(2,128)S(1)}, f32[2,256]{1,0:T(2,128)}, u32[]{:S(2)}) copy-start(f32[2,256]{1,0:T(2,128)} %refs_20_.3) | copy-start | bytes 6148
  61.0 0.7 %copy-start.22 = (f32[2,256]{1,0:T(2,128)S(1)}, f32[2,256]{1,0:T(2,128)}, u32[]{:S(2)}) copy-start(f32[2,256]{1,0:T(2,128)} %refs_19_.3) | copy-start | bytes 6148
  61.1 0.7 %copy-start.21 = (f32[2,256]{1,0:T(2,128)S(1)}, f32[2,256]{1,0:T(2,128)}, u32[]{:S(2)}) copy-start(f32[2,256]{1,0:T(2,128)} %refs_18_.3) | copy-start | bytes 6148

commit v13 on v11

--- a/solution.py
+++ b/solution.py
@@ -182,11 +182,21 @@
             self.arrivals += MEMBERS
 
 
+OPERANDS = 23
+FIRST, SECOND = 3, 16
+
+
 def main_kernel(lay, *refs):
+    n_in = OPERANDS
+    sources, held = refs[:n_in], refs[n_in : 2 * n_in]
     (
-        replay, model, requests, member, live, noise, sac_h, sac_m, dyn_h, dyn_m, crit_in, act_in,
-        dyn_in, crit_out, act_out, dyn_out, biases, targ_in, targ_hidden, targ_out, targ_bias,
-        sac_g, sac_x, dyn_x, dyn_s, small, count,
+        sac_h, requests, member, replay, live, model, noise, biases, targ_in, crit_in, act_in, targ_bias,
+        targ_hidden, crit_out, targ_out, act_out, dyn_h, dyn_m, crit_out_m, crit_out_v, sac_m, dyn_in, dyn_out,
+    ) = held
+    loads = refs[2 * n_in]
+    refs = refs[2 * n_in + 1 :]
+    (
+        sac_g, sac_x, dyn_x, dyn_s, small, count, crit_rows,
         wg, lists, asked, dhg, dmg, bk, xs, nz, ys, w1f, w1t, w1n, w2t, w2h, heads, head_t, head_f,
         rowbuf, wide, headcol, acc_h, acc_w, acc_c, acc_a, acc_m, acc_l, grid_0, grid_1, grid_2, core_0, core_1,
         core_2, from_0, from_1, from_2, zr_0, zr_1, zr_2, zf_0, zf_1, zf_2, sum_0, sum_1, sum_2, mg, mat, dcols, dacc_h, dacc_w, dacc_o, dacc_m, dacc_b, dacc_l, xt, dmat,
@@ -240,9 +250,20 @@
         at = recv.at[here_at[name]]
         on_plane(view, view, at, at, sibling).wait_recv()
 
+    copies = [
+        pltpu.make_async_copy(src, dst, loads.at[at]) for at, (src, dst) in enumerate(zip(sources, held))
+    ]
+
+    def arrived(begin, end):
+        for copy in copies[begin:end]:
+            copy.wait()
+
     barrier = pltpu.get_barrier_semaphore()
     plane_peers(lambda peer: pl.semaphore_signal(barrier, inc=1, device_id={"dp": peer}, device_id_type=MESH))
     line_peers(lambda peer: pl.semaphore_signal(barrier, inc=1, device_id={"blk": peer}, device_id_type=MESH))
+    for copy in copies:
+        copy.start()
+    arrived(0, FIRST)
     wg[0] = sac_h[...].astype(BF16)
     lists[0] = requests[...]
     lists[1] = member[...]
@@ -275,6 +296,7 @@
     def dyn_m_copy(peer):
         return on_line(dyn_m.at[dyn_e], dmg.at[z], send.at[sent["dyn m"]], recv.at[here_at["dyn m"]], peer)
 
+    arrived(FIRST, SECOND)
     alive = live[...].astype(F32).reshape(1, lay.model)
     data = replay[...]
     sums = jnp.sum(data[0:24], axis=1, keepdims=True)
@@ -301,14 +323,11 @@
     slots = in_lanes(0)
     wanted = jnp.maximum(slots, 0.0).astype(jnp.int32)
     hot = (rows_of((lay.replay, lay.real)) == wanted).astype(BF16)
-    padded = jnp.concatenate([data[0:40], jnp.zeros((8, lay.replay), F32)], 0)
-    tail = jnp.concatenate([data[40:FEAT], jnp.zeros((14, lay.replay), F32)], 0)
-    parts = [jnp.concatenate(pair, 0) for pair in zip(pieces(padded), pieces(tail))]
-    chosen = dot(jnp.concatenate(parts, 0), hot)
-    chosen = chosen[0:64] + chosen[64:128] + chosen[128:192]
+    padded = jnp.concatenate([data, jnp.zeros((48 - FEAT, lay.replay), F32)], 0)
+    chosen = dot(jnp.concatenate(pieces(padded), 0), hot)
+    chosen = chosen[0:48] + chosen[48:96] + chosen[96:144]
     mine = me * n_blk
-    bk[mine, 0:40, 0 : lay.real] = chosen[0:40]
-    bk[mine, 40:FEAT, 0 : lay.real] = chosen[48:50]
+    bk[mine, 0:FEAT, 0 : lay.real] = chosen[0:FEAT]
     bk[mine, 42:43, 0 : lay.real] = (slots >= 0.0).astype(F32)
     bk[mine, 43:44, 0 : lay.real] = in_lanes(1)
     bk[mine, 44:48, 0 : lay.real] = jnp.zeros((4, lay.real), F32)
@@ -335,6 +354,12 @@
 
     plane_peers(lambda peer: block_own(peer).start())
     line_peers(lambda peer: block_line(peer).start())
+
+    arrived(SECOND, n_in)
+    crit_rows[0:2, :] = crit_out[...]
+    crit_rows[2:4, :] = crit_out_m[...]
+    crit_rows[4:6, :] = crit_out_v[...]
+    crit_rows[6:8, :] = jnp.zeros((2, HSAC), F32)
 
     @pl.when(is_dyn)
     def _():
@@ -988,6 +1013,11 @@
         tiles_on(k).wait_send()
 
 
+def ordered(lay, n_in, n_out, *refs):
+    inputs, outputs, scratch = refs[:n_in], refs[n_in : n_in + n_out], refs[n_in + n_out :]
+    main_kernel(lay, *inputs, *scratch[: n_in + 1], *outputs, *scratch[n_in + 1 :])
+
+
 def adamw(weights, first, second, gradient):
     first = BETA_FIRST * first + (1.0 - BETA_FIRST) * gradient
     second = BETA_SECOND * second + (1.0 - BETA_SECOND) * gradient * gradient
@@ -999,8 +1029,8 @@
 
 def update_kernel(lay, *refs):
     (
-        sac_g, sac_x, dyn_x, dyn_s, small, count, sac_h, dyn_h, dyn_m,
-        ci, ci_m, ci_v, ai, ai_m, ai_v, di, di_m, di_v, co, co_m, co_v, ao, ao_m, ao_v,
+        sac_g, sac_x, dyn_x, dyn_s, small, count, crit_rows, sac_h, dyn_h, dyn_m,
+        ci, ci_m, ci_v, ai, ai_m, ai_v, di, di_m, di_v, ao, ao_m, ao_v,
         do, do_m, do_v, bi, bi_m, bi_v,
         sac_new, sac_mom, dyn_new, dyn_mom, ci_n, ci_mn, ci_vn, ai_n, ai_mn, ai_vn, di_n, di_mn,
         di_vn, co_n, co_mn, co_vn, ao_n, ao_mn, ao_vn, do_n, do_mn, do_vn, bi_n, bi_mn, bi_vn,
@@ -1044,7 +1074,8 @@
     for at, row in ((slice(0, ACT), slice(1, 1 + ACT)), (slice(ACT, 2 * ACT), slice(9, 9 + ACT))):
         store((ao_n, ao_mn, ao_vn), at, adamw(ao[at], ao_m[at], ao_v[at], grad[row] / total))
     grad = rows(R_OUT, 8)
-    store((co_n, co_mn, co_vn), ..., adamw(co[...], co_m[...], co_v[...], grad[0:2] / total))
+    held = [crit_rows[2 * at : 2 * at + 2, :] for at in range(3)]
+    store((co_n, co_mn, co_vn), ..., adamw(*held, grad[0:2] / total))
     bg[:, CB2 : CB2 + HSAC] = grad[2:3]
     bg[:, CB2 + HSAC : CB2 + 2 * HSAC] = grad[3:4]
     bg[:, AB2 : AB2 + HSAC] = grad[4:5]
@@ -1104,10 +1135,10 @@
         return pltpu.with_memory_space_constraint(value, pltpu.VMEM)
 
     inputs = (
-        replay, model_rows, requests, member_of, model_live, jnp.transpose(noise, (2, 0, 1)),
-        sac_hidden, sac_hidden_mom, dyn_hidden, dyn_hidden_mom, flip(crit_in), act_in, dyn_in,
-        crit_out, swap(act_out), swap(dyn_out), biases, flip(targ_in), targ_hidden, targ_out,
-        targ_bias,
+        sac_hidden, requests, member_of, replay, model_live, model_rows, jnp.transpose(noise, (2, 0, 1)),
+        biases, flip(targ_in), flip(crit_in), act_in, targ_bias, targ_hidden, crit_out, targ_out,
+        swap(act_out), dyn_hidden, dyn_hidden_mom, crit_out_m, crit_out_v, sac_hidden_mom, dyn_in,
+        swap(dyn_out),
     )
     shape = jax.ShapeDtypeStruct
     rows, drows = lay.rows, lay.drows
@@ -1118,6 +1149,7 @@
         pltpu.VMEM((MEMBERS, D_ROWS, HSAC), F32),
         pltpu.VMEM((32, 8, 128), F32),
         pltpu.VMEM((8, 128), F32),
+        pltpu.VMEM((8, HSAC), F32),
     )
 
     def vm(*dims, kind=F32):
@@ -1174,13 +1206,15 @@
         vm(HSAC, 48, kind=BF16),
     ]
     scratch += [pltpu.SemaphoreType.DMA((lay.departures,)), pltpu.SemaphoreType.DMA((lay.arrivals,))]
+    held = [pltpu.VMEM(value.shape, value.dtype) for value in inputs]
+    held.append(pltpu.SemaphoreType.DMA((len(inputs),)))
     varying = 4 * (lay.n_dev * 48 * lay.width + 72 * lay.batch + 48 * lay.replay)
     gathered = pl.pallas_call(
-        functools.partial(main_kernel, lay),
+        functools.partial(ordered, lay, len(inputs), len(out_shape)),
         out_shape=out_shape,
-        in_specs=[spec] * len(inputs),
+        in_specs=[pl.BlockSpec(memory_space=pl.ANY)] * len(inputs),
         out_specs=[spec] * len(out_shape),
-        scratch_shapes=scratch,
+        scratch_shapes=held + scratch,
         compiler_params=pltpu.CompilerParams(
             collective_id=0, has_side_effects=True, vmem_limit_bytes=26 * 2**20 + varying
         ),
@@ -1189,11 +1223,12 @@
     params = (
         sac_hidden, dyn_hidden, dyn_hidden_mom,
         flip(crit_in), flip(crit_in_m), flip(crit_in_v), act_in, act_in_m, act_in_v,
-        dyn_in, dyn_in_m, dyn_in_v, crit_out, crit_out_m, crit_out_v,
+        dyn_in, dyn_in_m, dyn_in_v,
         swap(act_out), swap(act_out_m), swap(act_out_v),
         swap(dyn_out), swap(dyn_out_m), swap(dyn_out_v), biases, biases_m, biases_v,
     )
-    new_shape = [shape(sac_hidden.shape, F32)] + [shape(value.shape, F32) for value in params]
+    new_shape = [shape(sac_hidden.shape, F32)] + [shape(value.shape, F32) for value in params[:12]]
+    new_shape += [shape(crit_out.shape, F32)] * 3 + [shape(value.shape, F32) for value in params[12:]]
     new_shape += [shape((1, 1), F32)] * 2
     out = pl.pallas_call(
         functools.partial(update_kernel, lay),

time: 61.7 us -> 59.1 us (0.958)
  Pallas kernels: 59.7 us -> 57.1 us
    pallas_call x1, Pallas kernels: 57.6 us -> 54.8 us  [shards(): pl.pallas_call(functools.partial(ordered, lay, len(inputs), len(out_shape...]
where the time goes in v13:
time: 59.1 us; the launch traced here: 58.3 us
  Pallas kernels  57.1 us (97%)
  between operations  1.18 us (2%)
    pallas_call x1, Pallas kernels, shards(): pl.pallas_call(functools.partial(ordered, lay, len(inputs), len(out_shape...  54.8 us
    pallas_call x1, Pallas kernels, shards(): pl.pallas_call(functools.partial(update_kernel, lay), out_shape=tuple(new...  2.22 us

profile of v13, /device:TPU:0, one launch (start us, length us, event | category | flops | bytes accessed | tf_op | source)
XLA Modules:
  0.0 58.3 jit_solution(16282003281969004917)
XLA Ops:
  0.7 0.0 copy-start
  0.7 0.0 copy-start.1
  0.7 0.0 copy-start.2
  0.7 0.0 copy-start.3
  0.7 0.0 copy-start.4
  0.7 0.0 copy-start.5
  0.7 0.0 copy-start.6
  0.7 0.0 copy-start.7
  0.8 0.0 copy-start.8
  0.8 0.0 copy-start.9
  0.8 0.0 copy-start.10
  0.8 0.0 copy-start.11
  0.8 0.0 copy-start.12
  0.8 0.0 copy-start.13
  0.8 0.0 copy-start.14
  0.8 0.0 copy-start.15
  0.8 0.0 copy-start.16
  0.8 0.0 copy-start.17
  0.9 0.0 copy-start.18
  0.9 0.0 copy-start.19
  0.9 0.0 copy-start.20
  0.9 54.8 %step.1 = (f32[2,3,8,8,128]{4,3,2,1,0:T(8,128)S(1)}, f32[3,64,256]{2,1,0:T(8,128)S(1)}, f32[7,50,200]{2,1,0:T(8,128)S(1)}, f32[7,128,256]{2,1,0:T(8,128)S(1)}, f...) custom-call(f32[3,64,256]{2,1,0:T(8,128)} %refs_7_.3, s32[8,8]{1,0:T(8,128)} %refs_1_.1, ...), custom_call_target="tpu_custom_call" | custom-call | tf_op jit(solution)/shard_map/step/pallas_call | solution.py:1212
  55.7 0.0 copy-done
  55.7 0.0 copy-done.1
  55.8 0.0 copy-done.2
  55.8 0.0 copy-done.3
  55.8 0.0 copy-done.4
  55.8 0.0 copy-done.5
  55.8 0.0 copy-done.6
  55.8 0.0 copy-done.7
  55.8 0.0 copy-done.8
  55.8 0.0 copy-done.9
  55.8 0.0 copy-done.10
  55.8 0.0 copy-done.11
  55.9 0.0 copy-done.12
  55.9 0.0 copy-done.13
  55.9 0.0 copy-done.14
  55.9 0.0 copy-done.15
  55.9 0.0 copy-done.16
  55.9 0.0 copy-done.17
  55.9 0.0 copy-done.18
  55.9 0.0 copy-done.19
  55.9 0.0 copy-done.20
  55.9 2.2 %update.1 = (f32[3,64,256]{2,1,0:T(8,128)}, f32[3,64,256]{2,1,0:T(8,128)}, f32[7,50,200]{2,1,0:T(8,128)}, f32[7,50,200]{2,1,0:T(8,128)}, f32[23,2,256]{2,1,0:T(2...) custom-call(f32[2,3,8,8,128]{4,3,2,1,0:T(8,128)S(1)} %get-tuple-elem, ...), custom_call_target="tpu_custom_call" | custom-call | tf_op jit(solution)/shard_map/update/pallas_call | solution.py:1233
Async XLA Ops:
  0.7 55.1 %copy-start = (f32[7,50,200]{2,1,0:T(8,128)S(1)}, f32[7,50,200]{2,1,0:T(8,128)}, u32[]{:S(2)}) copy-start(f32[7,50,200]{2,1,0:T(8,128)} %refs_8_.1) | copy-start | bytes 840004
  0.7 55.1 %copy-start.1 = (f32[7,50,200]{2,1,0:T(8,128)S(1)}, f32[7,50,200]{2,1,0:T(8,128)}, u32[]{:S(2)}) copy-start(f32[7,50,200]{2,1,0:T(8,128)} %refs_9_.1) | copy-start | bytes 840004
  0.7 55.1 %copy-start.2 = (f32[7,200,36]{1,2,0:T(8,128)S(1)}, f32[7,200,36]{1,2,0:T(8,128)}, u32[]{:S(2)}) copy-start(f32[7,200,36]{1,2,0:T(8,128)} %param.60) | copy-start | bytes 604804
  0.7 55.1 %copy-start.3 = (f32[3,64,256]{2,1,0:T(8,128)S(1)}, f32[3,64,256]{2,1,0:T(8,128)}, u32[]{:S(2)}) copy-start(f32[3,64,256]{2,1,0:T(8,128)} %refs_7_.3) | copy-start | bytes 589828
  0.7 55.1 %copy-start.4 = (f32[7,23,200]{2,1,0:T(8,128)S(1)}, f32[7,23,200]{2,1,0:T(8,128)}, u32[]{:S(2)}) copy-start(f32[7,23,200]{2,1,0:T(8,128)} %refs_16_.3) | copy-start | bytes 386404
  0.7 55.1 %copy-start.5 = (f32[7,200,36]{1,2,0:T(8,128)S(1)}, f32[7,200,36]{1,2,0:T(8,128)}, u32[]{:S(2)}) copy-start(f32[7,200,36]{1,2,0:T(8,128)} %param.61) | copy-start | bytes 604804
  0.7 55.1 %copy-start.6 = (f32[7,200,36]{1,2,0:T(8,128)S(1)}, f32[7,200,36]{1,2,0:T(8,128)}, u32[]{:S(2)}) copy-start(f32[7,200,36]{1,2,0:T(8,128)} %param.62) | copy-start | bytes 604804
  0.7 55.1 %copy-start.7 = (f32[2,23,256]{2,0,1:T(2,128)S(1)}, f32[2,23,256]{2,0,1:T(2,128)}, u32[]{:S(2)}) copy-start(f32[2,23,256]{2,0,1:T(2,128)} %param.45) | copy-start | bytes 141316
  0.8 55.1 %copy-start.8 = (f32[7,23,200]{2,1,0:T(8,128)S(1)}, f32[7,23,200]{2,1,0:T(8,128)}, u32[]{:S(2)}) copy-start(f32[7,23,200]{2,1,0:T(8,128)} %refs_17_.3) | copy-start | bytes 386404
  0.8 55.1 %copy-start.9 = (f32[7,23,200]{2,1,0:T(8,128)S(1)}, f32[7,23,200]{2,1,0:T(8,128)}, u32[]{:S(2)}) copy-start(f32[7,23,200]{2,1,0:T(8,128)} %refs_18_.3) | copy-start | bytes 386404
  0.8 55.1 %copy-start.10 = (f32[17,256]{1,0:T(8,128)S(1)}, f32[17,256]{1,0:T(8,128)}, u32[]{:S(2)}) copy-start(f32[17,256]{1,0:T(8,128)} %refs_13_.3) | copy-start | bytes 52228
  0.8 55.1 %copy-start.11 = (f32[4639]{0:T(1024)S(1)}, f32[4639]{0:T(1024)}, u32[]{:S(2)}) copy-start(f32[4639]{0:T(1024)} %refs_25_.1) | copy-start | bytes 55672
  0.8 55.1 %copy-start.12 = (f32[256,12]{0,1:T(8,128)S(1)}, f32[256,12]{0,1:T(8,128)}, u32[]{:S(2)}) copy-start(f32[256,12]{0,1:T(8,128)} %param.57) | copy-start | bytes 36868
  0.8 55.1 %copy-start.13 = (f32[2,23,256]{2,0,1:T(2,128)S(1)}, f32[2,23,256]{2,0,1:T(2,128)}, u32[]{:S(2)}) copy-start(f32[2,23,256]{2,0,1:T(2,128)} %param.46) | copy-start | bytes 141316
  0.8 55.1 %copy-start.14 = (f32[2,23,256]{2,0,1:T(2,128)S(1)}, f32[2,23,256]{2,0,1:T(2,128)}, u32[]{:S(2)}) copy-start(f32[2,23,256]{2,0,1:T(2,128)} %param.47) | copy-start | bytes 141316
  0.8 55.1 %copy-start.15 = (f32[17,256]{1,0:T(8,128)S(1)}, f32[17,256]{1,0:T(8,128)}, u32[]{:S(2)}) copy-start(f32[17,256]{1,0:T(8,128)} %refs_14_.3) | copy-start | bytes 52228
  0.8 55.1 %copy-start.16 = (f32[17,256]{1,0:T(8,128)S(1)}, f32[17,256]{1,0:T(8,128)}, u32[]{:S(2)}) copy-start(f32[17,256]{1,0:T(8,128)} %refs_15_.1) | copy-start | bytes 52228
  0.8 55.1 %copy-start.17 = (f32[4639]{0:T(1024)S(1)}, f32[4639]{0:T(1024)}, u32[]{:S(2)}) copy-start(f32[4639]{0:T(1024)} %refs_26_.1) | copy-start | bytes 55672
  0.9 55.1 %copy-start.18 = (f32[4639]{0:T(1024)S(1)}, f32[4639]{0:T(1024)}, u32[]{:S(2)}) copy-start(f32[4639]{0:T(1024)} %refs_27_.1) | copy-start | bytes 55672
  0.9 55.1 %copy-start.19 = (f32[256,12]{0,1:T(8,128)S(1)}, f32[256,12]{0,1:T(8,128)}, u32[]{:S(2)}) copy-start(f32[256,12]{0,1:T(8,128)} %param.58) | copy-start | bytes 36868
  0.9 55.1 %copy-start.20 = (f32[256,12]{0,1:T(8,128)S(1)}, f32[256,12]{0,1:T(8,128)}, u32[]{:S(2)}) copy-start(f32[256,12]{0,1:T(8,128)} %param.59) | copy-start | bytes 36868

commit v14 on v13

--- a/solution.py
+++ b/solution.py
@@ -22,7 +22,7 @@
 CAP = 8
 CRITIC_TILE = 640
 ACTOR_TILE = 640
-DYN_TILE = 512
+DYN_TILE = 1024
 ROWS = 32
 
 DISCOUNT = 0.99
@@ -801,11 +801,7 @@
         for ref in (dacc_h, dacc_w, dacc_o, dacc_m, dacc_b, dacc_l):
             ref[...] = jnp.zeros_like(ref)
 
-    in_dyn = {}
-    for at, event in (
-        (1, chains[0][2]), (1, chains[1][1]), (2, chains[2][3]), (dyn_tiles - 1, chains[1][2]),
-    ):
-        in_dyn.setdefault(min(at, dyn_tiles - 1), []).append(event)
+    in_dyn = {min(1, dyn_tiles - 1): [chains[0][2], chains[1][1], chains[2][3]]}
 
     @pl.loop(0, dyn_tiles)
     def _(tile):
@@ -914,8 +910,8 @@
             mat[k, at, half * 128 : (half + 1) * 128] = piece / total
         normalise(mat.at[k])
 
+    chains[1][2]()
     chains[2][4]()
-    chains[0][3]()
 
     @pl.when(is_dyn)
     def _():
@@ -944,10 +940,9 @@
         normalise(dmat)
 
     def sum_end(step):
-        @pl.when(step == 3)
-        def _():
-            chains[0][4]()
-            chains[1][3]()
+        pl.when(step == 1)(chains[0][3])
+        pl.when(step == 3)(chains[1][3])
+        pl.when(step == NS_ITERS - 1)(chains[0][4])
 
     take_matrix(2)
 
@@ -986,6 +981,7 @@
         pl.when(step == 2)(functools.partial(hand_on, "pack"))
         pl.when(step == NS_ITERS - 1)(functools.partial(hand_on, "x"))
 
+    sent_early()
     chains[1][4]()
     for k in range(2):
         take_matrix(k)
@@ -998,7 +994,6 @@
                 kept = mg[k, lax.rem(chunk, 2), chunk // 2]
                 sac_g[half, k, piece * lay.mat : (piece + 1) * lay.mat] = kept
 
-    sent_early()
     small_on().wait_recv()
     from_sibling("pack")
     from_sibling("x")
@@ -1037,14 +1032,26 @@
         loss, counted, bg,
     ) = refs
     total = count[0:1, 0:1]
+
+    def store(outs, at, values):
+        for out, value in zip(outs, values):
+            out[at] = value
+
+    @pl.loop(0, MEMBERS)
+    def _(e):
+        grad = dyn_s[e, 0:IN, 0:HDYN] / total
+        store((di_n, di_mn, di_vn), e, adamw(di[e], di_m[e], di_v[e], grad))
+        grad = dyn_s[e, D_OUT : D_OUT + DOUT, 0:HDYN] / total
+        store((do_n, do_mn, do_vn), e, adamw(do[e], do_m[e], do_v[e], grad))
+        grad = dyn_s[e, D_HID : D_HID + dyn_m.shape[1], 0:HDYN] / total
+        dyn_mom[e] = MOMENTUM * dyn_m[e] + grad
+        dyn_new[e] = dyn_h[e] * (1.0 - MUON_RATE * MUON_DECAY) - MUON_RATE * dyn_x[e]
+
     for k in range(3):
         for side in range(2):
             tiles = sac_g[side, k].reshape(sac_mom.shape[1], 128)
             sac_mom[k, :, side * 128 : (side + 1) * 128] = tiles / total
     sac_new[...] = sac_h[...] * (1.0 - MUON_RATE * MUON_DECAY) - MUON_RATE * sac_x[...]
-    dyn_rows = dyn_s[:, D_HID : D_HID + dyn_m.shape[1], 0:HDYN]
-    dyn_mom[...] = MOMENTUM * dyn_m[...] + dyn_rows / total.reshape(1, 1, 1)
-    dyn_new[...] = dyn_h[...] * (1.0 - MUON_RATE * MUON_DECAY) - MUON_RATE * dyn_x[...]
 
     def rows(row, number):
         def tile(at):
@@ -1056,10 +1063,6 @@
             at = side * (R_SMALL // 8) + row // 8
             sides.append(jnp.concatenate([tile(at + more) for more in range(-(-number // 8))], 0))
         return jnp.concatenate(sides, 1)
-
-    def store(outs, at, values):
-        for out, value in zip(outs, values):
-            out[at] = value
 
     outs = (ci_n, ci_mn, ci_vn)
     for k in range(2):
@@ -1097,10 +1100,6 @@
         bg[:, DB2 + HDYN * e : DB2 + HDYN * (e + 1)] = pack[D_B2 : D_B2 + 1, 0:HDYN]
         bg[:, DB3 + DOUT * e : DB3 + DOUT * e + HALF] = pack[D_B3 : D_B3 + 1, 0:HALF]
         bg[:, DB3 + DOUT * e + HALF : DB3 + DOUT * (e + 1)] = pack[D_B3 : D_B3 + 1, 24 : 24 + HALF]
-        grad = pack[0:IN, 0:HDYN] / total
-        store((di_n, di_mn, di_vn), e, adamw(di[e], di_m[e], di_v[e], grad))
-        grad = pack[D_OUT : D_OUT + DOUT, 0:HDYN] / total
-        store((do_n, do_mn, do_vn), e, adamw(do[e], do_m[e], do_v[e], grad))
     bg[:, MAXLV : MAXLV + HALF] = up
     bg[:, MINLV : MINLV + HALF] = low
     lane = lax.broadcasted_iota(jnp.int32, (1, NB), 1)

time: 59.1 us -> 60.1 us (1.017)
  the two profiles are of different devices: /device:TPU:0 before, /device:TPU:11 now
where the time goes in v14:
time: 60.1 us; the launch traced here: 59.9 us
  Pallas kernels  58.8 us (98%)
  between operations  1.02 us (2%)
    pallas_call x1, Pallas kernels, shards(): pl.pallas_call(functools.partial(ordered, lay, len(inputs), len(out_shape...  56.2 us
    pallas_call x1, Pallas kernels, shards(): pl.pallas_call(functools.partial(update_kernel, lay), out_shape=tuple(new...  2.59 us

profile of v14, /device:TPU:11, one launch (start us, length us, event | category | flops | bytes accessed | tf_op | source)
XLA Modules:
  0.0 59.9 jit_solution(4845957209185023666)
XLA Ops:
  0.7 0.0 copy-start
  0.7 0.0 copy-start.1
  0.7 0.0 copy-start.2
  0.7 0.0 copy-start.3
  0.7 0.0 copy-start.4
  0.7 0.0 copy-start.5
  0.7 0.0 copy-start.6
  0.7 0.0 copy-start.7
  0.8 0.0 copy-start.8
  0.8 0.0 copy-start.9
  0.8 0.0 copy-start.10
  0.8 0.0 copy-start.11
  0.8 0.0 copy-start.12
  0.8 0.0 copy-start.13
  0.8 0.0 copy-start.14
  0.8 0.0 copy-start.15
  0.8 0.0 copy-start.16
  0.8 0.0 copy-start.17
  0.9 0.0 copy-start.18
  0.9 0.0 copy-start.19
  0.9 0.0 copy-start.20
  0.9 56.2 %step.1 = (f32[2,3,8,8,128]{4,3,2,1,0:T(8,128)S(1)}, f32[3,64,256]{2,1,0:T(8,128)S(1)}, f32[7,50,200]{2,1,0:T(8,128)S(1)}, f32[7,128,256]{2,1,0:T(8,128)S(1)}, f...) custom-call(f32[3,64,256]{2,1,0:T(8,128)} %refs_7_.3, s32[8,8]{1,0:T(8,128)} %refs_1_.1, ...), custom_call_target="tpu_custom_call" | custom-call | tf_op jit(solution)/shard_map/step/pallas_call | solution.py:1211
  57.1 0.0 copy-done
  57.1 0.0 copy-done.1
  57.1 0.0 copy-done.2
  57.1 0.0 copy-done.3
  57.2 0.0 copy-done.4
  57.2 0.0 copy-done.5
  57.2 0.0 copy-done.6
  57.2 0.0 copy-done.7
  57.2 0.0 copy-done.8
  57.2 0.0 copy-done.9
  57.2 0.0 copy-done.10
  57.2 0.0 copy-done.11
  57.2 0.0 copy-done.12
  57.2 0.0 copy-done.13
  57.3 0.0 copy-done.14
  57.3 0.0 copy-done.15
  57.3 0.0 copy-done.16
  57.3 0.0 copy-done.17
  57.3 0.0 copy-done.18
  57.3 0.0 copy-done.19
  57.3 0.0 copy-done.20
  57.3 2.6 %update.1 = (f32[3,64,256]{2,1,0:T(8,128)}, f32[3,64,256]{2,1,0:T(8,128)}, f32[7,50,200]{2,1,0:T(8,128)}, f32[7,50,200]{2,1,0:T(8,128)}, f32[23,2,256]{2,1,0:T(2...) custom-call(f32[2,3,8,8,128]{4,3,2,1,0:T(8,128)S(1)} %get-tuple-elem, ...), custom_call_target="tpu_custom_call" | custom-call | tf_op jit(solution)/shard_map/update/pallas_call | solution.py:1232
Async XLA Ops:
  0.7 56.4 %copy-start = (f32[7,50,200]{2,1,0:T(8,128)S(1)}, f32[7,50,200]{2,1,0:T(8,128)}, u32[]{:S(2)}) copy-start(f32[7,50,200]{2,1,0:T(8,128)} %refs_8_.1) | copy-start | bytes 840004
  0.7 56.4 %copy-start.1 = (f32[7,50,200]{2,1,0:T(8,128)S(1)}, f32[7,50,200]{2,1,0:T(8,128)}, u32[]{:S(2)}) copy-start(f32[7,50,200]{2,1,0:T(8,128)} %refs_9_.1) | copy-start | bytes 840004
  0.7 56.4 %copy-start.2 = (f32[7,200,36]{1,2,0:T(8,128)S(1)}, f32[7,200,36]{1,2,0:T(8,128)}, u32[]{:S(2)}) copy-start(f32[7,200,36]{1,2,0:T(8,128)} %param.60) | copy-start | bytes 604804
  0.7 56.4 %copy-start.3 = (f32[3,64,256]{2,1,0:T(8,128)S(1)}, f32[3,64,256]{2,1,0:T(8,128)}, u32[]{:S(2)}) copy-start(f32[3,64,256]{2,1,0:T(8,128)} %refs_7_.3) | copy-start | bytes 589828
  0.7 56.4 %copy-start.4 = (f32[7,23,200]{2,1,0:T(8,128)S(1)}, f32[7,23,200]{2,1,0:T(8,128)}, u32[]{:S(2)}) copy-start(f32[7,23,200]{2,1,0:T(8,128)} %refs_16_.3) | copy-start | bytes 386404
  0.7 56.4 %copy-start.5 = (f32[7,200,36]{1,2,0:T(8,128)S(1)}, f32[7,200,36]{1,2,0:T(8,128)}, u32[]{:S(2)}) copy-start(f32[7,200,36]{1,2,0:T(8,128)} %param.61) | copy-start | bytes 604804
  0.7 56.4 %copy-start.6 = (f32[7,200,36]{1,2,0:T(8,128)S(1)}, f32[7,200,36]{1,2,0:T(8,128)}, u32[]{:S(2)}) copy-start(f32[7,200,36]{1,2,0:T(8,128)} %param.62) | copy-start | bytes 604804
  0.7 56.4 %copy-start.7 = (f32[2,23,256]{2,0,1:T(2,128)S(1)}, f32[2,23,256]{2,0,1:T(2,128)}, u32[]{:S(2)}) copy-start(f32[2,23,256]{2,0,1:T(2,128)} %param.45) | copy-start | bytes 141316
  0.8 56.4 %copy-start.8 = (f32[7,23,200]{2,1,0:T(8,128)S(1)}, f32[7,23,200]{2,1,0:T(8,128)}, u32[]{:S(2)}) copy-start(f32[7,23,200]{2,1,0:T(8,128)} %refs_17_.3) | copy-start | bytes 386404
  0.8 56.4 %copy-start.9 = (f32[7,23,200]{2,1,0:T(8,128)S(1)}, f32[7,23,200]{2,1,0:T(8,128)}, u32[]{:S(2)}) copy-start(f32[7,23,200]{2,1,0:T(8,128)} %refs_18_.3) | copy-start | bytes 386404
  0.8 56.4 %copy-start.10 = (f32[17,256]{1,0:T(8,128)S(1)}, f32[17,256]{1,0:T(8,128)}, u32[]{:S(2)}) copy-start(f32[17,256]{1,0:T(8,128)} %refs_13_.3) | copy-start | bytes 52228
  0.8 56.4 %copy-start.11 = (f32[4639]{0:T(1024)S(1)}, f32[4639]{0:T(1024)}, u32[]{:S(2)}) copy-start(f32[4639]{0:T(1024)} %refs_25_.1) | copy-start | bytes 55672
  0.8 56.4 %copy-start.12 = (f32[256,12]{0,1:T(8,128)S(1)}, f32[256,12]{0,1:T(8,128)}, u32[]{:S(2)}) copy-start(f32[256,12]{0,1:T(8,128)} %param.57) | copy-start | bytes 36868
  0.8 56.4 %copy-start.13 = (f32[2,23,256]{2,0,1:T(2,128)S(1)}, f32[2,23,256]{2,0,1:T(2,128)}, u32[]{:S(2)}) copy-start(f32[2,23,256]{2,0,1:T(2,128)} %param.46) | copy-start | bytes 141316
  0.8 56.4 %copy-start.14 = (f32[2,23,256]{2,0,1:T(2,128)S(1)}, f32[2,23,256]{2,0,1:T(2,128)}, u32[]{:S(2)}) copy-start(f32[2,23,256]{2,0,1:T(2,128)} %param.47) | copy-start | bytes 141316
  0.8 56.4 %copy-start.15 = (f32[17,256]{1,0:T(8,128)S(1)}, f32[17,256]{1,0:T(8,128)}, u32[]{:S(2)}) copy-start(f32[17,256]{1,0:T(8,128)} %refs_14_.3) | copy-start | bytes 52228
  0.8 56.4 %copy-start.16 = (f32[17,256]{1,0:T(8,128)S(1)}, f32[17,256]{1,0:T(8,128)}, u32[]{:S(2)}) copy-start(f32[17,256]{1,0:T(8,128)} %refs_15_.1) | copy-start | bytes 52228
  0.8 56.4 %copy-start.17 = (f32[4639]{0:T(1024)S(1)}, f32[4639]{0:T(1024)}, u32[]{:S(2)}) copy-start(f32[4639]{0:T(1024)} %refs_26_.1) | copy-start | bytes 55672
  0.9 56.4 %copy-start.18 = (f32[4639]{0:T(1024)S(1)}, f32[4639]{0:T(1024)}, u32[]{:S(2)}) copy-start(f32[4639]{0:T(1024)} %refs_27_.1) | copy-start | bytes 55672
  0.9 56.4 %copy-start.19 = (f32[256,12]{0,1:T(8,128)S(1)}, f32[256,12]{0,1:T(8,128)}, u32[]{:S(2)}) copy-start(f32[256,12]{0,1:T(8,128)} %param.58) | copy-start | bytes 36868
  0.9 56.4 %copy-start.20 = (f32[256,12]{0,1:T(8,128)S(1)}, f32[256,12]{0,1:T(8,128)}, u32[]{:S(2)}) copy-start(f32[256,12]{0,1:T(8,128)} %param.59) | copy-start | bytes 36868

commit v15 on v13

--- a/solution.py
+++ b/solution.py
@@ -197,7 +197,7 @@
     refs = refs[2 * n_in + 1 :]
     (
         sac_g, sac_x, dyn_x, dyn_s, small, count, crit_rows,
-        wg, lists, asked, dhg, dmg, bk, xs, nz, ys, w1f, w1t, w1n, w2t, w2h, heads, head_t, head_f,
+        wg, lists, asked, dhg, dmg, bk, xs, nz, ys, ahead, w1f, w1t, w1n, w2t, w2h, heads, head_t, head_f,
         rowbuf, wide, headcol, acc_h, acc_w, acc_c, acc_a, acc_m, acc_l, grid_0, grid_1, grid_2, core_0, core_1,
         core_2, from_0, from_1, from_2, zr_0, zr_1, zr_2, zf_0, zf_1, zf_2, sum_0, sum_1, sum_2, mg, mat, dcols, dacc_h, dacc_w, dacc_o, dacc_m, dacc_b, dacc_l, xt, dmat,
         dpack, drow_x, bias, dhead, dhead_t, *rest,
@@ -667,6 +667,9 @@
         now_f = framed(0, IN, where)
         now_in = now_f.astype(BF16)
         weight = xs[42:43, where]
+        next_action, next_prob, _, _, _ = policy(framed(24, OBS, where).astype(BF16), 1, where)
+        ahead[0:8, where] = next_action
+        ys[1:2, where] = next_prob
         action, log_prob, bent, moved, (a1, da1, a2, da2) = policy(now_in, 0, where)
         judged_in = with_action(now_f, action)
         loss = alpha * log_prob - log_alpha * (log_prob + TARGET_ENTROPY)
@@ -703,11 +706,10 @@
 
         where = place_of(step, CRITIC_TILE)
         now_in = framed(0, IN, where).astype(BF16)
-        next_f = framed(24, OBS, where)
         reward = xs[23:24, where]
         done = xs[41:42, where]
-        next_action, next_prob, _, _, _ = policy(next_f.astype(BF16), 1, where)
-        aim_in = with_action(next_f, next_action)
+        aim_in = with_action(framed(24, OBS, where), ahead[0:8, where])
+        next_prob = ys[1:2, where]
         aim = jnp.minimum(critic(aim_in, 0)[0], critic(aim_in, 1)[0])
         target = reward + DISCOUNT * (1.0 - done) * (aim - alpha * next_prob)
         ys[0:1, where] = target
@@ -986,6 +988,7 @@
         pl.when(step == 2)(functools.partial(hand_on, "pack"))
         pl.when(step == NS_ITERS - 1)(functools.partial(hand_on, "x"))
 
+    sent_early()
     chains[1][4]()
     for k in range(2):
         take_matrix(k)
@@ -998,7 +1001,6 @@
                 kept = mg[k, lax.rem(chunk, 2), chunk // 2]
                 sac_g[half, k, piece * lay.mat : (piece + 1) * lay.mat] = kept
 
-    sent_early()
     small_on().wait_recv()
     from_sibling("pack")
     from_sibling("x")
@@ -1164,6 +1166,7 @@
         vm(lay.n_dev, 48, lay.width),
         vm(56, lay.batch),
         vm(2, 8, lay.batch),
+        vm(8, lay.batch),
         vm(8, lay.batch),
         vm(5, 32, HSAC),
         vm(5, HSAC, 32, kind=BF16),

time: 59.1 us -> 58.9 us (level)
  no operation moved by 1% of the time
where the time goes in v15:
time: 58.9 us; the launch traced here: 58.1 us
  Pallas kernels  56.9 us (97%)
  between operations  1.18 us (2%)
    pallas_call x1, Pallas kernels, shards(): pl.pallas_call(functools.partial(ordered, lay, len(inputs), len(out_shape...  54.6 us
    pallas_call x1, Pallas kernels, shards(): pl.pallas_call(functools.partial(update_kernel, lay), out_shape=tuple(new...  2.22 us

profile of v15, /device:TPU:0, one launch (start us, length us, event | category | flops | bytes accessed | tf_op | source)
XLA Modules:
  0.0 58.1 jit_solution(15249940389014054625)
XLA Ops:
  0.7 0.0 copy-start
  0.7 0.0 copy-start.1
  0.7 0.0 copy-start.2
  0.7 0.0 copy-start.3
  0.7 0.0 copy-start.4
  0.7 0.0 copy-start.5
  0.7 0.0 copy-start.6
  0.7 0.0 copy-start.7
  0.8 0.0 copy-start.8
  0.8 0.0 copy-start.9
  0.8 0.0 copy-start.10
  0.8 0.0 copy-start.11
  0.8 0.0 copy-start.12
  0.8 0.0 copy-start.13
  0.8 0.0 copy-start.14
  0.8 0.0 copy-start.15
  0.8 0.0 copy-start.16
  0.8 0.0 copy-start.17
  0.9 0.0 copy-start.18
  0.9 0.0 copy-start.19
  0.9 0.0 copy-start.20
  0.9 54.6 %step.1 = (f32[2,3,8,8,128]{4,3,2,1,0:T(8,128)S(1)}, f32[3,64,256]{2,1,0:T(8,128)S(1)}, f32[7,50,200]{2,1,0:T(8,128)S(1)}, f32[7,128,256]{2,1,0:T(8,128)S(1)}, f...) custom-call(f32[3,64,256]{2,1,0:T(8,128)} %refs_7_.3, s32[8,8]{1,0:T(8,128)} %refs_1_.1, ...), custom_call_target="tpu_custom_call" | custom-call | tf_op jit(solution)/shard_map/step/pallas_call | solution.py:1215
  55.5 0.0 copy-done
  55.5 0.0 copy-done.1
  55.6 0.0 copy-done.2
  55.6 0.0 copy-done.3
  55.6 0.0 copy-done.4
  55.6 0.0 copy-done.5
  55.6 0.0 copy-done.6
  55.6 0.0 copy-done.7
  55.6 0.0 copy-done.8
  55.6 0.0 copy-done.9
  55.6 0.0 copy-done.10
  55.6 0.0 copy-done.11
  55.7 0.0 copy-done.12
  55.7 0.0 copy-done.13
  55.7 0.0 copy-done.14
  55.7 0.0 copy-done.15
  55.7 0.0 copy-done.16
  55.7 0.0 copy-done.17
  55.7 0.0 copy-done.18
  55.7 0.0 copy-done.19
  55.7 0.0 copy-done.20
  55.8 2.2 %update.1 = (f32[3,64,256]{2,1,0:T(8,128)}, f32[3,64,256]{2,1,0:T(8,128)}, f32[7,50,200]{2,1,0:T(8,128)}, f32[7,50,200]{2,1,0:T(8,128)}, f32[23,2,256]{2,1,0:T(2...) custom-call(f32[2,3,8,8,128]{4,3,2,1,0:T(8,128)S(1)} %get-tuple-elem, ...), custom_call_target="tpu_custom_call" | custom-call | tf_op jit(solution)/shard_map/update/pallas_call | solution.py:1236
Async XLA Ops:
  0.7 54.9 %copy-start = (f32[7,50,200]{2,1,0:T(8,128)S(1)}, f32[7,50,200]{2,1,0:T(8,128)}, u32[]{:S(2)}) copy-start(f32[7,50,200]{2,1,0:T(8,128)} %refs_8_.1) | copy-start | bytes 840004
  0.7 54.9 %copy-start.1 = (f32[7,50,200]{2,1,0:T(8,128)S(1)}, f32[7,50,200]{2,1,0:T(8,128)}, u32[]{:S(2)}) copy-start(f32[7,50,200]{2,1,0:T(8,128)} %refs_9_.1) | copy-start | bytes 840004
  0.7 54.9 %copy-start.2 = (f32[7,200,36]{1,2,0:T(8,128)S(1)}, f32[7,200,36]{1,2,0:T(8,128)}, u32[]{:S(2)}) copy-start(f32[7,200,36]{1,2,0:T(8,128)} %param.60) | copy-start | bytes 604804
  0.7 54.9 %copy-start.3 = (f32[3,64,256]{2,1,0:T(8,128)S(1)}, f32[3,64,256]{2,1,0:T(8,128)}, u32[]{:S(2)}) copy-start(f32[3,64,256]{2,1,0:T(8,128)} %refs_7_.3) | copy-start | bytes 589828
  0.7 54.9 %copy-start.4 = (f32[7,23,200]{2,1,0:T(8,128)S(1)}, f32[7,23,200]{2,1,0:T(8,128)}, u32[]{:S(2)}) copy-start(f32[7,23,200]{2,1,0:T(8,128)} %refs_16_.3) | copy-start | bytes 386404
  0.7 54.9 %copy-start.5 = (f32[7,200,36]{1,2,0:T(8,128)S(1)}, f32[7,200,36]{1,2,0:T(8,128)}, u32[]{:S(2)}) copy-start(f32[7,200,36]{1,2,0:T(8,128)} %param.61) | copy-start | bytes 604804
  0.7 54.9 %copy-start.6 = (f32[7,200,36]{1,2,0:T(8,128)S(1)}, f32[7,200,36]{1,2,0:T(8,128)}, u32[]{:S(2)}) copy-start(f32[7,200,36]{1,2,0:T(8,128)} %param.62) | copy-start | bytes 604804
  0.7 54.9 %copy-start.7 = (f32[2,23,256]{2,0,1:T(2,128)S(1)}, f32[2,23,256]{2,0,1:T(2,128)}, u32[]{:S(2)}) copy-start(f32[2,23,256]{2,0,1:T(2,128)} %param.45) | copy-start | bytes 141316
  0.8 54.9 %copy-start.8 = (f32[7,23,200]{2,1,0:T(8,128)S(1)}, f32[7,23,200]{2,1,0:T(8,128)}, u32[]{:S(2)}) copy-start(f32[7,23,200]{2,1,0:T(8,128)} %refs_17_.3) | copy-start | bytes 386404
  0.8 54.9 %copy-start.9 = (f32[7,23,200]{2,1,0:T(8,128)S(1)}, f32[7,23,200]{2,1,0:T(8,128)}, u32[]{:S(2)}) copy-start(f32[7,23,200]{2,1,0:T(8,128)} %refs_18_.3) | copy-start | bytes 386404
  0.8 54.9 %copy-start.10 = (f32[17,256]{1,0:T(8,128)S(1)}, f32[17,256]{1,0:T(8,128)}, u32[]{:S(2)}) copy-start(f32[17,256]{1,0:T(8,128)} %refs_13_.3) | copy-start | bytes 52228
  0.8 54.9 %copy-start.11 = (f32[4639]{0:T(1024)S(1)}, f32[4639]{0:T(1024)}, u32[]{:S(2)}) copy-start(f32[4639]{0:T(1024)} %refs_25_.1) | copy-start | bytes 55672
  0.8 54.9 %copy-start.12 = (f32[256,12]{0,1:T(8,128)S(1)}, f32[256,12]{0,1:T(8,128)}, u32[]{:S(2)}) copy-start(f32[256,12]{0,1:T(8,128)} %param.57) | copy-start | bytes 36868
  0.8 54.9 %copy-start.13 = (f32[2,23,256]{2,0,1:T(2,128)S(1)}, f32[2,23,256]{2,0,1:T(2,128)}, u32[]{:S(2)}) copy-start(f32[2,23,256]{2,0,1:T(2,128)} %param.46) | copy-start | bytes 141316
  0.8 54.9 %copy-start.14 = (f32[2,23,256]{2,0,1:T(2,128)S(1)}, f32[2,23,256]{2,0,1:T(2,128)}, u32[]{:S(2)}) copy-start(f32[2,23,256]{2,0,1:T(2,128)} %param.47) | copy-start | bytes 141316
  0.8 54.9 %copy-start.15 = (f32[17,256]{1,0:T(8,128)S(1)}, f32[17,256]{1,0:T(8,128)}, u32[]{:S(2)}) copy-start(f32[17,256]{1,0:T(8,128)} %refs_14_.3) | copy-start | bytes 52228
  0.8 54.9 %copy-start.16 = (f32[17,256]{1,0:T(8,128)S(1)}, f32[17,256]{1,0:T(8,128)}, u32[]{:S(2)}) copy-start(f32[17,256]{1,0:T(8,128)} %refs_15_.1) | copy-start | bytes 52228
  0.8 54.9 %copy-start.17 = (f32[4639]{0:T(1024)S(1)}, f32[4639]{0:T(1024)}, u32[]{:S(2)}) copy-start(f32[4639]{0:T(1024)} %refs_26_.1) | copy-start | bytes 55672
  0.9 54.9 %copy-start.18 = (f32[4639]{0:T(1024)S(1)}, f32[4639]{0:T(1024)}, u32[]{:S(2)}) copy-start(f32[4639]{0:T(1024)} %refs_27_.1) | copy-start | bytes 55672
  0.9 54.9 %copy-start.19 = (f32[256,12]{0,1:T(8,128)S(1)}, f32[256,12]{0,1:T(8,128)}, u32[]{:S(2)}) copy-start(f32[256,12]{0,1:T(8,128)} %param.58) | copy-start | bytes 36868
  0.9 54.9 %copy-start.20 = (f32[256,12]{0,1:T(8,128)S(1)}, f32[256,12]{0,1:T(8,128)}, u32[]{:S(2)}) copy-start(f32[256,12]{0,1:T(8,128)} %param.59) | copy-start | bytes 36868

commit v16 on v15

--- a/solution.py
+++ b/solution.py
@@ -71,11 +71,12 @@
     return high, (v - high.astype(F32)).astype(BF16)
 
 
-def product(a, b, dims=NN):
+def product(a, b, dims=NN, cuts=1):
     left = jnp.concatenate([a[0], a[0], a[1]], 1)
     right = jnp.concatenate([b[0], b[1], b[0]], dims[0][1][0])
-    half = left.shape[0] // 2
-    return jnp.concatenate([dot(left[:half], right, dims), dot(left[half:], right, dims)], 0)
+    rows = left.shape[0] // cuts
+    done = [dot(left[at * rows : (at + 1) * rows], right, dims) for at in range(cuts)]
+    return done[0] if cuts == 1 else jnp.concatenate(done, 0)
 
 
 def softplus(v):
@@ -123,22 +124,42 @@
     return lax.broadcasted_iota(jnp.int32, shape, 0)
 
 
+def blend(gram, square):
+    return split(COEF_CUBIC * gram + COEF_QUINTIC * square)
+
+
 def schulz(refs, steps, before=None):
+    cuts = 2 if len(refs) == 1 else 1
+
     @pl.loop(0, steps)
     def _(step):
         if before is not None:
             before(step)
         matrices = [ref[...] for ref in refs]
         parts = [split(matrix) for matrix in matrices]
-        grams = [product(part, part, NT) for part in parts]
+        grams = [product(part, part, NT, cuts) for part in parts]
         halves = [split(gram) for gram in grams]
-        squares = [product(half, half) for half in halves]
-        blends = [
-            split(COEF_CUBIC * gram + COEF_QUINTIC * square) for gram, square in zip(grams, squares)
-        ]
-        moved = [product(blend, part) for blend, part in zip(blends, parts)]
+        squares = [product(half, half, NN, cuts) for half in halves]
+        blends = [blend(gram, square) for gram, square in zip(grams, squares)]
+        moved = [product(mix, part, NN, cuts) for mix, part in zip(blends, parts)]
         for ref, matrix, move in zip(refs, matrices, moved):
             ref[...] = COEF_LINEAR * matrix + move
+
+
+def schulz_rows(refs, windows, held):
+    cuts = 2 if len(refs) == 1 else 1
+    parts = [split(ref[...]) for ref in refs]
+    grams = [product(part, part, NT, cuts) for part in parts]
+    for at, gram in enumerate(grams):
+        held[at] = gram
+    halves = [split(gram) for gram in grams]
+    grams = [held[at, window] for at, window in enumerate(windows)]
+    squares = [product(split(gram), half) for gram, half in zip(grams, halves)]
+    blends = [blend(gram, square) for gram, square in zip(grams, squares)]
+    moved = [product(mix, part) for mix, part in zip(blends, parts)]
+    return [
+        COEF_LINEAR * ref[window, :] + move for ref, window, move in zip(refs, windows, moved)
+    ]
 
 
 def normalise(ref):
@@ -199,7 +220,7 @@
         sac_g, sac_x, dyn_x, dyn_s, small, count, crit_rows,
         wg, lists, asked, dhg, dmg, bk, xs, nz, ys, ahead, w1f, w1t, w1n, w2t, w2h, heads, head_t, head_f,
         rowbuf, wide, headcol, acc_h, acc_w, acc_c, acc_a, acc_m, acc_l, grid_0, grid_1, grid_2, core_0, core_1,
-        core_2, from_0, from_1, from_2, zr_0, zr_1, zr_2, zf_0, zf_1, zf_2, sum_0, sum_1, sum_2, mg, mat, dcols, dacc_h, dacc_w, dacc_o, dacc_m, dacc_b, dacc_l, xt, dmat,
+        core_2, from_0, from_1, from_2, zr_0, zr_1, zr_2, zf_0, zf_1, zf_2, sum_0, sum_1, sum_2, mg, mat, gram, dcols, dacc_h, dacc_w, dacc_o, dacc_m, dacc_b, dacc_l, xt, dmat,
         dpack, drow_x, bias, dhead, dhead_t, *rest,
     ) = refs
     send, recv = rest
@@ -905,6 +926,14 @@
         return rows
 
     mine_rows = pl.ds(pl.multiple_of(z * lay.rows, lay.rows), lay.rows)
+    dyn_window = pl.ds(pl.multiple_of(z * lay.drows // 8 * 8, 8), -(-(lay.drows + 7) // 8) * 8)
+
+    def from_window(value):
+        rows = value[0 : lay.drows, 0:HDYN]
+        for block in range(1, n_blk):
+            begin = block * lay.drows % 8
+            rows = jnp.where(z == block, value[begin : begin + lay.drows, 0:HDYN], rows)
+        return rows
 
     def take_matrix(k):
         tiles_on(k).wait_recv()
@@ -955,15 +984,18 @@
 
     @pl.when(is_dyn)
     def _():
-        schulz([dmat, mat.at[2]], NS_ITERS, sum_end)
-        rows = line_rows(dmat)
+        both = [dmat, mat.at[2]]
+        schulz(both, NS_ITERS - 1, sum_end)
+        window, sac_x[2] = schulz_rows(both, [dyn_window, mine_rows], gram)
+        rows = from_window(window)
         drow_x[...] = rows
         dyn_x[dyn_e] = rows
         give("x", drow_x)
 
     @pl.when(jnp.logical_not(is_dyn))
     def _():
-        schulz([mat.at[2]], NS_ITERS, sum_end)
+        schulz([mat.at[2]], NS_ITERS - 1, sum_end)
+        (sac_x[2],) = schulz_rows([mat.at[2]], [mine_rows], gram)
 
     def sent_early():
         has_sent(wg.at[pl.ds(0, n_blk - 1), :, half_rows], "hidden")
@@ -986,15 +1018,16 @@
 
     def pass_on(step):
         pl.when(step == 2)(functools.partial(hand_on, "pack"))
-        pl.when(step == NS_ITERS - 1)(functools.partial(hand_on, "x"))
 
     sent_early()
     chains[1][4]()
     for k in range(2):
         take_matrix(k)
-    schulz([mat.at[0], mat.at[1]], NS_ITERS, pass_on)
+    both = [mat.at[0], mat.at[1]]
+    schulz(both, NS_ITERS - 1, pass_on)
+    hand_on("x")
+    sac_x[0], sac_x[1] = schulz_rows(both, [mine_rows, mine_rows], gram)
     for k in range(3):
-        sac_x[k] = mat[k, mine_rows, :]
         for half in range(2):
             for piece in range(lay.rows // 8 // lay.mat):
                 chunk = (half * 32 + z * (lay.rows // 8)) // lay.mat + piece
@@ -1193,6 +1226,7 @@
         *[vm(chunk, 8, 128) for chunk in lay.chunks],
         vm(3, 2, lay.half, lay.mat, 8, 128),
         vm(3, HSAC, HSAC),
+        vm(2, HSAC, HSAC),
         vm(HSAC, 8),
         vm(HSAC + 16, HSAC),
         vm(32, HSAC),

time: 58.9 us -> 58.6 us (level)
  no operation moved by 1% of the time
where the time goes in v16:
time: 58.6 us; the launch traced here: 57.9 us
  Pallas kernels  56.7 us (97%)
  between operations  1.18 us (2%)
    pallas_call x1, Pallas kernels, shards(): pl.pallas_call(functools.partial(ordered, lay, len(inputs), len(out_shape...  54.4 us
    pallas_call x1, Pallas kernels, shards(): pl.pallas_call(functools.partial(update_kernel, lay), out_shape=tuple(new...  2.22 us

profile of v16, /device:TPU:0, one launch (start us, length us, event | category | flops | bytes accessed | tf_op | source)
XLA Modules:
  0.0 57.9 jit_solution(12886010407020726113)
XLA Ops:
  0.7 0.0 copy-start
  0.7 0.0 copy-start.1
  0.7 0.0 copy-start.2
  0.7 0.0 copy-start.3
  0.7 0.0 copy-start.4
  0.7 0.0 copy-start.5
  0.7 0.0 copy-start.6
  0.7 0.0 copy-start.7
  0.8 0.0 copy-start.8
  0.8 0.0 copy-start.9
  0.8 0.0 copy-start.10
  0.8 0.0 copy-start.11
  0.8 0.0 copy-start.12
  0.8 0.0 copy-start.13
  0.8 0.0 copy-start.14
  0.8 0.0 copy-start.15
  0.8 0.0 copy-start.16
  0.8 0.0 copy-start.17
  0.9 0.0 copy-start.18
  0.9 0.0 copy-start.19
  0.9 0.0 copy-start.20
  0.9 54.4 %step.1 = (f32[2,3,8,8,128]{4,3,2,1,0:T(8,128)S(1)}, f32[3,64,256]{2,1,0:T(8,128)S(1)}, f32[7,50,200]{2,1,0:T(8,128)S(1)}, f32[7,128,256]{2,1,0:T(8,128)S(1)}, f...) custom-call(f32[3,64,256]{2,1,0:T(8,128)} %refs_7_.3, s32[8,8]{1,0:T(8,128)} %refs_1_.1, ...), custom_call_target="tpu_custom_call" | custom-call | tf_op jit(solution)/shard_map/step/pallas_call | solution.py:1249
  55.3 0.0 copy-done
  55.4 0.0 copy-done.1
  55.4 0.0 copy-done.2
  55.4 0.0 copy-done.3
  55.4 0.0 copy-done.4
  55.4 0.0 copy-done.5
  55.4 0.0 copy-done.6
  55.4 0.0 copy-done.7
  55.4 0.0 copy-done.8
  55.4 0.0 copy-done.9
  55.4 0.0 copy-done.10
  55.5 0.0 copy-done.11
  55.5 0.0 copy-done.12
  55.5 0.0 copy-done.13
  55.5 0.0 copy-done.14
  55.5 0.0 copy-done.15
  55.5 0.0 copy-done.16
  55.5 0.0 copy-done.17
  55.5 0.0 copy-done.18
  55.5 0.0 copy-done.19
  55.5 0.0 copy-done.20
  55.6 2.2 %update.1 = (f32[3,64,256]{2,1,0:T(8,128)}, f32[3,64,256]{2,1,0:T(8,128)}, f32[7,50,200]{2,1,0:T(8,128)}, f32[7,50,200]{2,1,0:T(8,128)}, f32[23,2,256]{2,1,0:T(2...) custom-call(f32[2,3,8,8,128]{4,3,2,1,0:T(8,128)S(1)} %get-tuple-elem, ...), custom_call_target="tpu_custom_call" | custom-call | tf_op jit(solution)/shard_map/update/pallas_call | solution.py:1270
Async XLA Ops:
  0.7 54.7 %copy-start = (f32[7,50,200]{2,1,0:T(8,128)S(1)}, f32[7,50,200]{2,1,0:T(8,128)}, u32[]{:S(2)}) copy-start(f32[7,50,200]{2,1,0:T(8,128)} %refs_8_.1) | copy-start | bytes 840004
  0.7 54.7 %copy-start.1 = (f32[7,50,200]{2,1,0:T(8,128)S(1)}, f32[7,50,200]{2,1,0:T(8,128)}, u32[]{:S(2)}) copy-start(f32[7,50,200]{2,1,0:T(8,128)} %refs_9_.1) | copy-start | bytes 840004
  0.7 54.7 %copy-start.2 = (f32[7,200,36]{1,2,0:T(8,128)S(1)}, f32[7,200,36]{1,2,0:T(8,128)}, u32[]{:S(2)}) copy-start(f32[7,200,36]{1,2,0:T(8,128)} %param.60) | copy-start | bytes 604804
  0.7 54.7 %copy-start.3 = (f32[3,64,256]{2,1,0:T(8,128)S(1)}, f32[3,64,256]{2,1,0:T(8,128)}, u32[]{:S(2)}) copy-start(f32[3,64,256]{2,1,0:T(8,128)} %refs_7_.3) | copy-start | bytes 589828
  0.7 54.7 %copy-start.4 = (f32[7,23,200]{2,1,0:T(8,128)S(1)}, f32[7,23,200]{2,1,0:T(8,128)}, u32[]{:S(2)}) copy-start(f32[7,23,200]{2,1,0:T(8,128)} %refs_16_.3) | copy-start | bytes 386404
  0.7 54.7 %copy-start.5 = (f32[7,200,36]{1,2,0:T(8,128)S(1)}, f32[7,200,36]{1,2,0:T(8,128)}, u32[]{:S(2)}) copy-start(f32[7,200,36]{1,2,0:T(8,128)} %param.61) | copy-start | bytes 604804
  0.7 54.7 %copy-start.6 = (f32[7,200,36]{1,2,0:T(8,128)S(1)}, f32[7,200,36]{1,2,0:T(8,128)}, u32[]{:S(2)}) copy-start(f32[7,200,36]{1,2,0:T(8,128)} %param.62) | copy-start | bytes 604804
  0.7 54.7 %copy-start.7 = (f32[2,23,256]{2,0,1:T(2,128)S(1)}, f32[2,23,256]{2,0,1:T(2,128)}, u32[]{:S(2)}) copy-start(f32[2,23,256]{2,0,1:T(2,128)} %param.45) | copy-start | bytes 141316
  0.8 54.7 %copy-start.8 = (f32[7,23,200]{2,1,0:T(8,128)S(1)}, f32[7,23,200]{2,1,0:T(8,128)}, u32[]{:S(2)}) copy-start(f32[7,23,200]{2,1,0:T(8,128)} %refs_17_.3) | copy-start | bytes 386404
  0.8 54.7 %copy-start.9 = (f32[7,23,200]{2,1,0:T(8,128)S(1)}, f32[7,23,200]{2,1,0:T(8,128)}, u32[]{:S(2)}) copy-start(f32[7,23,200]{2,1,0:T(8,128)} %refs_18_.3) | copy-start | bytes 386404
  0.8 54.7 %copy-start.10 = (f32[17,256]{1,0:T(8,128)S(1)}, f32[17,256]{1,0:T(8,128)}, u32[]{:S(2)}) copy-start(f32[17,256]{1,0:T(8,128)} %refs_13_.3) | copy-start | bytes 52228
  0.8 54.7 %copy-start.11 = (f32[4639]{0:T(1024)S(1)}, f32[4639]{0:T(1024)}, u32[]{:S(2)}) copy-start(f32[4639]{0:T(1024)} %refs_25_.1) | copy-start | bytes 55672
  0.8 54.7 %copy-start.12 = (f32[256,12]{0,1:T(8,128)S(1)}, f32[256,12]{0,1:T(8,128)}, u32[]{:S(2)}) copy-start(f32[256,12]{0,1:T(8,128)} %param.57) | copy-start | bytes 36868
  0.8 54.7 %copy-start.13 = (f32[2,23,256]{2,0,1:T(2,128)S(1)}, f32[2,23,256]{2,0,1:T(2,128)}, u32[]{:S(2)}) copy-start(f32[2,23,256]{2,0,1:T(2,128)} %param.46) | copy-start | bytes 141316
  0.8 54.7 %copy-start.14 = (f32[2,23,256]{2,0,1:T(2,128)S(1)}, f32[2,23,256]{2,0,1:T(2,128)}, u32[]{:S(2)}) copy-start(f32[2,23,256]{2,0,1:T(2,128)} %param.47) | copy-start | bytes 141316
  0.8 54.7 %copy-start.15 = (f32[17,256]{1,0:T(8,128)S(1)}, f32[17,256]{1,0:T(8,128)}, u32[]{:S(2)}) copy-start(f32[17,256]{1,0:T(8,128)} %refs_14_.3) | copy-start | bytes 52228
  0.8 54.7 %copy-start.16 = (f32[17,256]{1,0:T(8,128)S(1)}, f32[17,256]{1,0:T(8,128)}, u32[]{:S(2)}) copy-start(f32[17,256]{1,0:T(8,128)} %refs_15_.1) | copy-start | bytes 52228
  0.8 54.7 %copy-start.17 = (f32[4639]{0:T(1024)S(1)}, f32[4639]{0:T(1024)}, u32[]{:S(2)}) copy-start(f32[4639]{0:T(1024)} %refs_26_.1) | copy-start | bytes 55672
  0.9 54.7 %copy-start.18 = (f32[4639]{0:T(1024)S(1)}, f32[4639]{0:T(1024)}, u32[]{:S(2)}) copy-start(f32[4639]{0:T(1024)} %refs_27_.1) | copy-start | bytes 55672
  0.9 54.7 %copy-start.19 = (f32[256,12]{0,1:T(8,128)S(1)}, f32[256,12]{0,1:T(8,128)}, u32[]{:S(2)}) copy-start(f32[256,12]{0,1:T(8,128)} %param.58) | copy-start | bytes 36868
  0.9 54.7 %copy-start.20 = (f32[256,12]{0,1:T(8,128)S(1)}, f32[256,12]{0,1:T(8,128)}, u32[]{:S(2)}) copy-start(f32[256,12]{0,1:T(8,128)} %param.59) | copy-start | bytes 36868

commit v17 on v16

--- a/solution.py
+++ b/solution.py
@@ -638,24 +638,21 @@
             mg[part, core, like] = whole
 
     def chain(group):
-        def end():
-            for part in (1, 3) if group == 1 else (group,):
-                fold_end(part)
-
         def turn():
             has_come(mg.at[group, 0, pl.ds(0, lay.half - 1)], ("tiles", group))
             tiles_on(group).start()
-            if group == 1:
-                has_come(small.at[pl.ds(0, (lay.half - 1) * lay.sml)], "small")
-                small_on().start()
 
         return [
             lambda: core_sum(group).start(),
             lambda: fold_core(group),
             lambda: fold_plane(group),
-            end,
+            lambda: fold_end(group),
             turn,
         ]
+
+    def small_turn():
+        has_come(small.at[pl.ds(0, (lay.half - 1) * lay.sml)], "small")
+        small_on().start()
 
     chains = [chain(group) for group in range(3)]
     per = DYN_TILE // lay.real
@@ -761,7 +758,9 @@
 
     @pl.loop(0, critic_tiles)
     def _(step):
-        take({critic_tiles - 1: [chains[0][1], chains[2][2]]}, step)
+        slots = {0: [chains[2][2]]}
+        slots.setdefault(critic_tiles - 1, []).append(chains[0][1])
+        take(slots, step)
         where = place_of(step, CRITIC_TILE)
         critic_pass(1, framed(0, IN, where).astype(BF16), where, ys[0:1, where])
 
@@ -826,7 +825,8 @@
 
     in_dyn = {}
     for at, event in (
-        (1, chains[0][2]), (1, chains[1][1]), (2, chains[2][3]), (dyn_tiles - 1, chains[1][2]),
+        (1, chains[0][2]), (1, chains[1][1]), (1, chains[2][3]),
+        (dyn_tiles - 1, chains[1][2]), (dyn_tiles - 1, chains[2][4]),
     ):
         in_dyn.setdefault(min(at, dyn_tiles - 1), []).append(event)
 
@@ -945,7 +945,6 @@
             mat[k, at, half * 128 : (half + 1) * 128] = piece / total
         normalise(mat.at[k])
 
-    chains[2][4]()
     chains[0][3]()
 
     @pl.when(is_dyn)
@@ -975,10 +974,12 @@
         normalise(dmat)
 
     def sum_end(step):
-        @pl.when(step == 3)
+        @pl.when(step == 2)
         def _():
             chains[0][4]()
             chains[1][3]()
+
+        pl.when(step == 3)(functools.partial(fold_end, 3))
 
     take_matrix(2)
 
@@ -986,6 +987,7 @@
     def _():
         both = [dmat, mat.at[2]]
         schulz(both, NS_ITERS - 1, sum_end)
+        chains[1][4]()
         window, sac_x[2] = schulz_rows(both, [dyn_window, mine_rows], gram)
         rows = from_window(window)
         drow_x[...] = rows
@@ -995,6 +997,7 @@
     @pl.when(jnp.logical_not(is_dyn))
     def _():
         schulz([mat.at[2]], NS_ITERS - 1, sum_end)
+        chains[1][4]()
         (sac_x[2],) = schulz_rows([mat.at[2]], [mine_rows], gram)
 
     def sent_early():
@@ -1017,10 +1020,10 @@
             has_sent(line_bytes(part), ("line sum", part))
 
     def pass_on(step):
+        pl.when(step == 1)(small_turn)
         pl.when(step == 2)(functools.partial(hand_on, "pack"))
 
     sent_early()
-    chains[1][4]()
     for k in range(2):
         take_matrix(k)
     both = [mat.at[0], mat.at[1]]

time: 58.6 us -> 59.4 us (1.014)
  Pallas kernels: 56.7 us -> 57.4 us
    pallas_call x1, Pallas kernels: 54.4 us -> 55.2 us  [shards(): pl.pallas_call(functools.partial(ordered, lay, len(inputs), len(out_shape...]
where the time goes in v17:
time: 59.4 us; the launch traced here: 58.7 us
  Pallas kernels  57.4 us (97%)
  between operations  1.18 us (2%)
    pallas_call x1, Pallas kernels, shards(): pl.pallas_call(functools.partial(ordered, lay, len(inputs), len(out_shape...  55.2 us
    pallas_call x1, Pallas kernels, shards(): pl.pallas_call(functools.partial(update_kernel, lay), out_shape=tuple(new...  2.22 us

profile of v17, /device:TPU:0, one launch (start us, length us, event | category | flops | bytes accessed | tf_op | source)
XLA Modules:
  0.0 58.7 jit_solution(9112921407975805437)
XLA Ops:
  0.7 0.0 copy-start
  0.7 0.0 copy-start.1
  0.7 0.0 copy-start.2
  0.7 0.0 copy-start.3
  0.7 0.0 copy-start.4
  0.7 0.0 copy-start.5
  0.7 0.0 copy-start.6
  0.7 0.0 copy-start.7
  0.8 0.0 copy-start.8
  0.8 0.0 copy-start.9
  0.8 0.0 copy-start.10
  0.8 0.0 copy-start.11
  0.8 0.0 copy-start.12
  0.8 0.0 copy-start.13
  0.8 0.0 copy-start.14
  0.8 0.0 copy-start.15
  0.8 0.0 copy-start.16
  0.8 0.0 copy-start.17
  0.9 0.0 copy-start.18
  0.9 0.0 copy-start.19
  0.9 0.0 copy-start.20
  0.9 55.2 %step.1 = (f32[2,3,8,8,128]{4,3,2,1,0:T(8,128)S(1)}, f32[3,64,256]{2,1,0:T(8,128)S(1)}, f32[7,50,200]{2,1,0:T(8,128)S(1)}, f32[7,128,256]{2,1,0:T(8,128)S(1)}, f...) custom-call(f32[3,64,256]{2,1,0:T(8,128)} %refs_7_.3, s32[8,8]{1,0:T(8,128)} %refs_1_.1, ...), custom_call_target="tpu_custom_call" | custom-call | tf_op jit(solution)/shard_map/step/pallas_call | solution.py:1252
  56.1 0.0 copy-done
  56.1 0.0 copy-done.1
  56.1 0.0 copy-done.2
  56.1 0.0 copy-done.3
  56.1 0.0 copy-done.4
  56.1 0.0 copy-done.5
  56.1 0.0 copy-done.6
  56.1 0.0 copy-done.7
  56.2 0.0 copy-done.8
  56.2 0.0 copy-done.9
  56.2 0.0 copy-done.10
  56.2 0.0 copy-done.11
  56.2 0.0 copy-done.12
  56.2 0.0 copy-done.13
  56.2 0.0 copy-done.14
  56.2 0.0 copy-done.15
  56.2 0.0 copy-done.16
  56.2 0.0 copy-done.17
  56.3 0.0 copy-done.18
  56.3 0.0 copy-done.19
  56.3 0.0 copy-done.20
  56.3 2.2 %update.1 = (f32[3,64,256]{2,1,0:T(8,128)}, f32[3,64,256]{2,1,0:T(8,128)}, f32[7,50,200]{2,1,0:T(8,128)}, f32[7,50,200]{2,1,0:T(8,128)}, f32[23,2,256]{2,1,0:T(2...) custom-call(f32[2,3,8,8,128]{4,3,2,1,0:T(8,128)S(1)} %get-tuple-elem, ...), custom_call_target="tpu_custom_call" | custom-call | tf_op jit(solution)/shard_map/update/pallas_call | solution.py:1273
Async XLA Ops:
  0.7 55.4 %copy-start = (f32[7,50,200]{2,1,0:T(8,128)S(1)}, f32[7,50,200]{2,1,0:T(8,128)}, u32[]{:S(2)}) copy-start(f32[7,50,200]{2,1,0:T(8,128)} %refs_8_.1) | copy-start | bytes 840004
  0.7 55.4 %copy-start.1 = (f32[7,50,200]{2,1,0:T(8,128)S(1)}, f32[7,50,200]{2,1,0:T(8,128)}, u32[]{:S(2)}) copy-start(f32[7,50,200]{2,1,0:T(8,128)} %refs_9_.1) | copy-start | bytes 840004
  0.7 55.4 %copy-start.2 = (f32[7,200,36]{1,2,0:T(8,128)S(1)}, f32[7,200,36]{1,2,0:T(8,128)}, u32[]{:S(2)}) copy-start(f32[7,200,36]{1,2,0:T(8,128)} %param.60) | copy-start | bytes 604804
  0.7 55.4 %copy-start.3 = (f32[3,64,256]{2,1,0:T(8,128)S(1)}, f32[3,64,256]{2,1,0:T(8,128)}, u32[]{:S(2)}) copy-start(f32[3,64,256]{2,1,0:T(8,128)} %refs_7_.3) | copy-start | bytes 589828
  0.7 55.4 %copy-start.4 = (f32[7,23,200]{2,1,0:T(8,128)S(1)}, f32[7,23,200]{2,1,0:T(8,128)}, u32[]{:S(2)}) copy-start(f32[7,23,200]{2,1,0:T(8,128)} %refs_16_.3) | copy-start | bytes 386404
  0.7 55.4 %copy-start.5 = (f32[7,200,36]{1,2,0:T(8,128)S(1)}, f32[7,200,36]{1,2,0:T(8,128)}, u32[]{:S(2)}) copy-start(f32[7,200,36]{1,2,0:T(8,128)} %param.61) | copy-start | bytes 604804
  0.7 55.4 %copy-start.6 = (f32[7,200,36]{1,2,0:T(8,128)S(1)}, f32[7,200,36]{1,2,0:T(8,128)}, u32[]{:S(2)}) copy-start(f32[7,200,36]{1,2,0:T(8,128)} %param.62) | copy-start | bytes 604804
  0.7 55.4 %copy-start.7 = (f32[2,23,256]{2,0,1:T(2,128)S(1)}, f32[2,23,256]{2,0,1:T(2,128)}, u32[]{:S(2)}) copy-start(f32[2,23,256]{2,0,1:T(2,128)} %param.45) | copy-start | bytes 141316
  0.8 55.4 %copy-start.8 = (f32[7,23,200]{2,1,0:T(8,128)S(1)}, f32[7,23,200]{2,1,0:T(8,128)}, u32[]{:S(2)}) copy-start(f32[7,23,200]{2,1,0:T(8,128)} %refs_17_.3) | copy-start | bytes 386404
  0.8 55.4 %copy-start.9 = (f32[7,23,200]{2,1,0:T(8,128)S(1)}, f32[7,23,200]{2,1,0:T(8,128)}, u32[]{:S(2)}) copy-start(f32[7,23,200]{2,1,0:T(8,128)} %refs_18_.3) | copy-start | bytes 386404
  0.8 55.4 %copy-start.10 = (f32[17,256]{1,0:T(8,128)S(1)}, f32[17,256]{1,0:T(8,128)}, u32[]{:S(2)}) copy-start(f32[17,256]{1,0:T(8,128)} %refs_13_.3) | copy-start | bytes 52228
  0.8 55.4 %copy-start.11 = (f32[4639]{0:T(1024)S(1)}, f32[4639]{0:T(1024)}, u32[]{:S(2)}) copy-start(f32[4639]{0:T(1024)} %refs_25_.1) | copy-start | bytes 55672
  0.8 55.4 %copy-start.12 = (f32[256,12]{0,1:T(8,128)S(1)}, f32[256,12]{0,1:T(8,128)}, u32[]{:S(2)}) copy-start(f32[256,12]{0,1:T(8,128)} %param.57) | copy-start | bytes 36868
  0.8 55.4 %copy-start.13 = (f32[2,23,256]{2,0,1:T(2,128)S(1)}, f32[2,23,256]{2,0,1:T(2,128)}, u32[]{:S(2)}) copy-start(f32[2,23,256]{2,0,1:T(2,128)} %param.46) | copy-start | bytes 141316
  0.8 55.4 %copy-start.14 = (f32[2,23,256]{2,0,1:T(2,128)S(1)}, f32[2,23,256]{2,0,1:T(2,128)}, u32[]{:S(2)}) copy-start(f32[2,23,256]{2,0,1:T(2,128)} %param.47) | copy-start | bytes 141316
  0.8 55.4 %copy-start.15 = (f32[17,256]{1,0:T(8,128)S(1)}, f32[17,256]{1,0:T(8,128)}, u32[]{:S(2)}) copy-start(f32[17,256]{1,0:T(8,128)} %refs_14_.3) | copy-start | bytes 52228
  0.8 55.4 %copy-start.16 = (f32[17,256]{1,0:T(8,128)S(1)}, f32[17,256]{1,0:T(8,128)}, u32[]{:S(2)}) copy-start(f32[17,256]{1,0:T(8,128)} %refs_15_.1) | copy-start | bytes 52228
  0.8 55.4 %copy-start.17 = (f32[4639]{0:T(1024)S(1)}, f32[4639]{0:T(1024)}, u32[]{:S(2)}) copy-start(f32[4639]{0:T(1024)} %refs_26_.1) | copy-start | bytes 55672
  0.9 55.4 %copy-start.18 = (f32[4639]{0:T(1024)S(1)}, f32[4639]{0:T(1024)}, u32[]{:S(2)}) copy-start(f32[4639]{0:T(1024)} %refs_27_.1) | copy-start | bytes 55672
  0.9 55.4 %copy-start.19 = (f32[256,12]{0,1:T(8,128)S(1)}, f32[256,12]{0,1:T(8,128)}, u32[]{:S(2)}) copy-start(f32[256,12]{0,1:T(8,128)} %param.58) | copy-start | bytes 36868
  0.9 55.4 %copy-start.20 = (f32[256,12]{0,1:T(8,128)S(1)}, f32[256,12]{0,1:T(8,128)}, u32[]{:S(2)}) copy-start(f32[256,12]{0,1:T(8,128)} %param.59) | copy-start | bytes 36868

commit v18 on v16

--- a/solution.py
+++ b/solution.py
@@ -23,7 +23,7 @@
 CRITIC_TILE = 640
 ACTOR_TILE = 640
 DYN_TILE = 512
-ROWS = 32
+ROWS = 16
 
 DISCOUNT = 0.99
 TARGET_ENTROPY = -6.0

time: 58.6 us -> 58.6 us (level)
  no operation moved by 1% of the time
where the time goes in v18:
time: 58.6 us; the launch traced here: 57.9 us
  Pallas kernels  56.7 us (97%)
  between operations  1.18 us (2%)
    pallas_call x1, Pallas kernels, shards(): pl.pallas_call(functools.partial(ordered, lay, len(inputs), len(out_shape...  54.4 us
    pallas_call x1, Pallas kernels, shards(): pl.pallas_call(functools.partial(update_kernel, lay), out_shape=tuple(new...  2.22 us

profile of v18, /device:TPU:0, one launch (start us, length us, event | category | flops | bytes accessed | tf_op | source)
XLA Modules:
  0.0 57.9 jit_solution(12886010407020726113)
XLA Ops:
  0.7 0.0 copy-start
  0.7 0.0 copy-start.1
  0.7 0.0 copy-start.2
  0.7 0.0 copy-start.3
  0.7 0.0 copy-start.4
  0.7 0.0 copy-start.5
  0.7 0.0 copy-start.6
  0.7 0.0 copy-start.7
  0.8 0.0 copy-start.8
  0.8 0.0 copy-start.9
  0.8 0.0 copy-start.10
  0.8 0.0 copy-start.11
  0.8 0.0 copy-start.12
  0.8 0.0 copy-start.13
  0.8 0.0 copy-start.14
  0.8 0.0 copy-start.15
  0.8 0.0 copy-start.16
  0.8 0.0 copy-start.17
  0.9 0.0 copy-start.18
  0.9 0.0 copy-start.19
  0.9 0.0 copy-start.20
  0.9 54.4 %step.1 = (f32[2,3,8,8,128]{4,3,2,1,0:T(8,128)S(1)}, f32[3,64,256]{2,1,0:T(8,128)S(1)}, f32[7,50,200]{2,1,0:T(8,128)S(1)}, f32[7,128,256]{2,1,0:T(8,128)S(1)}, f...) custom-call(f32[3,64,256]{2,1,0:T(8,128)} %refs_7_.3, s32[8,8]{1,0:T(8,128)} %refs_1_.1, ...), custom_call_target="tpu_custom_call" | custom-call | tf_op jit(solution)/shard_map/step/pallas_call | solution.py:1249
  55.3 0.0 copy-done
  55.4 0.0 copy-done.1
  55.4 0.0 copy-done.2
  55.4 0.0 copy-done.3
  55.4 0.0 copy-done.4
  55.4 0.0 copy-done.5
  55.4 0.0 copy-done.6
  55.4 0.0 copy-done.7
  55.4 0.0 copy-done.8
  55.4 0.0 copy-done.9
  55.4 0.0 copy-done.10
  55.5 0.0 copy-done.11
  55.5 0.0 copy-done.12
  55.5 0.0 copy-done.13
  55.5 0.0 copy-done.14
  55.5 0.0 copy-done.15
  55.5 0.0 copy-done.16
  55.5 0.0 copy-done.17
  55.5 0.0 copy-done.18
  55.5 0.0 copy-done.19
  55.5 0.0 copy-done.20
  55.6 2.2 %update.1 = (f32[3,64,256]{2,1,0:T(8,128)}, f32[3,64,256]{2,1,0:T(8,128)}, f32[7,50,200]{2,1,0:T(8,128)}, f32[7,50,200]{2,1,0:T(8,128)}, f32[23,2,256]{2,1,0:T(2...) custom-call(f32[2,3,8,8,128]{4,3,2,1,0:T(8,128)S(1)} %get-tuple-elem, ...), custom_call_target="tpu_custom_call" | custom-call | tf_op jit(solution)/shard_map/update/pallas_call | solution.py:1270
Async XLA Ops:
  0.7 54.7 %copy-start = (f32[7,50,200]{2,1,0:T(8,128)S(1)}, f32[7,50,200]{2,1,0:T(8,128)}, u32[]{:S(2)}) copy-start(f32[7,50,200]{2,1,0:T(8,128)} %refs_8_.1) | copy-start | bytes 840004
  0.7 54.7 %copy-start.1 = (f32[7,50,200]{2,1,0:T(8,128)S(1)}, f32[7,50,200]{2,1,0:T(8,128)}, u32[]{:S(2)}) copy-start(f32[7,50,200]{2,1,0:T(8,128)} %refs_9_.1) | copy-start | bytes 840004
  0.7 54.7 %copy-start.2 = (f32[7,200,36]{1,2,0:T(8,128)S(1)}, f32[7,200,36]{1,2,0:T(8,128)}, u32[]{:S(2)}) copy-start(f32[7,200,36]{1,2,0:T(8,128)} %param.60) | copy-start | bytes 604804
  0.7 54.7 %copy-start.3 = (f32[3,64,256]{2,1,0:T(8,128)S(1)}, f32[3,64,256]{2,1,0:T(8,128)}, u32[]{:S(2)}) copy-start(f32[3,64,256]{2,1,0:T(8,128)} %refs_7_.3) | copy-start | bytes 589828
  0.7 54.7 %copy-start.4 = (f32[7,23,200]{2,1,0:T(8,128)S(1)}, f32[7,23,200]{2,1,0:T(8,128)}, u32[]{:S(2)}) copy-start(f32[7,23,200]{2,1,0:T(8,128)} %refs_16_.3) | copy-start | bytes 386404
  0.7 54.7 %copy-start.5 = (f32[7,200,36]{1,2,0:T(8,128)S(1)}, f32[7,200,36]{1,2,0:T(8,128)}, u32[]{:S(2)}) copy-start(f32[7,200,36]{1,2,0:T(8,128)} %param.61) | copy-start | bytes 604804
  0.7 54.7 %copy-start.6 = (f32[7,200,36]{1,2,0:T(8,128)S(1)}, f32[7,200,36]{1,2,0:T(8,128)}, u32[]{:S(2)}) copy-start(f32[7,200,36]{1,2,0:T(8,128)} %param.62) | copy-start | bytes 604804
  0.7 54.7 %copy-start.7 = (f32[2,23,256]{2,0,1:T(2,128)S(1)}, f32[2,23,256]{2,0,1:T(2,128)}, u32[]{:S(2)}) copy-start(f32[2,23,256]{2,0,1:T(2,128)} %param.45) | copy-start | bytes 141316
  0.8 54.7 %copy-start.8 = (f32[7,23,200]{2,1,0:T(8,128)S(1)}, f32[7,23,200]{2,1,0:T(8,128)}, u32[]{:S(2)}) copy-start(f32[7,23,200]{2,1,0:T(8,128)} %refs_17_.3) | copy-start | bytes 386404
  0.8 54.7 %copy-start.9 = (f32[7,23,200]{2,1,0:T(8,128)S(1)}, f32[7,23,200]{2,1,0:T(8,128)}, u32[]{:S(2)}) copy-start(f32[7,23,200]{2,1,0:T(8,128)} %refs_18_.3) | copy-start | bytes 386404
  0.8 54.7 %copy-start.10 = (f32[17,256]{1,0:T(8,128)S(1)}, f32[17,256]{1,0:T(8,128)}, u32[]{:S(2)}) copy-start(f32[17,256]{1,0:T(8,128)} %refs_13_.3) | copy-start | bytes 52228
  0.8 54.7 %copy-start.11 = (f32[4639]{0:T(1024)S(1)}, f32[4639]{0:T(1024)}, u32[]{:S(2)}) copy-start(f32[4639]{0:T(1024)} %refs_25_.1) | copy-start | bytes 55672
  0.8 54.7 %copy-start.12 = (f32[256,12]{0,1:T(8,128)S(1)}, f32[256,12]{0,1:T(8,128)}, u32[]{:S(2)}) copy-start(f32[256,12]{0,1:T(8,128)} %param.57) | copy-start | bytes 36868
  0.8 54.7 %copy-start.13 = (f32[2,23,256]{2,0,1:T(2,128)S(1)}, f32[2,23,256]{2,0,1:T(2,128)}, u32[]{:S(2)}) copy-start(f32[2,23,256]{2,0,1:T(2,128)} %param.46) | copy-start | bytes 141316
  0.8 54.7 %copy-start.14 = (f32[2,23,256]{2,0,1:T(2,128)S(1)}, f32[2,23,256]{2,0,1:T(2,128)}, u32[]{:S(2)}) copy-start(f32[2,23,256]{2,0,1:T(2,128)} %param.47) | copy-start | bytes 141316
  0.8 54.7 %copy-start.15 = (f32[17,256]{1,0:T(8,128)S(1)}, f32[17,256]{1,0:T(8,128)}, u32[]{:S(2)}) copy-start(f32[17,256]{1,0:T(8,128)} %refs_14_.3) | copy-start | bytes 52228
  0.8 54.7 %copy-start.16 = (f32[17,256]{1,0:T(8,128)S(1)}, f32[17,256]{1,0:T(8,128)}, u32[]{:S(2)}) copy-start(f32[17,256]{1,0:T(8,128)} %refs_15_.1) | copy-start | bytes 52228
  0.8 54.7 %copy-start.17 = (f32[4639]{0:T(1024)S(1)}, f32[4639]{0:T(1024)}, u32[]{:S(2)}) copy-start(f32[4639]{0:T(1024)} %refs_26_.1) | copy-start | bytes 55672
  0.9 54.7 %copy-start.18 = (f32[4639]{0:T(1024)S(1)}, f32[4639]{0:T(1024)}, u32[]{:S(2)}) copy-start(f32[4639]{0:T(1024)} %refs_27_.1) | copy-start | bytes 55672
  0.9 54.7 %copy-start.19 = (f32[256,12]{0,1:T(8,128)S(1)}, f32[256,12]{0,1:T(8,128)}, u32[]{:S(2)}) copy-start(f32[256,12]{0,1:T(8,128)} %param.58) | copy-start | bytes 36868
  0.9 54.7 %copy-start.20 = (f32[256,12]{0,1:T(8,128)S(1)}, f32[256,12]{0,1:T(8,128)}, u32[]{:S(2)}) copy-start(f32[256,12]{0,1:T(8,128)} %param.59) | copy-start | bytes 36868

commit v19 on v16

--- a/solution.py
+++ b/solution.py
@@ -21,7 +21,7 @@
 STEP = 10
 CAP = 8
 CRITIC_TILE = 640
-ACTOR_TILE = 640
+ACTOR_TILE = 1280
 DYN_TILE = 512
 ROWS = 32
 

time: 58.6 us -> 57.3 us (0.978)
  Pallas kernels: 56.7 us -> 55.9 us
    pallas_call x1, Pallas kernels: 54.4 us -> 53.7 us  [shards(): pl.pallas_call(functools.partial(ordered, lay, len(inputs), len(out_shape...]
where the time goes in v19:
time: 57.3 us; the launch traced here: 57.2 us
  Pallas kernels  55.9 us (98%)
  between operations  1.18 us (2%)
    pallas_call x1, Pallas kernels, shards(): pl.pallas_call(functools.partial(ordered, lay, len(inputs), len(out_shape...  53.7 us
    pallas_call x1, Pallas kernels, shards(): pl.pallas_call(functools.partial(update_kernel, lay), out_shape=tuple(new...  2.22 us

profile of v19, /device:TPU:0, one launch (start us, length us, event | category | flops | bytes accessed | tf_op | source)
XLA Modules:
  0.0 57.2 jit_solution(9565702285329174623)
XLA Ops:
  0.7 0.0 copy-start
  0.7 0.0 copy-start.1
  0.7 0.0 copy-start.2
  0.7 0.0 copy-start.3
  0.7 0.0 copy-start.4
  0.7 0.0 copy-start.5
  0.7 0.0 copy-start.6
  0.7 0.0 copy-start.7
  0.8 0.0 copy-start.8
  0.8 0.0 copy-start.9
  0.8 0.0 copy-start.10
  0.8 0.0 copy-start.11
  0.8 0.0 copy-start.12
  0.8 0.0 copy-start.13
  0.8 0.0 copy-start.14
  0.8 0.0 copy-start.15
  0.8 0.0 copy-start.16
  0.8 0.0 copy-start.17
  0.9 0.0 copy-start.18
  0.9 0.0 copy-start.19
  0.9 0.0 copy-start.20
  0.9 53.7 %step.1 = (f32[2,3,8,8,128]{4,3,2,1,0:T(8,128)S(1)}, f32[3,64,256]{2,1,0:T(8,128)S(1)}, f32[7,50,200]{2,1,0:T(8,128)S(1)}, f32[7,128,256]{2,1,0:T(8,128)S(1)}, f...) custom-call(f32[3,64,256]{2,1,0:T(8,128)} %refs_7_.3, s32[8,8]{1,0:T(8,128)} %refs_1_.1, ...), custom_call_target="tpu_custom_call" | custom-call | tf_op jit(solution)/shard_map/step/pallas_call | solution.py:1249
  54.6 0.0 copy-done
  54.6 0.0 copy-done.1
  54.6 0.0 copy-done.2
  54.6 0.0 copy-done.3
  54.6 0.0 copy-done.4
  54.6 0.0 copy-done.5
  54.7 0.0 copy-done.6
  54.7 0.0 copy-done.7
  54.7 0.0 copy-done.8
  54.7 0.0 copy-done.9
  54.7 0.0 copy-done.10
  54.7 0.0 copy-done.11
  54.7 0.0 copy-done.12
  54.7 0.0 copy-done.13
  54.7 0.0 copy-done.14
  54.7 0.0 copy-done.15
  54.8 0.0 copy-done.16
  54.8 0.0 copy-done.17
  54.8 0.0 copy-done.18
  54.8 0.0 copy-done.19
  54.8 0.0 copy-done.20
  54.8 2.2 %update.1 = (f32[3,64,256]{2,1,0:T(8,128)}, f32[3,64,256]{2,1,0:T(8,128)}, f32[7,50,200]{2,1,0:T(8,128)}, f32[7,50,200]{2,1,0:T(8,128)}, f32[23,2,256]{2,1,0:T(2...) custom-call(f32[2,3,8,8,128]{4,3,2,1,0:T(8,128)S(1)} %get-tuple-elem, ...), custom_call_target="tpu_custom_call" | custom-call | tf_op jit(solution)/shard_map/update/pallas_call | solution.py:1270
Async XLA Ops:
  0.7 53.9 %copy-start = (f32[7,50,200]{2,1,0:T(8,128)S(1)}, f32[7,50,200]{2,1,0:T(8,128)}, u32[]{:S(2)}) copy-start(f32[7,50,200]{2,1,0:T(8,128)} %refs_8_.1) | copy-start | bytes 840004
  0.7 53.9 %copy-start.1 = (f32[7,50,200]{2,1,0:T(8,128)S(1)}, f32[7,50,200]{2,1,0:T(8,128)}, u32[]{:S(2)}) copy-start(f32[7,50,200]{2,1,0:T(8,128)} %refs_9_.1) | copy-start | bytes 840004
  0.7 53.9 %copy-start.2 = (f32[7,200,36]{1,2,0:T(8,128)S(1)}, f32[7,200,36]{1,2,0:T(8,128)}, u32[]{:S(2)}) copy-start(f32[7,200,36]{1,2,0:T(8,128)} %param.60) | copy-start | bytes 604804
  0.7 53.9 %copy-start.3 = (f32[3,64,256]{2,1,0:T(8,128)S(1)}, f32[3,64,256]{2,1,0:T(8,128)}, u32[]{:S(2)}) copy-start(f32[3,64,256]{2,1,0:T(8,128)} %refs_7_.3) | copy-start | bytes 589828
  0.7 53.9 %copy-start.4 = (f32[7,23,200]{2,1,0:T(8,128)S(1)}, f32[7,23,200]{2,1,0:T(8,128)}, u32[]{:S(2)}) copy-start(f32[7,23,200]{2,1,0:T(8,128)} %refs_16_.3) | copy-start | bytes 386404
  0.7 53.9 %copy-start.5 = (f32[7,200,36]{1,2,0:T(8,128)S(1)}, f32[7,200,36]{1,2,0:T(8,128)}, u32[]{:S(2)}) copy-start(f32[7,200,36]{1,2,0:T(8,128)} %param.61) | copy-start | bytes 604804
  0.7 53.9 %copy-start.6 = (f32[7,200,36]{1,2,0:T(8,128)S(1)}, f32[7,200,36]{1,2,0:T(8,128)}, u32[]{:S(2)}) copy-start(f32[7,200,36]{1,2,0:T(8,128)} %param.62) | copy-start | bytes 604804
  0.7 53.9 %copy-start.7 = (f32[2,23,256]{2,0,1:T(2,128)S(1)}, f32[2,23,256]{2,0,1:T(2,128)}, u32[]{:S(2)}) copy-start(f32[2,23,256]{2,0,1:T(2,128)} %param.45) | copy-start | bytes 141316
  0.8 53.9 %copy-start.8 = (f32[7,23,200]{2,1,0:T(8,128)S(1)}, f32[7,23,200]{2,1,0:T(8,128)}, u32[]{:S(2)}) copy-start(f32[7,23,200]{2,1,0:T(8,128)} %refs_17_.3) | copy-start | bytes 386404
  0.8 53.9 %copy-start.9 = (f32[7,23,200]{2,1,0:T(8,128)S(1)}, f32[7,23,200]{2,1,0:T(8,128)}, u32[]{:S(2)}) copy-start(f32[7,23,200]{2,1,0:T(8,128)} %refs_18_.3) | copy-start | bytes 386404
  0.8 53.9 %copy-start.10 = (f32[17,256]{1,0:T(8,128)S(1)}, f32[17,256]{1,0:T(8,128)}, u32[]{:S(2)}) copy-start(f32[17,256]{1,0:T(8,128)} %refs_13_.3) | copy-start | bytes 52228
  0.8 53.9 %copy-start.11 = (f32[4639]{0:T(1024)S(1)}, f32[4639]{0:T(1024)}, u32[]{:S(2)}) copy-start(f32[4639]{0:T(1024)} %refs_25_.1) | copy-start | bytes 55672
  0.8 53.9 %copy-start.12 = (f32[256,12]{0,1:T(8,128)S(1)}, f32[256,12]{0,1:T(8,128)}, u32[]{:S(2)}) copy-start(f32[256,12]{0,1:T(8,128)} %param.57) | copy-start | bytes 36868
  0.8 53.9 %copy-start.13 = (f32[2,23,256]{2,0,1:T(2,128)S(1)}, f32[2,23,256]{2,0,1:T(2,128)}, u32[]{:S(2)}) copy-start(f32[2,23,256]{2,0,1:T(2,128)} %param.46) | copy-start | bytes 141316
  0.8 53.9 %copy-start.14 = (f32[2,23,256]{2,0,1:T(2,128)S(1)}, f32[2,23,256]{2,0,1:T(2,128)}, u32[]{:S(2)}) copy-start(f32[2,23,256]{2,0,1:T(2,128)} %param.47) | copy-start | bytes 141316
  0.8 53.9 %copy-start.15 = (f32[17,256]{1,0:T(8,128)S(1)}, f32[17,256]{1,0:T(8,128)}, u32[]{:S(2)}) copy-start(f32[17,256]{1,0:T(8,128)} %refs_14_.3) | copy-start | bytes 52228
  0.8 53.9 %copy-start.16 = (f32[17,256]{1,0:T(8,128)S(1)}, f32[17,256]{1,0:T(8,128)}, u32[]{:S(2)}) copy-start(f32[17,256]{1,0:T(8,128)} %refs_15_.1) | copy-start | bytes 52228
  0.8 53.9 %copy-start.17 = (f32[4639]{0:T(1024)S(1)}, f32[4639]{0:T(1024)}, u32[]{:S(2)}) copy-start(f32[4639]{0:T(1024)} %refs_26_.1) | copy-start | bytes 55672
  0.9 53.9 %copy-start.18 = (f32[4639]{0:T(1024)S(1)}, f32[4639]{0:T(1024)}, u32[]{:S(2)}) copy-start(f32[4639]{0:T(1024)} %refs_27_.1) | copy-start | bytes 55672
  0.9 53.9 %copy-start.19 = (f32[256,12]{0,1:T(8,128)S(1)}, f32[256,12]{0,1:T(8,128)}, u32[]{:S(2)}) copy-start(f32[256,12]{0,1:T(8,128)} %param.58) | copy-start | bytes 36868
  0.9 53.9 %copy-start.20 = (f32[256,12]{0,1:T(8,128)S(1)}, f32[256,12]{0,1:T(8,128)}, u32[]{:S(2)}) copy-start(f32[256,12]{0,1:T(8,128)} %param.59) | copy-start | bytes 36868
